TPU v7x, 32 devices: a whole 2x2x4 slice. The times are simulated.
32 devices in a mesh: seq: 8 (over z, x), head: 4 (over y, core).
Axes of the slice: x: 2, y: 2, z: 4, core: 2. Of those that a mesh axis runs over, the one named last changes fastest.
Arguments:
- queries: bfloat16 [2048, 16, 128], P(('seq', 'head')), may hold values from -6 to 6
- key_vectors: bfloat16 [2048, 16, 128], P(('seq', 'head')), may hold values from -6 to 6
- value_vectors: bfloat16 [2048, 32, 128], P(('seq', 'head')), may hold values from -6 to 6
- output_gate: bfloat16 [2048, 32, 128], P(('seq', 'head')), may hold values from -6 to 6
- write_strength: bfloat16 [2048, 32], P(('seq', 'head'))
- norm_gain: bfloat16 [128], replicated, may hold values from 0.099609375 to 1.8984375
- output_weight: bfloat16 [4096, 2048], P('head'), may hold values from -0.09375 to 0.09375
Outputs:
- projected: bfloat16 [2048, 2048], P(('seq', 'head'))
All inputs are finite; a program needn't handle non-finite values.
Results may differ from a plain program's by a relative error of at most 0.017.
Values may be sent and summed in bfloat16 or wider, within the bound.
No kernel may reach another device: no remote copies, remote signals or barrier semaphores. Data moves between devices by JAX's collectives and lax.ppermute only.
A program may use at most 128 MiB of HBM per device.

v0:
```python
import functools

import jax
import jax.numpy as jnp
from jax import lax
from jax.experimental import pallas as pl
from jax.experimental.pallas import tpu as pltpu
from jax.sharding import Mesh, PartitionSpec as P

SPAN = 128
EPSILON = 1e-06
F32 = jnp.float32
BF16 = jnp.bfloat16
ROW_TILE = 16
VMEM = pl.BlockSpec(memory_space=pltpu.VMEM)
SMEM = pl.BlockSpec(memory_space=pltpu.SMEM)
ANY = pl.BlockSpec(memory_space=pl.ANY)
LIGHT = pl.CostEstimate(flops=1, bytes_accessed=1, transcendentals=0)


def dot(left, right):
    return jnp.dot(left, right, preferred_element_type=F32)


def dot_nt(left, right):
    return lax.dot_general(left, right, (((1,), (1,)), ((), ())), preferred_element_type=F32)


def params(megabytes=24):
    return pltpu.CompilerParams(vmem_limit_bytes=megabytes * 2**20)


def turned(values):
    return jnp.transpose(values, (1, 0, 2))


def position():
    return lax.axis_index("sub"), lax.axis_index("head")


def pack_kernel(sub, q_hbm, k_hbm, v_hbm, b_hbm, out_ref, q_ref, k_ref, v_ref, b_ref, done):
    tokens, key_heads, width = q_hbm.shape
    ratio = v_hbm.shape[1] // key_heads
    n_head = key_heads // sub
    copies = [
        pltpu.make_async_copy(source, target, done.at[number])
        for number, (source, target) in enumerate(
            ((b_hbm, b_ref), (k_hbm, k_ref), (q_hbm, q_ref), (v_hbm, v_ref))
        )
    ]
    for copy in copies:
        copy.start()
    heads = [(peer % n_head) * sub + peer // n_head for peer in range(key_heads)]
    copies[0].wait()
    strength = jnp.concatenate([b_ref[...].astype(F32)] * (width // tokens), axis=1)
    strength = jnp.concatenate([strength, jnp.zeros((ROW_TILE, width), F32)], axis=0)
    for peer, head in enumerate(heads):
        tile = strength[head * ratio : head * ratio + ROW_TILE]
        out_ref[peer, (2 + ratio) * tokens :] = tile.astype(BF16)
    copies[1].wait()
    rows = turned(k_ref[...])
    for peer, head in enumerate(heads):
        out_ref[peer, tokens : 2 * tokens] = rows[head]
    copies[2].wait()
    rows = turned(q_ref[...])
    for peer, head in enumerate(heads):
        out_ref[peer, 0:tokens] = rows[head]
    copies[3].wait()
    rows = turned(v_ref[...])
    for peer, head in enumerate(heads):
        for r in range(ratio):
            out_ref[peer, (2 + r) * tokens : (3 + r) * tokens] = rows[head * ratio + r]


def gate_kernel(gate_ref, gain_ref, *refs):
    unused, along_head = position()
    out_refs, gates = refs[:-1], refs[-1]
    gate = gate_ref[...].astype(F32)
    gated = gain_ref[...].astype(F32)[:, None] * (gate / (1.0 + jnp.exp(-gate)))
    gates[...] = turned(gated.astype(BF16))
    for distance, out_ref in enumerate(out_refs):
        heads = out_ref.shape[0]
        out_ref[...] = gates[pl.ds((along_head ^ distance) * heads, heads)]


def block_rows(got_ref, block, per, tokens, part):
    rows = got_ref[pl.ds(block * per, per), part * tokens : (part + 1) * tokens]
    return rows.reshape(per * tokens, rows.shape[-1])


def block_inverse(below):
    size = below[0].shape[0]
    rows = lax.broadcasted_iota(jnp.int32, (size, size), 0)
    cols = lax.broadcasted_iota(jnp.int32, (size, size), 1)
    zero = jnp.zeros((size, size), F32)
    step = 1
    solved = None
    while step < size:
        joins = (rows // (2 * step) == cols // (2 * step)) & (rows // step > cols // step)
        parts = [jnp.where(joins, matrix, zero) for matrix in below]
        if step == 1:
            solved = [
                jnp.where(rows == cols, jnp.ones_like(zero), -part).astype(BF16) for part in parts
            ]
        else:
            inner = [dot(part.astype(BF16), now).astype(BF16) for part, now in zip(parts, solved)]
            solved = [now - dot(now, mid).astype(BF16) for now, mid in zip(solved, inner)]
        step *= 2
    return solved


def factor_kernel(tokens, ratio, n_head, got_ref, *refs):
    state_ref, w_ref, u_ref, trans_ref, prefix_ref = refs[n_head : n_head + 5]
    add_ref = refs[-1]
    width = got_ref.shape[-1]
    per = SPAN // tokens
    blocks = got_ref.shape[0] // per
    rows = lax.broadcasted_iota(jnp.int32, (SPAN, SPAN), 0)
    cols = lax.broadcasted_iota(jnp.int32, (SPAN, SPAN), 1)
    lane = lax.broadcasted_iota(jnp.int32, (1, SPAN), 1)
    first = (2 + ratio) * tokens
    below, held = [], []
    for block in range(blocks):
        key = block_rows(got_ref, block, per, tokens, 1)
        gram = dot_nt(key, key)
        squares = jnp.where(rows == cols, gram, 0.0)
        key_row = lax.rsqrt(jnp.sum(squares, 0, keepdims=True) + EPSILON)
        key_col = lax.rsqrt(jnp.sum(squares, 1, keepdims=True) + EPSILON)
        lower = jnp.where(rows > cols, gram, 0.0) * key_row
        for r in range(ratio):
            strength = jnp.zeros((1, SPAN), F32)
            for place in range(per):
                piece = got_ref[block * per + place, first : first + ROW_TILE].astype(F32)[r : r + 1]
                strength = jnp.where(lane // tokens == place, piece, strength)
            scaled_col = jnp.sum(jnp.where(rows == cols, strength * key_row, 0.0), 1, keepdims=True)
            below.append(lower * scaled_col)
            held.append((block, r, key, key_col, key_row, strength))
    solved = block_inverse(below)
    for now, (block, r, key, key_col, key_row, strength) in zip(solved, held):
        value = block_rows(got_ref, block, per, tokens, 2 + r)
        weighted = now.astype(F32) * key_col * strength
        u_now = dot(weighted.astype(BF16), value)
        w_now = dot((weighted * key_row).astype(BF16), key).astype(BF16)
        both = dot(key.T, jnp.concatenate([w_now, u_now.astype(BF16)], axis=1))
        w_ref[block, r] = w_now
        u_ref[block, r] = u_now
        trans_ref[block, r] = both[:, :width].astype(BF16)
        add_ref[block, r] = both[:, width:]

    states = [jnp.zeros((width, width), F32) for r in range(ratio)]
    for block in range(blocks):
        for r in range(ratio):
            held = states[r].astype(BF16)
            prefix_ref[block, r] = held
            if block == 0:
                states[r] = add_ref[block, r]
            else:
                states[r] = states[r] + add_ref[block, r] - dot(trans_ref[block, r], held)
    for r in range(ratio):
        state_ref[r] = states[r].astype(state_ref.dtype)


def spread_kernel(
    tokens, ratio, got_ref, w_ref, u_ref, trans_ref, prefix_ref, local_ref, reach_ref, total_ref
):
    width = got_ref.shape[-1]
    per = SPAN // tokens
    blocks = got_ref.shape[0] // per
    rows = lax.broadcasted_iota(jnp.int32, (SPAN, SPAN), 0)
    cols = lax.broadcasted_iota(jnp.int32, (SPAN, SPAN), 1)
    wide_rows = lax.broadcasted_iota(jnp.int32, (width, width), 0)
    wide_cols = lax.broadcasted_iota(jnp.int32, (width, width), 1)
    identity = jnp.where(wide_rows == wide_cols, 1.0, 0.0).astype(F32)
    carried = [identity for r in range(ratio)]
    for block in range(blocks):
        query = block_rows(got_ref, block, per, tokens, 0)
        key = block_rows(got_ref, block, per, tokens, 1)
        scores = jnp.where(rows >= cols, dot_nt(query, key), 0.0).astype(BF16)
        query_f = query.astype(F32)
        squares = jnp.sum(query_f * query_f, 1, keepdims=True)
        unit = lax.rsqrt(squares + EPSILON) * width ** (-0.5)
        left = jnp.concatenate([query, scores], axis=1)
        for r in range(ratio):
            held = carried[r].astype(BF16)
            if block == 0:
                carried[r] = identity - trans_ref[block, r].astype(F32)
            else:
                carried[r] = carried[r] - dot(trans_ref[block, r], held)
            starts = jnp.concatenate([prefix_ref[block, r], held], axis=1)
            passed = dot(w_ref[block, r], starts)
            corrected = jnp.concatenate([u_ref[block, r] - passed[:, :width], -passed[:, width:]], axis=1)
            right = jnp.concatenate([starts, corrected.astype(BF16)], axis=0)
            out = dot(left, right) * unit
            local_ref[r, block] = out[:, :width]
            reach_ref[r, block] = out[:, width:].astype(BF16)
    for r in range(ratio):
        total_ref[r] = carried[r]


def join_kernel(state_ref, local_ref, reach_ref, *out_refs):
    ratio, blocks, span, width = local_ref.shape
    pieces, parts = out_refs[0].shape[0], len(out_refs) // 2
    along_sub, along_head = position()
    upper = along_head // (lax.axis_size("head") // 2)
    for number, out_ref in enumerate(out_refs):
        target = along_sub ^ (number % parts)
        for piece in range(pieces):
            block = (target * 2 + (upper ^ (1 - number // parts))) * pieces + piece
            for r in range(ratio):
                core = local_ref[r, block] + dot(reach_ref[r, block], state_ref[r].astype(BF16))
                mean_square = jnp.mean(core * core, 1, keepdims=True)
                out_ref[piece, r] = (core * lax.rsqrt(mean_square + EPSILON)).astype(BF16)


def project_kernel(parts, shares, *refs):
    normed_refs, gate_refs = refs[:parts], refs[parts : parts + shares]
    weight_ref, *send_refs, keep_ref, rows_ref = refs[parts + 2 * shares :]
    pieces, ratio, span, width = normed_refs[0].shape
    tokens = gate_refs[0].shape[1]
    per = span // tokens
    along_sub, along_head = position()
    for distance, normed_ref in enumerate(normed_refs):
        source = along_sub ^ distance
        for apart, gate_ref in enumerate(gate_refs):
            share = (along_head ^ apart) & (shares - 1)
            first = ((1 - apart % 2) * (shares // 2) + share // 2) * tokens
            place = pl.ds(pl.multiple_of(first, tokens), tokens)
            from_rows = pl.ds(pl.multiple_of(share % per * tokens, tokens), tokens)
            for r in range(ratio):
                lanes = pl.ds(pl.multiple_of((source * ratio + r) * width, width), width)
                normed = normed_ref[share // per, r, from_rows].astype(F32)
                gate = gate_ref[source * ratio + r].astype(F32)
                rows_ref[place, lanes] = (normed * gate).astype(BF16)
    out = dot(rows_ref[...], weight_ref[...]).reshape((2,) + keep_ref.shape)
    first = 0
    for send_ref in send_refs:
        columns = send_ref.shape[-1]
        send_ref[...] = out[0, :, :, first : first + columns].astype(BF16)
        first += columns
    keep_ref[...] = out[1]


def sum_kernel(keep_ref, *refs):
    out_ref = refs[-1]
    first = 0
    for number, got_ref in enumerate(refs[:-1]):
        columns = got_ref.shape[-1]
        if first == keep_ref.shape[-1]:
            break
        total = keep_ref[:, :, first : first + columns] + got_ref[...].astype(F32)
        for more_ref in refs[:-1]:
            if more_ref.shape[-1] == keep_ref.shape[-1] and more_ref is not got_ref:
                total = total + more_ref[:, :, first : first + columns].astype(F32)
        out_ref[:, :, first : first + columns] = total.astype(out_ref.dtype)
        first += columns


def per_device(
    outer, sub, n_head, queries, key_vectors, value_vectors, output_gate, write_strength, norm_gain, output_weight
):
    tokens, key_heads, width = queries.shape
    value_heads = value_vectors.shape[1]
    ratio = value_heads // key_heads
    sources = sub * n_head
    shard = tokens * sources
    blocks = shard // SPAN
    shard_tokens = tokens * n_head
    shape = jax.ShapeDtypeStruct

    with jax.named_scope("pack"):
        slab = ((2 + ratio) * tokens + ROW_TILE, width)
        packed = pl.pallas_call(
            functools.partial(pack_kernel, sub),
            out_shape=shape((sources,) + slab, BF16),
            in_specs=[ANY] * 4,
            out_specs=VMEM,
            scratch_shapes=[
                pltpu.VMEM(queries.shape, BF16),
                pltpu.VMEM(key_vectors.shape, BF16),
                pltpu.VMEM(value_vectors.shape, BF16),
                pltpu.VMEM((value_heads, tokens), BF16),
                pltpu.SemaphoreType.DMA((4,)),
            ],
            compiler_params=params(60),
        )(queries, key_vectors, value_vectors, write_strength.T)
    got = lax.all_to_all(packed, ("sub", "head"), split_axis=0, concat_axis=0, tiled=True)

    heads = sub * ratio
    with jax.named_scope("gates"):
        gates = pl.pallas_call(
            gate_kernel,
            out_shape=[shape((heads, tokens, width), BF16)] * n_head,
            in_specs=[VMEM] * 2,
            out_specs=[VMEM] * n_head,
            scratch_shapes=[pltpu.VMEM((value_heads, tokens, width), BF16)],
            compiler_params=params(),
            cost_estimate=LIGHT,
        )(output_gate, norm_gain.reshape(1, width))

    state_type = BF16 if outer == 2 else F32
    square = (blocks, ratio, width, width)
    with jax.named_scope("factors"):
        state, w, u, trans, prefix, *gates = pl.pallas_call(
            functools.partial(factor_kernel, tokens, ratio, n_head),
            out_shape=[
                shape((ratio, width, width), state_type),
                shape((blocks, ratio, SPAN, width), BF16),
                shape((blocks, ratio, SPAN, width), F32),
                shape(square, BF16),
                shape(square, BF16),
            ]
            + [shape((heads, tokens, width), BF16)] * n_head,
            in_specs=[VMEM] + [ANY] * n_head,
            out_specs=[VMEM] * 5 + [ANY] * n_head,
            input_output_aliases={1 + number: 5 + number for number in range(n_head)},
            scratch_shapes=[pltpu.VMEM(square, F32)],
            compiler_params=params(),
            cost_estimate=LIGHT,
        )(got, *gates)

    onward = [(here, here + 1) for here in range(outer - 1)]
    incoming = lax.ppermute(state, "outer", onward)
    for distance in reversed(range(1, n_head)):
        pairs = [(here, here ^ distance) for here in range(n_head)]
        gates[distance] = lax.ppermute(gates[distance], "head", pairs)
    with jax.named_scope("spread"):
        local, reach, total = pl.pallas_call(
            functools.partial(spread_kernel, tokens, ratio),
            out_shape=[
                shape((ratio, blocks, SPAN, width), F32),
                shape((ratio, blocks, SPAN, width), BF16),
                shape((ratio, width, width), F32),
            ],
            in_specs=[VMEM] * 5,
            out_specs=[VMEM] * 3,
            compiler_params=params(),
            cost_estimate=LIGHT,
        )(got, w, u, trans, prefix)
    for hop in range(outer - 2):
        passed = jnp.einsum("hde,hef->hdf", total, incoming, precision=lax.Precision.HIGHEST)
        incoming = lax.ppermute(state + passed, "outer", onward)

    pieces = shard_tokens // SPAN // 2
    columns = output_weight.shape[1]
    quarter = (n_head // 4, tokens, columns)
    by_core = [(here, here ^ 1) for here in range(n_head)]
    half = n_head // 2
    with jax.named_scope("join"):
        normed = pl.pallas_call(
            join_kernel,
            out_shape=[shape((pieces, ratio, SPAN, width), BF16)] * (2 * sub),
            in_specs=[VMEM] * 3,
            out_specs=[VMEM] * (2 * sub),
            compiler_params=params(),
            cost_estimate=LIGHT,
        )(incoming, local, reach)
    for kept in range(2):
        mine = list(normed[kept * sub : (kept + 1) * sub])
        for distance in reversed(range(1, sub)):
            pairs = [(here, here ^ distance) for here in range(sub)]
            mine[distance] = lax.ppermute(mine[distance], "sub", pairs)
        cuts = 1 + kept
        with jax.named_scope("project"):
            *sends, keep = pl.pallas_call(
                functools.partial(project_kernel, sub, half),
                out_shape=[shape(quarter[:-1] + (columns // cuts,), BF16)] * cuts + [shape(quarter, F32)],
                in_specs=[VMEM] * (sub + half) + [ANY] * half + [VMEM],
                out_specs=[VMEM] * (cuts + 1),
                scratch_shapes=[pltpu.VMEM((shard_tokens // 2, heads * width), BF16)],
                compiler_params=params(),
                cost_estimate=LIGHT,
            )(*mine, *gates[half * (1 - kept) :], *gates[: half * (1 - kept)], output_weight)
        arrived = [lax.ppermute(send, "head", by_core) for send in sends]
        last = n_head == 4 and kept == 1
        with jax.named_scope("sum"):
            summed = pl.pallas_call(
                sum_kernel,
                out_shape=shape(quarter, F32 if kept and not last else BF16),
                in_specs=[VMEM] * (1 + cuts + kept),
                out_specs=VMEM,
                compiler_params=params(),
                cost_estimate=LIGHT,
            )(keep, *arrived, *([passed_on] if kept else []))
        if not kept:
            passed_on = lax.ppermute(summed, "head", [(here, here ^ half) for here in range(n_head)])
    bit = 2
    while bit < half:
        mine = (lax.axis_index("head") // bit) % 2
        split = summed.reshape((summed.shape[0] // 2, 2) + summed.shape[1:])
        send = lax.dynamic_index_in_dim(split, 1 - mine, 1, False).astype(BF16)
        keep = lax.dynamic_index_in_dim(split, mine, 1, False)
        summed = keep + lax.ppermute(send, "head", [(here, here ^ bit) for here in range(n_head)]).astype(F32)
        bit *= 2
    return summed[0].astype(BF16)


def solution(mesh):
    n_seq, n_head = mesh.shape["seq"], mesh.shape["head"]

    def run(queries, key_vectors, value_vectors, output_gate, write_strength, norm_gain, output_weight):
        sub = queries.shape[1] // n_head
        outer = n_seq // sub
        split = Mesh(mesh.devices.reshape(outer, sub, n_head), ("outer", "sub", "head"))
        every = ("outer", "sub", "head")
        placed = (
            P(every, None, None),
            P(every, None, None),
            P(every, None, None),
            P(every, None, None),
            P(every, None),
            P(),
            P("head", None),
        )
        return jax.shard_map(
            functools.partial(per_device, outer, sub, n_head),
            mesh=split,
            in_specs=placed,
            out_specs=P(every, None),
            check_vma=False,
        )(queries, key_vectors, value_vectors, output_gate, write_strength, norm_gain, output_weight)

    return run
```

profile of v0, /device:TPU:0, one launch (start us, length us, event | category | flops | bytes accessed | tf_op | source)
XLA Modules:
  0.0 59.5 jit_solution(8409312940568876467)
XLA Ops:
  0.0 2.4 %pack.1 = bf16[16,272,128]{2,1,0:T(8,128)(2,1)} custom-call(bf16[64,16,128]{2,1,0:T(8,128)(2,1)} %q_hbm.1, bf16[64,16,128]{2,1,0:T(8,128)(2,1)} %k_hbm.1, bf16[64,32,128]{2,1,0:T(8,128)(2,1)} %v_hbm.1, bf16[32,64]{1,0:T(8,128)(2,1)} %bitcast.4), custom_call_target="tpu_custom_call" | custom-call | tf_op jit(solution)/shard_map/pack/pallas_call | solution.py:272
  2.5 6.4 %all-to-all-start = ((bf16[16,272,128]{2,1,0:T(8,128)(2,1)}), bf16[16,272,128]{2,1,0:T(8,128)(2,1)S(1)}, u32[]{:S(2)}, u32[]{:S(2)}) async-start(bf16[16,272,128]{2,1,0:T(8,128)(2,1)} %pack.1), calls=%async_computation | async-start | bytes 2228224 | tf_op jit(solution)/shard_map/all_to_all | solution.py:286
  8.9 0.6 gates.1
  9.5 16.3 %all-to-all-done.got_ref = bf16[16,272,128]{2,1,0:T(8,128)(2,1)S(1)} async-done(((bf16[16,272,128]{2,1,0:T(8,128)(2,1)}), bf16[16,272,128]{2,1,0:T(8,128)(2,1)S(1)}, u32[]{:S(2)}, u32[]{:S(2)}) %all-to-all-start) | async-done | bytes 1114144 | tf_op jit(solution)/shard_map/all_to_all | solution.py:286
  25.9 3.8 %factors.1 = (bf16[2,128,128]{2,1,0:T(8,128)(2,1)S(1)}, bf16[8,2,128,128]{3,2,1,0:T(8,128)(2,1)S(1)}, f32[8,2,128,128]{3,2,1,0:T(8,128)S(1)}, bf16[8,2,128,128]{...) custom-call(bf16[16,272,128]{2,1,0:T(8,128)(2,1)S(1)} %all-to-all-do, ...), custom_call_target="tpu_custom_call", output_to_operand_aliasing={{5}: (1, {}), {6}: (2, {}), {7}: (3, {}), {8}: (4, {})} | custom-call | flops 1 | bytes 1 | tf_op jit(solution)/shard_map/factors/pallas_call | solution.py:303
  29.7 0.1 collective-permute-start.4
  29.7 4.5 %collective-permute-start = (bf16[2,128,128]{2,1,0:T(8,128)(2,1)S(1)}, bf16[2,128,128]{2,1,0:T(8,128)(2,1)S(1)}, u32[]{:S(2)}, u32[]{:S(2)}) collective-permute-start(bf16[2,128,128]{2,1,0:T(8,128)(2,1)S(1)} %get-tuple-element.37), channel_id=1, source_target_pairs={{0,16},{1,17},{2,18},{3,19},{4,20},{5,21},{6,22},{7,23},{8,24},{9,... | collective-permute-start | bytes 196616 | tf_op jit(solution)/shard_map/ppermute | solution.py:322
  34.2 0.1 collective-permute-start.5
  34.3 1.5 %collective-permute-start.6 = (bf16[8,64,128]{2,1,0:T(8,128)(2,1)S(1)}, bf16[8,64,128]{2,1,0:T(8,128)(2,1)S(1)}, u32[]{:S(2)}, u32[]{:S(2)}) collective-permute-start(bf16[8,64,128]{2,1,0:T(8,128)(2,1)S(1)} %get-tuple-element.51), channel_id=1, source_target_pairs={{0,3},{1,2},{2,1},{3,0},{4,7},{5,6},{6,5},{7,4},{8,11},{9,10},{10,... | collective-permute-start | bytes 393224 | tf_op jit(solution)/shard_map/ppermute | solution.py:325
  35.9 2.3 %spread.1 = (f32[2,8,128,128]{3,2,1,0:T(8,128)S(1)}, bf16[2,8,128,128]{3,2,1,0:T(8,128)(2,1)S(1)}, f32[2,128,128]{2,1,0:T(8,128)}) custom-call(bf16[16,272,128]{2,1,0:T(8,128)(2,1)S(1)} %all-to-all-done.got_ref, bf16[8,2,128,128]{3,2,1,0:T(8,128)(2,1)S(1)} %get-tuple-element.38.w_ref, f32[8,2,128,128]{3,2,1,0:T(8,128)S(1)} %get-tuple-element.39.u_ref, ...), custom_call_target="tpu_custom_call" | custom-call | flops 1 | bytes 1 | tf_op jit(solution)/shard_map/spread/pallas_call | solution.py:327
  38.1 0.5 join.1
  38.6 0.4 collective-permute-start.9
  39.1 2.0 %collective-permute-start.10 = (bf16[1,2,128,128]{3,2,1,0:T(8,128)(2,1)S(1)}, bf16[1,2,128,128]{3,2,1,0:T(8,128)(2,1)S(1)}, u32[]{:S(2)}, u32[]{:S(2)}) collective-permute-start(bf16[1,2,128,128]{3,2,1,0:T(8,128)(2,1)S(1)} %get-tuple-element.57), channel_id=1, source_target_pairs={{0,8},{4,12},{8,0},{12,4},{1,9},{5,13},{9,1},{13,5},{2,10},{6,14},... | collective-permute-start | bytes 196616 | tf_op jit(solution)/shard_map/ppermute | solution.py:361
  41.1 1.1 %collective-permute-start.11 = (bf16[1,2,128,128]{3,2,1,0:T(8,128)(2,1)S(1)}, bf16[1,2,128,128]{3,2,1,0:T(8,128)(2,1)S(1)}, u32[]{:S(2)}, u32[]{:S(2)}) collective-permute-start(bf16[1,2,128,128]{3,2,1,0:T(8,128)(2,1)S(1)} %get-tuple-element.58), channel_id=1, source_target_pairs={{0,12},{4,8},{8,4},{12,0},{1,13},{5,9},{9,5},{13,1},{2,14},{6,10},... | collective-permute-start | bytes 196616 | tf_op jit(solution)/shard_map/ppermute | solution.py:361
  42.2 1.1 %collective-permute-done.9.refs_1_ = bf16[1,2,128,128]{3,2,1,0:T(8,128)(2,1)S(1)} collective-permute-done((bf16[1,2,128,128]{3,2,1,0:T(8,128)(2,1)S(1)}, bf16[1,2,128,128]{3,2,1,0:T(8,128)(2,1)S(1)}, u32[]{:S(2)}, u32[]{:S(2)}) %collective-permute-start.9) | collective-permute-done | bytes 65568 | tf_op jit(solution)/shard_map/ppermute | solution.py:361
  43.3 0.5 collective-permute-done.10.refs_2_
  43.8 2.4 %collective-permute-done.11.refs_3_ = bf16[1,2,128,128]{3,2,1,0:T(8,128)(2,1)S(1)} collective-permute-done((bf16[1,2,128,128]{3,2,1,0:T(8,128)(2,1)S(1)}, bf16[1,2,128,128]{3,2,1,0:T(8,128)(2,1)S(1)}, u32[]{:S(2)}, u32[]{:S(2)}) %collective-permute-start.11) | collective-permute-done | bytes 65568 | tf_op jit(solution)/shard_map/ppermute | solution.py:361
  46.2 0.8 %project.3 = (bf16[1,64,2048]{2,1,0:T(8,128)(2,1)S(1)}, f32[1,64,2048]{2,1,0:T(8,128)S(1)}) custom-call(bf16[1,2,128,128]{3,2,1,0:T(8,128)(2,1)S(1)} %get-tuple-element.55.refs_0_, bf16[1,2,128,128]{3,2,1,0:T(8,128)(2,1)S(1)} %collective-permute-done.9.refs_1_, bf16[1,2,128,128]{3,2,1,0:T(8,128)(2,1)S(1)} %collective-permute-done.10.refs_2_, ...), custom_call_target="tpu_custom_call" | custom-call | flops 1 | bytes 1 | tf_op jit(solution)/shard_map/project/pallas_call | solution.py:364
  47.0 0.1 collective-permute-start.12
  47.1 1.5 %collective-permute-done.12.refs_0_ = bf16[1,64,2048]{2,1,0:T(8,128)(2,1)S(1)} collective-permute-done((bf16[1,64,2048]{2,1,0:T(8,128)(2,1)S(1)}, bf16[1,64,2048]{2,1,0:T(8,128)(2,1)S(1)}, u32[]{:S(2)}, u32[]{:S(2)}) %collective-permute-start.12) | collective-permute-done | bytes 262176 | tf_op jit(solution)/shard_map/ppermute | solution.py:373
  48.7 0.5 collective-permute-start.13
  49.2 1.1 %collective-permute-start.1 = (bf16[1,2,128,128]{3,2,1,0:T(8,128)(2,1)S(1)}, bf16[1,2,128,128]{3,2,1,0:T(8,128)(2,1)S(1)}, u32[]{:S(2)}, u32[]{:S(2)}) collective-permute-start(bf16[1,2,128,128]{3,2,1,0:T(8,128)(2,1)S(1)} %get-tuple-element.45), channel_id=1, source_target_pairs={{0,4},{4,0},{8,12},{12,8},{1,5},{5,1},{9,13},{13,9},{2,6},{6,2},{1... | collective-permute-start | bytes 196616 | tf_op jit(solution)/shard_map/ppermute | solution.py:361
  50.3 0.9 %collective-permute-start.2 = (bf16[1,2,128,128]{3,2,1,0:T(8,128)(2,1)S(1)}, bf16[1,2,128,128]{3,2,1,0:T(8,128)(2,1)S(1)}, u32[]{:S(2)}, u32[]{:S(2)}) collective-permute-start(bf16[1,2,128,128]{3,2,1,0:T(8,128)(2,1)S(1)} %get-tuple-element.46), channel_id=1, source_target_pairs={{0,8},{4,12},{8,0},{12,4},{1,9},{5,13},{9,1},{13,5},{2,10},{6,14},... | collective-permute-start | bytes 196616 | tf_op jit(solution)/shard_map/ppermute | solution.py:361
  51.2 1.5 %collective-permute-start.3 = (bf16[1,2,128,128]{3,2,1,0:T(8,128)(2,1)S(1)}, bf16[1,2,128,128]{3,2,1,0:T(8,128)(2,1)S(1)}, u32[]{:S(2)}, u32[]{:S(2)}) collective-permute-start(bf16[1,2,128,128]{3,2,1,0:T(8,128)(2,1)S(1)} %get-tuple-element.47), channel_id=1, source_target_pairs={{0,12},{4,8},{8,4},{12,0},{1,13},{5,9},{9,5},{13,1},{2,14},{6,10},... | collective-permute-start | bytes 196616 | tf_op jit(solution)/shard_map/ppermute | solution.py:361
  52.7 0.8 %collective-permute-done.1.refs_1_ = bf16[1,2,128,128]{3,2,1,0:T(8,128)(2,1)S(1)} collective-permute-done((bf16[1,2,128,128]{3,2,1,0:T(8,128)(2,1)S(1)}, bf16[1,2,128,128]{3,2,1,0:T(8,128)(2,1)S(1)}, u32[]{:S(2)}, u32[]{:S(2)}) %collective-permute-start.1) | collective-permute-done | bytes 65568 | tf_op jit(solution)/shard_map/ppermute | solution.py:361
  53.5 1.4 %collective-permute-done.2.refs_2_ = bf16[1,2,128,128]{3,2,1,0:T(8,128)(2,1)S(1)} collective-permute-done((bf16[1,2,128,128]{3,2,1,0:T(8,128)(2,1)S(1)}, bf16[1,2,128,128]{3,2,1,0:T(8,128)(2,1)S(1)}, u32[]{:S(2)}, u32[]{:S(2)}) %collective-permute-start.2) | collective-permute-done | bytes 65568 | tf_op jit(solution)/shard_map/ppermute | solution.py:361
  54.9 1.5 %collective-permute-done.3.refs_3_ = bf16[1,2,128,128]{3,2,1,0:T(8,128)(2,1)S(1)} collective-permute-done((bf16[1,2,128,128]{3,2,1,0:T(8,128)(2,1)S(1)}, bf16[1,2,128,128]{3,2,1,0:T(8,128)(2,1)S(1)}, u32[]{:S(2)}, u32[]{:S(2)}) %collective-permute-start.3) | collective-permute-done | bytes 65568 | tf_op jit(solution)/shard_map/ppermute | solution.py:361
  56.3 0.8 %project.2 = (bf16[1,64,1024]{2,1,0:T(8,128)(2,1)S(1)}, bf16[1,64,1024]{2,1,0:T(8,128)(2,1)S(1)}, f32[1,64,2048]{2,1,0:T(8,128)S(1)}) custom-call(bf16[1,2,128,128]{3,2,1,0:T(8,128)(2,1)S(1)} %get-tuple-element.44.refs_0_, bf16[1,2,128,128]{3,2,1,0:T(8,128)(2,1)S(1)} %collective-permute-done.1.refs_1_, ...), custom_call_target="tpu_custom_call" | custom-call | flops 1 | bytes 1 | tf_op jit(solution)/shard_map/project/pallas_call | solution.py:364
  57.2 0.5 collective-permute-start.8
  57.7 0.8 %collective-permute-done.7.refs_0_ = bf16[1,64,1024]{2,1,0:T(8,128)(2,1)S(1)} collective-permute-done((bf16[1,64,1024]{2,1,0:T(8,128)(2,1)S(1)}, bf16[1,64,1024]{2,1,0:T(8,128)(2,1)S(1)}, u32[]{:S(2)}, u32[]{:S(2)}) %collective-permute-start.7) | collective-permute-done | bytes 131104 | tf_op jit(solution)/shard_map/ppermute | solution.py:373
  58.5 0.2 collective-permute-done.8.refs_1_
  58.7 0.8 %sum.3 = bf16[1,64,2048]{2,1,0:T(8,128)(2,1)} custom-call(f32[1,64,2048]{2,1,0:T(8,128)S(1)} %get-tuple-element.52.keep_ref, bf16[1,64,1024]{2,1,0:T(8,128)(2,1)S(1)} %collective-permute-done.7.refs_0_, bf16[1,64,1024]{2,1,0:T(8,128)(2,1)S(1)} %collective-permute-done.8.refs_1_, bf16[1,64,2048]{2,1,0:T(8,128)(2,1)S(1)} %collective-permute-done.13.refs_2_), custom_call_target="tpu_custom_call" | custom-call | flops 1 | bytes 1 | tf_op jit(solution)/shard_map/sum/pallas_call | solution.py:376
  (13 shorter events, 0.1 us)
Async XLA Ops:
  2.5 6.5 %copy-start.1 = (bf16[64,32,128]{2,1,0:T(8,128)(2,1)S(1)}, bf16[64,32,128]{2,1,0:T(8,128)(2,1)}, u32[]{:S(2)}) copy-start(bf16[64,32,128]{2,1,0:T(8,128)(2,1)} %gate_ref.1) | copy-start | bytes 1572868
  2.5 6.5 %copy-start.2 = (bf16[128]{0:T(256)(128)(2,1)S(1)}, bf16[128]{0:T(256)(128)(2,1)}, u32[]{:S(2)}) copy-start(bf16[128]{0:T(256)(128)(2,1)} %param.12) | copy-start | bytes 772
  2.5 23.4 %all-to-all-start = ((bf16[16,272,128]{2,1,0:T(8,128)(2,1)}), bf16[16,272,128]{2,1,0:T(8,128)(2,1)S(1)}, u32[]{:S(2)}, u32[]{:S(2)}) async-start(bf16[16,272,128]{2,1,0:T(8,128)(2,1)} %pack.1), calls=%async_computation | async-start | bytes 2228224 | tf_op jit(solution)/shard_map/all_to_all | solution.py:286
  29.7 11.4 %collective-permute-start.4 = (bf16[8,64,128]{2,1,0:T(8,128)(2,1)S(1)}, bf16[8,64,128]{2,1,0:T(8,128)(2,1)S(1)}, u32[]{:S(2)}, u32[]{:S(2)}) collective-permute-start(bf16[8,64,128]{2,1,0:T(8,128)(2,1)S(1)} %get-tuple-element.49), channel_id=1, source_target_pairs={{0,1},{1,0},{2,3},{3,2},{4,5},{5,4},{6,7},{7,6},{8,9},{9,8},{10,11... | collective-permute-start | bytes 393224 | tf_op jit(solution)/shard_map/ppermute | solution.py:325
  29.7 8.4 %collective-permute-start = (bf16[2,128,128]{2,1,0:T(8,128)(2,1)S(1)}, bf16[2,128,128]{2,1,0:T(8,128)(2,1)S(1)}, u32[]{:S(2)}, u32[]{:S(2)}) collective-permute-start(bf16[2,128,128]{2,1,0:T(8,128)(2,1)S(1)} %get-tuple-element.37), channel_id=1, source_target_pairs={{0,16},{1,17},{2,18},{3,19},{4,20},{5,21},{6,22},{7,23},{8,24},{9,... | collective-permute-start | bytes 196616 | tf_op jit(solution)/shard_map/ppermute | solution.py:322
  34.2 8.0 %collective-permute-start.5 = (bf16[8,64,128]{2,1,0:T(8,128)(2,1)S(1)}, bf16[8,64,128]{2,1,0:T(8,128)(2,1)S(1)}, u32[]{:S(2)}, u32[]{:S(2)}) collective-permute-start(bf16[8,64,128]{2,1,0:T(8,128)(2,1)S(1)} %get-tuple-element.50), channel_id=1, source_target_pairs={{0,2},{1,3},{2,0},{3,1},{4,6},{5,7},{6,4},{7,5},{8,10},{9,11},{10,... | collective-permute-start | bytes 393224 | tf_op jit(solution)/shard_map/ppermute | solution.py:325
  34.3 7.9 %collective-permute-start.6 = (bf16[8,64,128]{2,1,0:T(8,128)(2,1)S(1)}, bf16[8,64,128]{2,1,0:T(8,128)(2,1)S(1)}, u32[]{:S(2)}, u32[]{:S(2)}) collective-permute-start(bf16[8,64,128]{2,1,0:T(8,128)(2,1)S(1)} %get-tuple-element.51), channel_id=1, source_target_pairs={{0,3},{1,2},{2,1},{3,0},{4,7},{5,6},{6,5},{7,4},{8,11},{9,10},{10,... | collective-permute-start | bytes 393224 | tf_op jit(solution)/shard_map/ppermute | solution.py:325
  35.9 10.4 %copy-start = (bf16[1024,2048]{1,0:T(8,128)(2,1)S(1)}, bf16[1024,2048]{1,0:T(8,128)(2,1)}, u32[]{:S(2)}) copy-start(bf16[1024,2048]{1,0:T(8,128)(2,1)} %refs_8_.3) | copy-start | bytes 12582916
  38.6 4.6 %collective-permute-start.9 = (bf16[1,2,128,128]{3,2,1,0:T(8,128)(2,1)S(1)}, bf16[1,2,128,128]{3,2,1,0:T(8,128)(2,1)S(1)}, u32[]{:S(2)}, u32[]{:S(2)}) collective-permute-start(bf16[1,2,128,128]{3,2,1,0:T(8,128)(2,1)S(1)} %get-tuple-element.56), channel_id=1, source_target_pairs={{0,4},{4,0},{8,12},{12,8},{1,5},{5,1},{9,13},{13,9},{2,6},{6,2},{1... | collective-permute-start | bytes 196616 | tf_op jit(solution)/shard_map/ppermute | solution.py:361
  39.1 4.7 %collective-permute-start.10 = (bf16[1,2,128,128]{3,2,1,0:T(8,128)(2,1)S(1)}, bf16[1,2,128,128]{3,2,1,0:T(8,128)(2,1)S(1)}, u32[]{:S(2)}, u32[]{:S(2)}) collective-permute-start(bf16[1,2,128,128]{3,2,1,0:T(8,128)(2,1)S(1)} %get-tuple-element.57), channel_id=1, source_target_pairs={{0,8},{4,12},{8,0},{12,4},{1,9},{5,13},{9,1},{13,5},{2,10},{6,14},... | collective-permute-start | bytes 196616 | tf_op jit(solution)/shard_map/ppermute | solution.py:361
  41.1 5.2 %collective-permute-start.11 = (bf16[1,2,128,128]{3,2,1,0:T(8,128)(2,1)S(1)}, bf16[1,2,128,128]{3,2,1,0:T(8,128)(2,1)S(1)}, u32[]{:S(2)}, u32[]{:S(2)}) collective-permute-start(bf16[1,2,128,128]{3,2,1,0:T(8,128)(2,1)S(1)} %get-tuple-element.58), channel_id=1, source_target_pairs={{0,12},{4,8},{8,4},{12,0},{1,13},{5,9},{9,5},{13,1},{2,14},{6,10},... | collective-permute-start | bytes 196616 | tf_op jit(solution)/shard_map/ppermute | solution.py:361
  47.0 1.6 %collective-permute-start.12 = (bf16[1,64,2048]{2,1,0:T(8,128)(2,1)S(1)}, bf16[1,64,2048]{2,1,0:T(8,128)(2,1)S(1)}, u32[]{:S(2)}, u32[]{:S(2)}) collective-permute-start(bf16[1,64,2048]{2,1,0:T(8,128)(2,1)S(1)} %get-tuple-element.60), channel_id=1, source_target_pairs={{0,1},{1,0},{2,3},{3,2},{4,5},{5,4},{6,7},{7,6},{8,9},{9,8},{10,11... | collective-permute-start | bytes 786440 | tf_op jit(solution)/shard_map/ppermute | solution.py:373
  48.7 10.1 %collective-permute-start.13 = (bf16[1,64,2048]{2,1,0:T(8,128)(2,1)S(1)}, bf16[1,64,2048]{2,1,0:T(8,128)(2,1)S(1)}, u32[]{:S(2)}, u32[]{:S(2)}) collective-permute-start(bf16[1,64,2048]{2,1,0:T(8,128)(2,1)S(1)} %sum.2), channel_id=1, source_target_pairs={{0,2},{1,3},{2,0},{3,1},{4,6},{5,7},{6,4},{7,5},{8,10},{9,11},{10,... | collective-permute-start | bytes 786440 | tf_op jit(solution)/shard_map/ppermute | solution.py:385
  49.2 4.3 %collective-permute-start.1 = (bf16[1,2,128,128]{3,2,1,0:T(8,128)(2,1)S(1)}, bf16[1,2,128,128]{3,2,1,0:T(8,128)(2,1)S(1)}, u32[]{:S(2)}, u32[]{:S(2)}) collective-permute-start(bf16[1,2,128,128]{3,2,1,0:T(8,128)(2,1)S(1)} %get-tuple-element.45), channel_id=1, source_target_pairs={{0,4},{4,0},{8,12},{12,8},{1,5},{5,1},{9,13},{13,9},{2,6},{6,2},{1... | collective-permute-start | bytes 196616 | tf_op jit(solution)/shard_map/ppermute | solution.py:361
  50.3 4.5 %collective-permute-start.2 = (bf16[1,2,128,128]{3,2,1,0:T(8,128)(2,1)S(1)}, bf16[1,2,128,128]{3,2,1,0:T(8,128)(2,1)S(1)}, u32[]{:S(2)}, u32[]{:S(2)}) collective-permute-start(bf16[1,2,128,128]{3,2,1,0:T(8,128)(2,1)S(1)} %get-tuple-element.46), channel_id=1, source_target_pairs={{0,8},{4,12},{8,0},{12,4},{1,9},{5,13},{9,1},{13,5},{2,10},{6,14},... | collective-permute-start | bytes 196616 | tf_op jit(solution)/shard_map/ppermute | solution.py:361
  51.2 5.2 %collective-permute-start.3 = (bf16[1,2,128,128]{3,2,1,0:T(8,128)(2,1)S(1)}, bf16[1,2,128,128]{3,2,1,0:T(8,128)(2,1)S(1)}, u32[]{:S(2)}, u32[]{:S(2)}) collective-permute-start(bf16[1,2,128,128]{3,2,1,0:T(8,128)(2,1)S(1)} %get-tuple-element.47), channel_id=1, source_target_pairs={{0,12},{4,8},{8,4},{12,0},{1,13},{5,9},{9,5},{13,1},{2,14},{6,10},... | collective-permute-start | bytes 196616 | tf_op jit(solution)/shard_map/ppermute | solution.py:361
  57.1 1.4 %collective-permute-start.7 = (bf16[1,64,1024]{2,1,0:T(8,128)(2,1)S(1)}, bf16[1,64,1024]{2,1,0:T(8,128)(2,1)S(1)}, u32[]{:S(2)}, u32[]{:S(2)}) collective-permute-start(bf16[1,64,1024]{2,1,0:T(8,128)(2,1)S(1)} %get-tuple-element.53), channel_id=1, source_target_pairs={{0,1},{1,0},{2,3},{3,2},{4,5},{5,4},{6,7},{7,6},{8,9},{9,8},{10,11... | collective-permute-start | bytes 393224 | tf_op jit(solution)/shard_map/ppermute | solution.py:373
  57.2 1.5 %collective-permute-start.8 = (bf16[1,64,1024]{2,1,0:T(8,128)(2,1)S(1)}, bf16[1,64,1024]{2,1,0:T(8,128)(2,1)S(1)}, u32[]{:S(2)}, u32[]{:S(2)}) collective-permute-start(bf16[1,64,1024]{2,1,0:T(8,128)(2,1)S(1)} %get-tuple-element.54), channel_id=1, source_target_pairs={{0,1},{1,0},{2,3},{3,2},{4,5},{5,4},{6,7},{7,6},{8,9},{9,8},{10,11... | collective-permute-start | bytes 393224 | tf_op jit(solution)/shard_map/ppermute | solution.py:373
where the time goes:
time: 59.8 us; the launch traced here: 59.5 us
  waiting for transfers between devices  26.5 us (44%)
  starting transfers between devices  20.8 us (35%)
  Pallas kernels  12 us (20%)
    all_to_all x1, waiting for transfers between devices, per_device(): lax.all_to_all(packed, ('sub', 'head'), split_axis=0, concat_axis=0, tile...  16.3 us
    ppermute x6, waiting for transfers between devices, per_device(): mine[distance] = lax.ppermute(mine[distance], 'sub', pairs)  7.65 us
    ppermute x6, starting transfers between devices, per_device(): mine[distance] = lax.ppermute(mine[distance], 'sub', pairs)  7.04 us
    all_to_all x1, starting transfers between devices, per_device(): lax.all_to_all(packed, ('sub', 'head'), split_axis=0, concat_axis=0, tile...  6.43 us
    ppermute x1, starting transfers between devices, per_device(): incoming = lax.ppermute(state, 'outer', onward)  4.5 us
    pallas_call x1, Pallas kernels, per_device(): pl.pallas_call(functools.partial(factor_kernel, tokens, ratio, n_head), o...  3.77 us
    ppermute x3, waiting for transfers between devices, per_device(): arrived = [lax.ppermute(send, 'head', by_core) for send in sends]  2.55 us
    pallas_call x1, Pallas kernels, per_device(): pl.pallas_call(functools.partial(pack_kernel, sub), out_shape=shape((sour...  2.45 us
  transfers between devices with their start and end apart: 15, of which 10 were waited for; matrix products, arithmetic and copies ran while one was open for 0% of the time, Pallas kernels for 7%

commit v1 on v0

--- a/solution.py
+++ b/solution.py
@@ -88,23 +88,40 @@
     return rows.reshape(per * tokens, rows.shape[-1])
 
 
-def block_inverse(below):
-    size = below[0].shape[0]
-    rows = lax.broadcasted_iota(jnp.int32, (size, size), 0)
-    cols = lax.broadcasted_iota(jnp.int32, (size, size), 1)
-    zero = jnp.zeros((size, size), F32)
+def beside(matrices):
+    return jnp.concatenate(matrices, axis=1)
+
+
+def diagonal(matrices):
+    zero = jnp.zeros_like(matrices[0])
+    return jnp.concatenate(
+        [beside([m if row == col else zero for col, m in enumerate(matrices)]) for row in range(len(matrices))], axis=0
+    )
+
+
+def parts_of(wide, count):
+    width = wide.shape[1] // count
+    return [wide[:, part * width : (part + 1) * width] for part in range(count)]
+
+
+def block_inverse(below, count):
+    size, wide = below[0].shape
+    rows = lax.broadcasted_iota(jnp.int32, (size, wide), 0)
+    cols = lax.broadcasted_iota(jnp.int32, (size, wide), 1) % size
     step = 1
     solved = None
     while step < size:
         joins = (rows // (2 * step) == cols // (2 * step)) & (rows // step > cols // step)
-        parts = [jnp.where(joins, matrix, zero) for matrix in below]
+        parts = [jnp.where(joins, matrix, 0.0) for matrix in below]
         if step == 1:
+            solved = [jnp.where(rows == cols, 1.0, -part).astype(BF16) for part in parts]
+        else:
+            inner = [
+                dot(part.astype(BF16), diagonal(parts_of(now, count))).astype(BF16) for part, now in zip(parts, solved)
+            ]
             solved = [
-                jnp.where(rows == cols, jnp.ones_like(zero), -part).astype(BF16) for part in parts
+                now - dot(now, diagonal(parts_of(mid, count))).astype(BF16) for now, mid in zip(solved, inner)
             ]
-        else:
-            inner = [dot(part.astype(BF16), now).astype(BF16) for part, now in zip(parts, solved)]
-            solved = [now - dot(now, mid).astype(BF16) for now, mid in zip(solved, inner)]
         step *= 2
     return solved
 
@@ -127,25 +144,34 @@
         key_row = lax.rsqrt(jnp.sum(squares, 0, keepdims=True) + EPSILON)
         key_col = lax.rsqrt(jnp.sum(squares, 1, keepdims=True) + EPSILON)
         lower = jnp.where(rows > cols, gram, 0.0) * key_row
+        strengths, systems = [], []
         for r in range(ratio):
             strength = jnp.zeros((1, SPAN), F32)
             for place in range(per):
                 piece = got_ref[block * per + place, first : first + ROW_TILE].astype(F32)[r : r + 1]
                 strength = jnp.where(lane // tokens == place, piece, strength)
             scaled_col = jnp.sum(jnp.where(rows == cols, strength * key_row, 0.0), 1, keepdims=True)
-            below.append(lower * scaled_col)
-            held.append((block, r, key, key_col, key_row, strength))
-    solved = block_inverse(below)
-    for now, (block, r, key, key_col, key_row, strength) in zip(solved, held):
-        value = block_rows(got_ref, block, per, tokens, 2 + r)
-        weighted = now.astype(F32) * key_col * strength
-        u_now = dot(weighted.astype(BF16), value)
-        w_now = dot((weighted * key_row).astype(BF16), key).astype(BF16)
-        both = dot(key.T, jnp.concatenate([w_now, u_now.astype(BF16)], axis=1))
-        w_ref[block, r] = w_now
-        u_ref[block, r] = u_now
-        trans_ref[block, r] = both[:, :width].astype(BF16)
-        add_ref[block, r] = both[:, width:]
+            systems.append(lower * scaled_col)
+            strengths.append(strength)
+        below.append(beside(systems))
+        held.append((block, key, key_col, key_row, strengths))
+    solved = block_inverse(below, ratio)
+    for now, (block, key, key_col, key_row, strengths) in zip(solved, held):
+        products = []
+        for r, inverse in enumerate(parts_of(now, ratio)):
+            value = block_rows(got_ref, block, per, tokens, 2 + r)
+            weighted = inverse.astype(F32) * key_col * strengths[r]
+            left = beside([(weighted * key_row).astype(BF16), weighted.astype(BF16)])
+            w_now, u_now = parts_of(dot(left, diagonal([key, value])), 2)
+            w_now = w_now.astype(BF16)
+            w_ref[block, r] = w_now
+            u_ref[block, r] = u_now
+            products += [w_now, u_now.astype(BF16)]
+        key_t = key.T
+        for r in range(ratio):
+            trans, add = parts_of(dot(key_t, beside(products[2 * r : 2 * r + 2])), 2)
+            trans_ref[block, r] = trans.astype(BF16)
+            add_ref[block, r] = add
 
     states = [jnp.zeros((width, width), F32) for r in range(ratio)]
     for block in range(blocks):
@@ -197,29 +223,33 @@
         total_ref[r] = carried[r]
 
 
-def join_kernel(state_ref, local_ref, reach_ref, *out_refs):
+def join_kernel(order, state_ref, local_ref, reach_ref, *out_refs):
     ratio, blocks, span, width = local_ref.shape
-    pieces, parts = out_refs[0].shape[0], len(out_refs) // 2
+    pieces = out_refs[0].shape[1]
     along_sub, along_head = position()
     upper = along_head // (lax.axis_size("head") // 2)
-    for number, out_ref in enumerate(out_refs):
-        target = along_sub ^ (number % parts)
-        for piece in range(pieces):
-            block = (target * 2 + (upper ^ (1 - number // parts))) * pieces + piece
-            for r in range(ratio):
-                core = local_ref[r, block] + dot(reach_ref[r, block], state_ref[r].astype(BF16))
-                mean_square = jnp.mean(core * core, 1, keepdims=True)
-                out_ref[piece, r] = (core * lax.rsqrt(mean_square + EPSILON)).astype(BF16)
-
-
-def project_kernel(parts, shares, *refs):
+    follows = lax.axis_index("outer") > 0
+    states = [jnp.where(follows, state_ref[r].astype(F32), 0.0).astype(BF16) for r in range(ratio)]
+    for distance, out_ref in zip(order, out_refs):
+        target = along_sub ^ distance
+        for kept in range(2):
+            for piece in range(pieces):
+                block = (target * 2 + (upper ^ (1 - kept))) * pieces + piece
+                for r in range(ratio):
+                    core = local_ref[r, block] + dot(reach_ref[r, block], states[r])
+                    mean_square = jnp.mean(core * core, 1, keepdims=True)
+                    out_ref[kept, piece, r] = (core * lax.rsqrt(mean_square + EPSILON)).astype(BF16)
+
+
+def project_kernel(order, shares, kept, *refs):
+    parts = len(order)
     normed_refs, gate_refs = refs[:parts], refs[parts : parts + shares]
     weight_ref, *send_refs, keep_ref, rows_ref = refs[parts + 2 * shares :]
-    pieces, ratio, span, width = normed_refs[0].shape
+    unused, pieces, ratio, span, width = normed_refs[0].shape
     tokens = gate_refs[0].shape[1]
     per = span // tokens
     along_sub, along_head = position()
-    for distance, normed_ref in enumerate(normed_refs):
+    for distance, normed_ref in zip(order, normed_refs):
         source = along_sub ^ distance
         for apart, gate_ref in enumerate(gate_refs):
             share = (along_head ^ apart) & (shares - 1)
@@ -228,7 +258,7 @@
             from_rows = pl.ds(pl.multiple_of(share % per * tokens, tokens), tokens)
             for r in range(ratio):
                 lanes = pl.ds(pl.multiple_of((source * ratio + r) * width, width), width)
-                normed = normed_ref[share // per, r, from_rows].astype(F32)
+                normed = normed_ref[kept, share // per, r, from_rows].astype(F32)
                 gate = gate_ref[source * ratio + r].astype(F32)
                 rows_ref[place, lanes] = (normed * gate).astype(BF16)
     out = dot(rows_ref[...], weight_ref[...]).reshape((2,) + keep_ref.shape)
@@ -318,7 +348,7 @@
             cost_estimate=LIGHT,
         )(got, *gates)
 
-    onward = [(here, here + 1) for here in range(outer - 1)]
+    onward = [(here, (here + 1) % outer) for here in range(outer)]
     incoming = lax.ppermute(state, "outer", onward)
     for distance in reversed(range(1, n_head)):
         pairs = [(here, here ^ distance) for here in range(n_head)]
@@ -337,6 +367,7 @@
             cost_estimate=LIGHT,
         )(got, w, u, trans, prefix)
     for hop in range(outer - 2):
+        incoming = jnp.where(lax.axis_index("outer") == 0, 0.0, incoming)
         passed = jnp.einsum("hde,hef->hdf", total, incoming, precision=lax.Precision.HIGHEST)
         incoming = lax.ppermute(state + passed, "outer", onward)
 
@@ -345,31 +376,32 @@
     quarter = (n_head // 4, tokens, columns)
     by_core = [(here, here ^ 1) for here in range(n_head)]
     half = n_head // 2
+    order = [0] + sorted(range(1, sub), reverse=True)
     with jax.named_scope("join"):
         normed = pl.pallas_call(
-            join_kernel,
-            out_shape=[shape((pieces, ratio, SPAN, width), BF16)] * (2 * sub),
+            functools.partial(join_kernel, order),
+            out_shape=[shape((2, pieces, ratio, SPAN, width), BF16)] * sub,
             in_specs=[VMEM] * 3,
-            out_specs=[VMEM] * (2 * sub),
+            out_specs=[VMEM] * sub,
             compiler_params=params(),
             cost_estimate=LIGHT,
         )(incoming, local, reach)
+    normed = [
+        lax.ppermute(part, "sub", [(here, here ^ distance) for here in range(sub)]) if distance else part
+        for distance, part in zip(order, normed)
+    ]
     for kept in range(2):
-        mine = list(normed[kept * sub : (kept + 1) * sub])
-        for distance in reversed(range(1, sub)):
-            pairs = [(here, here ^ distance) for here in range(sub)]
-            mine[distance] = lax.ppermute(mine[distance], "sub", pairs)
         cuts = 1 + kept
         with jax.named_scope("project"):
             *sends, keep = pl.pallas_call(
-                functools.partial(project_kernel, sub, half),
+                functools.partial(project_kernel, order, half, kept),
                 out_shape=[shape(quarter[:-1] + (columns // cuts,), BF16)] * cuts + [shape(quarter, F32)],
                 in_specs=[VMEM] * (sub + half) + [ANY] * half + [VMEM],
                 out_specs=[VMEM] * (cuts + 1),
                 scratch_shapes=[pltpu.VMEM((shard_tokens // 2, heads * width), BF16)],
                 compiler_params=params(),
                 cost_estimate=LIGHT,
-            )(*mine, *gates[half * (1 - kept) :], *gates[: half * (1 - kept)], output_weight)
+            )(*normed, *gates[half * (1 - kept) :], *gates[: half * (1 - kept)], output_weight)
         arrived = [lax.ppermute(send, "head", by_core) for send in sends]
         last = n_head == 4 and kept == 1
         with jax.named_scope("sum"):

time: 59.8 us -> 60.1 us (level)
  starting transfers between devices: 20.8 us -> 15.4 us
  waiting for transfers between devices: 26.5 us -> 30.6 us
  Pallas kernels: 12 us -> 13.7 us
    ppermute x1, waiting for transfers between devices: 0.01 us -> 5.51 us  [per_device(): lax.ppermute(summed, 'head', [(here, here ^ half) for here in range(n_hea...]
    ppermute x6 -> x3, starting transfers between devices: 7.04 us -> 3.55 us  [per_device(): lax.ppermute(part, 'sub', [(here, here ^ distance) for here in range(sub)])]
    ppermute x1, starting transfers between devices: 4.5 us -> 2.66 us  [per_device(): incoming = lax.ppermute(state, 'outer', onward)]
    ppermute x6 -> x3, waiting for transfers between devices: 7.65 us -> 5.92 us  [per_device(): lax.ppermute(part, 'sub', [(here, here ^ distance) for here in range(sub)])]
    pallas_call x1, Pallas kernels: 3.77 us -> 5.49 us  [per_device(): pl.pallas_call(functools.partial(factor_kernel, tokens, ratio, n_head), o...]
  transfers between devices with their start and end apart: 15 -> 12, of which waited for: 10 -> 9; matrix products, arithmetic and copies ran while one was open for 0% -> 0% of each run, Pallas kernels for 7% -> 7%
where the time goes in v1:
time: 60.1 us; the launch traced here: 59.8 us
  waiting for transfers between devices  30.6 us (51%)
  starting transfers between devices  15.4 us (26%)
  Pallas kernels  13.7 us (23%)
    all_to_all x1, waiting for transfers between devices, per_device(): lax.all_to_all(packed, ('sub', 'head'), split_axis=0, concat_axis=0, tile...  16.3 us
    all_to_all x1, starting transfers between devices, per_device(): lax.all_to_all(packed, ('sub', 'head'), split_axis=0, concat_axis=0, tile...  6.43 us
    ppermute x3, waiting for transfers between devices, per_device(): lax.ppermute(part, 'sub', [(here, here ^ distance) for here in range(sub)])  5.92 us
    ppermute x1, waiting for transfers between devices, per_device(): lax.ppermute(summed, 'head', [(here, here ^ half) for here in range(n_hea...  5.51 us
    pallas_call x1, Pallas kernels, per_device(): pl.pallas_call(functools.partial(factor_kernel, tokens, ratio, n_head), o...  5.49 us
    ppermute x3, starting transfers between devices, per_device(): lax.ppermute(part, 'sub', [(here, here ^ distance) for here in range(sub)])  3.55 us
    ppermute x1, starting transfers between devices, per_device(): incoming = lax.ppermute(state, 'outer', onward)  2.66 us
    ppermute x3, waiting for transfers between devices, per_device(): arrived = [lax.ppermute(send, 'head', by_core) for send in sends]  2.5 us
  transfers between devices with their start and end apart: 12, of which 9 were waited for; matrix products, arithmetic and copies ran while one was open for 0% of the time, Pallas kernels for 7%

profile of v1, /device:TPU:0, one launch (start us, length us, event | category | flops | bytes accessed | tf_op | source)
XLA Modules:
  0.0 59.8 jit_solution(12455252138563331602)
XLA Ops:
  0.0 2.4 %pack.1 = bf16[16,272,128]{2,1,0:T(8,128)(2,1)} custom-call(bf16[64,16,128]{2,1,0:T(8,128)(2,1)} %q_hbm.1, bf16[64,16,128]{2,1,0:T(8,128)(2,1)} %k_hbm.1, bf16[64,32,128]{2,1,0:T(8,128)(2,1)} %v_hbm.1, bf16[32,64]{1,0:T(8,128)(2,1)} %bitcast.4), custom_call_target="tpu_custom_call" | custom-call | tf_op jit(solution)/shard_map/pack/pallas_call | solution.py:302
  2.5 0.0 copy-start.1
  2.5 0.0 copy-start.2
  2.5 6.4 %all-to-all-start = ((bf16[16,272,128]{2,1,0:T(8,128)(2,1)}), bf16[16,272,128]{2,1,0:T(8,128)(2,1)S(1)}, u32[]{:S(2)}, u32[]{:S(2)}) async-start(bf16[16,272,128]{2,1,0:T(8,128)(2,1)} %pack.1), calls=%async_computation | async-start | bytes 2228224 | tf_op jit(solution)/shard_map/all_to_all | solution.py:316
  8.9 0.6 gates.1
  9.5 16.3 %all-to-all-done.got_ref = bf16[16,272,128]{2,1,0:T(8,128)(2,1)S(1)} async-done(((bf16[16,272,128]{2,1,0:T(8,128)(2,1)}), bf16[16,272,128]{2,1,0:T(8,128)(2,1)S(1)}, u32[]{:S(2)}, u32[]{:S(2)}) %all-to-all-start) | async-done | bytes 1114144 | tf_op jit(solution)/shard_map/all_to_all | solution.py:316
  25.9 5.5 %factors.1 = (bf16[2,128,128]{2,1,0:T(8,128)(2,1)S(1)}, bf16[8,2,128,128]{3,2,1,0:T(8,128)(2,1)S(1)}, f32[8,2,128,128]{3,2,1,0:T(8,128)S(1)}, bf16[8,2,128,128]{...) custom-call(bf16[16,272,128]{2,1,0:T(8,128)(2,1)S(1)} %all-to-all-do, ...), custom_call_target="tpu_custom_call", output_to_operand_aliasing={{5}: (1, {}), {6}: (2, {}), {7}: (3, {}), {8}: (4, {})} | custom-call | flops 1 | bytes 1 | tf_op jit(solution)/shard_map/factors/pallas_call | solution.py:333
  31.4 0.1 collective-permute-start.4
  31.4 2.7 %collective-permute-start = (bf16[2,128,128]{2,1,0:T(8,128)(2,1)S(1)}, bf16[2,128,128]{2,1,0:T(8,128)(2,1)S(1)}, u32[]{:S(2)}, u32[]{:S(2)}) collective-permute-start(bf16[2,128,128]{2,1,0:T(8,128)(2,1)S(1)} %get-tuple-element.33), channel_id=1, source_target_pairs={{0,16},{16,0},{1,17},{17,1},{2,18},{18,2},{3,19},{19,3},{4,20},{20... | collective-permute-start | bytes 196616 | tf_op jit(solution)/shard_map/ppermute | solution.py:352
  34.1 0.0 collective-permute-start.5
  34.1 1.5 %collective-permute-start.6 = (bf16[8,64,128]{2,1,0:T(8,128)(2,1)S(1)}, bf16[8,64,128]{2,1,0:T(8,128)(2,1)S(1)}, u32[]{:S(2)}, u32[]{:S(2)}) collective-permute-start(bf16[8,64,128]{2,1,0:T(8,128)(2,1)S(1)} %get-tuple-element.47), channel_id=1, source_target_pairs={{0,3},{1,2},{2,1},{3,0},{4,7},{5,6},{6,5},{7,4},{8,11},{9,10},{10,... | collective-permute-start | bytes 393224 | tf_op jit(solution)/shard_map/ppermute | solution.py:355
  35.6 2.3 %spread.1 = (f32[2,8,128,128]{3,2,1,0:T(8,128)S(1)}, bf16[2,8,128,128]{3,2,1,0:T(8,128)(2,1)S(1)}, f32[2,128,128]{2,1,0:T(8,128)}) custom-call(bf16[16,272,128]{2,1,0:T(8,128)(2,1)S(1)} %all-to-all-done.got_ref, bf16[8,2,128,128]{3,2,1,0:T(8,128)(2,1)S(1)} %get-tuple-element.34.w_ref, f32[8,2,128,128]{3,2,1,0:T(8,128)S(1)} %get-tuple-element.35.u_ref, ...), custom_call_target="tpu_custom_call" | custom-call | flops 1 | bytes 1 | tf_op jit(solution)/shard_map/spread/pallas_call | solution.py:357
  37.9 0.3 collective-permute-done.state_ref
  38.2 0.5 join.1
  38.7 1.5 %collective-permute-start.1 = (bf16[2,1,2,128,128]{4,3,2,1,0:T(8,128)(2,1)S(1)}, bf16[2,1,2,128,128]{4,3,2,1,0:T(8,128)(2,1)S(1)}, u32[]{:S(2)}, u32[]{:S(2)}) collective-permute-start(bf16[2,1,2,128,128]{4,3,2,1,0:T(8,128)(2,1)S(1)} %get-tuple-element.41), channel_id=1, source_target_pairs={{0,12},{4,8},{8,4},{12,0},{1,13},{5,9},{9,5},{13,1},{2,14},{6,10},... | collective-permute-start | bytes 393224 | tf_op jit(solution)/shard_map/ppermute | solution.py:390
  40.2 0.0 collective-permute-start.2
  40.3 0.0 collective-permute-done.4.refs_5_.refs_7_
  40.3 2.0 %collective-permute-start.3 = (bf16[2,1,2,128,128]{4,3,2,1,0:T(8,128)(2,1)S(1)}, bf16[2,1,2,128,128]{4,3,2,1,0:T(8,128)(2,1)S(1)}, u32[]{:S(2)}, u32[]{:S(2)}) collective-permute-start(bf16[2,1,2,128,128]{4,3,2,1,0:T(8,128)(2,1)S(1)} %get-tuple-element.43), channel_id=1, source_target_pairs={{0,4},{4,0},{8,12},{12,8},{1,5},{5,1},{9,13},{13,9},{2,6},{6,2},{1... | collective-permute-start | bytes 393224 | tf_op jit(solution)/shard_map/ppermute | solution.py:390
  42.3 3.7 %collective-permute-done.1.refs_1_ = bf16[2,1,2,128,128]{4,3,2,1,0:T(8,128)(2,1)S(1)} collective-permute-done((bf16[2,1,2,128,128]{4,3,2,1,0:T(8,128)(2,1)S(1)}, bf16[2,1,2,128,128]{4,3,2,1,0:T(8,128)(2,1)S(1)}, u32[]{:S(2)}, u32[]{:S(2)}) %collective-permute-start.1) | collective-permute-done | bytes 131104 | tf_op jit(solution)/shard_map/ppermute | solution.py:390
  46.0 0.6 %collective-permute-done.2.refs_2_ = bf16[2,1,2,128,128]{4,3,2,1,0:T(8,128)(2,1)S(1)} collective-permute-done((bf16[2,1,2,128,128]{4,3,2,1,0:T(8,128)(2,1)S(1)}, bf16[2,1,2,128,128]{4,3,2,1,0:T(8,128)(2,1)S(1)}, u32[]{:S(2)}, u32[]{:S(2)}) %collective-permute-start.2) | collective-permute-done | bytes 131104 | tf_op jit(solution)/shard_map/ppermute | solution.py:390
  46.6 1.6 %collective-permute-done.3.refs_3_ = bf16[2,1,2,128,128]{4,3,2,1,0:T(8,128)(2,1)S(1)} collective-permute-done((bf16[2,1,2,128,128]{4,3,2,1,0:T(8,128)(2,1)S(1)}, bf16[2,1,2,128,128]{4,3,2,1,0:T(8,128)(2,1)S(1)}, u32[]{:S(2)}, u32[]{:S(2)}) %collective-permute-start.3) | collective-permute-done | bytes 131104 | tf_op jit(solution)/shard_map/ppermute | solution.py:390
  48.2 0.8 %project.3 = (bf16[1,64,2048]{2,1,0:T(8,128)(2,1)S(1)}, f32[1,64,2048]{2,1,0:T(8,128)S(1)}) custom-call(bf16[2,1,2,128,128]{4,3,2,1,0:T(8,128)(2,1)S(1)} %get-tuple-element.40.refs_0_, bf16[2,1,2,128,128]{4,3,2,1,0:T(8,128)(2,1)S(1)} %collective-permute-done.1.refs_1_, bf16[2,1,2,128,128]{4,3,2,1,0:T(8,128)(2,1)S(1)} %collective-permute-done.2.refs_2_, ...), custom_call_target="tpu_custom_call" | custom-call | flops 1 | bytes 1 | tf_op jit(solution)/shard_map/project/pallas_call | solution.py:396
  49.0 0.1 collective-permute-start.9
  49.1 1.5 %collective-permute-done.9.refs_0_ = bf16[1,64,2048]{2,1,0:T(8,128)(2,1)S(1)} collective-permute-done((bf16[1,64,2048]{2,1,0:T(8,128)(2,1)S(1)}, bf16[1,64,2048]{2,1,0:T(8,128)(2,1)S(1)}, u32[]{:S(2)}, u32[]{:S(2)}) %collective-permute-start.9) | collective-permute-done | bytes 262176 | tf_op jit(solution)/shard_map/ppermute | solution.py:405
  50.6 0.5 collective-permute-start.10
  51.2 0.8 %project.2 = (bf16[1,64,1024]{2,1,0:T(8,128)(2,1)S(1)}, bf16[1,64,1024]{2,1,0:T(8,128)(2,1)S(1)}, f32[1,64,2048]{2,1,0:T(8,128)S(1)}) custom-call(bf16[2,1,2,128,128]{4,3,2,1,0:T(8,128)(2,1)S(1)} %get-tuple-element.40.refs_0_, bf16[2,1,2,128,128]{4,3,2,1,0:T(8,128)(2,1)S(1)} %collective-permute-done.1.refs_1_, ...), custom_call_target="tpu_custom_call" | custom-call | flops 1 | bytes 1 | tf_op jit(solution)/shard_map/project/pallas_call | solution.py:396
  51.9 0.1 collective-permute-start.7
  52.0 0.5 collective-permute-start.8
  52.5 0.8 %collective-permute-done.7.refs_0_ = bf16[1,64,1024]{2,1,0:T(8,128)(2,1)S(1)} collective-permute-done((bf16[1,64,1024]{2,1,0:T(8,128)(2,1)S(1)}, bf16[1,64,1024]{2,1,0:T(8,128)(2,1)S(1)}, u32[]{:S(2)}, u32[]{:S(2)}) %collective-permute-start.7) | collective-permute-done | bytes 131104 | tf_op jit(solution)/shard_map/ppermute | solution.py:405
  53.4 0.2 collective-permute-done.8.refs_1_
  53.5 5.5 %collective-permute-done.10.refs_2_ = bf16[1,64,2048]{2,1,0:T(8,128)(2,1)S(1)} collective-permute-done((bf16[1,64,2048]{2,1,0:T(8,128)(2,1)S(1)}, bf16[1,64,2048]{2,1,0:T(8,128)(2,1)S(1)}, u32[]{:S(2)}, u32[]{:S(2)}) %collective-permute-start.10) | collective-permute-done | bytes 262176 | tf_op jit(solution)/shard_map/ppermute | solution.py:417
  59.1 0.8 %sum.3 = bf16[1,64,2048]{2,1,0:T(8,128)(2,1)} custom-call(f32[1,64,2048]{2,1,0:T(8,128)S(1)} %get-tuple-element.48.keep_ref, bf16[1,64,1024]{2,1,0:T(8,128)(2,1)S(1)} %collective-permute-done.7.refs_0_, bf16[1,64,1024]{2,1,0:T(8,128)(2,1)S(1)} %collective-permute-done.8.refs_1_, bf16[1,64,2048]{2,1,0:T(8,128)(2,1)S(1)} %collective-permute-done.10.refs_2_), custom_call_target="tpu_custom_call" | custom-call | flops 1 | bytes 1 | tf_op jit(solution)/shard_map/sum/pallas_call | solution.py:408
  (7 shorter events, 0.1 us)
Async XLA Ops:
  2.5 6.5 %copy-start.1 = (bf16[64,32,128]{2,1,0:T(8,128)(2,1)S(1)}, bf16[64,32,128]{2,1,0:T(8,128)(2,1)}, u32[]{:S(2)}) copy-start(bf16[64,32,128]{2,1,0:T(8,128)(2,1)} %gate_ref.1) | copy-start | bytes 1572868
  2.5 6.5 %copy-start.2 = (bf16[128]{0:T(256)(128)(2,1)S(1)}, bf16[128]{0:T(256)(128)(2,1)}, u32[]{:S(2)}) copy-start(bf16[128]{0:T(256)(128)(2,1)} %param.12) | copy-start | bytes 772
  2.5 23.4 %all-to-all-start = ((bf16[16,272,128]{2,1,0:T(8,128)(2,1)}), bf16[16,272,128]{2,1,0:T(8,128)(2,1)S(1)}, u32[]{:S(2)}, u32[]{:S(2)}) async-start(bf16[16,272,128]{2,1,0:T(8,128)(2,1)} %pack.1), calls=%async_computation | async-start | bytes 2228224 | tf_op jit(solution)/shard_map/all_to_all | solution.py:316
  31.4 8.9 %collective-permute-start.4 = (bf16[8,64,128]{2,1,0:T(8,128)(2,1)S(1)}, bf16[8,64,128]{2,1,0:T(8,128)(2,1)S(1)}, u32[]{:S(2)}, u32[]{:S(2)}) collective-permute-start(bf16[8,64,128]{2,1,0:T(8,128)(2,1)S(1)} %get-tuple-element.45), channel_id=1, source_target_pairs={{0,1},{1,0},{2,3},{3,2},{4,5},{5,4},{6,7},{7,6},{8,9},{9,8},{10,11... | collective-permute-start | bytes 393224 | tf_op jit(solution)/shard_map/ppermute | solution.py:355
  31.4 6.8 %collective-permute-start = (bf16[2,128,128]{2,1,0:T(8,128)(2,1)S(1)}, bf16[2,128,128]{2,1,0:T(8,128)(2,1)S(1)}, u32[]{:S(2)}, u32[]{:S(2)}) collective-permute-start(bf16[2,128,128]{2,1,0:T(8,128)(2,1)S(1)} %get-tuple-element.33), channel_id=1, source_target_pairs={{0,16},{16,0},{1,17},{17,1},{2,18},{18,2},{3,19},{19,3},{4,20},{20... | collective-permute-start | bytes 196616 | tf_op jit(solution)/shard_map/ppermute | solution.py:352
  34.1 8.2 %collective-permute-start.5 = (bf16[8,64,128]{2,1,0:T(8,128)(2,1)S(1)}, bf16[8,64,128]{2,1,0:T(8,128)(2,1)S(1)}, u32[]{:S(2)}, u32[]{:S(2)}) collective-permute-start(bf16[8,64,128]{2,1,0:T(8,128)(2,1)S(1)} %get-tuple-element.46), channel_id=1, source_target_pairs={{0,2},{1,3},{2,0},{3,1},{4,6},{5,7},{6,4},{7,5},{8,10},{9,11},{10,... | collective-permute-start | bytes 393224 | tf_op jit(solution)/shard_map/ppermute | solution.py:355
  34.1 8.2 %collective-permute-start.6 = (bf16[8,64,128]{2,1,0:T(8,128)(2,1)S(1)}, bf16[8,64,128]{2,1,0:T(8,128)(2,1)S(1)}, u32[]{:S(2)}, u32[]{:S(2)}) collective-permute-start(bf16[8,64,128]{2,1,0:T(8,128)(2,1)S(1)} %get-tuple-element.47), channel_id=1, source_target_pairs={{0,3},{1,2},{2,1},{3,0},{4,7},{5,6},{6,5},{7,4},{8,11},{9,10},{10,... | collective-permute-start | bytes 393224 | tf_op jit(solution)/shard_map/ppermute | solution.py:355
  35.6 12.6 %copy-start = (bf16[1024,2048]{1,0:T(8,128)(2,1)S(1)}, bf16[1024,2048]{1,0:T(8,128)(2,1)}, u32[]{:S(2)}) copy-start(bf16[1024,2048]{1,0:T(8,128)(2,1)} %refs_8_.3) | copy-start | bytes 12582916
  38.7 7.3 %collective-permute-start.1 = (bf16[2,1,2,128,128]{4,3,2,1,0:T(8,128)(2,1)S(1)}, bf16[2,1,2,128,128]{4,3,2,1,0:T(8,128)(2,1)S(1)}, u32[]{:S(2)}, u32[]{:S(2)}) collective-permute-start(bf16[2,1,2,128,128]{4,3,2,1,0:T(8,128)(2,1)S(1)} %get-tuple-element.41), channel_id=1, source_target_pairs={{0,12},{4,8},{8,4},{12,0},{1,13},{5,9},{9,5},{13,1},{2,14},{6,10},... | collective-permute-start | bytes 393224 | tf_op jit(solution)/shard_map/ppermute | solution.py:390
  40.2 6.4 %collective-permute-start.2 = (bf16[2,1,2,128,128]{4,3,2,1,0:T(8,128)(2,1)S(1)}, bf16[2,1,2,128,128]{4,3,2,1,0:T(8,128)(2,1)S(1)}, u32[]{:S(2)}, u32[]{:S(2)}) collective-permute-start(bf16[2,1,2,128,128]{4,3,2,1,0:T(8,128)(2,1)S(1)} %get-tuple-element.42), channel_id=1, source_target_pairs={{0,8},{4,12},{8,0},{12,4},{1,9},{5,13},{9,1},{13,5},{2,10},{6,14},... | collective-permute-start | bytes 393224 | tf_op jit(solution)/shard_map/ppermute | solution.py:390
  40.3 7.9 %collective-permute-start.3 = (bf16[2,1,2,128,128]{4,3,2,1,0:T(8,128)(2,1)S(1)}, bf16[2,1,2,128,128]{4,3,2,1,0:T(8,128)(2,1)S(1)}, u32[]{:S(2)}, u32[]{:S(2)}) collective-permute-start(bf16[2,1,2,128,128]{4,3,2,1,0:T(8,128)(2,1)S(1)} %get-tuple-element.43), channel_id=1, source_target_pairs={{0,4},{4,0},{8,12},{12,8},{1,5},{5,1},{9,13},{13,9},{2,6},{6,2},{1... | collective-permute-start | bytes 393224 | tf_op jit(solution)/shard_map/ppermute | solution.py:390
  49.0 1.6 %collective-permute-start.9 = (bf16[1,64,2048]{2,1,0:T(8,128)(2,1)S(1)}, bf16[1,64,2048]{2,1,0:T(8,128)(2,1)S(1)}, u32[]{:S(2)}, u32[]{:S(2)}) collective-permute-start(bf16[1,64,2048]{2,1,0:T(8,128)(2,1)S(1)} %get-tuple-element.52), channel_id=1, source_target_pairs={{0,1},{1,0},{2,3},{3,2},{4,5},{5,4},{6,7},{7,6},{8,9},{9,8},{10,11... | collective-permute-start | bytes 786440 | tf_op jit(solution)/shard_map/ppermute | solution.py:405
  50.6 8.4 %collective-permute-start.10 = (bf16[1,64,2048]{2,1,0:T(8,128)(2,1)S(1)}, bf16[1,64,2048]{2,1,0:T(8,128)(2,1)S(1)}, u32[]{:S(2)}, u32[]{:S(2)}) collective-permute-start(bf16[1,64,2048]{2,1,0:T(8,128)(2,1)S(1)} %sum.2), channel_id=1, source_target_pairs={{0,2},{1,3},{2,0},{3,1},{4,6},{5,7},{6,4},{7,5},{8,10},{9,11},{10,... | collective-permute-start | bytes 786440 | tf_op jit(solution)/shard_map/ppermute | solution.py:417
  51.9 1.4 %collective-permute-start.7 = (bf16[1,64,1024]{2,1,0:T(8,128)(2,1)S(1)}, bf16[1,64,1024]{2,1,0:T(8,128)(2,1)S(1)}, u32[]{:S(2)}, u32[]{:S(2)}) collective-permute-start(bf16[1,64,1024]{2,1,0:T(8,128)(2,1)S(1)} %get-tuple-element.49), channel_id=1, source_target_pairs={{0,1},{1,0},{2,3},{3,2},{4,5},{5,4},{6,7},{7,6},{8,9},{9,8},{10,11... | collective-permute-start | bytes 393224 | tf_op jit(solution)/shard_map/ppermute | solution.py:405
  52.0 1.5 %collective-permute-start.8 = (bf16[1,64,1024]{2,1,0:T(8,128)(2,1)S(1)}, bf16[1,64,1024]{2,1,0:T(8,128)(2,1)S(1)}, u32[]{:S(2)}, u32[]{:S(2)}) collective-permute-start(bf16[1,64,1024]{2,1,0:T(8,128)(2,1)S(1)} %get-tuple-element.50), channel_id=1, source_target_pairs={{0,1},{1,0},{2,3},{3,2},{4,5},{5,4},{6,7},{7,6},{8,9},{9,8},{10,11... | collective-permute-start | bytes 393224 | tf_op jit(solution)/shard_map/ppermute | solution.py:405

commit v2 on v1

--- a/solution.py
+++ b/solution.py
@@ -38,12 +38,12 @@
     return lax.axis_index("sub"), lax.axis_index("head")
 
 
-def pack_kernel(sub, q_hbm, k_hbm, v_hbm, b_hbm, out_ref, q_ref, k_ref, v_ref, b_ref, done):
+def pack_kernel(sub, q_hbm, k_hbm, v_hbm, b_hbm, out_hbm, q_ref, k_ref, v_ref, b_ref, out_ref, came, left):
     tokens, key_heads, width = q_hbm.shape
     ratio = v_hbm.shape[1] // key_heads
     n_head = key_heads // sub
     copies = [
-        pltpu.make_async_copy(source, target, done.at[number])
+        pltpu.make_async_copy(source, target, came.at[number])
         for number, (source, target) in enumerate(
             ((b_hbm, b_ref), (k_hbm, k_ref), (q_hbm, q_ref), (v_hbm, v_ref))
         )
@@ -51,25 +51,34 @@
     for copy in copies:
         copy.start()
     heads = [(peer % n_head) * sub + peer // n_head for peer in range(key_heads)]
+    leaving = []
+
+    def leave(first, size):
+        rows = pl.ds(first, size)
+        leaving.append(pltpu.make_async_copy(out_ref.at[:, rows], out_hbm.at[:, rows], left.at[len(leaving)]))
+        leaving[-1].start()
+
     copies[0].wait()
     strength = jnp.concatenate([b_ref[...].astype(F32)] * (width // tokens), axis=1)
     strength = jnp.concatenate([strength, jnp.zeros((ROW_TILE, width), F32)], axis=0)
     for peer, head in enumerate(heads):
         tile = strength[head * ratio : head * ratio + ROW_TILE]
         out_ref[peer, (2 + ratio) * tokens :] = tile.astype(BF16)
-    copies[1].wait()
-    rows = turned(k_ref[...])
-    for peer, head in enumerate(heads):
-        out_ref[peer, tokens : 2 * tokens] = rows[head]
-    copies[2].wait()
-    rows = turned(q_ref[...])
-    for peer, head in enumerate(heads):
-        out_ref[peer, 0:tokens] = rows[head]
+    leave((2 + ratio) * tokens, ROW_TILE)
+    for place, copy, ref in ((1, copies[1], k_ref), (0, copies[2], q_ref)):
+        copy.wait()
+        rows = turned(ref[...])
+        for peer, head in enumerate(heads):
+            out_ref[peer, place * tokens : (place + 1) * tokens] = rows[head]
+        leave(place * tokens, tokens)
     copies[3].wait()
     rows = turned(v_ref[...])
-    for peer, head in enumerate(heads):
-        for r in range(ratio):
+    for r in range(ratio):
+        for peer, head in enumerate(heads):
             out_ref[peer, (2 + r) * tokens : (3 + r) * tokens] = rows[head * ratio + r]
+        leave((2 + r) * tokens, tokens)
+    for copy in leaving:
+        copy.wait()
 
 
 def gate_kernel(gate_ref, gain_ref, *refs):
@@ -92,42 +101,48 @@
     return jnp.concatenate(matrices, axis=1)
 
 
-def diagonal(matrices):
-    zero = jnp.zeros_like(matrices[0])
-    return jnp.concatenate(
-        [beside([m if row == col else zero for col, m in enumerate(matrices)]) for row in range(len(matrices))], axis=0
-    )
-
-
 def parts_of(wide, count):
     width = wide.shape[1] // count
     return [wide[:, part * width : (part + 1) * width] for part in range(count)]
 
 
-def block_inverse(below, count):
-    size, wide = below[0].shape
-    rows = lax.broadcasted_iota(jnp.int32, (size, wide), 0)
-    cols = lax.broadcasted_iota(jnp.int32, (size, wide), 1) % size
+def block_inverse(below):
+    size = below[0].shape[0]
+    half = size // 2
+    rows = lax.broadcasted_iota(jnp.int32, (half, size), 0)
+    cols = lax.broadcasted_iota(jnp.int32, (half, size), 1)
+    first = cols < half
+    cols = cols % half
+
+    def stacked(wide):
+        return jnp.concatenate(parts_of(wide, 2), axis=0)
+
+    def side(tall):
+        return jnp.where(first, tall[:half], tall[half:])
+
+    systems = [side(matrix) for matrix in below]
     step = 1
     solved = None
-    while step < size:
+    while step < half:
         joins = (rows // (2 * step) == cols // (2 * step)) & (rows // step > cols // step)
-        parts = [jnp.where(joins, matrix, 0.0) for matrix in below]
+        parts = [jnp.where(joins, system, 0.0) for system in systems]
         if step == 1:
             solved = [jnp.where(rows == cols, 1.0, -part).astype(BF16) for part in parts]
         else:
-            inner = [
-                dot(part.astype(BF16), diagonal(parts_of(now, count))).astype(BF16) for part, now in zip(parts, solved)
-            ]
-            solved = [
-                now - dot(now, diagonal(parts_of(mid, count))).astype(BF16) for now, mid in zip(solved, inner)
-            ]
+            inner = [side(dot(stacked(part).astype(BF16), now)).astype(BF16) for part, now in zip(parts, solved)]
+            solved = [now - side(dot(stacked(now), mid)).astype(BF16) for now, mid in zip(solved, inner)]
         step *= 2
-    return solved
+    joined = []
+    for matrix, now in zip(below, solved):
+        inner = dot(matrix[half:, :half].astype(BF16), now).astype(BF16)
+        outer = dot(now[:, half:], inner).astype(BF16)
+        zero = jnp.zeros_like(now)
+        joined.append(jnp.concatenate([jnp.where(first, now, zero), jnp.where(first, -outer, now)], axis=0))
+    return joined
 
 
 def factor_kernel(tokens, ratio, n_head, got_ref, *refs):
-    state_ref, w_ref, u_ref, trans_ref, prefix_ref = refs[n_head : n_head + 5]
+    state_ref, both_ref, trans_ref, prefix_ref = refs[n_head : n_head + 4]
     add_ref = refs[-1]
     width = got_ref.shape[-1]
     per = SPAN // tokens
@@ -144,32 +159,30 @@
         key_row = lax.rsqrt(jnp.sum(squares, 0, keepdims=True) + EPSILON)
         key_col = lax.rsqrt(jnp.sum(squares, 1, keepdims=True) + EPSILON)
         lower = jnp.where(rows > cols, gram, 0.0) * key_row
-        strengths, systems = [], []
+        strengths = []
         for r in range(ratio):
             strength = jnp.zeros((1, SPAN), F32)
             for place in range(per):
                 piece = got_ref[block * per + place, first : first + ROW_TILE].astype(F32)[r : r + 1]
                 strength = jnp.where(lane // tokens == place, piece, strength)
             scaled_col = jnp.sum(jnp.where(rows == cols, strength * key_row, 0.0), 1, keepdims=True)
-            systems.append(lower * scaled_col)
+            below.append(lower * scaled_col)
             strengths.append(strength)
-        below.append(beside(systems))
         held.append((block, key, key_col, key_row, strengths))
-    solved = block_inverse(below, ratio)
-    for now, (block, key, key_col, key_row, strengths) in zip(solved, held):
-        products = []
-        for r, inverse in enumerate(parts_of(now, ratio)):
+    solved = block_inverse(below)
+    for number, (block, key, key_col, key_row, strengths) in enumerate(held):
+        weighted = [
+            inverse.astype(F32) * key_col * strength
+            for inverse, strength in zip(solved[number * ratio : (number + 1) * ratio], strengths)
+        ]
+        w_all = dot(jnp.concatenate([(part * key_row).astype(BF16) for part in weighted], axis=0), key).astype(BF16)
+        key_t = key.T
+        for r, part in enumerate(weighted):
             value = block_rows(got_ref, block, per, tokens, 2 + r)
-            weighted = inverse.astype(F32) * key_col * strengths[r]
-            left = beside([(weighted * key_row).astype(BF16), weighted.astype(BF16)])
-            w_now, u_now = parts_of(dot(left, diagonal([key, value])), 2)
-            w_now = w_now.astype(BF16)
-            w_ref[block, r] = w_now
-            u_ref[block, r] = u_now
-            products += [w_now, u_now.astype(BF16)]
-        key_t = key.T
-        for r in range(ratio):
-            trans, add = parts_of(dot(key_t, beside(products[2 * r : 2 * r + 2])), 2)
+            u_now = dot(part.astype(BF16), value).astype(BF16)
+            both = beside([w_all[r * SPAN : (r + 1) * SPAN], u_now])
+            both_ref[block, r] = both
+            trans, add = parts_of(dot(key_t, both), 2)
             trans_ref[block, r] = trans.astype(BF16)
             add_ref[block, r] = add
 
@@ -187,7 +200,7 @@
 
 
 def spread_kernel(
-    tokens, ratio, got_ref, w_ref, u_ref, trans_ref, prefix_ref, local_ref, reach_ref, total_ref
+    tokens, ratio, total_too, got_ref, both_ref, trans_ref, prefix_ref, local_ref, reach_ref, total_ref
 ):
     width = got_ref.shape[-1]
     per = SPAN // tokens
@@ -205,20 +218,18 @@
         query_f = query.astype(F32)
         squares = jnp.sum(query_f * query_f, 1, keepdims=True)
         unit = lax.rsqrt(squares + EPSILON) * width ** (-0.5)
-        left = jnp.concatenate([query, scores], axis=1)
-        for r in range(ratio):
+        passed = dot(scores, beside([both_ref[block, r] for r in range(ratio)]))
+        for r, part in enumerate(parts_of(passed, ratio)):
+            through, added = parts_of(part, 2)
             held = carried[r].astype(BF16)
             if block == 0:
                 carried[r] = identity - trans_ref[block, r].astype(F32)
-            else:
+            elif total_too or block < blocks - 1:
                 carried[r] = carried[r] - dot(trans_ref[block, r], held)
-            starts = jnp.concatenate([prefix_ref[block, r], held], axis=1)
-            passed = dot(w_ref[block, r], starts)
-            corrected = jnp.concatenate([u_ref[block, r] - passed[:, :width], -passed[:, width:]], axis=1)
-            right = jnp.concatenate([starts, corrected.astype(BF16)], axis=0)
-            out = dot(left, right) * unit
-            local_ref[r, block] = out[:, :width]
-            reach_ref[r, block] = out[:, width:].astype(BF16)
+            starts = beside([prefix_ref[block, r], held])
+            out = dot((query_f - through).astype(BF16), starts)
+            local_ref[r, block] = (out[:, :width] + added) * unit
+            reach_ref[r, block] = (out[:, width:] * unit).astype(BF16)
     for r in range(ratio):
         total_ref[r] = carried[r]
 
@@ -303,13 +314,15 @@
             functools.partial(pack_kernel, sub),
             out_shape=shape((sources,) + slab, BF16),
             in_specs=[ANY] * 4,
-            out_specs=VMEM,
+            out_specs=ANY,
             scratch_shapes=[
                 pltpu.VMEM(queries.shape, BF16),
                 pltpu.VMEM(key_vectors.shape, BF16),
                 pltpu.VMEM(value_vectors.shape, BF16),
                 pltpu.VMEM((value_heads, tokens), BF16),
+                pltpu.VMEM((sources,) + slab, BF16),
                 pltpu.SemaphoreType.DMA((4,)),
+                pltpu.SemaphoreType.DMA((3 + ratio,)),
             ],
             compiler_params=params(60),
         )(queries, key_vectors, value_vectors, write_strength.T)
@@ -330,19 +343,18 @@
     state_type = BF16 if outer == 2 else F32
     square = (blocks, ratio, width, width)
     with jax.named_scope("factors"):
-        state, w, u, trans, prefix, *gates = pl.pallas_call(
+        state, both, trans, prefix, *gates = pl.pallas_call(
             functools.partial(factor_kernel, tokens, ratio, n_head),
             out_shape=[
                 shape((ratio, width, width), state_type),
-                shape((blocks, ratio, SPAN, width), BF16),
-                shape((blocks, ratio, SPAN, width), F32),
+                shape((blocks, ratio, SPAN, 2 * width), BF16),
                 shape(square, BF16),
                 shape(square, BF16),
             ]
             + [shape((heads, tokens, width), BF16)] * n_head,
             in_specs=[VMEM] + [ANY] * n_head,
-            out_specs=[VMEM] * 5 + [ANY] * n_head,
-            input_output_aliases={1 + number: 5 + number for number in range(n_head)},
+            out_specs=[VMEM] * 4 + [ANY] * n_head,
+            input_output_aliases={1 + number: 4 + number for number in range(n_head)},
             scratch_shapes=[pltpu.VMEM(square, F32)],
             compiler_params=params(),
             cost_estimate=LIGHT,
@@ -355,17 +367,17 @@
         gates[distance] = lax.ppermute(gates[distance], "head", pairs)
     with jax.named_scope("spread"):
         local, reach, total = pl.pallas_call(
-            functools.partial(spread_kernel, tokens, ratio),
+            functools.partial(spread_kernel, tokens, ratio, outer > 2),
             out_shape=[
                 shape((ratio, blocks, SPAN, width), F32),
                 shape((ratio, blocks, SPAN, width), BF16),
                 shape((ratio, width, width), F32),
             ],
-            in_specs=[VMEM] * 5,
+            in_specs=[VMEM] * 4,
             out_specs=[VMEM] * 3,
             compiler_params=params(),
             cost_estimate=LIGHT,
-        )(got, w, u, trans, prefix)
+        )(got, both, trans, prefix)
     for hop in range(outer - 2):
         incoming = jnp.where(lax.axis_index("outer") == 0, 0.0, incoming)
         passed = jnp.einsum("hde,hef->hdf", total, incoming, precision=lax.Precision.HIGHEST)

time: 60.1 us -> 59.9 us (level)
    pallas_call x1, Pallas kernels: 2.27 us -> 2.87 us  [per_device(): pl.pallas_call(functools.partial(spread_kernel, tokens, ratio, outer > 2)...]
  transfers between devices with their start and end apart: 12 -> 12, of which waited for: 9 -> 8; matrix products, arithmetic and copies ran while one was open for 0% -> 0% of each run, Pallas kernels for 7% -> 8%
where the time goes in v2:
time: 59.9 us; the launch traced here: 59.7 us
  waiting for transfers between devices  30.6 us (51%)
  starting transfers between devices  15.4 us (26%)
  Pallas kernels  13.6 us (23%)
    all_to_all x1, waiting for transfers between devices, per_device(): lax.all_to_all(packed, ('sub', 'head'), split_axis=0, concat_axis=0, tile...  16.3 us
    all_to_all x1, starting transfers between devices, per_device(): lax.all_to_all(packed, ('sub', 'head'), split_axis=0, concat_axis=0, tile...  6.43 us
    ppermute x3, waiting for transfers between devices, per_device(): lax.ppermute(part, 'sub', [(here, here ^ distance) for here in range(sub)])  6.23 us
    ppermute x1, waiting for transfers between devices, per_device(): lax.ppermute(summed, 'head', [(here, here ^ half) for here in range(n_hea...  5.55 us
    pallas_call x1, Pallas kernels, per_device(): pl.pallas_call(functools.partial(factor_kernel, tokens, ratio, n_head), o...  4.93 us
    ppermute x3, starting transfers between devices, per_device(): lax.ppermute(part, 'sub', [(here, here ^ distance) for here in range(sub)])  3.55 us
    pallas_call x1, Pallas kernels, per_device(): pl.pallas_call(functools.partial(spread_kernel, tokens, ratio, outer > 2)...  2.87 us
    ppermute x1, starting transfers between devices, per_device(): incoming = lax.ppermute(state, 'outer', onward)  2.66 us
  transfers between devices with their start and end apart: 12, of which 8 were waited for; matrix products, arithmetic and copies ran while one was open for 0% of the time, Pallas kernels for 8%

profile of v2, /device:TPU:0, one launch (start us, length us, event | category | flops | bytes accessed | tf_op | source)
XLA Modules:
  0.0 59.7 jit_solution(13601697716204253262)
XLA Ops:
  0.0 2.3 %pack.1 = bf16[16,272,128]{2,1,0:T(8,128)(2,1)} custom-call(bf16[64,16,128]{2,1,0:T(8,128)(2,1)} %q_hbm.1, bf16[64,16,128]{2,1,0:T(8,128)(2,1)} %k_hbm.1, bf16[64,32,128]{2,1,0:T(8,128)(2,1)} %v_hbm.1, bf16[32,64]{1,0:T(8,128)(2,1)} %bitcast.4), custom_call_target="tpu_custom_call" | custom-call | tf_op jit(solution)/shard_map/pack/pallas_call | solution.py:313
  2.3 0.0 copy-start.1
  2.3 0.0 copy-start.2
  2.3 6.4 %all-to-all-start = ((bf16[16,272,128]{2,1,0:T(8,128)(2,1)}), bf16[16,272,128]{2,1,0:T(8,128)(2,1)S(1)}, u32[]{:S(2)}, u32[]{:S(2)}) async-start(bf16[16,272,128]{2,1,0:T(8,128)(2,1)} %pack.1), calls=%async_computation | async-start | bytes 2228224 | tf_op jit(solution)/shard_map/all_to_all | solution.py:329
  8.7 0.6 gates.1
  9.3 16.3 %all-to-all-done.got_ref = bf16[16,272,128]{2,1,0:T(8,128)(2,1)S(1)} async-done(((bf16[16,272,128]{2,1,0:T(8,128)(2,1)}), bf16[16,272,128]{2,1,0:T(8,128)(2,1)S(1)}, u32[]{:S(2)}, u32[]{:S(2)}) %all-to-all-start) | async-done | bytes 1114144 | tf_op jit(solution)/shard_map/all_to_all | solution.py:329
  25.7 4.9 %factors.1 = (bf16[2,128,128]{2,1,0:T(8,128)(2,1)S(1)}, bf16[8,2,128,256]{3,2,1,0:T(8,128)(2,1)S(1)}, bf16[8,2,128,128]{3,2,1,0:T(8,128)(2,1)S(1)}, bf16[8,2,128...) custom-call(bf16[16,272,128]{2,1,0:T(8,128)(2,1)S(1)} %all-to-all-do, ...), custom_call_target="tpu_custom_call", output_to_operand_aliasing={{4}: (1, {}), {5}: (2, {}), {6}: (3, {}), {7}: (4, {})} | custom-call | flops 1 | bytes 1 | tf_op jit(solution)/shard_map/factors/pallas_call | solution.py:346
  30.6 0.1 collective-permute-start.4
  30.7 2.7 %collective-permute-start = (bf16[2,128,128]{2,1,0:T(8,128)(2,1)S(1)}, bf16[2,128,128]{2,1,0:T(8,128)(2,1)S(1)}, u32[]{:S(2)}, u32[]{:S(2)}) collective-permute-start(bf16[2,128,128]{2,1,0:T(8,128)(2,1)S(1)} %get-tuple-element.32), channel_id=1, source_target_pairs={{0,16},{16,0},{1,17},{17,1},{2,18},{18,2},{3,19},{19,3},{4,20},{20... | collective-permute-start | bytes 196616 | tf_op jit(solution)/shard_map/ppermute | solution.py:364
  33.4 0.0 collective-permute-start.5
  33.4 1.5 %collective-permute-start.6 = (bf16[8,64,128]{2,1,0:T(8,128)(2,1)S(1)}, bf16[8,64,128]{2,1,0:T(8,128)(2,1)S(1)}, u32[]{:S(2)}, u32[]{:S(2)}) collective-permute-start(bf16[8,64,128]{2,1,0:T(8,128)(2,1)S(1)} %get-tuple-element.45), channel_id=1, source_target_pairs={{0,3},{1,2},{2,1},{3,0},{4,7},{5,6},{6,5},{7,4},{8,11},{9,10},{10,... | collective-permute-start | bytes 393224 | tf_op jit(solution)/shard_map/ppermute | solution.py:367
  34.9 2.9 %spread.1 = (f32[2,8,128,128]{3,2,1,0:T(8,128)S(1)}, bf16[2,8,128,128]{3,2,1,0:T(8,128)(2,1)S(1)}, f32[2,128,128]{2,1,0:T(8,128)}) custom-call(bf16[16,272,128]{2,1,0:T(8,128)(2,1)S(1)} %all-to-all-done.got_ref, bf16[8,2,128,256]{3,2,1,0:T(8,128)(2,1)S(1)} %get-tuple-element.33.both_ref, bf16[8,2,128,128]{3,2,1,0:T(8,128)(2,1)S(1)} %get-tuple-element.34.trans_ref, ...), custom_call_target="tpu_custom_call" | custom-call | flops 1 | bytes 1 | tf_op jit(solution)/shard_map/spread/pallas_call | solution.py:369
  37.7 0.0 collective-permute-done.state_ref
  37.8 0.5 join.1
  38.3 1.8 %collective-permute-start.1 = (bf16[2,1,2,128,128]{4,3,2,1,0:T(8,128)(2,1)S(1)}, bf16[2,1,2,128,128]{4,3,2,1,0:T(8,128)(2,1)S(1)}, u32[]{:S(2)}, u32[]{:S(2)}) collective-permute-start(bf16[2,1,2,128,128]{4,3,2,1,0:T(8,128)(2,1)S(1)} %get-tuple-element.39), channel_id=1, source_target_pairs={{0,12},{4,8},{8,4},{12,0},{1,13},{5,9},{9,5},{13,1},{2,14},{6,10},... | collective-permute-start | bytes 393224 | tf_op jit(solution)/shard_map/ppermute | solution.py:402
  40.1 0.0 collective-permute-start.2
  40.1 0.0 collective-permute-done.4.refs_5_.refs_7_
  40.1 1.7 %collective-permute-start.3 = (bf16[2,1,2,128,128]{4,3,2,1,0:T(8,128)(2,1)S(1)}, bf16[2,1,2,128,128]{4,3,2,1,0:T(8,128)(2,1)S(1)}, u32[]{:S(2)}, u32[]{:S(2)}) collective-permute-start(bf16[2,1,2,128,128]{4,3,2,1,0:T(8,128)(2,1)S(1)} %get-tuple-element.41), channel_id=1, source_target_pairs={{0,4},{4,0},{8,12},{12,8},{1,5},{5,1},{9,13},{13,9},{2,6},{6,2},{1... | collective-permute-start | bytes 393224 | tf_op jit(solution)/shard_map/ppermute | solution.py:402
  41.8 3.7 %collective-permute-done.1.refs_1_ = bf16[2,1,2,128,128]{4,3,2,1,0:T(8,128)(2,1)S(1)} collective-permute-done((bf16[2,1,2,128,128]{4,3,2,1,0:T(8,128)(2,1)S(1)}, bf16[2,1,2,128,128]{4,3,2,1,0:T(8,128)(2,1)S(1)}, u32[]{:S(2)}, u32[]{:S(2)}) %collective-permute-start.1) | collective-permute-done | bytes 131104 | tf_op jit(solution)/shard_map/ppermute | solution.py:402
  45.6 1.0 %collective-permute-done.2.refs_2_ = bf16[2,1,2,128,128]{4,3,2,1,0:T(8,128)(2,1)S(1)} collective-permute-done((bf16[2,1,2,128,128]{4,3,2,1,0:T(8,128)(2,1)S(1)}, bf16[2,1,2,128,128]{4,3,2,1,0:T(8,128)(2,1)S(1)}, u32[]{:S(2)}, u32[]{:S(2)}) %collective-permute-start.2) | collective-permute-done | bytes 131104 | tf_op jit(solution)/shard_map/ppermute | solution.py:402
  46.5 1.6 %collective-permute-done.3.refs_3_ = bf16[2,1,2,128,128]{4,3,2,1,0:T(8,128)(2,1)S(1)} collective-permute-done((bf16[2,1,2,128,128]{4,3,2,1,0:T(8,128)(2,1)S(1)}, bf16[2,1,2,128,128]{4,3,2,1,0:T(8,128)(2,1)S(1)}, u32[]{:S(2)}, u32[]{:S(2)}) %collective-permute-start.3) | collective-permute-done | bytes 131104 | tf_op jit(solution)/shard_map/ppermute | solution.py:402
  48.1 0.8 %project.3 = (bf16[1,64,2048]{2,1,0:T(8,128)(2,1)S(1)}, f32[1,64,2048]{2,1,0:T(8,128)S(1)}) custom-call(bf16[2,1,2,128,128]{4,3,2,1,0:T(8,128)(2,1)S(1)} %get-tuple-element.38.refs_0_, bf16[2,1,2,128,128]{4,3,2,1,0:T(8,128)(2,1)S(1)} %collective-permute-done.1.refs_1_, bf16[2,1,2,128,128]{4,3,2,1,0:T(8,128)(2,1)S(1)} %collective-permute-done.2.refs_2_, ...), custom_call_target="tpu_custom_call" | custom-call | flops 1 | bytes 1 | tf_op jit(solution)/shard_map/project/pallas_call | solution.py:408
  48.9 0.1 collective-permute-start.9
  49.0 1.5 %collective-permute-done.9.refs_0_ = bf16[1,64,2048]{2,1,0:T(8,128)(2,1)S(1)} collective-permute-done((bf16[1,64,2048]{2,1,0:T(8,128)(2,1)S(1)}, bf16[1,64,2048]{2,1,0:T(8,128)(2,1)S(1)}, u32[]{:S(2)}, u32[]{:S(2)}) %collective-permute-start.9) | collective-permute-done | bytes 262176 | tf_op jit(solution)/shard_map/ppermute | solution.py:417
  50.5 0.5 collective-permute-start.10
  51.0 0.8 %project.2 = (bf16[1,64,1024]{2,1,0:T(8,128)(2,1)S(1)}, bf16[1,64,1024]{2,1,0:T(8,128)(2,1)S(1)}, f32[1,64,2048]{2,1,0:T(8,128)S(1)}) custom-call(bf16[2,1,2,128,128]{4,3,2,1,0:T(8,128)(2,1)S(1)} %get-tuple-element.38.refs_0_, bf16[2,1,2,128,128]{4,3,2,1,0:T(8,128)(2,1)S(1)} %collective-permute-done.1.refs_1_, ...), custom_call_target="tpu_custom_call" | custom-call | flops 1 | bytes 1 | tf_op jit(solution)/shard_map/project/pallas_call | solution.py:408
  51.8 0.1 collective-permute-start.7
  51.8 0.5 collective-permute-start.8
  52.3 0.8 %collective-permute-done.7.refs_0_ = bf16[1,64,1024]{2,1,0:T(8,128)(2,1)S(1)} collective-permute-done((bf16[1,64,1024]{2,1,0:T(8,128)(2,1)S(1)}, bf16[1,64,1024]{2,1,0:T(8,128)(2,1)S(1)}, u32[]{:S(2)}, u32[]{:S(2)}) %collective-permute-start.7) | collective-permute-done | bytes 131104 | tf_op jit(solution)/shard_map/ppermute | solution.py:417
  53.2 0.2 collective-permute-done.8.refs_1_
  53.4 5.6 %collective-permute-done.10.refs_2_ = bf16[1,64,2048]{2,1,0:T(8,128)(2,1)S(1)} collective-permute-done((bf16[1,64,2048]{2,1,0:T(8,128)(2,1)S(1)}, bf16[1,64,2048]{2,1,0:T(8,128)(2,1)S(1)}, u32[]{:S(2)}, u32[]{:S(2)}) %collective-permute-start.10) | collective-permute-done | bytes 262176 | tf_op jit(solution)/shard_map/ppermute | solution.py:429
  58.9 0.8 %sum.3 = bf16[1,64,2048]{2,1,0:T(8,128)(2,1)} custom-call(f32[1,64,2048]{2,1,0:T(8,128)S(1)} %get-tuple-element.46.keep_ref, bf16[1,64,1024]{2,1,0:T(8,128)(2,1)S(1)} %collective-permute-done.7.refs_0_, bf16[1,64,1024]{2,1,0:T(8,128)(2,1)S(1)} %collective-permute-done.8.refs_1_, bf16[1,64,2048]{2,1,0:T(8,128)(2,1)S(1)} %collective-permute-done.10.refs_2_), custom_call_target="tpu_custom_call" | custom-call | flops 1 | bytes 1 | tf_op jit(solution)/shard_map/sum/pallas_call | solution.py:420
  (7 shorter events, 0.1 us)
Async XLA Ops:
  2.3 6.5 %copy-start.1 = (bf16[64,32,128]{2,1,0:T(8,128)(2,1)S(1)}, bf16[64,32,128]{2,1,0:T(8,128)(2,1)}, u32[]{:S(2)}) copy-start(bf16[64,32,128]{2,1,0:T(8,128)(2,1)} %gate_ref.1) | copy-start | bytes 1572868
  2.3 6.5 %copy-start.2 = (bf16[128]{0:T(256)(128)(2,1)S(1)}, bf16[128]{0:T(256)(128)(2,1)}, u32[]{:S(2)}) copy-start(bf16[128]{0:T(256)(128)(2,1)} %param.12) | copy-start | bytes 772
  2.3 23.4 %all-to-all-start = ((bf16[16,272,128]{2,1,0:T(8,128)(2,1)}), bf16[16,272,128]{2,1,0:T(8,128)(2,1)S(1)}, u32[]{:S(2)}, u32[]{:S(2)}) async-start(bf16[16,272,128]{2,1,0:T(8,128)(2,1)} %pack.1), calls=%async_computation | async-start | bytes 2228224 | tf_op jit(solution)/shard_map/all_to_all | solution.py:329
  30.6 9.5 %collective-permute-start.4 = (bf16[8,64,128]{2,1,0:T(8,128)(2,1)S(1)}, bf16[8,64,128]{2,1,0:T(8,128)(2,1)S(1)}, u32[]{:S(2)}, u32[]{:S(2)}) collective-permute-start(bf16[8,64,128]{2,1,0:T(8,128)(2,1)S(1)} %get-tuple-element.43), channel_id=1, source_target_pairs={{0,1},{1,0},{2,3},{3,2},{4,5},{5,4},{6,7},{7,6},{8,9},{9,8},{10,11... | collective-permute-start | bytes 393224 | tf_op jit(solution)/shard_map/ppermute | solution.py:367
  30.7 7.0 %collective-permute-start = (bf16[2,128,128]{2,1,0:T(8,128)(2,1)S(1)}, bf16[2,128,128]{2,1,0:T(8,128)(2,1)S(1)}, u32[]{:S(2)}, u32[]{:S(2)}) collective-permute-start(bf16[2,128,128]{2,1,0:T(8,128)(2,1)S(1)} %get-tuple-element.32), channel_id=1, source_target_pairs={{0,16},{16,0},{1,17},{17,1},{2,18},{18,2},{3,19},{19,3},{4,20},{20... | collective-permute-start | bytes 196616 | tf_op jit(solution)/shard_map/ppermute | solution.py:364
  33.4 8.5 %collective-permute-start.5 = (bf16[8,64,128]{2,1,0:T(8,128)(2,1)S(1)}, bf16[8,64,128]{2,1,0:T(8,128)(2,1)S(1)}, u32[]{:S(2)}, u32[]{:S(2)}) collective-permute-start(bf16[8,64,128]{2,1,0:T(8,128)(2,1)S(1)} %get-tuple-element.44), channel_id=1, source_target_pairs={{0,2},{1,3},{2,0},{3,1},{4,6},{5,7},{6,4},{7,5},{8,10},{9,11},{10,... | collective-permute-start | bytes 393224 | tf_op jit(solution)/shard_map/ppermute | solution.py:367
  33.4 8.5 %collective-permute-start.6 = (bf16[8,64,128]{2,1,0:T(8,128)(2,1)S(1)}, bf16[8,64,128]{2,1,0:T(8,128)(2,1)S(1)}, u32[]{:S(2)}, u32[]{:S(2)}) collective-permute-start(bf16[8,64,128]{2,1,0:T(8,128)(2,1)S(1)} %get-tuple-element.45), channel_id=1, source_target_pairs={{0,3},{1,2},{2,1},{3,0},{4,7},{5,6},{6,5},{7,4},{8,11},{9,10},{10,... | collective-permute-start | bytes 393224 | tf_op jit(solution)/shard_map/ppermute | solution.py:367
  34.9 13.2 %copy-start = (bf16[1024,2048]{1,0:T(8,128)(2,1)S(1)}, bf16[1024,2048]{1,0:T(8,128)(2,1)}, u32[]{:S(2)}) copy-start(bf16[1024,2048]{1,0:T(8,128)(2,1)} %refs_8_.3) | copy-start | bytes 12582916
  38.3 7.3 %collective-permute-start.1 = (bf16[2,1,2,128,128]{4,3,2,1,0:T(8,128)(2,1)S(1)}, bf16[2,1,2,128,128]{4,3,2,1,0:T(8,128)(2,1)S(1)}, u32[]{:S(2)}, u32[]{:S(2)}) collective-permute-start(bf16[2,1,2,128,128]{4,3,2,1,0:T(8,128)(2,1)S(1)} %get-tuple-element.39), channel_id=1, source_target_pairs={{0,12},{4,8},{8,4},{12,0},{1,13},{5,9},{9,5},{13,1},{2,14},{6,10},... | collective-permute-start | bytes 393224 | tf_op jit(solution)/shard_map/ppermute | solution.py:402
  40.1 6.4 %collective-permute-start.2 = (bf16[2,1,2,128,128]{4,3,2,1,0:T(8,128)(2,1)S(1)}, bf16[2,1,2,128,128]{4,3,2,1,0:T(8,128)(2,1)S(1)}, u32[]{:S(2)}, u32[]{:S(2)}) collective-permute-start(bf16[2,1,2,128,128]{4,3,2,1,0:T(8,128)(2,1)S(1)} %get-tuple-element.40), channel_id=1, source_target_pairs={{0,8},{4,12},{8,0},{12,4},{1,9},{5,13},{9,1},{13,5},{2,10},{6,14},... | collective-permute-start | bytes 393224 | tf_op jit(solution)/shard_map/ppermute | solution.py:402
  40.1 7.9 %collective-permute-start.3 = (bf16[2,1,2,128,128]{4,3,2,1,0:T(8,128)(2,1)S(1)}, bf16[2,1,2,128,128]{4,3,2,1,0:T(8,128)(2,1)S(1)}, u32[]{:S(2)}, u32[]{:S(2)}) collective-permute-start(bf16[2,1,2,128,128]{4,3,2,1,0:T(8,128)(2,1)S(1)} %get-tuple-element.41), channel_id=1, source_target_pairs={{0,4},{4,0},{8,12},{12,8},{1,5},{5,1},{9,13},{13,9},{2,6},{6,2},{1... | collective-permute-start | bytes 393224 | tf_op jit(solution)/shard_map/ppermute | solution.py:402
  48.9 1.6 %collective-permute-start.9 = (bf16[1,64,2048]{2,1,0:T(8,128)(2,1)S(1)}, bf16[1,64,2048]{2,1,0:T(8,128)(2,1)S(1)}, u32[]{:S(2)}, u32[]{:S(2)}) collective-permute-start(bf16[1,64,2048]{2,1,0:T(8,128)(2,1)S(1)} %get-tuple-element.50), channel_id=1, source_target_pairs={{0,1},{1,0},{2,3},{3,2},{4,5},{5,4},{6,7},{7,6},{8,9},{9,8},{10,11... | collective-permute-start | bytes 786440 | tf_op jit(solution)/shard_map/ppermute | solution.py:417
  50.5 8.4 %collective-permute-start.10 = (bf16[1,64,2048]{2,1,0:T(8,128)(2,1)S(1)}, bf16[1,64,2048]{2,1,0:T(8,128)(2,1)S(1)}, u32[]{:S(2)}, u32[]{:S(2)}) collective-permute-start(bf16[1,64,2048]{2,1,0:T(8,128)(2,1)S(1)} %sum.2), channel_id=1, source_target_pairs={{0,2},{1,3},{2,0},{3,1},{4,6},{5,7},{6,4},{7,5},{8,10},{9,11},{10,... | collective-permute-start | bytes 786440 | tf_op jit(solution)/shard_map/ppermute | solution.py:429
  51.8 1.4 %collective-permute-start.7 = (bf16[1,64,1024]{2,1,0:T(8,128)(2,1)S(1)}, bf16[1,64,1024]{2,1,0:T(8,128)(2,1)S(1)}, u32[]{:S(2)}, u32[]{:S(2)}) collective-permute-start(bf16[1,64,1024]{2,1,0:T(8,128)(2,1)S(1)} %get-tuple-element.47), channel_id=1, source_target_pairs={{0,1},{1,0},{2,3},{3,2},{4,5},{5,4},{6,7},{7,6},{8,9},{9,8},{10,11... | collective-permute-start | bytes 393224 | tf_op jit(solution)/shard_map/ppermute | solution.py:417
  51.8 1.5 %collective-permute-start.8 = (bf16[1,64,1024]{2,1,0:T(8,128)(2,1)S(1)}, bf16[1,64,1024]{2,1,0:T(8,128)(2,1)S(1)}, u32[]{:S(2)}, u32[]{:S(2)}) collective-permute-start(bf16[1,64,1024]{2,1,0:T(8,128)(2,1)S(1)} %get-tuple-element.48), channel_id=1, source_target_pairs={{0,1},{1,0},{2,3},{3,2},{4,5},{5,4},{6,7},{7,6},{8,9},{9,8},{10,11... | collective-permute-start | bytes 393224 | tf_op jit(solution)/shard_map/ppermute | solution.py:417

commit v3 on v2

--- a/solution.py
+++ b/solution.py
@@ -108,42 +108,27 @@
 
 def block_inverse(below):
     size = below[0].shape[0]
-    half = size // 2
-    rows = lax.broadcasted_iota(jnp.int32, (half, size), 0)
-    cols = lax.broadcasted_iota(jnp.int32, (half, size), 1)
-    first = cols < half
-    cols = cols % half
-
-    def stacked(wide):
-        return jnp.concatenate(parts_of(wide, 2), axis=0)
-
-    def side(tall):
-        return jnp.where(first, tall[:half], tall[half:])
-
-    systems = [side(matrix) for matrix in below]
+    rows = lax.broadcasted_iota(jnp.int32, (size, size), 0)
+    cols = lax.broadcasted_iota(jnp.int32, (size, size), 1)
+    zero = jnp.zeros((size, size), F32)
     step = 1
     solved = None
-    while step < half:
+    while step < size:
         joins = (rows // (2 * step) == cols // (2 * step)) & (rows // step > cols // step)
-        parts = [jnp.where(joins, system, 0.0) for system in systems]
+        parts = [jnp.where(joins, matrix, zero) for matrix in below]
         if step == 1:
-            solved = [jnp.where(rows == cols, 1.0, -part).astype(BF16) for part in parts]
+            solved = [
+                jnp.where(rows == cols, jnp.ones_like(zero), -part).astype(BF16) for part in parts
+            ]
         else:
-            inner = [side(dot(stacked(part).astype(BF16), now)).astype(BF16) for part, now in zip(parts, solved)]
-            solved = [now - side(dot(stacked(now), mid)).astype(BF16) for now, mid in zip(solved, inner)]
+            inner = [dot(part.astype(BF16), now).astype(BF16) for part, now in zip(parts, solved)]
+            solved = [now - dot(now, mid).astype(BF16) for now, mid in zip(solved, inner)]
         step *= 2
-    joined = []
-    for matrix, now in zip(below, solved):
-        inner = dot(matrix[half:, :half].astype(BF16), now).astype(BF16)
-        outer = dot(now[:, half:], inner).astype(BF16)
-        zero = jnp.zeros_like(now)
-        joined.append(jnp.concatenate([jnp.where(first, now, zero), jnp.where(first, -outer, now)], axis=0))
-    return joined
-
-
-def factor_kernel(tokens, ratio, n_head, got_ref, *refs):
-    state_ref, both_ref, trans_ref, prefix_ref = refs[n_head : n_head + 4]
-    add_ref = refs[-1]
+    return solved
+
+
+def factor_kernel(tokens, ratio, n_head, total_too, got_ref, *refs):
+    state_ref, w_ref, u_ref, *tree_refs = refs[n_head : len(refs) - n_head]
     width = got_ref.shape[-1]
     per = SPAN // tokens
     blocks = got_ref.shape[0] // per
@@ -170,68 +155,101 @@
             strengths.append(strength)
         held.append((block, key, key_col, key_row, strengths))
     solved = block_inverse(below)
-    for number, (block, key, key_col, key_row, strengths) in enumerate(held):
-        weighted = [
-            inverse.astype(F32) * key_col * strength
-            for inverse, strength in zip(solved[number * ratio : (number + 1) * ratio], strengths)
-        ]
-        w_all = dot(jnp.concatenate([(part * key_row).astype(BF16) for part in weighted], axis=0), key).astype(BF16)
-        key_t = key.T
-        for r, part in enumerate(weighted):
-            value = block_rows(got_ref, block, per, tokens, 2 + r)
-            u_now = dot(part.astype(BF16), value).astype(BF16)
-            both = beside([w_all[r * SPAN : (r + 1) * SPAN], u_now])
-            both_ref[block, r] = both
-            trans, add = parts_of(dot(key_t, both), 2)
-            trans_ref[block, r] = trans.astype(BF16)
-            add_ref[block, r] = add
-
-    states = [jnp.zeros((width, width), F32) for r in range(ratio)]
+    flat = [(block, r) for block in range(blocks) for r in range(ratio)]
+    weighted = []
+    for inverse, (block, r) in zip(solved, flat):
+        unused, key, key_col, key_row, strengths = held[block]
+        weighted.append(inverse.astype(F32) * key_col * strengths[r])
+    for part, (block, r) in zip(weighted, flat):
+        value = block_rows(got_ref, block, per, tokens, 2 + r)
+        u_ref[block, r] = dot(part.astype(BF16), value)
+    for part, (block, r) in zip(weighted, flat):
+        unused, key, key_col, key_row, strengths = held[block]
+        w_ref[block, r] = dot((part * key_row).astype(BF16), key).astype(BF16)
+    turns, adds = [], []
     for block in range(blocks):
+        key_t = held[block][1].T
         for r in range(ratio):
-            held = states[r].astype(BF16)
-            prefix_ref[block, r] = held
-            if block == 0:
-                states[r] = add_ref[block, r]
+            turn, add = parts_of(dot(key_t, beside([w_ref[block, r], u_ref[block, r].astype(BF16)])), 2)
+            turns.append(turn)
+            adds.append(add)
+
+    level = 0
+    while len(adds) > ratio:
+        count = len(adds) // ratio
+        trans_ref, add_ref = tree_refs[2 * level : 2 * level + 2]
+        for number in range(len(adds)):
+            trans_ref[number // ratio, number % ratio] = turns[number].astype(BF16)
+            add_ref[number // ratio, number % ratio] = adds[number]
+        longer_turns, longer_adds = [], []
+        for pair in range(count // 2):
+            for r in range(ratio):
+                left, right = 2 * pair * ratio + r, (2 * pair + 1) * ratio + r
+                if count > 2 or total_too:
+                    both = beside([turns[left], adds[left]])
+                    turn, add = parts_of(both - dot(turns[right].astype(BF16), both.astype(BF16)), 2)
+                    longer_turns.append(turns[right] + turn)
+                else:
+                    add = adds[left] - dot(turns[right].astype(BF16), adds[left].astype(BF16))
+                longer_adds.append(add + adds[right])
+        turns, adds = longer_turns, longer_adds
+        level += 1
+    for r in range(ratio):
+        state_ref[r] = adds[r].astype(state_ref.dtype)
+        if total_too:
+            tree_refs[-1][r] = turns[r]
+
+
+def tree_starts(ratio, width, tree_refs):
+    rows = lax.broadcasted_iota(jnp.int32, (width, 2 * width), 0)
+    cols = lax.broadcasted_iota(jnp.int32, (width, 2 * width), 1)
+    neutral = jnp.where(cols == rows + width, 1.0, 0.0).astype(F32)
+    starts = [None] * ratio
+    for level in reversed(range(len(tree_refs) // 2)):
+        trans_ref, add_ref = tree_refs[2 * level : 2 * level + 2]
+        longer = []
+        for number, start in enumerate(starts):
+            place, r = 2 * (number // ratio), number % ratio
+            add = beside([add_ref[place, r], jnp.zeros((width, width), F32)])
+            if start is None:
+                turn = beside([jnp.zeros((width, width), F32), trans_ref[place, r].astype(F32)])
+                longer.append((start, neutral - turn + add))
             else:
-                states[r] = states[r] + add_ref[block, r] - dot(trans_ref[block, r], held)
-    for r in range(ratio):
-        state_ref[r] = states[r].astype(state_ref.dtype)
-
-
-def spread_kernel(
-    tokens, ratio, total_too, got_ref, both_ref, trans_ref, prefix_ref, local_ref, reach_ref, total_ref
-):
+                longer.append((start, start - dot(trans_ref[place, r], start.astype(BF16)) + add))
+        starts = []
+        for pair in range(len(longer) // ratio):
+            for side in range(2):
+                starts += [longer[pair * ratio + r][side] for r in range(ratio)]
+    return [neutral if start is None else start for start in starts]
+
+
+def spread_kernel(tokens, ratio, got_ref, w_ref, u_ref, *refs):
+    tree_refs, (local_ref, reach_ref) = refs[:-2], refs[-2:]
     width = got_ref.shape[-1]
     per = SPAN // tokens
     blocks = got_ref.shape[0] // per
     rows = lax.broadcasted_iota(jnp.int32, (SPAN, SPAN), 0)
     cols = lax.broadcasted_iota(jnp.int32, (SPAN, SPAN), 1)
-    wide_rows = lax.broadcasted_iota(jnp.int32, (width, width), 0)
-    wide_cols = lax.broadcasted_iota(jnp.int32, (width, width), 1)
-    identity = jnp.where(wide_rows == wide_cols, 1.0, 0.0).astype(F32)
-    carried = [identity for r in range(ratio)]
+    starts = [start.astype(BF16) for start in tree_starts(ratio, width, tree_refs)]
+    lefts, units = [], []
     for block in range(blocks):
         query = block_rows(got_ref, block, per, tokens, 0)
         key = block_rows(got_ref, block, per, tokens, 1)
         scores = jnp.where(rows >= cols, dot_nt(query, key), 0.0).astype(BF16)
         query_f = query.astype(F32)
         squares = jnp.sum(query_f * query_f, 1, keepdims=True)
-        unit = lax.rsqrt(squares + EPSILON) * width ** (-0.5)
-        passed = dot(scores, beside([both_ref[block, r] for r in range(ratio)]))
-        for r, part in enumerate(parts_of(passed, ratio)):
-            through, added = parts_of(part, 2)
-            held = carried[r].astype(BF16)
-            if block == 0:
-                carried[r] = identity - trans_ref[block, r].astype(F32)
-            elif total_too or block < blocks - 1:
-                carried[r] = carried[r] - dot(trans_ref[block, r], held)
-            starts = beside([prefix_ref[block, r], held])
-            out = dot((query_f - through).astype(BF16), starts)
-            local_ref[r, block] = (out[:, :width] + added) * unit
-            reach_ref[r, block] = (out[:, width:] * unit).astype(BF16)
-    for r in range(ratio):
-        total_ref[r] = carried[r]
+        units.append(lax.rsqrt(squares + EPSILON) * width ** (-0.5))
+        lefts.append(beside([query, scores]))
+    flat = [(block, r) for block in range(blocks) for r in range(ratio)]
+    rights = []
+    for start, (block, r) in zip(starts, flat):
+        through, reached = parts_of(dot(w_ref[block, r], start), 2)
+        corrected = beside([u_ref[block, r] - through, -reached]).astype(BF16)
+        rights.append(jnp.concatenate([start, corrected], axis=0))
+    for right, (block, r) in zip(rights, flat):
+        out = dot(lefts[block], right) * units[block]
+        local_ref[r, block] = out[:, :width]
+        reach_ref[r, block] = out[:, width:].astype(BF16)
 
 
 def join_kernel(order, state_ref, local_ref, reach_ref, *out_refs):
@@ -341,24 +359,30 @@
         )(output_gate, norm_gain.reshape(1, width))
 
     state_type = BF16 if outer == 2 else F32
-    square = (blocks, ratio, width, width)
     with jax.named_scope("factors"):
-        state, both, trans, prefix, *gates = pl.pallas_call(
-            functools.partial(factor_kernel, tokens, ratio, n_head),
-            out_shape=[
-                shape((ratio, width, width), state_type),
-                shape((blocks, ratio, SPAN, 2 * width), BF16),
-                shape(square, BF16),
-                shape(square, BF16),
-            ]
-            + [shape((heads, tokens, width), BF16)] * n_head,
+        depths = []
+        while blocks >> len(depths) > 1:
+            depths.append(blocks >> len(depths))
+        tree = []
+        for depth in depths:
+            tree += [shape((depth, ratio, width, width), BF16), shape((depth, ratio, width, width), F32)]
+        if outer > 2:
+            tree.append(shape((ratio, width, width), F32))
+        out_shape = [
+            shape((ratio, width, width), state_type),
+            shape((blocks, ratio, SPAN, width), BF16),
+            shape((blocks, ratio, SPAN, width), F32),
+        ] + tree
+        state, w, u, *rest = pl.pallas_call(
+            functools.partial(factor_kernel, tokens, ratio, n_head, outer > 2),
+            out_shape=out_shape + [shape((heads, tokens, width), BF16)] * n_head,
             in_specs=[VMEM] + [ANY] * n_head,
-            out_specs=[VMEM] * 4 + [ANY] * n_head,
-            input_output_aliases={1 + number: 4 + number for number in range(n_head)},
-            scratch_shapes=[pltpu.VMEM(square, F32)],
+            out_specs=[VMEM] * len(out_shape) + [ANY] * n_head,
+            input_output_aliases={1 + number: len(out_shape) + number for number in range(n_head)},
             compiler_params=params(),
             cost_estimate=LIGHT,
         )(got, *gates)
+        tree, gates = rest[:-n_head], rest[-n_head:]
 
     onward = [(here, (here + 1) % outer) for here in range(outer)]
     incoming = lax.ppermute(state, "outer", onward)
@@ -366,22 +390,21 @@
         pairs = [(here, here ^ distance) for here in range(n_head)]
         gates[distance] = lax.ppermute(gates[distance], "head", pairs)
     with jax.named_scope("spread"):
-        local, reach, total = pl.pallas_call(
-            functools.partial(spread_kernel, tokens, ratio, outer > 2),
+        local, reach = pl.pallas_call(
+            functools.partial(spread_kernel, tokens, ratio),
             out_shape=[
                 shape((ratio, blocks, SPAN, width), F32),
                 shape((ratio, blocks, SPAN, width), BF16),
-                shape((ratio, width, width), F32),
             ],
-            in_specs=[VMEM] * 4,
-            out_specs=[VMEM] * 3,
+            in_specs=[VMEM] * (3 + 2 * len(depths)),
+            out_specs=[VMEM] * 2,
             compiler_params=params(),
             cost_estimate=LIGHT,
-        )(got, both, trans, prefix)
+        )(got, w, u, *tree[: 2 * len(depths)])
     for hop in range(outer - 2):
         incoming = jnp.where(lax.axis_index("outer") == 0, 0.0, incoming)
-        passed = jnp.einsum("hde,hef->hdf", total, incoming, precision=lax.Precision.HIGHEST)
-        incoming = lax.ppermute(state + passed, "outer", onward)
+        turned_by = jnp.einsum("hde,hef->hdf", tree[-1], incoming, precision=lax.Precision.HIGHEST)
+        incoming = lax.ppermute(state + incoming - turned_by, "outer", onward)
 
     pieces = shard_tokens // SPAN // 2
     columns = output_weight.shape[1]

time: 59.9 us -> 57.5 us (0.960)
  Pallas kernels: 13.6 us -> 10.2 us
  waiting for transfers between devices: 30.6 us -> 32 us
    pallas_call x2, Pallas kernels: 7.8 us -> 4.45 us  [the longest x1 3.38 us: per_device(): pl.pallas_call(functools.partial(factor_kernel, tokens, ratio, n_head, ou...]
    ppermute x1, waiting for transfers between devices: 0.01 us -> 1.5 us  [per_device(): incoming = lax.ppermute(state, 'outer', onward)]
  transfers between devices with their start and end apart: 12 -> 12, of which waited for: 8 -> 8; matrix products, arithmetic and copies ran while one was open for 0% -> 0% of each run, Pallas kernels for 8% -> 5%
where the time goes in v3:
time: 57.5 us; the launch traced here: 57.3 us
  waiting for transfers between devices  32 us (56%)
  starting transfers between devices  15 us (26%)
  Pallas kernels  10.2 us (18%)
    all_to_all x1, waiting for transfers between devices, per_device(): lax.all_to_all(packed, ('sub', 'head'), split_axis=0, concat_axis=0, tile...  16.3 us
    all_to_all x1, starting transfers between devices, per_device(): lax.all_to_all(packed, ('sub', 'head'), split_axis=0, concat_axis=0, tile...  6.43 us
    ppermute x1, waiting for transfers between devices, per_device(): lax.ppermute(summed, 'head', [(here, here ^ half) for here in range(n_hea...  5.94 us
    ppermute x3, waiting for transfers between devices, per_device(): lax.ppermute(part, 'sub', [(here, here ^ distance) for here in range(sub)])  5.67 us
    ppermute x3, starting transfers between devices, per_device(): lax.ppermute(part, 'sub', [(here, here ^ distance) for here in range(sub)])  3.55 us
    pallas_call x1, Pallas kernels, per_device(): pl.pallas_call(functools.partial(factor_kernel, tokens, ratio, n_head, ou...  3.38 us
    ppermute x1, starting transfers between devices, per_device(): incoming = lax.ppermute(state, 'outer', onward)  2.67 us
    ppermute x3, waiting for transfers between devices, per_device(): arrived = [lax.ppermute(send, 'head', by_core) for send in sends]  2.54 us
  transfers between devices with their start and end apart: 12, of which 8 were waited for; matrix products, arithmetic and copies ran while one was open for 0% of the time, Pallas kernels for 5%

profile of v3, /device:TPU:0, one launch (start us, length us, event | category | flops | bytes accessed | tf_op | source)
XLA Modules:
  0.0 57.3 jit_solution(8602519791553261355)
XLA Ops:
  0.0 2.3 %pack.1 = bf16[16,272,128]{2,1,0:T(8,128)(2,1)} custom-call(bf16[64,16,128]{2,1,0:T(8,128)(2,1)} %q_hbm.1, bf16[64,16,128]{2,1,0:T(8,128)(2,1)} %k_hbm.1, bf16[64,32,128]{2,1,0:T(8,128)(2,1)} %v_hbm.1, bf16[32,64]{1,0:T(8,128)(2,1)} %bitcast.4), custom_call_target="tpu_custom_call" | custom-call | tf_op jit(solution)/shard_map/pack/pallas_call | solution.py:331
  2.3 0.0 copy-start.1
  2.3 0.0 copy-start.2
  2.3 6.4 %all-to-all-start = ((bf16[16,272,128]{2,1,0:T(8,128)(2,1)}), bf16[16,272,128]{2,1,0:T(8,128)(2,1)S(1)}, u32[]{:S(2)}, u32[]{:S(2)}) async-start(bf16[16,272,128]{2,1,0:T(8,128)(2,1)} %pack.1), calls=%async_computation | async-start | bytes 2228224 | tf_op jit(solution)/shard_map/all_to_all | solution.py:347
  8.7 0.6 %gates.1 = (bf16[8,64,128]{2,1,0:T(8,128)(2,1)S(1)}, bf16[8,64,128]{2,1,0:T(8,128)(2,1)S(1)}, bf16[8,64,128]{2,1,0:T(8,128)(2,1)S(1)}, bf16[8,64,128]{2,1,0:T(8,128)(2,1)S(1)}) custom-call(bf16[64,32,128]{2,1,0:T(8,128)(2,1)S(1)} %copy-done.1, bf16[1,128]{1,0:T(2,128)(2,1)S(1)} %bitcast.3), custom_call_target="tpu_custom_call" | custom-call | flops 1 | bytes 1 | tf_op jit(solution)/shard_map/gates/pallas_call | solution.py:351
  9.3 16.3 %all-to-all-done.got_ref = bf16[16,272,128]{2,1,0:T(8,128)(2,1)S(1)} async-done(((bf16[16,272,128]{2,1,0:T(8,128)(2,1)}), bf16[16,272,128]{2,1,0:T(8,128)(2,1)S(1)}, u32[]{:S(2)}, u32[]{:S(2)}) %all-to-all-start) | async-done | bytes 1114144 | tf_op jit(solution)/shard_map/all_to_all | solution.py:347
  25.7 3.4 %factors.1 = (bf16[2,128,128]{2,1,0:T(8,128)(2,1)S(1)}, bf16[8,2,128,128]{3,2,1,0:T(8,128)(2,1)S(1)}, f32[8,2,128,128]{3,2,1,0:T(8,128)S(1)}, bf16[8,2,128,128]{...) custom-call(bf16[16,272,128]{2,1,0:T(8,128)(2,1)S(1)} %all-to-all-do, ...), custom_call_target="tpu_custom_call", output_to_operand_aliasing={{9}: (1, {}), {10}: (2, {}), {11}: (3, {}), {12}: (4, {})} | custom-call | flops 1 | bytes 1 | tf_op jit(solution)/shard_map/factors/pallas_call | solution.py:376
  29.1 0.1 collective-permute-start.4
  29.1 2.7 %collective-permute-start = (bf16[2,128,128]{2,1,0:T(8,128)(2,1)S(1)}, bf16[2,128,128]{2,1,0:T(8,128)(2,1)S(1)}, u32[]{:S(2)}, u32[]{:S(2)}) collective-permute-start(bf16[2,128,128]{2,1,0:T(8,128)(2,1)S(1)} %get-tuple-element.37), channel_id=1, source_target_pairs={{0,16},{16,0},{1,17},{17,1},{2,18},{18,2},{3,19},{19,3},{4,20},{20... | collective-permute-start | bytes 196616 | tf_op jit(solution)/shard_map/ppermute | solution.py:388
  31.8 0.0 collective-permute-start.5
  31.8 1.5 %collective-permute-start.6 = (bf16[8,64,128]{2,1,0:T(8,128)(2,1)S(1)}, bf16[8,64,128]{2,1,0:T(8,128)(2,1)S(1)}, u32[]{:S(2)}, u32[]{:S(2)}) collective-permute-start(bf16[8,64,128]{2,1,0:T(8,128)(2,1)S(1)} %get-tuple-element.55), channel_id=1, source_target_pairs={{0,3},{1,2},{2,1},{3,0},{4,7},{5,6},{6,5},{7,4},{8,11},{9,10},{10,... | collective-permute-start | bytes 393224 | tf_op jit(solution)/shard_map/ppermute | solution.py:391
  33.3 1.1 %spread.1 = (f32[2,8,128,128]{3,2,1,0:T(8,128)S(1)}, bf16[2,8,128,128]{3,2,1,0:T(8,128)(2,1)S(1)}) custom-call(bf16[16,272,128]{2,1,0:T(8,128)(2,1)S(1)} %all-to-all-done.got_ref, bf16[8,2,128,128]{3,2,1,0:T(8,128)(2,1)S(1)} %get-tuple-element.38.w_ref, f32[8,2,128,128]{3,2,1,0:T(8,128)S(1)} %get-tuple-element.39.u_ref, ...), custom_call_target="tpu_custom_call" | custom-call | flops 1 | bytes 1 | tf_op jit(solution)/shard_map/spread/pallas_call | solution.py:393
  34.4 1.5 %collective-permute-done.state_ref = bf16[2,128,128]{2,1,0:T(8,128)(2,1)S(1)} collective-permute-done((bf16[2,128,128]{2,1,0:T(8,128)(2,1)S(1)}, bf16[2,128,128]{2,1,0:T(8,128)(2,1)S(1)}, u32[]{:S(2)}, u32[]{:S(2)}) %collective-permute-start) | collective-permute-done | bytes 65568 | tf_op jit(solution)/shard_map/ppermute | solution.py:388
  35.9 0.5 join.1
  36.4 0.5 collective-permute-start.1
  36.9 0.0 collective-permute-start.2
  36.9 0.0 collective-permute-done.4.refs_5_.refs_7_
  36.9 3.1 %collective-permute-start.3 = (bf16[2,1,2,128,128]{4,3,2,1,0:T(8,128)(2,1)S(1)}, bf16[2,1,2,128,128]{4,3,2,1,0:T(8,128)(2,1)S(1)}, u32[]{:S(2)}, u32[]{:S(2)}) collective-permute-start(bf16[2,1,2,128,128]{4,3,2,1,0:T(8,128)(2,1)S(1)} %get-tuple-element.51), channel_id=1, source_target_pairs={{0,4},{4,0},{8,12},{12,8},{1,5},{5,1},{9,13},{13,9},{2,6},{6,2},{1... | collective-permute-start | bytes 393224 | tf_op jit(solution)/shard_map/ppermute | solution.py:425
  40.0 3.8 %collective-permute-done.1.refs_1_ = bf16[2,1,2,128,128]{4,3,2,1,0:T(8,128)(2,1)S(1)} collective-permute-done((bf16[2,1,2,128,128]{4,3,2,1,0:T(8,128)(2,1)S(1)}, bf16[2,1,2,128,128]{4,3,2,1,0:T(8,128)(2,1)S(1)}, u32[]{:S(2)}, u32[]{:S(2)}) %collective-permute-start.1) | collective-permute-done | bytes 131104 | tf_op jit(solution)/shard_map/ppermute | solution.py:425
  43.8 0.0 collective-permute-done.2.refs_2_
  43.8 1.9 %collective-permute-done.3.refs_3_ = bf16[2,1,2,128,128]{4,3,2,1,0:T(8,128)(2,1)S(1)} collective-permute-done((bf16[2,1,2,128,128]{4,3,2,1,0:T(8,128)(2,1)S(1)}, bf16[2,1,2,128,128]{4,3,2,1,0:T(8,128)(2,1)S(1)}, u32[]{:S(2)}, u32[]{:S(2)}) %collective-permute-start.3) | collective-permute-done | bytes 131104 | tf_op jit(solution)/shard_map/ppermute | solution.py:425
  45.7 0.8 %project.3 = (bf16[1,64,2048]{2,1,0:T(8,128)(2,1)S(1)}, f32[1,64,2048]{2,1,0:T(8,128)S(1)}) custom-call(bf16[2,1,2,128,128]{4,3,2,1,0:T(8,128)(2,1)S(1)} %get-tuple-element.48.refs_0_, bf16[2,1,2,128,128]{4,3,2,1,0:T(8,128)(2,1)S(1)} %collective-permute-done.1.refs_1_, bf16[2,1,2,128,128]{4,3,2,1,0:T(8,128)(2,1)S(1)} %collective-permute-done.2.refs_2_, ...), custom_call_target="tpu_custom_call" | custom-call | flops 1 | bytes 1 | tf_op jit(solution)/shard_map/project/pallas_call | solution.py:431
  46.5 0.1 collective-permute-start.9
  46.5 1.5 %collective-permute-done.9.refs_0_ = bf16[1,64,2048]{2,1,0:T(8,128)(2,1)S(1)} collective-permute-done((bf16[1,64,2048]{2,1,0:T(8,128)(2,1)S(1)}, bf16[1,64,2048]{2,1,0:T(8,128)(2,1)S(1)}, u32[]{:S(2)}, u32[]{:S(2)}) %collective-permute-start.9) | collective-permute-done | bytes 262176 | tf_op jit(solution)/shard_map/ppermute | solution.py:440
  48.1 0.1 collective-permute-start.10
  48.2 0.8 %project.2 = (bf16[1,64,1024]{2,1,0:T(8,128)(2,1)S(1)}, bf16[1,64,1024]{2,1,0:T(8,128)(2,1)S(1)}, f32[1,64,2048]{2,1,0:T(8,128)S(1)}) custom-call(bf16[2,1,2,128,128]{4,3,2,1,0:T(8,128)(2,1)S(1)} %get-tuple-element.48.refs_0_, bf16[2,1,2,128,128]{4,3,2,1,0:T(8,128)(2,1)S(1)} %collective-permute-done.1.refs_1_, ...), custom_call_target="tpu_custom_call" | custom-call | flops 1 | bytes 1 | tf_op jit(solution)/shard_map/project/pallas_call | solution.py:431
  49.0 0.2 collective-permute-start.7
  49.2 0.4 collective-permute-start.8
  49.6 0.8 %collective-permute-done.7.refs_0_ = bf16[1,64,1024]{2,1,0:T(8,128)(2,1)S(1)} collective-permute-done((bf16[1,64,1024]{2,1,0:T(8,128)(2,1)S(1)}, bf16[1,64,1024]{2,1,0:T(8,128)(2,1)S(1)}, u32[]{:S(2)}, u32[]{:S(2)}) %collective-permute-start.7) | collective-permute-done | bytes 131104 | tf_op jit(solution)/shard_map/ppermute | solution.py:440
  50.4 0.2 collective-permute-done.8.refs_1_
  50.6 5.9 %collective-permute-done.10.refs_2_ = bf16[1,64,2048]{2,1,0:T(8,128)(2,1)S(1)} collective-permute-done((bf16[1,64,2048]{2,1,0:T(8,128)(2,1)S(1)}, bf16[1,64,2048]{2,1,0:T(8,128)(2,1)S(1)}, u32[]{:S(2)}, u32[]{:S(2)}) %collective-permute-start.10) | collective-permute-done | bytes 262176 | tf_op jit(solution)/shard_map/ppermute | solution.py:452
  56.5 0.8 %sum.3 = bf16[1,64,2048]{2,1,0:T(8,128)(2,1)} custom-call(f32[1,64,2048]{2,1,0:T(8,128)S(1)} %get-tuple-element.56.keep_ref, bf16[1,64,1024]{2,1,0:T(8,128)(2,1)S(1)} %collective-permute-done.7.refs_0_, bf16[1,64,1024]{2,1,0:T(8,128)(2,1)S(1)} %collective-permute-done.8.refs_1_, bf16[1,64,2048]{2,1,0:T(8,128)(2,1)S(1)} %collective-permute-done.10.refs_2_), custom_call_target="tpu_custom_call" | custom-call | flops 1 | bytes 1 | tf_op jit(solution)/shard_map/sum/pallas_call | solution.py:443
  (7 shorter events, 0.1 us)
Async XLA Ops:
  2.3 6.5 %copy-start.1 = (bf16[64,32,128]{2,1,0:T(8,128)(2,1)S(1)}, bf16[64,32,128]{2,1,0:T(8,128)(2,1)}, u32[]{:S(2)}) copy-start(bf16[64,32,128]{2,1,0:T(8,128)(2,1)} %gate_ref.1) | copy-start | bytes 1572868
  2.3 6.5 %copy-start.2 = (bf16[128]{0:T(256)(128)(2,1)S(1)}, bf16[128]{0:T(256)(128)(2,1)}, u32[]{:S(2)}) copy-start(bf16[128]{0:T(256)(128)(2,1)} %param.12) | copy-start | bytes 772
  2.3 23.4 %all-to-all-start = ((bf16[16,272,128]{2,1,0:T(8,128)(2,1)}), bf16[16,272,128]{2,1,0:T(8,128)(2,1)S(1)}, u32[]{:S(2)}, u32[]{:S(2)}) async-start(bf16[16,272,128]{2,1,0:T(8,128)(2,1)} %pack.1), calls=%async_computation | async-start | bytes 2228224 | tf_op jit(solution)/shard_map/all_to_all | solution.py:347
  29.1 7.9 %collective-permute-start.4 = (bf16[8,64,128]{2,1,0:T(8,128)(2,1)S(1)}, bf16[8,64,128]{2,1,0:T(8,128)(2,1)S(1)}, u32[]{:S(2)}, u32[]{:S(2)}) collective-permute-start(bf16[8,64,128]{2,1,0:T(8,128)(2,1)S(1)} %get-tuple-element.53), channel_id=1, source_target_pairs={{0,1},{1,0},{2,3},{3,2},{4,5},{5,4},{6,7},{7,6},{8,9},{9,8},{10,11... | collective-permute-start | bytes 393224 | tf_op jit(solution)/shard_map/ppermute | solution.py:391
  29.1 6.8 %collective-permute-start = (bf16[2,128,128]{2,1,0:T(8,128)(2,1)S(1)}, bf16[2,128,128]{2,1,0:T(8,128)(2,1)S(1)}, u32[]{:S(2)}, u32[]{:S(2)}) collective-permute-start(bf16[2,128,128]{2,1,0:T(8,128)(2,1)S(1)} %get-tuple-element.37), channel_id=1, source_target_pairs={{0,16},{16,0},{1,17},{17,1},{2,18},{18,2},{3,19},{19,3},{4,20},{20... | collective-permute-start | bytes 196616 | tf_op jit(solution)/shard_map/ppermute | solution.py:388
  31.8 8.2 %collective-permute-start.5 = (bf16[8,64,128]{2,1,0:T(8,128)(2,1)S(1)}, bf16[8,64,128]{2,1,0:T(8,128)(2,1)S(1)}, u32[]{:S(2)}, u32[]{:S(2)}) collective-permute-start(bf16[8,64,128]{2,1,0:T(8,128)(2,1)S(1)} %get-tuple-element.54), channel_id=1, source_target_pairs={{0,2},{1,3},{2,0},{3,1},{4,6},{5,7},{6,4},{7,5},{8,10},{9,11},{10,... | collective-permute-start | bytes 393224 | tf_op jit(solution)/shard_map/ppermute | solution.py:391
  31.8 8.2 %collective-permute-start.6 = (bf16[8,64,128]{2,1,0:T(8,128)(2,1)S(1)}, bf16[8,64,128]{2,1,0:T(8,128)(2,1)S(1)}, u32[]{:S(2)}, u32[]{:S(2)}) collective-permute-start(bf16[8,64,128]{2,1,0:T(8,128)(2,1)S(1)} %get-tuple-element.55), channel_id=1, source_target_pairs={{0,3},{1,2},{2,1},{3,0},{4,7},{5,6},{6,5},{7,4},{8,11},{9,10},{10,... | collective-permute-start | bytes 393224 | tf_op jit(solution)/shard_map/ppermute | solution.py:391
  33.3 12.3 %copy-start = (bf16[1024,2048]{1,0:T(8,128)(2,1)S(1)}, bf16[1024,2048]{1,0:T(8,128)(2,1)}, u32[]{:S(2)}) copy-start(bf16[1024,2048]{1,0:T(8,128)(2,1)} %refs_8_.3) | copy-start | bytes 12582916
  36.4 7.3 %collective-permute-start.1 = (bf16[2,1,2,128,128]{4,3,2,1,0:T(8,128)(2,1)S(1)}, bf16[2,1,2,128,128]{4,3,2,1,0:T(8,128)(2,1)S(1)}, u32[]{:S(2)}, u32[]{:S(2)}) collective-permute-start(bf16[2,1,2,128,128]{4,3,2,1,0:T(8,128)(2,1)S(1)} %get-tuple-element.49), channel_id=1, source_target_pairs={{0,12},{4,8},{8,4},{12,0},{1,13},{5,9},{9,5},{13,1},{2,14},{6,10},... | collective-permute-start | bytes 393224 | tf_op jit(solution)/shard_map/ppermute | solution.py:425
  36.9 6.8 %collective-permute-start.2 = (bf16[2,1,2,128,128]{4,3,2,1,0:T(8,128)(2,1)S(1)}, bf16[2,1,2,128,128]{4,3,2,1,0:T(8,128)(2,1)S(1)}, u32[]{:S(2)}, u32[]{:S(2)}) collective-permute-start(bf16[2,1,2,128,128]{4,3,2,1,0:T(8,128)(2,1)S(1)} %get-tuple-element.50), channel_id=1, source_target_pairs={{0,8},{4,12},{8,0},{12,4},{1,9},{5,13},{9,1},{13,5},{2,10},{6,14},... | collective-permute-start | bytes 393224 | tf_op jit(solution)/shard_map/ppermute | solution.py:425
  36.9 8.7 %collective-permute-start.3 = (bf16[2,1,2,128,128]{4,3,2,1,0:T(8,128)(2,1)S(1)}, bf16[2,1,2,128,128]{4,3,2,1,0:T(8,128)(2,1)S(1)}, u32[]{:S(2)}, u32[]{:S(2)}) collective-permute-start(bf16[2,1,2,128,128]{4,3,2,1,0:T(8,128)(2,1)S(1)} %get-tuple-element.51), channel_id=1, source_target_pairs={{0,4},{4,0},{8,12},{12,8},{1,5},{5,1},{9,13},{13,9},{2,6},{6,2},{1... | collective-permute-start | bytes 393224 | tf_op jit(solution)/shard_map/ppermute | solution.py:425
  46.5 1.6 %collective-permute-start.9 = (bf16[1,64,2048]{2,1,0:T(8,128)(2,1)S(1)}, bf16[1,64,2048]{2,1,0:T(8,128)(2,1)S(1)}, u32[]{:S(2)}, u32[]{:S(2)}) collective-permute-start(bf16[1,64,2048]{2,1,0:T(8,128)(2,1)S(1)} %get-tuple-element.60), channel_id=1, source_target_pairs={{0,1},{1,0},{2,3},{3,2},{4,5},{5,4},{6,7},{7,6},{8,9},{9,8},{10,11... | collective-permute-start | bytes 786440 | tf_op jit(solution)/shard_map/ppermute | solution.py:440
  48.1 8.4 %collective-permute-start.10 = (bf16[1,64,2048]{2,1,0:T(8,128)(2,1)S(1)}, bf16[1,64,2048]{2,1,0:T(8,128)(2,1)S(1)}, u32[]{:S(2)}, u32[]{:S(2)}) collective-permute-start(bf16[1,64,2048]{2,1,0:T(8,128)(2,1)S(1)} %sum.2), channel_id=1, source_target_pairs={{0,2},{1,3},{2,0},{3,1},{4,6},{5,7},{6,4},{7,5},{8,10},{9,11},{10,... | collective-permute-start | bytes 786440 | tf_op jit(solution)/shard_map/ppermute | solution.py:452
  49.0 1.4 %collective-permute-start.7 = (bf16[1,64,1024]{2,1,0:T(8,128)(2,1)S(1)}, bf16[1,64,1024]{2,1,0:T(8,128)(2,1)S(1)}, u32[]{:S(2)}, u32[]{:S(2)}) collective-permute-start(bf16[1,64,1024]{2,1,0:T(8,128)(2,1)S(1)} %get-tuple-element.57), channel_id=1, source_target_pairs={{0,1},{1,0},{2,3},{3,2},{4,5},{5,4},{6,7},{7,6},{8,9},{9,8},{10,11... | collective-permute-start | bytes 393224 | tf_op jit(solution)/shard_map/ppermute | solution.py:440
  49.2 1.4 %collective-permute-start.8 = (bf16[1,64,1024]{2,1,0:T(8,128)(2,1)S(1)}, bf16[1,64,1024]{2,1,0:T(8,128)(2,1)S(1)}, u32[]{:S(2)}, u32[]{:S(2)}) collective-permute-start(bf16[1,64,1024]{2,1,0:T(8,128)(2,1)S(1)} %get-tuple-element.58), channel_id=1, source_target_pairs={{0,1},{1,0},{2,3},{3,2},{4,5},{5,4},{6,7},{7,6},{8,9},{9,8},{10,11... | collective-permute-start | bytes 393224 | tf_op jit(solution)/shard_map/ppermute | solution.py:440

commit v4 on v3

--- a/solution.py
+++ b/solution.py
@@ -128,7 +128,7 @@
 
 
 def factor_kernel(tokens, ratio, n_head, total_too, got_ref, *refs):
-    state_ref, w_ref, u_ref, *tree_refs = refs[n_head : len(refs) - n_head]
+    state_ref, w_ref, u_ref, *tree_refs = refs[n_head:]
     width = got_ref.shape[-1]
     per = SPAN // tokens
     blocks = got_ref.shape[0] // per
@@ -358,6 +358,11 @@
             cost_estimate=LIGHT,
         )(output_gate, norm_gain.reshape(1, width))
 
+    gates = list(gates)
+    for distance in reversed(range(1, n_head)):
+        pairs = [(here, here ^ distance) for here in range(n_head)]
+        gates[distance] = lax.ppermute(gates[distance], "head", pairs)
+
     state_type = BF16 if outer == 2 else F32
     with jax.named_scope("factors"):
         depths = []
@@ -373,22 +378,17 @@
             shape((blocks, ratio, SPAN, width), BF16),
             shape((blocks, ratio, SPAN, width), F32),
         ] + tree
-        state, w, u, *rest = pl.pallas_call(
+        state, w, u, *tree = pl.pallas_call(
             functools.partial(factor_kernel, tokens, ratio, n_head, outer > 2),
-            out_shape=out_shape + [shape((heads, tokens, width), BF16)] * n_head,
+            out_shape=out_shape,
             in_specs=[VMEM] + [ANY] * n_head,
-            out_specs=[VMEM] * len(out_shape) + [ANY] * n_head,
-            input_output_aliases={1 + number: len(out_shape) + number for number in range(n_head)},
+            out_specs=[VMEM] * len(out_shape),
             compiler_params=params(),
             cost_estimate=LIGHT,
         )(got, *gates)
-        tree, gates = rest[:-n_head], rest[-n_head:]
 
     onward = [(here, (here + 1) % outer) for here in range(outer)]
     incoming = lax.ppermute(state, "outer", onward)
-    for distance in reversed(range(1, n_head)):
-        pairs = [(here, here ^ distance) for here in range(n_head)]
-        gates[distance] = lax.ppermute(gates[distance], "head", pairs)
     with jax.named_scope("spread"):
         local, reach = pl.pallas_call(
             functools.partial(spread_kernel, tokens, ratio),

time: 57.5 us -> 59.6 us (1.037)
  starting transfers between devices: 15 us -> 16 us
  waiting for transfers between devices: 32 us -> 33 us
    ppermute x3, waiting for transfers between devices: 0.01 us -> 17.4 us  [per_device(): gates[distance] = lax.ppermute(gates[distance], 'head', pairs)]
    all_to_all x1, waiting for transfers between devices: 16.3 us -> 0.01 us  [per_device(): lax.all_to_all(packed, ('sub', 'head'), split_axis=0, concat_axis=0, tile...]
    ppermute x1, waiting for transfers between devices: 1.5 us -> 2.92 us  [per_device(): incoming = lax.ppermute(state, 'outer', onward)]
    ppermute x3, waiting for transfers between devices: 5.67 us -> 4.64 us  [per_device(): lax.ppermute(part, 'sub', [(here, here ^ distance) for here in range(sub)])]
  transfers between devices with their start and end apart: 12 -> 12, of which waited for: 8 -> 9; matrix products, arithmetic and copies ran while one was open for 0% -> 0% of each run, Pallas kernels for 5% -> 4%
where the time goes in v4:
time: 59.6 us; the launch traced here: 59.3 us
  waiting for transfers between devices  33 us (55%)
  starting transfers between devices  16 us (27%)
  Pallas kernels  10.2 us (17%)
    ppermute x3, waiting for transfers between devices, per_device(): gates[distance] = lax.ppermute(gates[distance], 'head', pairs)  17.4 us
    all_to_all x1, starting transfers between devices, per_device(): lax.all_to_all(packed, ('sub', 'head'), split_axis=0, concat_axis=0, tile...  6.43 us
    ppermute x1, waiting for transfers between devices, per_device(): lax.ppermute(summed, 'head', [(here, here ^ half) for here in range(n_hea...  5.43 us
    ppermute x3, waiting for transfers between devices, per_device(): lax.ppermute(part, 'sub', [(here, here ^ distance) for here in range(sub)])  4.64 us
    ppermute x3, starting transfers between devices, per_device(): lax.ppermute(part, 'sub', [(here, here ^ distance) for here in range(sub)])  3.55 us
    pallas_call x1, Pallas kernels, per_device(): pl.pallas_call(functools.partial(factor_kernel, tokens, ratio, n_head, ou...  3.38 us
    ppermute x1, waiting for transfers between devices, per_device(): incoming = lax.ppermute(state, 'outer', onward)  2.92 us
    ppermute x1, starting transfers between devices, per_device(): incoming = lax.ppermute(state, 'outer', onward)  2.67 us
  transfers between devices with their start and end apart: 12, of which 9 were waited for; matrix products, arithmetic and copies ran while one was open for 0% of the time, Pallas kernels for 4%

profile of v4, /device:TPU:0, one launch (start us, length us, event | category | flops | bytes accessed | tf_op | source)
XLA Modules:
  0.0 59.3 jit_solution(12305611343923824592)
XLA Ops:
  0.0 2.3 %pack.1 = bf16[16,272,128]{2,1,0:T(8,128)(2,1)} custom-call(bf16[64,16,128]{2,1,0:T(8,128)(2,1)} %q_hbm.1, bf16[64,16,128]{2,1,0:T(8,128)(2,1)} %k_hbm.1, bf16[64,32,128]{2,1,0:T(8,128)(2,1)} %v_hbm.1, bf16[32,64]{1,0:T(8,128)(2,1)} %bitcast.4), custom_call_target="tpu_custom_call" | custom-call | tf_op jit(solution)/shard_map/pack/pallas_call | solution.py:331
  2.3 0.0 copy-start.1
  2.3 0.0 copy-start.2
  2.3 6.4 %all-to-all-start = ((bf16[16,272,128]{2,1,0:T(8,128)(2,1)}), bf16[16,272,128]{2,1,0:T(8,128)(2,1)S(1)}, u32[]{:S(2)}, u32[]{:S(2)}) async-start(bf16[16,272,128]{2,1,0:T(8,128)(2,1)} %pack.1), calls=%async_computation | async-start | bytes 2228224 | tf_op jit(solution)/shard_map/all_to_all | solution.py:347
  8.7 0.6 %gates.1 = (bf16[8,64,128]{2,1,0:T(8,128)(2,1)S(1)}, bf16[8,64,128]{2,1,0:T(8,128)(2,1)S(1)}, bf16[8,64,128]{2,1,0:T(8,128)(2,1)S(1)}, bf16[8,64,128]{2,1,0:T(8,128)(2,1)S(1)}) custom-call(bf16[64,32,128]{2,1,0:T(8,128)(2,1)S(1)} %copy-done.1, bf16[1,128]{1,0:T(2,128)(2,1)S(1)} %bitcast.3), custom_call_target="tpu_custom_call" | custom-call | flops 1 | bytes 1 | tf_op jit(solution)/shard_map/gates/pallas_call | solution.py:351
  9.3 0.5 collective-permute-start
  9.8 1.7 %collective-permute-start.1 = (bf16[8,64,128]{2,1,0:T(8,128)(2,1)S(1)}, bf16[8,64,128]{2,1,0:T(8,128)(2,1)S(1)}, u32[]{:S(2)}, u32[]{:S(2)}) collective-permute-start(bf16[8,64,128]{2,1,0:T(8,128)(2,1)S(1)} %get-tuple-element.31), channel_id=1, source_target_pairs={{0,2},{1,3},{2,0},{3,1},{4,6},{5,7},{6,4},{7,5},{8,10},{9,11},{10,... | collective-permute-start | bytes 393224 | tf_op jit(solution)/shard_map/ppermute | solution.py:364
  11.5 0.0 collective-permute-start.2
  11.5 15.6 %collective-permute-done.1.refs_2_.refs_6_.refs_4_ = bf16[8,64,128]{2,1,0:T(8,128)(2,1)S(1)} collective-permute-done((bf16[8,64,128]{2,1,0:T(8,128)(2,1)S(1)}, bf16[8,64,128]{2,1,0:T(8,128)(2,1)S(1)}, u32[]{:S(2)}, u32[]{:S(2)}) %collective-permute-start.1) | collective-permute-done | bytes 131104 | tf_op jit(solution)/shard_map/ppermute | solution.py:364
  27.1 1.9 %collective-permute-done.2.refs_3_.refs_7_.refs_5_ = bf16[8,64,128]{2,1,0:T(8,128)(2,1)S(1)} collective-permute-done((bf16[8,64,128]{2,1,0:T(8,128)(2,1)S(1)}, bf16[8,64,128]{2,1,0:T(8,128)(2,1)S(1)}, u32[]{:S(2)}, u32[]{:S(2)}) %collective-permute-start.2) | collective-permute-done | bytes 131104 | tf_op jit(solution)/shard_map/ppermute | solution.py:364
  28.9 3.4 %factors.1 = (bf16[2,128,128]{2,1,0:T(8,128)(2,1)S(1)}, bf16[8,2,128,128]{3,2,1,0:T(8,128)(2,1)S(1)}, f32[8,2,128,128]{3,2,1,0:T(8,128)S(1)}, bf16[8,2,128,128]{...) custom-call(bf16[16,272,128]{2,1,0:T(8,128)(2,1)S(1)} %all-to-all-do, ...), custom_call_target="tpu_custom_call" | custom-call | flops 1 | bytes 1 | tf_op jit(solution)/shard_map/factors/pallas_call | solution.py:381
  32.3 2.7 %collective-permute-start.3 = (bf16[2,128,128]{2,1,0:T(8,128)(2,1)S(1)}, bf16[2,128,128]{2,1,0:T(8,128)(2,1)S(1)}, u32[]{:S(2)}, u32[]{:S(2)}) collective-permute-start(bf16[2,128,128]{2,1,0:T(8,128)(2,1)S(1)} %get-tuple-element.33), channel_id=1, source_target_pairs={{0,16},{16,0},{1,17},{17,1},{2,18},{18,2},{3,19},{19,3},{4,20},{20... | collective-permute-start | bytes 196616 | tf_op jit(solution)/shard_map/ppermute | solution.py:391
  35.0 1.1 %spread.1 = (f32[2,8,128,128]{3,2,1,0:T(8,128)S(1)}, bf16[2,8,128,128]{3,2,1,0:T(8,128)(2,1)S(1)}) custom-call(bf16[16,272,128]{2,1,0:T(8,128)(2,1)S(1)} %all-to-all-done.got_ref, bf16[8,2,128,128]{3,2,1,0:T(8,128)(2,1)S(1)} %get-tuple-element.34.w_ref, f32[8,2,128,128]{3,2,1,0:T(8,128)S(1)} %get-tuple-element.35.u_ref, ...), custom_call_target="tpu_custom_call" | custom-call | flops 1 | bytes 1 | tf_op jit(solution)/shard_map/spread/pallas_call | solution.py:393
  36.1 2.9 %collective-permute-done.3.state_ref = bf16[2,128,128]{2,1,0:T(8,128)(2,1)S(1)} collective-permute-done((bf16[2,128,128]{2,1,0:T(8,128)(2,1)S(1)}, bf16[2,128,128]{2,1,0:T(8,128)(2,1)S(1)}, u32[]{:S(2)}, u32[]{:S(2)}) %collective-permute-start.3) | collective-permute-done | bytes 65568 | tf_op jit(solution)/shard_map/ppermute | solution.py:391
  39.0 0.5 join.1
  39.5 1.6 %collective-permute-start.4 = (bf16[2,1,2,128,128]{4,3,2,1,0:T(8,128)(2,1)S(1)}, bf16[2,1,2,128,128]{4,3,2,1,0:T(8,128)(2,1)S(1)}, u32[]{:S(2)}, u32[]{:S(2)}) collective-permute-start(bf16[2,1,2,128,128]{4,3,2,1,0:T(8,128)(2,1)S(1)} %get-tuple-element.45), channel_id=1, source_target_pairs={{0,12},{4,8},{8,4},{12,0},{1,13},{5,9},{9,5},{13,1},{2,14},{6,10},... | collective-permute-start | bytes 393224 | tf_op jit(solution)/shard_map/ppermute | solution.py:425
  41.2 1.3 %collective-permute-start.5 = (bf16[2,1,2,128,128]{4,3,2,1,0:T(8,128)(2,1)S(1)}, bf16[2,1,2,128,128]{4,3,2,1,0:T(8,128)(2,1)S(1)}, u32[]{:S(2)}, u32[]{:S(2)}) collective-permute-start(bf16[2,1,2,128,128]{4,3,2,1,0:T(8,128)(2,1)S(1)} %get-tuple-element.46), channel_id=1, source_target_pairs={{0,8},{4,12},{8,0},{12,4},{1,9},{5,13},{9,1},{13,5},{2,10},{6,14},... | collective-permute-start | bytes 393224 | tf_op jit(solution)/shard_map/ppermute | solution.py:425
  42.5 0.6 collective-permute-start.6
  43.1 3.3 %collective-permute-done.4.refs_1_ = bf16[2,1,2,128,128]{4,3,2,1,0:T(8,128)(2,1)S(1)} collective-permute-done((bf16[2,1,2,128,128]{4,3,2,1,0:T(8,128)(2,1)S(1)}, bf16[2,1,2,128,128]{4,3,2,1,0:T(8,128)(2,1)S(1)}, u32[]{:S(2)}, u32[]{:S(2)}) %collective-permute-start.4) | collective-permute-done | bytes 131104 | tf_op jit(solution)/shard_map/ppermute | solution.py:425
  46.3 1.4 %collective-permute-done.5.refs_2_ = bf16[2,1,2,128,128]{4,3,2,1,0:T(8,128)(2,1)S(1)} collective-permute-done((bf16[2,1,2,128,128]{4,3,2,1,0:T(8,128)(2,1)S(1)}, bf16[2,1,2,128,128]{4,3,2,1,0:T(8,128)(2,1)S(1)}, u32[]{:S(2)}, u32[]{:S(2)}) %collective-permute-start.5) | collective-permute-done | bytes 131104 | tf_op jit(solution)/shard_map/ppermute | solution.py:425
  47.7 0.0 collective-permute-done.6.refs_3_
  47.7 0.8 %project.3 = (bf16[1,64,2048]{2,1,0:T(8,128)(2,1)S(1)}, f32[1,64,2048]{2,1,0:T(8,128)S(1)}) custom-call(bf16[2,1,2,128,128]{4,3,2,1,0:T(8,128)(2,1)S(1)} %get-tuple-element.44.refs_0_, bf16[2,1,2,128,128]{4,3,2,1,0:T(8,128)(2,1)S(1)} %collective-permute-done.4.refs_1_, bf16[2,1,2,128,128]{4,3,2,1,0:T(8,128)(2,1)S(1)} %collective-permute-done.5.refs_2_, ...), custom_call_target="tpu_custom_call" | custom-call | flops 1 | bytes 1 | tf_op jit(solution)/shard_map/project/pallas_call | solution.py:431
  48.5 0.1 collective-permute-start.9
  48.6 1.5 %collective-permute-done.9.refs_0_ = bf16[1,64,2048]{2,1,0:T(8,128)(2,1)S(1)} collective-permute-done((bf16[1,64,2048]{2,1,0:T(8,128)(2,1)S(1)}, bf16[1,64,2048]{2,1,0:T(8,128)(2,1)S(1)}, u32[]{:S(2)}, u32[]{:S(2)}) %collective-permute-start.9) | collective-permute-done | bytes 262176 | tf_op jit(solution)/shard_map/ppermute | solution.py:440
  50.1 0.6 %collective-permute-start.10 = (bf16[1,64,2048]{2,1,0:T(8,128)(2,1)S(1)}, bf16[1,64,2048]{2,1,0:T(8,128)(2,1)S(1)}, u32[]{:S(2)}, u32[]{:S(2)}) collective-permute-start(bf16[1,64,2048]{2,1,0:T(8,128)(2,1)S(1)} %sum.2), channel_id=1, source_target_pairs={{0,2},{1,3},{2,0},{3,1},{4,6},{5,7},{6,4},{7,5},{8,10},{9,11},{10,... | collective-permute-start | bytes 786440 | tf_op jit(solution)/shard_map/ppermute | solution.py:452
  50.7 0.8 %project.2 = (bf16[1,64,1024]{2,1,0:T(8,128)(2,1)S(1)}, bf16[1,64,1024]{2,1,0:T(8,128)(2,1)S(1)}, f32[1,64,2048]{2,1,0:T(8,128)S(1)}) custom-call(bf16[2,1,2,128,128]{4,3,2,1,0:T(8,128)(2,1)S(1)} %get-tuple-element.44.refs_0_, bf16[2,1,2,128,128]{4,3,2,1,0:T(8,128)(2,1)S(1)} %collective-permute-done.4.refs_1_, ...), custom_call_target="tpu_custom_call" | custom-call | flops 1 | bytes 1 | tf_op jit(solution)/shard_map/project/pallas_call | solution.py:431
  51.5 0.1 collective-permute-start.7
  51.6 0.5 collective-permute-start.8
  52.1 0.8 %collective-permute-done.7.refs_0_ = bf16[1,64,1024]{2,1,0:T(8,128)(2,1)S(1)} collective-permute-done((bf16[1,64,1024]{2,1,0:T(8,128)(2,1)S(1)}, bf16[1,64,1024]{2,1,0:T(8,128)(2,1)S(1)}, u32[]{:S(2)}, u32[]{:S(2)}) %collective-permute-start.7) | collective-permute-done | bytes 131104 | tf_op jit(solution)/shard_map/ppermute | solution.py:440
  52.9 0.2 collective-permute-done.8.refs_1_
  53.1 5.4 %collective-permute-done.10.refs_2_ = bf16[1,64,2048]{2,1,0:T(8,128)(2,1)S(1)} collective-permute-done((bf16[1,64,2048]{2,1,0:T(8,128)(2,1)S(1)}, bf16[1,64,2048]{2,1,0:T(8,128)(2,1)S(1)}, u32[]{:S(2)}, u32[]{:S(2)}) %collective-permute-start.10) | collective-permute-done | bytes 262176 | tf_op jit(solution)/shard_map/ppermute | solution.py:452
  58.6 0.8 %sum.3 = bf16[1,64,2048]{2,1,0:T(8,128)(2,1)} custom-call(f32[1,64,2048]{2,1,0:T(8,128)S(1)} %get-tuple-element.48.keep_ref, bf16[1,64,1024]{2,1,0:T(8,128)(2,1)S(1)} %collective-permute-done.7.refs_0_, bf16[1,64,1024]{2,1,0:T(8,128)(2,1)S(1)} %collective-permute-done.8.refs_1_, bf16[1,64,2048]{2,1,0:T(8,128)(2,1)S(1)} %collective-permute-done.10.refs_2_), custom_call_target="tpu_custom_call" | custom-call | flops 1 | bytes 1 | tf_op jit(solution)/shard_map/sum/pallas_call | solution.py:443
  (7 shorter events, 0.1 us)
Async XLA Ops:
  2.3 6.5 %copy-start.1 = (bf16[64,32,128]{2,1,0:T(8,128)(2,1)S(1)}, bf16[64,32,128]{2,1,0:T(8,128)(2,1)}, u32[]{:S(2)}) copy-start(bf16[64,32,128]{2,1,0:T(8,128)(2,1)} %gate_ref.1) | copy-start | bytes 1572868
  2.3 6.5 %copy-start.2 = (bf16[128]{0:T(256)(128)(2,1)S(1)}, bf16[128]{0:T(256)(128)(2,1)}, u32[]{:S(2)}) copy-start(bf16[128]{0:T(256)(128)(2,1)} %param.12) | copy-start | bytes 772
  2.3 26.6 %all-to-all-start = ((bf16[16,272,128]{2,1,0:T(8,128)(2,1)}), bf16[16,272,128]{2,1,0:T(8,128)(2,1)S(1)}, u32[]{:S(2)}, u32[]{:S(2)}) async-start(bf16[16,272,128]{2,1,0:T(8,128)(2,1)} %pack.1), calls=%async_computation | async-start | bytes 2228224 | tf_op jit(solution)/shard_map/all_to_all | solution.py:347
  9.3 2.2 %collective-permute-start = (bf16[8,64,128]{2,1,0:T(8,128)(2,1)S(1)}, bf16[8,64,128]{2,1,0:T(8,128)(2,1)S(1)}, u32[]{:S(2)}, u32[]{:S(2)}) collective-permute-start(bf16[8,64,128]{2,1,0:T(8,128)(2,1)S(1)} %get-tuple-element.30), channel_id=1, source_target_pairs={{0,1},{1,0},{2,3},{3,2},{4,5},{5,4},{6,7},{7,6},{8,9},{9,8},{10,11... | collective-permute-start | bytes 393224 | tf_op jit(solution)/shard_map/ppermute | solution.py:364
  9.8 17.3 %collective-permute-start.1 = (bf16[8,64,128]{2,1,0:T(8,128)(2,1)S(1)}, bf16[8,64,128]{2,1,0:T(8,128)(2,1)S(1)}, u32[]{:S(2)}, u32[]{:S(2)}) collective-permute-start(bf16[8,64,128]{2,1,0:T(8,128)(2,1)S(1)} %get-tuple-element.31), channel_id=1, source_target_pairs={{0,2},{1,3},{2,0},{3,1},{4,6},{5,7},{6,4},{7,5},{8,10},{9,11},{10,... | collective-permute-start | bytes 393224 | tf_op jit(solution)/shard_map/ppermute | solution.py:364
  11.5 17.4 %collective-permute-start.2 = (bf16[8,64,128]{2,1,0:T(8,128)(2,1)S(1)}, bf16[8,64,128]{2,1,0:T(8,128)(2,1)S(1)}, u32[]{:S(2)}, u32[]{:S(2)}) collective-permute-start(bf16[8,64,128]{2,1,0:T(8,128)(2,1)S(1)} %get-tuple-element.32), channel_id=1, source_target_pairs={{0,3},{1,2},{2,1},{3,0},{4,7},{5,6},{6,5},{7,4},{8,11},{9,10},{10,... | collective-permute-start | bytes 393224 | tf_op jit(solution)/shard_map/ppermute | solution.py:364
  32.3 6.7 %collective-permute-start.3 = (bf16[2,128,128]{2,1,0:T(8,128)(2,1)S(1)}, bf16[2,128,128]{2,1,0:T(8,128)(2,1)S(1)}, u32[]{:S(2)}, u32[]{:S(2)}) collective-permute-start(bf16[2,128,128]{2,1,0:T(8,128)(2,1)S(1)} %get-tuple-element.33), channel_id=1, source_target_pairs={{0,16},{16,0},{1,17},{17,1},{2,18},{18,2},{3,19},{19,3},{4,20},{20... | collective-permute-start | bytes 196616 | tf_op jit(solution)/shard_map/ppermute | solution.py:391
  35.0 12.7 %copy-start = (bf16[1024,2048]{1,0:T(8,128)(2,1)S(1)}, bf16[1024,2048]{1,0:T(8,128)(2,1)}, u32[]{:S(2)}) copy-start(bf16[1024,2048]{1,0:T(8,128)(2,1)} %refs_8_.3) | copy-start | bytes 12582916
  39.5 6.8 %collective-permute-start.4 = (bf16[2,1,2,128,128]{4,3,2,1,0:T(8,128)(2,1)S(1)}, bf16[2,1,2,128,128]{4,3,2,1,0:T(8,128)(2,1)S(1)}, u32[]{:S(2)}, u32[]{:S(2)}) collective-permute-start(bf16[2,1,2,128,128]{4,3,2,1,0:T(8,128)(2,1)S(1)} %get-tuple-element.45), channel_id=1, source_target_pairs={{0,12},{4,8},{8,4},{12,0},{1,13},{5,9},{9,5},{13,1},{2,14},{6,10},... | collective-permute-start | bytes 393224 | tf_op jit(solution)/shard_map/ppermute | solution.py:425
  41.2 6.5 %collective-permute-start.5 = (bf16[2,1,2,128,128]{4,3,2,1,0:T(8,128)(2,1)S(1)}, bf16[2,1,2,128,128]{4,3,2,1,0:T(8,128)(2,1)S(1)}, u32[]{:S(2)}, u32[]{:S(2)}) collective-permute-start(bf16[2,1,2,128,128]{4,3,2,1,0:T(8,128)(2,1)S(1)} %get-tuple-element.46), channel_id=1, source_target_pairs={{0,8},{4,12},{8,0},{12,4},{1,9},{5,13},{9,1},{13,5},{2,10},{6,14},... | collective-permute-start | bytes 393224 | tf_op jit(solution)/shard_map/ppermute | solution.py:425
  42.5 5.2 %collective-permute-start.6 = (bf16[2,1,2,128,128]{4,3,2,1,0:T(8,128)(2,1)S(1)}, bf16[2,1,2,128,128]{4,3,2,1,0:T(8,128)(2,1)S(1)}, u32[]{:S(2)}, u32[]{:S(2)}) collective-permute-start(bf16[2,1,2,128,128]{4,3,2,1,0:T(8,128)(2,1)S(1)} %get-tuple-element.47), channel_id=1, source_target_pairs={{0,4},{4,0},{8,12},{12,8},{1,5},{5,1},{9,13},{13,9},{2,6},{6,2},{1... | collective-permute-start | bytes 393224 | tf_op jit(solution)/shard_map/ppermute | solution.py:425
  48.5 1.6 %collective-permute-start.9 = (bf16[1,64,2048]{2,1,0:T(8,128)(2,1)S(1)}, bf16[1,64,2048]{2,1,0:T(8,128)(2,1)S(1)}, u32[]{:S(2)}, u32[]{:S(2)}) collective-permute-start(bf16[1,64,2048]{2,1,0:T(8,128)(2,1)S(1)} %get-tuple-element.52), channel_id=1, source_target_pairs={{0,1},{1,0},{2,3},{3,2},{4,5},{5,4},{6,7},{7,6},{8,9},{9,8},{10,11... | collective-permute-start | bytes 786440 | tf_op jit(solution)/shard_map/ppermute | solution.py:440
  50.1 8.4 %collective-permute-start.10 = (bf16[1,64,2048]{2,1,0:T(8,128)(2,1)S(1)}, bf16[1,64,2048]{2,1,0:T(8,128)(2,1)S(1)}, u32[]{:S(2)}, u32[]{:S(2)}) collective-permute-start(bf16[1,64,2048]{2,1,0:T(8,128)(2,1)S(1)} %sum.2), channel_id=1, source_target_pairs={{0,2},{1,3},{2,0},{3,1},{4,6},{5,7},{6,4},{7,5},{8,10},{9,11},{10,... | collective-permute-start | bytes 786440 | tf_op jit(solution)/shard_map/ppermute | solution.py:452
  51.5 1.4 %collective-permute-start.7 = (bf16[1,64,1024]{2,1,0:T(8,128)(2,1)S(1)}, bf16[1,64,1024]{2,1,0:T(8,128)(2,1)S(1)}, u32[]{:S(2)}, u32[]{:S(2)}) collective-permute-start(bf16[1,64,1024]{2,1,0:T(8,128)(2,1)S(1)} %get-tuple-element.49), channel_id=1, source_target_pairs={{0,1},{1,0},{2,3},{3,2},{4,5},{5,4},{6,7},{7,6},{8,9},{9,8},{10,11... | collective-permute-start | bytes 393224 | tf_op jit(solution)/shard_map/ppermute | solution.py:440
  51.6 1.5 %collective-permute-start.8 = (bf16[1,64,1024]{2,1,0:T(8,128)(2,1)S(1)}, bf16[1,64,1024]{2,1,0:T(8,128)(2,1)S(1)}, u32[]{:S(2)}, u32[]{:S(2)}) collective-permute-start(bf16[1,64,1024]{2,1,0:T(8,128)(2,1)S(1)} %get-tuple-element.50), channel_id=1, source_target_pairs={{0,1},{1,0},{2,3},{3,2},{4,5},{5,4},{6,7},{7,6},{8,9},{9,8},{10,11... | collective-permute-start | bytes 393224 | tf_op jit(solution)/shard_map/ppermute | solution.py:440

commit v5 on v3

--- a/solution.py
+++ b/solution.py
@@ -38,10 +38,9 @@
     return lax.axis_index("sub"), lax.axis_index("head")
 
 
-def pack_kernel(sub, q_hbm, k_hbm, v_hbm, b_hbm, out_hbm, q_ref, k_ref, v_ref, b_ref, out_ref, came, left):
+def pack_kernel(q_hbm, k_hbm, v_hbm, b_hbm, out_hbm, q_ref, k_ref, v_ref, b_ref, out_ref, came, left):
     tokens, key_heads, width = q_hbm.shape
     ratio = v_hbm.shape[1] // key_heads
-    n_head = key_heads // sub
     copies = [
         pltpu.make_async_copy(source, target, came.at[number])
         for number, (source, target) in enumerate(
@@ -50,7 +49,7 @@
     ]
     for copy in copies:
         copy.start()
-    heads = [(peer % n_head) * sub + peer // n_head for peer in range(key_heads)]
+    heads = range(key_heads)
     leaving = []
 
     def leave(first, size):
@@ -92,9 +91,15 @@
         out_ref[...] = gates[pl.ds((along_head ^ distance) * heads, heads)]
 
 
-def block_rows(got_ref, block, per, tokens, part):
-    rows = got_ref[pl.ds(block * per, per), part * tokens : (part + 1) * tokens]
-    return rows.reshape(per * tokens, rows.shape[-1])
+def block_slabs(blocks, sub, sources):
+    n_head = sources // sub
+    places = [source % n_head * sub + source // n_head for source in range(sources)]
+    per = sources // blocks
+    return [places[block * per : (block + 1) * per] for block in range(blocks)]
+
+
+def block_rows(got_ref, slabs, tokens, part):
+    return jnp.concatenate([got_ref[slab, part * tokens : (part + 1) * tokens] for slab in slabs], axis=0)
 
 
 def beside(matrices):
@@ -127,18 +132,19 @@
     return solved
 
 
-def factor_kernel(tokens, ratio, n_head, total_too, got_ref, *refs):
+def factor_kernel(tokens, ratio, sub, n_head, total_too, got_ref, *refs):
     state_ref, w_ref, u_ref, *tree_refs = refs[n_head : len(refs) - n_head]
     width = got_ref.shape[-1]
     per = SPAN // tokens
     blocks = got_ref.shape[0] // per
+    slabs = block_slabs(blocks, sub, got_ref.shape[0])
     rows = lax.broadcasted_iota(jnp.int32, (SPAN, SPAN), 0)
     cols = lax.broadcasted_iota(jnp.int32, (SPAN, SPAN), 1)
     lane = lax.broadcasted_iota(jnp.int32, (1, SPAN), 1)
     first = (2 + ratio) * tokens
     below, held = [], []
     for block in range(blocks):
-        key = block_rows(got_ref, block, per, tokens, 1)
+        key = block_rows(got_ref, slabs[block], tokens, 1)
         gram = dot_nt(key, key)
         squares = jnp.where(rows == cols, gram, 0.0)
         key_row = lax.rsqrt(jnp.sum(squares, 0, keepdims=True) + EPSILON)
@@ -148,7 +154,7 @@
         for r in range(ratio):
             strength = jnp.zeros((1, SPAN), F32)
             for place in range(per):
-                piece = got_ref[block * per + place, first : first + ROW_TILE].astype(F32)[r : r + 1]
+                piece = got_ref[slabs[block][place], first : first + ROW_TILE].astype(F32)[r : r + 1]
                 strength = jnp.where(lane // tokens == place, piece, strength)
             scaled_col = jnp.sum(jnp.where(rows == cols, strength * key_row, 0.0), 1, keepdims=True)
             below.append(lower * scaled_col)
@@ -161,7 +167,7 @@
         unused, key, key_col, key_row, strengths = held[block]
         weighted.append(inverse.astype(F32) * key_col * strengths[r])
     for part, (block, r) in zip(weighted, flat):
-        value = block_rows(got_ref, block, per, tokens, 2 + r)
+        value = block_rows(got_ref, slabs[block], tokens, 2 + r)
         u_ref[block, r] = dot(part.astype(BF16), value)
     for part, (block, r) in zip(weighted, flat):
         unused, key, key_col, key_row, strengths = held[block]
@@ -223,18 +229,19 @@
     return [neutral if start is None else start for start in starts]
 
 
-def spread_kernel(tokens, ratio, got_ref, w_ref, u_ref, *refs):
+def spread_kernel(tokens, ratio, sub, got_ref, w_ref, u_ref, *refs):
     tree_refs, (local_ref, reach_ref) = refs[:-2], refs[-2:]
     width = got_ref.shape[-1]
     per = SPAN // tokens
     blocks = got_ref.shape[0] // per
+    slabs = block_slabs(blocks, sub, got_ref.shape[0])
     rows = lax.broadcasted_iota(jnp.int32, (SPAN, SPAN), 0)
     cols = lax.broadcasted_iota(jnp.int32, (SPAN, SPAN), 1)
     starts = [start.astype(BF16) for start in tree_starts(ratio, width, tree_refs)]
     lefts, units = [], []
     for block in range(blocks):
-        query = block_rows(got_ref, block, per, tokens, 0)
-        key = block_rows(got_ref, block, per, tokens, 1)
+        query = block_rows(got_ref, slabs[block], tokens, 0)
+        key = block_rows(got_ref, slabs[block], tokens, 1)
         scores = jnp.where(rows >= cols, dot_nt(query, key), 0.0).astype(BF16)
         query_f = query.astype(F32)
         squares = jnp.sum(query_f * query_f, 1, keepdims=True)
@@ -270,33 +277,31 @@
                     out_ref[kept, piece, r] = (core * lax.rsqrt(mean_square + EPSILON)).astype(BF16)
 
 
-def project_kernel(order, shares, kept, *refs):
+def project_kernel(order, shares, kept, mine, *refs):
     parts = len(order)
     normed_refs, gate_refs = refs[:parts], refs[parts : parts + shares]
-    weight_ref, *send_refs, keep_ref, rows_ref = refs[parts + 2 * shares :]
+    weight_ref, *out_refs, rows_ref = refs[parts + 2 * shares :]
     unused, pieces, ratio, span, width = normed_refs[0].shape
     tokens = gate_refs[0].shape[1]
     per = span // tokens
     along_sub, along_head = position()
     for distance, normed_ref in zip(order, normed_refs):
         source = along_sub ^ distance
-        for apart, gate_ref in enumerate(gate_refs):
+        for apart in range(1 - mine, shares, 2):
             share = (along_head ^ apart) & (shares - 1)
-            first = ((1 - apart % 2) * (shares // 2) + share // 2) * tokens
-            place = pl.ds(pl.multiple_of(first, tokens), tokens)
+            place = pl.ds(pl.multiple_of(share // 2 * tokens, tokens), tokens)
             from_rows = pl.ds(pl.multiple_of(share % per * tokens, tokens), tokens)
             for r in range(ratio):
                 lanes = pl.ds(pl.multiple_of((source * ratio + r) * width, width), width)
                 normed = normed_ref[kept, share // per, r, from_rows].astype(F32)
-                gate = gate_ref[source * ratio + r].astype(F32)
+                gate = gate_refs[apart][source * ratio + r].astype(F32)
                 rows_ref[place, lanes] = (normed * gate).astype(BF16)
-    out = dot(rows_ref[...], weight_ref[...]).reshape((2,) + keep_ref.shape)
     first = 0
-    for send_ref in send_refs:
-        columns = send_ref.shape[-1]
-        send_ref[...] = out[0, :, :, first : first + columns].astype(BF16)
+    for out_ref in out_refs:
+        columns = out_ref.shape[-1]
+        out = dot(rows_ref[...], weight_ref[:, first : first + columns])
+        out_ref[...] = out.reshape(out_ref.shape).astype(out_ref.dtype)
         first += columns
-    keep_ref[...] = out[1]
 
 
 def sum_kernel(keep_ref, *refs):
@@ -329,7 +334,7 @@
     with jax.named_scope("pack"):
         slab = ((2 + ratio) * tokens + ROW_TILE, width)
         packed = pl.pallas_call(
-            functools.partial(pack_kernel, sub),
+            pack_kernel,
             out_shape=shape((sources,) + slab, BF16),
             in_specs=[ANY] * 4,
             out_specs=ANY,
@@ -344,7 +349,7 @@
             ],
             compiler_params=params(60),
         )(queries, key_vectors, value_vectors, write_strength.T)
-    got = lax.all_to_all(packed, ("sub", "head"), split_axis=0, concat_axis=0, tiled=True)
+    got = lax.all_to_all(packed, ("head", "sub"), split_axis=0, concat_axis=0, tiled=True)
 
     heads = sub * ratio
     with jax.named_scope("gates"):
@@ -357,6 +362,10 @@
             compiler_params=params(),
             cost_estimate=LIGHT,
         )(output_gate, norm_gain.reshape(1, width))
+
+    by_core = [(here, here ^ 1) for here in range(n_head)]
+    gates = list(gates)
+    gates[1] = lax.ppermute(gates[1], "head", by_core)
 
     state_type = BF16 if outer == 2 else F32
     with jax.named_scope("factors"):
@@ -374,7 +383,7 @@
             shape((blocks, ratio, SPAN, width), F32),
         ] + tree
         state, w, u, *rest = pl.pallas_call(
-            functools.partial(factor_kernel, tokens, ratio, n_head, outer > 2),
+            functools.partial(factor_kernel, tokens, ratio, sub, n_head, outer > 2),
             out_shape=out_shape + [shape((heads, tokens, width), BF16)] * n_head,
             in_specs=[VMEM] + [ANY] * n_head,
             out_specs=[VMEM] * len(out_shape) + [ANY] * n_head,
@@ -386,12 +395,12 @@
 
     onward = [(here, (here + 1) % outer) for here in range(outer)]
     incoming = lax.ppermute(state, "outer", onward)
-    for distance in reversed(range(1, n_head)):
+    for distance in reversed(range(2, n_head)):
         pairs = [(here, here ^ distance) for here in range(n_head)]
         gates[distance] = lax.ppermute(gates[distance], "head", pairs)
     with jax.named_scope("spread"):
         local, reach = pl.pallas_call(
-            functools.partial(spread_kernel, tokens, ratio),
+            functools.partial(spread_kernel, tokens, ratio, sub),
             out_shape=[
                 shape((ratio, blocks, SPAN, width), F32),
                 shape((ratio, blocks, SPAN, width), BF16),
@@ -409,7 +418,6 @@
     pieces = shard_tokens // SPAN // 2
     columns = output_weight.shape[1]
     quarter = (n_head // 4, tokens, columns)
-    by_core = [(here, here ^ 1) for here in range(n_head)]
     half = n_head // 2
     order = [0] + sorted(range(1, sub), reverse=True)
     with jax.named_scope("join"):
@@ -427,16 +435,21 @@
     ]
     for kept in range(2):
         cuts = 1 + kept
-        with jax.named_scope("project"):
-            *sends, keep = pl.pallas_call(
-                functools.partial(project_kernel, order, half, kept),
-                out_shape=[shape(quarter[:-1] + (columns // cuts,), BF16)] * cuts + [shape(quarter, F32)],
-                in_specs=[VMEM] * (sub + half) + [ANY] * half + [VMEM],
-                out_specs=[VMEM] * (cuts + 1),
-                scratch_shapes=[pltpu.VMEM((shard_tokens // 2, heads * width), BF16)],
-                compiler_params=params(),
-                cost_estimate=LIGHT,
-            )(*normed, *gates[half * (1 - kept) :], *gates[: half * (1 - kept)], output_weight)
+        operands = [*normed, *gates[half * (1 - kept) :], *gates[: half * (1 - kept)], output_weight]
+        results = []
+        for mine in range(2):
+            pieces_of = 1 if mine else cuts
+            with jax.named_scope("project"):
+                results += pl.pallas_call(
+                    functools.partial(project_kernel, order, half, kept, mine),
+                    out_shape=[shape(quarter[:-1] + (columns // pieces_of,), F32 if mine else BF16)] * pieces_of,
+                    in_specs=[VMEM] * (sub + half) + [ANY] * half + [VMEM],
+                    out_specs=[VMEM] * pieces_of,
+                    scratch_shapes=[pltpu.VMEM((shard_tokens // 4, heads * width), BF16)],
+                    compiler_params=params(),
+                    cost_estimate=LIGHT,
+                )(*operands)
+        *sends, keep = results
         arrived = [lax.ppermute(send, "head", by_core) for send in sends]
         last = n_head == 4 and kept == 1
         with jax.named_scope("sum"):

time: 57.5 us -> 55.3 us (0.962)
  waiting for transfers between devices: 32 us -> 26.4 us
  Pallas kernels: 10.2 us -> 12.1 us
  starting transfers between devices: 15 us -> 16.4 us
    all_to_all x1, waiting for transfers between devices: 16.3 us -> 13.5 us  [per_device(): lax.all_to_all(packed, ('head', 'sub'), split_axis=0, concat_axis=0, tile...]
    pallas_call x5 -> x7, Pallas kernels: 8.27 us -> 10.2 us  [the longest x4 3.46 us: per_device(): pl.pallas_call(functools.partial(project_kernel, order, half, kept, mine)...]
    ppermute x3, waiting for transfers between devices: 2.54 us -> 0.8 us  [per_device(): arrived = [lax.ppermute(send, 'head', by_core) for send in sends]]
    ppermute x1, waiting for transfers between devices: 5.94 us -> 4.6 us  [per_device(): lax.ppermute(summed, 'head', [(here, here ^ half) for here in range(n_hea...]
    ppermute x1, starting transfers between devices: 0.07 us -> 1.34 us  [per_device(): lax.ppermute(summed, 'head', [(here, here ^ half) for here in range(n_hea...]
    ppermute x0 -> x1, waiting for transfers between devices: none -> 0.99 us  [per_device(): gates[1] = lax.ppermute(gates[1], 'head', by_core)]
    ppermute x3 -> x2, starting transfers between devices: 1.59 us -> 1.31 us  [per_device(): gates[distance] = lax.ppermute(gates[distance], 'head', pairs)]
  transfers between devices with their start and end apart: 12 -> 12, of which waited for: 8 -> 8; matrix products, arithmetic and copies ran while one was open for 0% -> 0% of each run, Pallas kernels for 5% -> 9%
where the time goes in v5:
time: 55.3 us; the launch traced here: 55.1 us
  waiting for transfers between devices  26.4 us (48%)
  starting transfers between devices  16.4 us (30%)
  Pallas kernels  12.1 us (22%)
    all_to_all x1, waiting for transfers between devices, per_device(): lax.all_to_all(packed, ('head', 'sub'), split_axis=0, concat_axis=0, tile...  13.5 us
    all_to_all x1, starting transfers between devices, per_device(): lax.all_to_all(packed, ('head', 'sub'), split_axis=0, concat_axis=0, tile...  6.43 us
    ppermute x3, waiting for transfers between devices, per_device(): lax.ppermute(part, 'sub', [(here, here ^ distance) for here in range(sub)])  5.41 us
    ppermute x1, waiting for transfers between devices, per_device(): lax.ppermute(summed, 'head', [(here, here ^ half) for here in range(n_hea...  4.6 us
    ppermute x3, starting transfers between devices, per_device(): lax.ppermute(part, 'sub', [(here, here ^ distance) for here in range(sub)])  3.55 us
    pallas_call x4, Pallas kernels, per_device(): pl.pallas_call(functools.partial(project_kernel, order, half, kept, mine)...  3.46 us
    pallas_call x1, Pallas kernels, per_device(): pl.pallas_call(functools.partial(factor_kernel, tokens, ratio, sub, n_hea...  3.39 us
    ppermute x1, starting transfers between devices, per_device(): incoming = lax.ppermute(state, 'outer', onward)  2.65 us
  transfers between devices with their start and end apart: 12, of which 8 were waited for; matrix products, arithmetic and copies ran while one was open for 0% of the time, Pallas kernels for 9%

profile of v5, /device:TPU:0, one launch (start us, length us, event | category | flops | bytes accessed | tf_op | source)
XLA Modules:
  0.0 55.1 jit_solution(8639407707898463772)
XLA Ops:
  0.0 2.2 %pack.1 = bf16[16,272,128]{2,1,0:T(8,128)(2,1)} custom-call(bf16[64,16,128]{2,1,0:T(8,128)(2,1)} %q_hbm.1, bf16[64,16,128]{2,1,0:T(8,128)(2,1)} %k_hbm.1, bf16[64,32,128]{2,1,0:T(8,128)(2,1)} %v_hbm.1, bf16[32,64]{1,0:T(8,128)(2,1)} %bitcast.4), custom_call_target="tpu_custom_call" | custom-call | tf_op jit(solution)/shard_map/pack/pallas_call | solution.py:336
  2.2 0.0 copy-start.1
  2.3 0.0 copy-start.2
  2.3 6.4 %all-to-all-start = ((bf16[16,272,128]{2,1,0:T(8,128)(2,1)}), bf16[16,272,128]{2,1,0:T(8,128)(2,1)S(1)}, u32[]{:S(2)}, u32[]{:S(2)}) async-start(bf16[16,272,128]{2,1,0:T(8,128)(2,1)} %pack.1), calls=%async_computation | async-start | bytes 2228224 | tf_op jit(solution)/shard_map/all_to_all | solution.py:352
  8.7 0.6 %gates.1 = (bf16[8,64,128]{2,1,0:T(8,128)(2,1)S(1)}, bf16[8,64,128]{2,1,0:T(8,128)(2,1)S(1)}, bf16[8,64,128]{2,1,0:T(8,128)(2,1)S(1)}, bf16[8,64,128]{2,1,0:T(8,128)(2,1)S(1)}) custom-call(bf16[64,32,128]{2,1,0:T(8,128)(2,1)S(1)} %copy-done.1, bf16[1,128]{1,0:T(2,128)(2,1)S(1)} %bitcast.3), custom_call_target="tpu_custom_call" | custom-call | flops 1 | bytes 1 | tf_op jit(solution)/shard_map/gates/pallas_call | solution.py:356
  9.3 0.5 collective-permute-start
  9.8 1.0 %collective-permute-done.refs_1_ = bf16[8,64,128]{2,1,0:T(8,128)(2,1)S(1)} collective-permute-done((bf16[8,64,128]{2,1,0:T(8,128)(2,1)S(1)}, bf16[8,64,128]{2,1,0:T(8,128)(2,1)S(1)}, u32[]{:S(2)}, u32[]{:S(2)}) %collective-permute-start) | collective-permute-done | bytes 131104 | tf_op jit(solution)/shard_map/ppermute | solution.py:368
  10.8 13.5 %all-to-all-done.got_ref = bf16[16,272,128]{2,1,0:T(8,128)(2,1)S(1)} async-done(((bf16[16,272,128]{2,1,0:T(8,128)(2,1)}), bf16[16,272,128]{2,1,0:T(8,128)(2,1)S(1)}, u32[]{:S(2)}, u32[]{:S(2)}) %all-to-all-start) | async-done | bytes 1114144 | tf_op jit(solution)/shard_map/all_to_all | solution.py:352
  24.3 3.4 %factors.1 = (bf16[2,128,128]{2,1,0:T(8,128)(2,1)S(1)}, bf16[8,2,128,128]{3,2,1,0:T(8,128)(2,1)S(1)}, f32[8,2,128,128]{3,2,1,0:T(8,128)S(1)}, bf16[8,2,128,128]{...) custom-call(bf16[16,272,128]{2,1,0:T(8,128)(2,1)S(1)} %all-to-all-do, ...), custom_call_target="tpu_custom_call", output_to_operand_aliasing={{9}: (1, {}), {10}: (2, {}), {11}: (3, {}), {12}: (4, {})} | custom-call | flops 1 | bytes 1 | tf_op jit(solution)/shard_map/factors/pallas_call | solution.py:385
  27.7 2.6 %collective-permute-start.1 = (bf16[2,128,128]{2,1,0:T(8,128)(2,1)S(1)}, bf16[2,128,128]{2,1,0:T(8,128)(2,1)S(1)}, u32[]{:S(2)}, u32[]{:S(2)}) collective-permute-start(bf16[2,128,128]{2,1,0:T(8,128)(2,1)S(1)} %get-tuple-element.34), channel_id=1, source_target_pairs={{0,16},{16,0},{1,17},{17,1},{2,18},{18,2},{3,19},{19,3},{4,20},{20... | collective-permute-start | bytes 196616 | tf_op jit(solution)/shard_map/ppermute | solution.py:397
  30.4 1.3 %collective-permute-start.5 = (bf16[8,64,128]{2,1,0:T(8,128)(2,1)S(1)}, bf16[8,64,128]{2,1,0:T(8,128)(2,1)S(1)}, u32[]{:S(2)}, u32[]{:S(2)}) collective-permute-start(bf16[8,64,128]{2,1,0:T(8,128)(2,1)S(1)} %get-tuple-element.51), channel_id=1, source_target_pairs={{0,2},{1,3},{2,0},{3,1},{4,6},{5,7},{6,4},{7,5},{8,10},{9,11},{10,... | collective-permute-start | bytes 393224 | tf_op jit(solution)/shard_map/ppermute | solution.py:400
  31.7 1.1 %spread.1 = (f32[2,8,128,128]{3,2,1,0:T(8,128)S(1)}, bf16[2,8,128,128]{3,2,1,0:T(8,128)(2,1)S(1)}) custom-call(bf16[16,272,128]{2,1,0:T(8,128)(2,1)S(1)} %all-to-all-done.got_ref, bf16[8,2,128,128]{3,2,1,0:T(8,128)(2,1)S(1)} %get-tuple-element.35.w_ref, f32[8,2,128,128]{3,2,1,0:T(8,128)S(1)} %get-tuple-element.36.u_ref, ...), custom_call_target="tpu_custom_call" | custom-call | flops 1 | bytes 1 | tf_op jit(solution)/shard_map/spread/pallas_call | solution.py:402
  32.7 1.1 %collective-permute-done.1.state_ref = bf16[2,128,128]{2,1,0:T(8,128)(2,1)S(1)} collective-permute-done((bf16[2,128,128]{2,1,0:T(8,128)(2,1)S(1)}, bf16[2,128,128]{2,1,0:T(8,128)(2,1)S(1)}, u32[]{:S(2)}, u32[]{:S(2)}) %collective-permute-start.1) | collective-permute-done | bytes 65568 | tf_op jit(solution)/shard_map/ppermute | solution.py:397
  33.9 0.5 join.1
  34.4 1.2 %collective-permute-start.2 = (bf16[2,1,2,128,128]{4,3,2,1,0:T(8,128)(2,1)S(1)}, bf16[2,1,2,128,128]{4,3,2,1,0:T(8,128)(2,1)S(1)}, u32[]{:S(2)}, u32[]{:S(2)}) collective-permute-start(bf16[2,1,2,128,128]{4,3,2,1,0:T(8,128)(2,1)S(1)} %get-tuple-element.46), channel_id=1, source_target_pairs={{0,12},{4,8},{8,4},{12,0},{1,13},{5,9},{9,5},{13,1},{2,14},{6,10},... | collective-permute-start | bytes 393224 | tf_op jit(solution)/shard_map/ppermute | solution.py:433
  35.6 1.9 %collective-permute-start.3 = (bf16[2,1,2,128,128]{4,3,2,1,0:T(8,128)(2,1)S(1)}, bf16[2,1,2,128,128]{4,3,2,1,0:T(8,128)(2,1)S(1)}, u32[]{:S(2)}, u32[]{:S(2)}) collective-permute-start(bf16[2,1,2,128,128]{4,3,2,1,0:T(8,128)(2,1)S(1)} %get-tuple-element.47), channel_id=1, source_target_pairs={{0,8},{4,12},{8,0},{12,4},{1,9},{5,13},{9,1},{13,5},{2,10},{6,14},... | collective-permute-start | bytes 393224 | tf_op jit(solution)/shard_map/ppermute | solution.py:433
  37.5 0.5 collective-permute-start.4
  37.9 0.0 collective-permute-done.5.refs_6_.refs_4_
  37.9 3.8 %collective-permute-done.2.refs_1_ = bf16[2,1,2,128,128]{4,3,2,1,0:T(8,128)(2,1)S(1)} collective-permute-done((bf16[2,1,2,128,128]{4,3,2,1,0:T(8,128)(2,1)S(1)}, bf16[2,1,2,128,128]{4,3,2,1,0:T(8,128)(2,1)S(1)}, u32[]{:S(2)}, u32[]{:S(2)}) %collective-permute-start.2) | collective-permute-done | bytes 131104 | tf_op jit(solution)/shard_map/ppermute | solution.py:433
  41.7 1.6 %collective-permute-done.3.refs_2_ = bf16[2,1,2,128,128]{4,3,2,1,0:T(8,128)(2,1)S(1)} collective-permute-done((bf16[2,1,2,128,128]{4,3,2,1,0:T(8,128)(2,1)S(1)}, bf16[2,1,2,128,128]{4,3,2,1,0:T(8,128)(2,1)S(1)}, u32[]{:S(2)}, u32[]{:S(2)}) %collective-permute-start.3) | collective-permute-done | bytes 131104 | tf_op jit(solution)/shard_map/ppermute | solution.py:433
  43.3 0.9 %project.7 = bf16[1,64,2048]{2,1,0:T(8,128)(2,1)S(1)} custom-call(bf16[2,1,2,128,128]{4,3,2,1,0:T(8,128)(2,1)S(1)} %get-tuple-element.45.refs_0_, bf16[2,1,2,128,128]{4,3,2,1,0:T(8,128)(2,1)S(1)} %collective-permute-done.2.refs_1_, bf16[2,1,2,128,128]{4,3,2,1,0:T(8,128)(2,1)S(1)} %collective-permute-done.3.refs_2_, ...), custom_call_target="tpu_custom_call" | custom-call | flops 1 | bytes 1 | tf_op jit(solution)/shard_map/project/pallas_call | solution.py:443
  44.2 0.1 collective-permute-start.9
  44.3 0.9 %project.6.keep_ref = f32[1,64,2048]{2,1,0:T(8,128)S(1)} custom-call(bf16[2,1,2,128,128]{4,3,2,1,0:T(8,128)(2,1)S(1)} %get-tuple-element.45.refs_0_, bf16[2,1,2,128,128]{4,3,2,1,0:T(8,128)(2,1)S(1)} %collective-permute-done.2.refs_1_, bf16[2,1,2,128,128]{4,3,2,1,0:T(8,128)(2,1)S(1)} %collective-permute-done.3.refs_2_, ...), custom_call_target="tpu_custom_call" | custom-call | flops 1 | bytes 1 | tf_op jit(solution)/shard_map/project/pallas_call | solution.py:443
  45.2 0.7 %collective-permute-done.9.refs_0_ = bf16[1,64,2048]{2,1,0:T(8,128)(2,1)S(1)} collective-permute-done((bf16[1,64,2048]{2,1,0:T(8,128)(2,1)S(1)}, bf16[1,64,2048]{2,1,0:T(8,128)(2,1)S(1)}, u32[]{:S(2)}, u32[]{:S(2)}) %collective-permute-start.9) | collective-permute-done | bytes 262176 | tf_op jit(solution)/shard_map/ppermute | solution.py:453
  45.9 1.3 %collective-permute-start.10 = (bf16[1,64,2048]{2,1,0:T(8,128)(2,1)S(1)}, bf16[1,64,2048]{2,1,0:T(8,128)(2,1)S(1)}, u32[]{:S(2)}, u32[]{:S(2)}) collective-permute-start(bf16[1,64,2048]{2,1,0:T(8,128)(2,1)S(1)} %sum.2), channel_id=1, source_target_pairs={{0,2},{1,3},{2,0},{3,1},{4,6},{5,7},{6,4},{7,5},{8,10},{9,11},{10,... | collective-permute-start | bytes 786440 | tf_op jit(solution)/shard_map/ppermute | solution.py:465
  47.2 0.9 %project.5 = (bf16[1,64,1024]{2,1,0:T(8,128)(2,1)S(1)}, bf16[1,64,1024]{2,1,0:T(8,128)(2,1)S(1)}) custom-call(bf16[2,1,2,128,128]{4,3,2,1,0:T(8,128)(2,1)S(1)} %get-tuple-element.45.refs_0_, bf16[2,1,2,128,128]{4,3,2,1,0:T(8,128)(2,1)S(1)} %collective-permute-done.2.refs_1_, bf16[2,1,2,128,128]{4,3,2,1,0:T(8,128)(2,1)S(1)} %collective-permute-done.3.refs_2_, ...), custom_call_target="tpu_custom_call" | custom-call | flops 1 | bytes 1 | tf_op jit(solution)/shard_map/project/pallas_call | solution.py:443
  48.1 0.1 collective-permute-start.7
  48.2 0.5 collective-permute-start.8
  48.7 0.9 %project.4.keep_ref = f32[1,64,2048]{2,1,0:T(8,128)S(1)} custom-call(bf16[2,1,2,128,128]{4,3,2,1,0:T(8,128)(2,1)S(1)} %get-tuple-element.45.refs_0_, bf16[2,1,2,128,128]{4,3,2,1,0:T(8,128)(2,1)S(1)} %collective-permute-done.2.refs_1_, bf16[2,1,2,128,128]{4,3,2,1,0:T(8,128)(2,1)S(1)} %collective-permute-done.3.refs_2_, ...), custom_call_target="tpu_custom_call" | custom-call | flops 1 | bytes 1 | tf_op jit(solution)/shard_map/project/pallas_call | solution.py:443
  49.5 0.1 collective-permute-done.8.refs_1_
  49.7 4.6 %collective-permute-done.10.refs_2_ = bf16[1,64,2048]{2,1,0:T(8,128)(2,1)S(1)} collective-permute-done((bf16[1,64,2048]{2,1,0:T(8,128)(2,1)S(1)}, bf16[1,64,2048]{2,1,0:T(8,128)(2,1)S(1)}, u32[]{:S(2)}, u32[]{:S(2)}) %collective-permute-start.10) | collective-permute-done | bytes 262176 | tf_op jit(solution)/shard_map/ppermute | solution.py:465
  54.3 0.8 %sum.3 = bf16[1,64,2048]{2,1,0:T(8,128)(2,1)} custom-call(f32[1,64,2048]{2,1,0:T(8,128)S(1)} %project.4.keep_ref, bf16[1,64,1024]{2,1,0:T(8,128)(2,1)S(1)} %collective-permute-done.7.refs_0_, bf16[1,64,1024]{2,1,0:T(8,128)(2,1)S(1)} %collective-permute-done.8.refs_1_, bf16[1,64,2048]{2,1,0:T(8,128)(2,1)S(1)} %collective-permute-done.10.refs_2_), custom_call_target="tpu_custom_call" | custom-call | flops 1 | bytes 1 | tf_op jit(solution)/shard_map/sum/pallas_call | solution.py:456
  (9 shorter events, 0.1 us)
Async XLA Ops:
  2.2 6.5 %copy-start.1 = (bf16[64,32,128]{2,1,0:T(8,128)(2,1)S(1)}, bf16[64,32,128]{2,1,0:T(8,128)(2,1)}, u32[]{:S(2)}) copy-start(bf16[64,32,128]{2,1,0:T(8,128)(2,1)} %gate_ref.1) | copy-start | bytes 1572868
  2.3 6.5 %copy-start.2 = (bf16[128]{0:T(256)(128)(2,1)S(1)}, bf16[128]{0:T(256)(128)(2,1)}, u32[]{:S(2)}) copy-start(bf16[128]{0:T(256)(128)(2,1)} %param.12) | copy-start | bytes 772
  2.3 22.0 %all-to-all-start = ((bf16[16,272,128]{2,1,0:T(8,128)(2,1)}), bf16[16,272,128]{2,1,0:T(8,128)(2,1)S(1)}, u32[]{:S(2)}, u32[]{:S(2)}) async-start(bf16[16,272,128]{2,1,0:T(8,128)(2,1)} %pack.1), calls=%async_computation | async-start | bytes 2228224 | tf_op jit(solution)/shard_map/all_to_all | solution.py:352
  9.3 1.5 %collective-permute-start = (bf16[8,64,128]{2,1,0:T(8,128)(2,1)S(1)}, bf16[8,64,128]{2,1,0:T(8,128)(2,1)S(1)}, u32[]{:S(2)}, u32[]{:S(2)}) collective-permute-start(bf16[8,64,128]{2,1,0:T(8,128)(2,1)S(1)} %get-tuple-element.31), channel_id=1, source_target_pairs={{0,1},{1,0},{2,3},{3,2},{4,5},{5,4},{6,7},{7,6},{8,9},{9,8},{10,11... | collective-permute-start | bytes 393224 | tf_op jit(solution)/shard_map/ppermute | solution.py:368
  27.7 6.2 %collective-permute-start.1 = (bf16[2,128,128]{2,1,0:T(8,128)(2,1)S(1)}, bf16[2,128,128]{2,1,0:T(8,128)(2,1)S(1)}, u32[]{:S(2)}, u32[]{:S(2)}) collective-permute-start(bf16[2,128,128]{2,1,0:T(8,128)(2,1)S(1)} %get-tuple-element.34), channel_id=1, source_target_pairs={{0,16},{16,0},{1,17},{17,1},{2,18},{18,2},{3,19},{19,3},{4,20},{20... | collective-permute-start | bytes 196616 | tf_op jit(solution)/shard_map/ppermute | solution.py:397
  30.4 7.6 %collective-permute-start.5 = (bf16[8,64,128]{2,1,0:T(8,128)(2,1)S(1)}, bf16[8,64,128]{2,1,0:T(8,128)(2,1)S(1)}, u32[]{:S(2)}, u32[]{:S(2)}) collective-permute-start(bf16[8,64,128]{2,1,0:T(8,128)(2,1)S(1)} %get-tuple-element.51), channel_id=1, source_target_pairs={{0,2},{1,3},{2,0},{3,1},{4,6},{5,7},{6,4},{7,5},{8,10},{9,11},{10,... | collective-permute-start | bytes 393224 | tf_op jit(solution)/shard_map/ppermute | solution.py:400
  31.7 6.3 %collective-permute-start.6 = (bf16[8,64,128]{2,1,0:T(8,128)(2,1)S(1)}, bf16[8,64,128]{2,1,0:T(8,128)(2,1)S(1)}, u32[]{:S(2)}, u32[]{:S(2)}) collective-permute-start(bf16[8,64,128]{2,1,0:T(8,128)(2,1)S(1)} %get-tuple-element.52), channel_id=1, source_target_pairs={{0,3},{1,2},{2,1},{3,0},{4,7},{5,6},{6,5},{7,4},{8,11},{9,10},{10,... | collective-permute-start | bytes 393224 | tf_op jit(solution)/shard_map/ppermute | solution.py:400
  31.7 11.7 %copy-start = (bf16[1024,2048]{1,0:T(8,128)(2,1)S(1)}, bf16[1024,2048]{1,0:T(8,128)(2,1)}, u32[]{:S(2)}) copy-start(bf16[1024,2048]{1,0:T(8,128)(2,1)} %refs_8_.7) | copy-start | bytes 12582916
  34.4 7.4 %collective-permute-start.2 = (bf16[2,1,2,128,128]{4,3,2,1,0:T(8,128)(2,1)S(1)}, bf16[2,1,2,128,128]{4,3,2,1,0:T(8,128)(2,1)S(1)}, u32[]{:S(2)}, u32[]{:S(2)}) collective-permute-start(bf16[2,1,2,128,128]{4,3,2,1,0:T(8,128)(2,1)S(1)} %get-tuple-element.46), channel_id=1, source_target_pairs={{0,12},{4,8},{8,4},{12,0},{1,13},{5,9},{9,5},{13,1},{2,14},{6,10},... | collective-permute-start | bytes 393224 | tf_op jit(solution)/shard_map/ppermute | solution.py:433
  35.6 7.8 %collective-permute-start.3 = (bf16[2,1,2,128,128]{4,3,2,1,0:T(8,128)(2,1)S(1)}, bf16[2,1,2,128,128]{4,3,2,1,0:T(8,128)(2,1)S(1)}, u32[]{:S(2)}, u32[]{:S(2)}) collective-permute-start(bf16[2,1,2,128,128]{4,3,2,1,0:T(8,128)(2,1)S(1)} %get-tuple-element.47), channel_id=1, source_target_pairs={{0,8},{4,12},{8,0},{12,4},{1,9},{5,13},{9,1},{13,5},{2,10},{6,14},... | collective-permute-start | bytes 393224 | tf_op jit(solution)/shard_map/ppermute | solution.py:433
  37.5 5.9 %collective-permute-start.4 = (bf16[2,1,2,128,128]{4,3,2,1,0:T(8,128)(2,1)S(1)}, bf16[2,1,2,128,128]{4,3,2,1,0:T(8,128)(2,1)S(1)}, u32[]{:S(2)}, u32[]{:S(2)}) collective-permute-start(bf16[2,1,2,128,128]{4,3,2,1,0:T(8,128)(2,1)S(1)} %get-tuple-element.48), channel_id=1, source_target_pairs={{0,4},{4,0},{8,12},{12,8},{1,5},{5,1},{9,13},{13,9},{2,6},{6,2},{1... | collective-permute-start | bytes 393224 | tf_op jit(solution)/shard_map/ppermute | solution.py:433
  44.2 1.6 %collective-permute-start.9 = (bf16[1,64,2048]{2,1,0:T(8,128)(2,1)S(1)}, bf16[1,64,2048]{2,1,0:T(8,128)(2,1)S(1)}, u32[]{:S(2)}, u32[]{:S(2)}) collective-permute-start(bf16[1,64,2048]{2,1,0:T(8,128)(2,1)S(1)} %project.7), channel_id=1, source_target_pairs={{0,1},{1,0},{2,3},{3,2},{4,5},{5,4},{6,7},{7,6},{8,9},{9,8},{10,11... | collective-permute-start | bytes 786440 | tf_op jit(solution)/shard_map/ppermute | solution.py:453
  45.9 8.4 %collective-permute-start.10 = (bf16[1,64,2048]{2,1,0:T(8,128)(2,1)S(1)}, bf16[1,64,2048]{2,1,0:T(8,128)(2,1)S(1)}, u32[]{:S(2)}, u32[]{:S(2)}) collective-permute-start(bf16[1,64,2048]{2,1,0:T(8,128)(2,1)S(1)} %sum.2), channel_id=1, source_target_pairs={{0,2},{1,3},{2,0},{3,1},{4,6},{5,7},{6,4},{7,5},{8,10},{9,11},{10,... | collective-permute-start | bytes 786440 | tf_op jit(solution)/shard_map/ppermute | solution.py:465
  48.1 1.4 %collective-permute-start.7 = (bf16[1,64,1024]{2,1,0:T(8,128)(2,1)S(1)}, bf16[1,64,1024]{2,1,0:T(8,128)(2,1)S(1)}, u32[]{:S(2)}, u32[]{:S(2)}) collective-permute-start(bf16[1,64,1024]{2,1,0:T(8,128)(2,1)S(1)} %get-tuple-element.53), channel_id=1, source_target_pairs={{0,1},{1,0},{2,3},{3,2},{4,5},{5,4},{6,7},{7,6},{8,9},{9,8},{10,11... | collective-permute-start | bytes 393224 | tf_op jit(solution)/shard_map/ppermute | solution.py:453
  48.2 1.5 %collective-permute-start.8 = (bf16[1,64,1024]{2,1,0:T(8,128)(2,1)S(1)}, bf16[1,64,1024]{2,1,0:T(8,128)(2,1)S(1)}, u32[]{:S(2)}, u32[]{:S(2)}) collective-permute-start(bf16[1,64,1024]{2,1,0:T(8,128)(2,1)S(1)} %get-tuple-element.54), channel_id=1, source_target_pairs={{0,1},{1,0},{2,3},{3,2},{4,5},{5,4},{6,7},{7,6},{8,9},{9,8},{10,11... | collective-permute-start | bytes 393224 | tf_op jit(solution)/shard_map/ppermute | solution.py:453

commit v6 on v5

--- a/solution.py
+++ b/solution.py
@@ -34,11 +34,29 @@
     return jnp.transpose(values, (1, 0, 2))
 
 
-def position():
-    return lax.axis_index("sub"), lax.axis_index("head")
-
-
-def pack_kernel(q_hbm, k_hbm, v_hbm, b_hbm, out_hbm, q_ref, k_ref, v_ref, b_ref, out_ref, came, left):
+def split_axis(name, size):
+    return tuple(f"{name}{bit}" for bit in reversed(range(size.bit_length() - 1)))
+
+
+def partner_order(sub, n_head):
+    heads = split_axis("head", n_head)
+    return heads[-1:] + heads[:-1] + split_axis("sub", sub)
+
+
+def partner(source, sub, n_head):
+    axes = split_axis("sub", sub) + split_axis("head", n_head)
+    bits = {name: source >> (len(axes) - 1 - number) & 1 for number, name in enumerate(axes)}
+    place = 0
+    for name in partner_order(sub, n_head):
+        place = 2 * place + bits[name]
+    return place
+
+
+def position(sub, n_head):
+    return lax.axis_index(split_axis("sub", sub)), lax.axis_index(split_axis("head", n_head))
+
+
+def pack_kernel(sub, q_hbm, k_hbm, v_hbm, b_hbm, out_hbm, q_ref, k_ref, v_ref, b_ref, out_ref, came, left):
     tokens, key_heads, width = q_hbm.shape
     ratio = v_hbm.shape[1] // key_heads
     copies = [
@@ -49,7 +67,10 @@
     ]
     for copy in copies:
         copy.start()
-    heads = range(key_heads)
+    n_head = key_heads // sub
+    heads = [head % sub * n_head + head // sub for head in range(key_heads)]
+    heads = [partner(source, sub, n_head) for source in heads]
+    heads = [heads.index(peer) for peer in range(key_heads)]
     leaving = []
 
     def leave(first, size):
@@ -80,20 +101,26 @@
         copy.wait()
 
 
-def gate_kernel(gate_ref, gain_ref, *refs):
-    unused, along_head = position()
-    out_refs, gates = refs[:-1], refs[-1]
+def gate_kernel(sub, n_head, gate_ref, gain_ref, own_ref, other_ref, *refs):
+    pair_refs, gates = refs[:-1], refs[-1]
+    heads = own_ref.shape[1]
+    unused, along_head = position(sub, n_head)
     gate = gate_ref[...].astype(F32)
     gated = gain_ref[...].astype(F32)[:, None] * (gate / (1.0 + jnp.exp(-gate)))
     gates[...] = turned(gated.astype(BF16))
-    for distance, out_ref in enumerate(out_refs):
-        heads = out_ref.shape[0]
-        out_ref[...] = gates[pl.ds((along_head ^ distance) * heads, heads)]
+
+    def group(distance):
+        return gates[pl.ds((along_head ^ distance) * heads, heads)]
+
+    own_ref[0] = group(0)
+    other_ref[0] = group(1)
+    for number, pair_ref in enumerate(pair_refs):
+        for core in range(2):
+            pair_ref[core] = group(2 * number + 2 + core)
 
 
 def block_slabs(blocks, sub, sources):
-    n_head = sources // sub
-    places = [source % n_head * sub + source // n_head for source in range(sources)]
+    places = [partner(source, sub, sources // sub) for source in range(sources)]
     per = sources // blocks
     return [places[block * per : (block + 1) * per] for block in range(blocks)]
 
@@ -132,8 +159,8 @@
     return solved
 
 
-def factor_kernel(tokens, ratio, sub, n_head, total_too, got_ref, *refs):
-    state_ref, w_ref, u_ref, *tree_refs = refs[n_head : len(refs) - n_head]
+def factor_kernel(tokens, ratio, sub, total_too, got_ref, after_ref, *refs):
+    state_ref, w_ref, u_ref, *tree_refs = refs
     width = got_ref.shape[-1]
     per = SPAN // tokens
     blocks = got_ref.shape[0] // per
@@ -229,8 +256,9 @@
     return [neutral if start is None else start for start in starts]
 
 
-def spread_kernel(tokens, ratio, sub, got_ref, w_ref, u_ref, *refs):
-    tree_refs, (local_ref, reach_ref) = refs[:-2], refs[-2:]
+def spread_kernel(tokens, ratio, sub, passing, got_ref, w_ref, u_ref, *refs):
+    refs = refs[: len(refs) - passing]
+    tree_refs, (local_ref, reach_ref) = refs[: len(refs) - passing - 2], refs[-2:]
     width = got_ref.shape[-1]
     per = SPAN // tokens
     blocks = got_ref.shape[0] // per
@@ -259,11 +287,11 @@
         reach_ref[r, block] = out[:, width:].astype(BF16)
 
 
-def join_kernel(order, state_ref, local_ref, reach_ref, *out_refs):
+def join_kernel(order, n_head, state_ref, local_ref, reach_ref, *out_refs):
     ratio, blocks, span, width = local_ref.shape
     pieces = out_refs[0].shape[1]
-    along_sub, along_head = position()
-    upper = along_head // (lax.axis_size("head") // 2)
+    along_sub, along_head = position(len(order), n_head)
+    upper = along_head // (n_head // 2)
     follows = lax.axis_index("outer") > 0
     states = [jnp.where(follows, state_ref[r].astype(F32), 0.0).astype(BF16) for r in range(ratio)]
     for distance, out_ref in zip(order, out_refs):
@@ -282,9 +310,9 @@
     normed_refs, gate_refs = refs[:parts], refs[parts : parts + shares]
     weight_ref, *out_refs, rows_ref = refs[parts + 2 * shares :]
     unused, pieces, ratio, span, width = normed_refs[0].shape
-    tokens = gate_refs[0].shape[1]
+    tokens = gate_refs[0].shape[2]
     per = span // tokens
-    along_sub, along_head = position()
+    along_sub, along_head = position(parts, 2 * shares)
     for distance, normed_ref in zip(order, normed_refs):
         source = along_sub ^ distance
         for apart in range(1 - mine, shares, 2):
@@ -294,7 +322,7 @@
             for r in range(ratio):
                 lanes = pl.ds(pl.multiple_of((source * ratio + r) * width, width), width)
                 normed = normed_ref[kept, share // per, r, from_rows].astype(F32)
-                gate = gate_refs[apart][source * ratio + r].astype(F32)
+                gate = gate_refs[apart][0, source * ratio + r].astype(F32)
                 rows_ref[place, lanes] = (normed * gate).astype(BF16)
     first = 0
     for out_ref in out_refs:
@@ -330,11 +358,12 @@
     blocks = shard // SPAN
     shard_tokens = tokens * n_head
     shape = jax.ShapeDtypeStruct
+    along_sub, along_head = split_axis("sub", sub), split_axis("head", n_head)
 
     with jax.named_scope("pack"):
         slab = ((2 + ratio) * tokens + ROW_TILE, width)
         packed = pl.pallas_call(
-            pack_kernel,
+            functools.partial(pack_kernel, sub),
             out_shape=shape((sources,) + slab, BF16),
             in_specs=[ANY] * 4,
             out_specs=ANY,
@@ -349,23 +378,22 @@
             ],
             compiler_params=params(60),
         )(queries, key_vectors, value_vectors, write_strength.T)
-    got = lax.all_to_all(packed, ("head", "sub"), split_axis=0, concat_axis=0, tiled=True)
+    got = lax.all_to_all(packed, partner_order(sub, n_head), split_axis=0, concat_axis=0, tiled=True)
 
     heads = sub * ratio
+    by_core = [(here, here ^ 1) for here in range(n_head)]
+    group = (heads, tokens, width)
     with jax.named_scope("gates"):
-        gates = pl.pallas_call(
-            gate_kernel,
-            out_shape=[shape((heads, tokens, width), BF16)] * n_head,
+        own_gates, other_gates, *pair_gates = pl.pallas_call(
+            functools.partial(gate_kernel, sub, n_head),
+            out_shape=[shape((1,) + group, BF16)] * 2 + [shape((2,) + group, BF16)] * (n_head // 2 - 1),
             in_specs=[VMEM] * 2,
-            out_specs=[VMEM] * n_head,
+            out_specs=[VMEM] * (n_head // 2 + 1),
             scratch_shapes=[pltpu.VMEM((value_heads, tokens, width), BF16)],
             compiler_params=params(),
             cost_estimate=LIGHT,
         )(output_gate, norm_gain.reshape(1, width))
-
-    by_core = [(here, here ^ 1) for here in range(n_head)]
-    gates = list(gates)
-    gates[1] = lax.ppermute(gates[1], "head", by_core)
+    other_gates = lax.ppermute(other_gates, along_head, by_core)
 
     state_type = BF16 if outer == 2 else F32
     with jax.named_scope("factors"):
@@ -382,34 +410,38 @@
             shape((blocks, ratio, SPAN, width), BF16),
             shape((blocks, ratio, SPAN, width), F32),
         ] + tree
-        state, w, u, *rest = pl.pallas_call(
-            functools.partial(factor_kernel, tokens, ratio, sub, n_head, outer > 2),
-            out_shape=out_shape + [shape((heads, tokens, width), BF16)] * n_head,
-            in_specs=[VMEM] + [ANY] * n_head,
-            out_specs=[VMEM] * len(out_shape) + [ANY] * n_head,
-            input_output_aliases={1 + number: len(out_shape) + number for number in range(n_head)},
+        state, w, u, *tree = pl.pallas_call(
+            functools.partial(factor_kernel, tokens, ratio, sub, outer > 2),
+            out_shape=out_shape,
+            in_specs=[VMEM, ANY],
+            out_specs=[VMEM] * len(out_shape),
             compiler_params=params(),
             cost_estimate=LIGHT,
-        )(got, *gates)
-        tree, gates = rest[:-n_head], rest[-n_head:]
+        )(got, other_gates)
 
     onward = [(here, (here + 1) % outer) for here in range(outer)]
     incoming = lax.ppermute(state, "outer", onward)
-    for distance in reversed(range(2, n_head)):
-        pairs = [(here, here ^ distance) for here in range(n_head)]
-        gates[distance] = lax.ppermute(gates[distance], "head", pairs)
     with jax.named_scope("spread"):
-        local, reach = pl.pallas_call(
-            functools.partial(spread_kernel, tokens, ratio, sub),
+        passing = len(pair_gates)
+        first = 3 + 2 * len(depths)
+        local, reach, *pair_gates = pl.pallas_call(
+            functools.partial(spread_kernel, tokens, ratio, sub, passing),
             out_shape=[
                 shape((ratio, blocks, SPAN, width), F32),
                 shape((ratio, blocks, SPAN, width), BF16),
-            ],
-            in_specs=[VMEM] * (3 + 2 * len(depths)),
-            out_specs=[VMEM] * 2,
+            ]
+            + [shape((2,) + group, BF16)] * passing,
+            in_specs=[VMEM] * first + [ANY] * passing,
+            out_specs=[VMEM] * 2 + [ANY] * passing,
+            input_output_aliases={first + number: 2 + number for number in range(passing)},
             compiler_params=params(),
             cost_estimate=LIGHT,
-        )(got, w, u, *tree[: 2 * len(depths)])
+        )(got, w, u, *tree[: 2 * len(depths)], *pair_gates)
+    gates = [own_gates, other_gates]
+    for number, pair in enumerate(pair_gates):
+        distance = 2 * number + 2
+        pair = lax.ppermute(pair, along_head, [(here, here ^ distance) for here in range(n_head)])
+        gates += [pair, lax.ppermute(pair[1:], along_head, by_core)]
     for hop in range(outer - 2):
         incoming = jnp.where(lax.axis_index("outer") == 0, 0.0, incoming)
         turned_by = jnp.einsum("hde,hef->hdf", tree[-1], incoming, precision=lax.Precision.HIGHEST)
@@ -422,7 +454,7 @@
     order = [0] + sorted(range(1, sub), reverse=True)
     with jax.named_scope("join"):
         normed = pl.pallas_call(
-            functools.partial(join_kernel, order),
+            functools.partial(join_kernel, order, n_head),
             out_shape=[shape((2, pieces, ratio, SPAN, width), BF16)] * sub,
             in_specs=[VMEM] * 3,
             out_specs=[VMEM] * sub,
@@ -430,7 +462,7 @@
             cost_estimate=LIGHT,
         )(incoming, local, reach)
     normed = [
-        lax.ppermute(part, "sub", [(here, here ^ distance) for here in range(sub)]) if distance else part
+        lax.ppermute(part, along_sub, [(here, here ^ distance) for here in range(sub)]) if distance else part
         for distance, part in zip(order, normed)
     ]
     for kept in range(2):
@@ -450,7 +482,7 @@
                     cost_estimate=LIGHT,
                 )(*operands)
         *sends, keep = results
-        arrived = [lax.ppermute(send, "head", by_core) for send in sends]
+        arrived = [lax.ppermute(send, along_head, by_core) for send in sends]
         last = n_head == 4 and kept == 1
         with jax.named_scope("sum"):
             summed = pl.pallas_call(
@@ -462,14 +494,14 @@
                 cost_estimate=LIGHT,
             )(keep, *arrived, *([passed_on] if kept else []))
         if not kept:
-            passed_on = lax.ppermute(summed, "head", [(here, here ^ half) for here in range(n_head)])
+            passed_on = lax.ppermute(summed, along_head, [(here, here ^ half) for here in range(n_head)])
     bit = 2
     while bit < half:
-        mine = (lax.axis_index("head") // bit) % 2
+        mine = (lax.axis_index(along_head) // bit) % 2
         split = summed.reshape((summed.shape[0] // 2, 2) + summed.shape[1:])
         send = lax.dynamic_index_in_dim(split, 1 - mine, 1, False).astype(BF16)
         keep = lax.dynamic_index_in_dim(split, mine, 1, False)
-        summed = keep + lax.ppermute(send, "head", [(here, here ^ bit) for here in range(n_head)]).astype(F32)
+        summed = keep + lax.ppermute(send, along_head, [(here, here ^ bit) for here in range(n_head)]).astype(F32)
         bit *= 2
     return summed[0].astype(BF16)
 
@@ -480,8 +512,9 @@
     def run(queries, key_vectors, value_vectors, output_gate, write_strength, norm_gain, output_weight):
         sub = queries.shape[1] // n_head
         outer = n_seq // sub
-        split = Mesh(mesh.devices.reshape(outer, sub, n_head), ("outer", "sub", "head"))
-        every = ("outer", "sub", "head")
+        along = split_axis("sub", sub) + split_axis("head", n_head)
+        split = Mesh(mesh.devices.reshape((outer,) + (2,) * len(along)), ("outer",) + along)
+        every = ("outer",) + along
         placed = (
             P(every, None, None),
             P(every, None, None),
@@ -489,7 +522,7 @@
             P(every, None, None),
             P(every, None),
             P(),
-            P("head", None),
+            P(split_axis("head", n_head), None),
         )
         return jax.shard_map(
             functools.partial(per_device, outer, sub, n_head),

time: 55.3 us -> 56.9 us (1.029)
  starting transfers between devices: 16.4 us -> 17.5 us
    ppermute x1, waiting for transfers between devices: 1.11 us -> 2.62 us  [per_device(): incoming = lax.ppermute(state, 'outer', onward)]
    ppermute x10, starting transfers between devices: 7.31 us -> 8.5 us  [the longest x3 3.64 us: per_device(): lax.ppermute(part, along_sub, [(here, here ^ distance) for here in range(...]
    ppermute x10, waiting for transfers between devices: 11.8 us -> 10.8 us  [the longest x3 4.87 us: per_device(): lax.ppermute(part, along_sub, [(here, here ^ distance) for here in range(...]
  transfers between devices with their start and end apart: 12 -> 12, of which waited for: 8 -> 9; matrix products, arithmetic and copies ran while one was open for 0% -> 0% of each run, Pallas kernels for 9% -> 7%
where the time goes in v6:
time: 56.9 us; the launch traced here: 56.6 us
  waiting for transfers between devices  26.8 us (47%)
  starting transfers between devices  17.5 us (31%)
  Pallas kernels  12.1 us (21%)
    all_to_all x1, waiting for transfers between devices, per_device(): lax.all_to_all(packed, partner_order(sub, n_head), split_axis=0, concat_a...  13.4 us
    all_to_all x1, starting transfers between devices, per_device(): lax.all_to_all(packed, partner_order(sub, n_head), split_axis=0, concat_a...  6.43 us
    ppermute x3, waiting for transfers between devices, per_device(): lax.ppermute(part, along_sub, [(here, here ^ distance) for here in range(...  4.87 us
    ppermute x1, waiting for transfers between devices, per_device(): lax.ppermute(summed, along_head, [(here, here ^ half) for here in range(n...  4.12 us
    ppermute x3, starting transfers between devices, per_device(): lax.ppermute(part, along_sub, [(here, here ^ distance) for here in range(...  3.64 us
    pallas_call x4, Pallas kernels, per_device(): pl.pallas_call(functools.partial(project_kernel, order, half, kept, mine)...  3.48 us
    pallas_call x1, Pallas kernels, per_device(): pl.pallas_call(functools.partial(factor_kernel, tokens, ratio, sub, outer...  3.39 us
    ppermute x1, waiting for transfers between devices, per_device(): incoming = lax.ppermute(state, 'outer', onward)  2.62 us
  transfers between devices with their start and end apart: 12, of which 9 were waited for; matrix products, arithmetic and copies ran while one was open for 0% of the time, Pallas kernels for 7%

profile of v6, /device:TPU:0, one launch (start us, length us, event | category | flops | bytes accessed | tf_op | source)
XLA Modules:
  0.0 56.6 jit_solution(4511716311856858660)
XLA Ops:
  0.0 2.2 %pack.1 = bf16[16,272,128]{2,1,0:T(8,128)(2,1)} custom-call(bf16[64,16,128]{2,1,0:T(8,128)(2,1)} %q_hbm.1, bf16[64,16,128]{2,1,0:T(8,128)(2,1)} %k_hbm.1, bf16[64,32,128]{2,1,0:T(8,128)(2,1)} %v_hbm.1, bf16[32,64]{1,0:T(8,128)(2,1)} %bitcast.4), custom_call_target="tpu_custom_call" | custom-call | tf_op jit(solution)/shard_map/pack/pallas_call | solution.py:365
  2.3 0.0 copy-start.2
  2.3 6.4 %all-to-all-start = ((bf16[16,272,128]{2,1,0:T(8,128)(2,1)}), bf16[16,272,128]{2,1,0:T(8,128)(2,1)S(1)}, u32[]{:S(2)}, u32[]{:S(2)}) async-start(bf16[16,272,128]{2,1,0:T(8,128)(2,1)} %pack.1), calls=%async_computation | async-start | bytes 2228224 | tf_op jit(solution)/shard_map/all_to_all | solution.py:381
  8.7 0.6 %gates.1 = (bf16[1,8,64,128]{3,2,1,0:T(8,128)(2,1)S(1)}, bf16[1,8,64,128]{3,2,1,0:T(8,128)(2,1)S(1)}, bf16[2,8,64,128]{3,2,1,0:T(8,128)(2,1)S(1)}) custom-call(bf16[64,32,128]{2,1,0:T(8,128)(2,1)S(1)} %copy-done.1, bf16[1,128]{1,0:T(2,128)(2,1)S(1)} %bitcast.3), custom_call_target="tpu_custom_call" | custom-call | flops 1 | bytes 1 | tf_op jit(solution)/shard_map/gates/pallas_call | solution.py:387
  9.3 0.5 collective-permute-start
  9.8 1.0 %collective-permute-done.after_ref.refs_5_.refs_7_ = bf16[1,8,64,128]{3,2,1,0:T(8,128)(2,1)S(1)} collective-permute-done((bf16[1,8,64,128]{3,2,1,0:T(8,128)(2,1)S(1)}, bf16[1,8,64,128]{3,2,1,0:T(8,128)(2,1)S(1)}, u32[]{:S(2)}, u32[]{:S(2)}) %collective-permute-start) | collective-permute-done | bytes 131104 | tf_op jit(solution)/shard_map/ppermute | solution.py:396
  10.8 13.4 %all-to-all-done.got_ref = bf16[16,272,128]{2,1,0:T(8,128)(2,1)S(1)} async-done(((bf16[16,272,128]{2,1,0:T(8,128)(2,1)}), bf16[16,272,128]{2,1,0:T(8,128)(2,1)S(1)}, u32[]{:S(2)}, u32[]{:S(2)}) %all-to-all-start) | async-done | bytes 1114144 | tf_op jit(solution)/shard_map/all_to_all | solution.py:381
  24.2 3.4 %factors.1 = (bf16[2,128,128]{2,1,0:T(8,128)(2,1)S(1)}, bf16[8,2,128,128]{3,2,1,0:T(8,128)(2,1)S(1)}, f32[8,2,128,128]{3,2,1,0:T(8,128)S(1)}, bf16[8,2,128,128]{...) custom-call(bf16[16,272,128]{2,1,0:T(8,128)(2,1)S(1)} %all-to-all-do, ...), custom_call_target="tpu_custom_call" | custom-call | flops 1 | bytes 1 | tf_op jit(solution)/shard_map/factors/pallas_call | solution.py:413
  27.6 0.0 copy-start
  27.6 1.1 %spread.1 = (f32[2,8,128,128]{3,2,1,0:T(8,128)S(1)}, bf16[2,8,128,128]{3,2,1,0:T(8,128)(2,1)S(1)}, bf16[2,8,64,128]{3,2,1,0:T(8,128)(2,1)S(1)}) custom-call(bf16[16,272,128]{2,1,0:T(8,128)(2,1)S(1)} %all-to-all-done.got_ref, bf16[8,2,128,128]{3,2,1,0:T(8,128)(2,1)S(1)} %get-tuple-element.28.w_ref, ...), custom_call_target="tpu_custom_call", output_to_operand_aliasing={{2}: (9, {})} | custom-call | flops 1 | bytes 1 | tf_op jit(solution)/shard_map/spread/pallas_call | solution.py:427
  28.7 1.2 %collective-permute-start.5 = (bf16[2,8,64,128]{3,2,1,0:T(8,128)(2,1)S(1)}, bf16[2,8,64,128]{3,2,1,0:T(8,128)(2,1)S(1)}, u32[]{:S(2)}, u32[]{:S(2)}) collective-permute-start(bf16[2,8,64,128]{3,2,1,0:T(8,128)(2,1)S(1)} %get-tuple-element.44), channel_id=1, source_target_pairs={{0,2},{1,3},{2,0},{3,1},{4,6},{5,7},{6,4},{7,5},{8,10},{9,11},{10,... | collective-permute-start | bytes 786440 | tf_op jit(solution)/shard_map/ppermute | solution.py:443
  29.8 2.6 %collective-permute-start.1 = (bf16[2,128,128]{2,1,0:T(8,128)(2,1)S(1)}, bf16[2,128,128]{2,1,0:T(8,128)(2,1)S(1)}, u32[]{:S(2)}, u32[]{:S(2)}) collective-permute-start(bf16[2,128,128]{2,1,0:T(8,128)(2,1)S(1)} %get-tuple-element.27), channel_id=1, source_target_pairs={{0,16},{16,0},{1,17},{17,1},{2,18},{18,2},{3,19},{19,3},{4,20},{20... | collective-permute-start | bytes 196616 | tf_op jit(solution)/shard_map/ppermute | solution.py:423
  32.4 2.6 %collective-permute-done.1.state_ref = bf16[2,128,128]{2,1,0:T(8,128)(2,1)S(1)} collective-permute-done((bf16[2,128,128]{2,1,0:T(8,128)(2,1)S(1)}, bf16[2,128,128]{2,1,0:T(8,128)(2,1)S(1)}, u32[]{:S(2)}, u32[]{:S(2)}) %collective-permute-start.1) | collective-permute-done | bytes 65568 | tf_op jit(solution)/shard_map/ppermute | solution.py:423
  35.1 0.5 join.1
  35.6 1.5 %collective-permute-start.2 = (bf16[2,1,2,128,128]{4,3,2,1,0:T(8,128)(2,1)S(1)}, bf16[2,1,2,128,128]{4,3,2,1,0:T(8,128)(2,1)S(1)}, u32[]{:S(2)}, u32[]{:S(2)}) collective-permute-start(bf16[2,1,2,128,128]{4,3,2,1,0:T(8,128)(2,1)S(1)} %get-tuple-element.40), channel_id=1, source_target_pairs={{0,12},{4,8},{8,4},{12,0},{1,13},{5,9},{9,5},{13,1},{2,14},{6,10},... | collective-permute-start | bytes 393224 | tf_op jit(solution)/shard_map/ppermute | solution.py:465
  37.1 2.1 %collective-permute-start.3 = (bf16[2,1,2,128,128]{4,3,2,1,0:T(8,128)(2,1)S(1)}, bf16[2,1,2,128,128]{4,3,2,1,0:T(8,128)(2,1)S(1)}, u32[]{:S(2)}, u32[]{:S(2)}) collective-permute-start(bf16[2,1,2,128,128]{4,3,2,1,0:T(8,128)(2,1)S(1)} %get-tuple-element.41), channel_id=1, source_target_pairs={{0,8},{4,12},{8,0},{12,4},{1,9},{5,13},{9,1},{13,5},{2,10},{6,14},... | collective-permute-start | bytes 393224 | tf_op jit(solution)/shard_map/ppermute | solution.py:465
  39.2 0.1 collective-permute-start.6
  39.3 2.3 %collective-permute-done.2.refs_1_ = bf16[2,1,2,128,128]{4,3,2,1,0:T(8,128)(2,1)S(1)} collective-permute-done((bf16[2,1,2,128,128]{4,3,2,1,0:T(8,128)(2,1)S(1)}, bf16[2,1,2,128,128]{4,3,2,1,0:T(8,128)(2,1)S(1)}, u32[]{:S(2)}, u32[]{:S(2)}) %collective-permute-start.2) | collective-permute-done | bytes 131104 | tf_op jit(solution)/shard_map/ppermute | solution.py:465
  41.6 2.1 %collective-permute-done.3.refs_2_ = bf16[2,1,2,128,128]{4,3,2,1,0:T(8,128)(2,1)S(1)} collective-permute-done((bf16[2,1,2,128,128]{4,3,2,1,0:T(8,128)(2,1)S(1)}, bf16[2,1,2,128,128]{4,3,2,1,0:T(8,128)(2,1)S(1)}, u32[]{:S(2)}, u32[]{:S(2)}) %collective-permute-start.3) | collective-permute-done | bytes 131104 | tf_op jit(solution)/shard_map/ppermute | solution.py:465
  43.7 0.5 collective-permute-done.4.refs_3_
  44.2 0.9 %project.7 = bf16[1,64,2048]{2,1,0:T(8,128)(2,1)S(1)} custom-call(bf16[2,1,2,128,128]{4,3,2,1,0:T(8,128)(2,1)S(1)} %get-tuple-element.39.refs_0_, bf16[2,1,2,128,128]{4,3,2,1,0:T(8,128)(2,1)S(1)} %collective-permute-done.2.refs_1_, bf16[2,1,2,128,128]{4,3,2,1,0:T(8,128)(2,1)S(1)} %collective-permute-done.3.refs_2_, ...), custom_call_target="tpu_custom_call" | custom-call | flops 1 | bytes 1 | tf_op jit(solution)/shard_map/project/pallas_call | solution.py:475
  45.1 0.1 collective-permute-start.9
  45.1 0.9 %project.6.keep_ref = f32[1,64,2048]{2,1,0:T(8,128)S(1)} custom-call(bf16[2,1,2,128,128]{4,3,2,1,0:T(8,128)(2,1)S(1)} %get-tuple-element.39.refs_0_, bf16[2,1,2,128,128]{4,3,2,1,0:T(8,128)(2,1)S(1)} %collective-permute-done.2.refs_1_, bf16[2,1,2,128,128]{4,3,2,1,0:T(8,128)(2,1)S(1)} %collective-permute-done.3.refs_2_, ...), custom_call_target="tpu_custom_call" | custom-call | flops 1 | bytes 1 | tf_op jit(solution)/shard_map/project/pallas_call | solution.py:475
  46.0 0.6 %collective-permute-done.9.refs_0_ = bf16[1,64,2048]{2,1,0:T(8,128)(2,1)S(1)} collective-permute-done((bf16[1,64,2048]{2,1,0:T(8,128)(2,1)S(1)}, bf16[1,64,2048]{2,1,0:T(8,128)(2,1)S(1)}, u32[]{:S(2)}, u32[]{:S(2)}) %collective-permute-start.9) | collective-permute-done | bytes 262176 | tf_op jit(solution)/shard_map/ppermute | solution.py:485
  46.7 2.5 %collective-permute-start.10 = (bf16[1,64,2048]{2,1,0:T(8,128)(2,1)S(1)}, bf16[1,64,2048]{2,1,0:T(8,128)(2,1)S(1)}, u32[]{:S(2)}, u32[]{:S(2)}) collective-permute-start(bf16[1,64,2048]{2,1,0:T(8,128)(2,1)S(1)} %sum.2), channel_id=1, source_target_pairs={{0,2},{1,3},{2,0},{3,1},{4,6},{5,7},{6,4},{7,5},{8,10},{9,11},{10,... | collective-permute-start | bytes 786440 | tf_op jit(solution)/shard_map/ppermute | solution.py:497
  49.2 0.9 %project.5 = (bf16[1,64,1024]{2,1,0:T(8,128)(2,1)S(1)}, bf16[1,64,1024]{2,1,0:T(8,128)(2,1)S(1)}) custom-call(bf16[2,1,2,128,128]{4,3,2,1,0:T(8,128)(2,1)S(1)} %get-tuple-element.39.refs_0_, bf16[2,1,2,128,128]{4,3,2,1,0:T(8,128)(2,1)S(1)} %collective-permute-done.2.refs_1_, bf16[2,1,2,128,128]{4,3,2,1,0:T(8,128)(2,1)S(1)} %collective-permute-done.3.refs_2_, ...), custom_call_target="tpu_custom_call" | custom-call | flops 1 | bytes 1 | tf_op jit(solution)/shard_map/project/pallas_call | solution.py:475
  50.1 0.1 collective-permute-start.7
  50.2 0.5 collective-permute-start.8
  50.7 0.9 %project.4.keep_ref = f32[1,64,2048]{2,1,0:T(8,128)S(1)} custom-call(bf16[2,1,2,128,128]{4,3,2,1,0:T(8,128)(2,1)S(1)} %get-tuple-element.39.refs_0_, bf16[2,1,2,128,128]{4,3,2,1,0:T(8,128)(2,1)S(1)} %collective-permute-done.2.refs_1_, bf16[2,1,2,128,128]{4,3,2,1,0:T(8,128)(2,1)S(1)} %collective-permute-done.3.refs_2_, ...), custom_call_target="tpu_custom_call" | custom-call | flops 1 | bytes 1 | tf_op jit(solution)/shard_map/project/pallas_call | solution.py:475
  51.6 0.1 collective-permute-done.8.refs_1_
  51.7 4.1 %collective-permute-done.10.refs_2_ = bf16[1,64,2048]{2,1,0:T(8,128)(2,1)S(1)} collective-permute-done((bf16[1,64,2048]{2,1,0:T(8,128)(2,1)S(1)}, bf16[1,64,2048]{2,1,0:T(8,128)(2,1)S(1)}, u32[]{:S(2)}, u32[]{:S(2)}) %collective-permute-start.10) | collective-permute-done | bytes 262176 | tf_op jit(solution)/shard_map/ppermute | solution.py:497
  55.8 0.8 %sum.3 = bf16[1,64,2048]{2,1,0:T(8,128)(2,1)} custom-call(f32[1,64,2048]{2,1,0:T(8,128)S(1)} %project.4.keep_ref, bf16[1,64,1024]{2,1,0:T(8,128)(2,1)S(1)} %collective-permute-done.7.refs_0_, bf16[1,64,1024]{2,1,0:T(8,128)(2,1)S(1)} %collective-permute-done.8.refs_1_, bf16[1,64,2048]{2,1,0:T(8,128)(2,1)S(1)} %collective-permute-done.10.refs_2_), custom_call_target="tpu_custom_call" | custom-call | flops 1 | bytes 1 | tf_op jit(solution)/shard_map/sum/pallas_call | solution.py:488
  (10 shorter events, 0.1 us)
Async XLA Ops:
  2.2 6.5 %copy-start.1 = (bf16[64,32,128]{2,1,0:T(8,128)(2,1)S(1)}, bf16[64,32,128]{2,1,0:T(8,128)(2,1)}, u32[]{:S(2)}) copy-start(bf16[64,32,128]{2,1,0:T(8,128)(2,1)} %gate_ref.1) | copy-start | bytes 1572868
  2.3 6.5 %copy-start.2 = (bf16[128]{0:T(256)(128)(2,1)S(1)}, bf16[128]{0:T(256)(128)(2,1)}, u32[]{:S(2)}) copy-start(bf16[128]{0:T(256)(128)(2,1)} %param.12) | copy-start | bytes 772
  2.3 21.9 %all-to-all-start = ((bf16[16,272,128]{2,1,0:T(8,128)(2,1)}), bf16[16,272,128]{2,1,0:T(8,128)(2,1)S(1)}, u32[]{:S(2)}, u32[]{:S(2)}) async-start(bf16[16,272,128]{2,1,0:T(8,128)(2,1)} %pack.1), calls=%async_computation | async-start | bytes 2228224 | tf_op jit(solution)/shard_map/all_to_all | solution.py:381
  9.3 1.5 %collective-permute-start = (bf16[1,8,64,128]{3,2,1,0:T(8,128)(2,1)S(1)}, bf16[1,8,64,128]{3,2,1,0:T(8,128)(2,1)S(1)}, u32[]{:S(2)}, u32[]{:S(2)}) collective-permute-start(bf16[1,8,64,128]{3,2,1,0:T(8,128)(2,1)S(1)} %get-tuple-element.26), channel_id=1, source_target_pairs={{0,1},{1,0},{2,3},{3,2},{4,5},{5,4},{6,7},{7,6},{8,9},{9,8},{10,11... | collective-permute-start | bytes 393224 | tf_op jit(solution)/shard_map/ppermute | solution.py:396
  27.6 16.6 %copy-start = (bf16[1024,2048]{1,0:T(8,128)(2,1)S(1)}, bf16[1024,2048]{1,0:T(8,128)(2,1)}, u32[]{:S(2)}) copy-start(bf16[1024,2048]{1,0:T(8,128)(2,1)} %refs_8_.7) | copy-start | bytes 12582916
  28.7 10.5 %collective-permute-start.5 = (bf16[2,8,64,128]{3,2,1,0:T(8,128)(2,1)S(1)}, bf16[2,8,64,128]{3,2,1,0:T(8,128)(2,1)S(1)}, u32[]{:S(2)}, u32[]{:S(2)}) collective-permute-start(bf16[2,8,64,128]{3,2,1,0:T(8,128)(2,1)S(1)} %get-tuple-element.44), channel_id=1, source_target_pairs={{0,2},{1,3},{2,0},{3,1},{4,6},{5,7},{6,4},{7,5},{8,10},{9,11},{10,... | collective-permute-start | bytes 786440 | tf_op jit(solution)/shard_map/ppermute | solution.py:443
  29.8 5.2 %collective-permute-start.1 = (bf16[2,128,128]{2,1,0:T(8,128)(2,1)S(1)}, bf16[2,128,128]{2,1,0:T(8,128)(2,1)S(1)}, u32[]{:S(2)}, u32[]{:S(2)}) collective-permute-start(bf16[2,128,128]{2,1,0:T(8,128)(2,1)S(1)} %get-tuple-element.27), channel_id=1, source_target_pairs={{0,16},{16,0},{1,17},{17,1},{2,18},{18,2},{3,19},{19,3},{4,20},{20... | collective-permute-start | bytes 196616 | tf_op jit(solution)/shard_map/ppermute | solution.py:423
  35.6 6.0 %collective-permute-start.2 = (bf16[2,1,2,128,128]{4,3,2,1,0:T(8,128)(2,1)S(1)}, bf16[2,1,2,128,128]{4,3,2,1,0:T(8,128)(2,1)S(1)}, u32[]{:S(2)}, u32[]{:S(2)}) collective-permute-start(bf16[2,1,2,128,128]{4,3,2,1,0:T(8,128)(2,1)S(1)} %get-tuple-element.40), channel_id=1, source_target_pairs={{0,12},{4,8},{8,4},{12,0},{1,13},{5,9},{9,5},{13,1},{2,14},{6,10},... | collective-permute-start | bytes 393224 | tf_op jit(solution)/shard_map/ppermute | solution.py:465
  37.1 6.6 %collective-permute-start.3 = (bf16[2,1,2,128,128]{4,3,2,1,0:T(8,128)(2,1)S(1)}, bf16[2,1,2,128,128]{4,3,2,1,0:T(8,128)(2,1)S(1)}, u32[]{:S(2)}, u32[]{:S(2)}) collective-permute-start(bf16[2,1,2,128,128]{4,3,2,1,0:T(8,128)(2,1)S(1)} %get-tuple-element.41), channel_id=1, source_target_pairs={{0,8},{4,12},{8,0},{12,4},{1,9},{5,13},{9,1},{13,5},{2,10},{6,14},... | collective-permute-start | bytes 393224 | tf_op jit(solution)/shard_map/ppermute | solution.py:465
  39.2 5.0 %collective-permute-start.4 = (bf16[2,1,2,128,128]{4,3,2,1,0:T(8,128)(2,1)S(1)}, bf16[2,1,2,128,128]{4,3,2,1,0:T(8,128)(2,1)S(1)}, u32[]{:S(2)}, u32[]{:S(2)}) collective-permute-start(bf16[2,1,2,128,128]{4,3,2,1,0:T(8,128)(2,1)S(1)} %get-tuple-element.42), channel_id=1, source_target_pairs={{0,4},{4,0},{8,12},{12,8},{1,5},{5,1},{9,13},{13,9},{2,6},{6,2},{1... | collective-permute-start | bytes 393224 | tf_op jit(solution)/shard_map/ppermute | solution.py:465
  39.2 5.0 %collective-permute-start.6 = (bf16[1,8,64,128]{3,2,1,0:T(8,128)(2,1)S(1)}, bf16[1,8,64,128]{3,2,1,0:T(8,128)(2,1)S(1)}, u32[]{:S(2)}, u32[]{:S(2)}) collective-permute-start(bf16[1,8,64,128]{3,2,1,0:T(8,128)(2,1)S(1)} %slice.4), channel_id=1, source_target_pairs={{0,1},{1,0},{2,3},{3,2},{4,5},{5,4},{6,7},{7,6},{8,9},{9,8},{10,11... | collective-permute-start | bytes 393224 | tf_op jit(solution)/shard_map/ppermute | solution.py:444
  45.1 1.6 %collective-permute-start.9 = (bf16[1,64,2048]{2,1,0:T(8,128)(2,1)S(1)}, bf16[1,64,2048]{2,1,0:T(8,128)(2,1)S(1)}, u32[]{:S(2)}, u32[]{:S(2)}) collective-permute-start(bf16[1,64,2048]{2,1,0:T(8,128)(2,1)S(1)} %project.7), channel_id=1, source_target_pairs={{0,1},{1,0},{2,3},{3,2},{4,5},{5,4},{6,7},{7,6},{8,9},{9,8},{10,11... | collective-permute-start | bytes 786440 | tf_op jit(solution)/shard_map/ppermute | solution.py:485
  46.7 9.1 %collective-permute-start.10 = (bf16[1,64,2048]{2,1,0:T(8,128)(2,1)S(1)}, bf16[1,64,2048]{2,1,0:T(8,128)(2,1)S(1)}, u32[]{:S(2)}, u32[]{:S(2)}) collective-permute-start(bf16[1,64,2048]{2,1,0:T(8,128)(2,1)S(1)} %sum.2), channel_id=1, source_target_pairs={{0,2},{1,3},{2,0},{3,1},{4,6},{5,7},{6,4},{7,5},{8,10},{9,11},{10,... | collective-permute-start | bytes 786440 | tf_op jit(solution)/shard_map/ppermute | solution.py:497
  50.1 1.5 %collective-permute-start.7 = (bf16[1,64,1024]{2,1,0:T(8,128)(2,1)S(1)}, bf16[1,64,1024]{2,1,0:T(8,128)(2,1)S(1)}, u32[]{:S(2)}, u32[]{:S(2)}) collective-permute-start(bf16[1,64,1024]{2,1,0:T(8,128)(2,1)S(1)} %get-tuple-element.45), channel_id=1, source_target_pairs={{0,1},{1,0},{2,3},{3,2},{4,5},{5,4},{6,7},{7,6},{8,9},{9,8},{10,11... | collective-permute-start | bytes 393224 | tf_op jit(solution)/shard_map/ppermute | solution.py:485
  50.2 1.5 %collective-permute-start.8 = (bf16[1,64,1024]{2,1,0:T(8,128)(2,1)S(1)}, bf16[1,64,1024]{2,1,0:T(8,128)(2,1)S(1)}, u32[]{:S(2)}, u32[]{:S(2)}) collective-permute-start(bf16[1,64,1024]{2,1,0:T(8,128)(2,1)S(1)} %get-tuple-element.46), channel_id=1, source_target_pairs={{0,1},{1,0},{2,3},{3,2},{4,5},{5,4},{6,7},{7,6},{8,9},{9,8},{10,11... | collective-permute-start | bytes 393224 | tf_op jit(solution)/shard_map/ppermute | solution.py:485

commit v7 on v6

--- a/solution.py
+++ b/solution.py
@@ -101,22 +101,21 @@
         copy.wait()
 
 
-def gate_kernel(sub, n_head, gate_ref, gain_ref, own_ref, other_ref, *refs):
-    pair_refs, gates = refs[:-1], refs[-1]
+def gate_kernel(sub, n_head, gate_ref, gain_ref, own_ref, swap_ref, gates):
     heads = own_ref.shape[1]
     unused, along_head = position(sub, n_head)
     gate = gate_ref[...].astype(F32)
     gated = gain_ref[...].astype(F32)[:, None] * (gate / (1.0 + jnp.exp(-gate)))
     gates[...] = turned(gated.astype(BF16))
-
-    def group(distance):
-        return gates[pl.ds((along_head ^ distance) * heads, heads)]
-
-    own_ref[0] = group(0)
-    other_ref[0] = group(1)
+    for number in range(n_head // 2):
+        own_ref[number] = gates[pl.ds((along_head ^ (2 * number)) * heads, heads)]
+        swap_ref[number] = gates[pl.ds((along_head ^ (2 * number + 1)) * heads, heads)]
+
+
+def pair_kernel(own_ref, swapped_ref, *pair_refs):
     for number, pair_ref in enumerate(pair_refs):
-        for core in range(2):
-            pair_ref[core] = group(2 * number + 2 + core)
+        pair_ref[0] = own_ref[number + 1]
+        pair_ref[1] = swapped_ref[number + 1]
 
 
 def block_slabs(blocks, sub, sources):
@@ -159,8 +158,8 @@
     return solved
 
 
-def factor_kernel(tokens, ratio, sub, total_too, got_ref, after_ref, *refs):
-    state_ref, w_ref, u_ref, *tree_refs = refs
+def factor_kernel(tokens, ratio, sub, passing, total_too, got_ref, *refs):
+    state_ref, w_ref, u_ref, *tree_refs = refs[passing : len(refs) - passing]
     width = got_ref.shape[-1]
     per = SPAN // tokens
     blocks = got_ref.shape[0] // per
@@ -256,9 +255,8 @@
     return [neutral if start is None else start for start in starts]
 
 
-def spread_kernel(tokens, ratio, sub, passing, got_ref, w_ref, u_ref, *refs):
-    refs = refs[: len(refs) - passing]
-    tree_refs, (local_ref, reach_ref) = refs[: len(refs) - passing - 2], refs[-2:]
+def spread_kernel(tokens, ratio, sub, got_ref, w_ref, u_ref, *refs):
+    tree_refs, (local_ref, reach_ref) = refs[:-2], refs[-2:]
     width = got_ref.shape[-1]
     per = SPAN // tokens
     blocks = got_ref.shape[0] // per
@@ -305,8 +303,8 @@
                     out_ref[kept, piece, r] = (core * lax.rsqrt(mean_square + EPSILON)).astype(BF16)
 
 
-def project_kernel(order, shares, kept, mine, *refs):
-    parts = len(order)
+def project_kernel(order, gate_places, kept, mine, *refs):
+    parts, shares = len(order), len(gate_places)
     normed_refs, gate_refs = refs[:parts], refs[parts : parts + shares]
     weight_ref, *out_refs, rows_ref = refs[parts + 2 * shares :]
     unused, pieces, ratio, span, width = normed_refs[0].shape
@@ -322,7 +320,7 @@
             for r in range(ratio):
                 lanes = pl.ds(pl.multiple_of((source * ratio + r) * width, width), width)
                 normed = normed_ref[kept, share // per, r, from_rows].astype(F32)
-                gate = gate_refs[apart][0, source * ratio + r].astype(F32)
+                gate = gate_refs[apart][gate_places[apart], source * ratio + r].astype(F32)
                 rows_ref[place, lanes] = (normed * gate).astype(BF16)
     first = 0
     for out_ref in out_refs:
@@ -383,17 +381,27 @@
     heads = sub * ratio
     by_core = [(here, here ^ 1) for here in range(n_head)]
     group = (heads, tokens, width)
+    half = n_head // 2
     with jax.named_scope("gates"):
-        own_gates, other_gates, *pair_gates = pl.pallas_call(
+        own_gates, swap = pl.pallas_call(
             functools.partial(gate_kernel, sub, n_head),
-            out_shape=[shape((1,) + group, BF16)] * 2 + [shape((2,) + group, BF16)] * (n_head // 2 - 1),
+            out_shape=[shape((half,) + group, BF16)] * 2,
             in_specs=[VMEM] * 2,
-            out_specs=[VMEM] * (n_head // 2 + 1),
+            out_specs=[VMEM] * 2,
             scratch_shapes=[pltpu.VMEM((value_heads, tokens, width), BF16)],
             compiler_params=params(),
             cost_estimate=LIGHT,
         )(output_gate, norm_gain.reshape(1, width))
-    other_gates = lax.ppermute(other_gates, along_head, by_core)
+    swapped = lax.ppermute(swap, along_head, by_core)
+    with jax.named_scope("pair"):
+        pairs = pl.pallas_call(
+            pair_kernel,
+            out_shape=[shape((2,) + group, BF16)] * (half - 1),
+            in_specs=[VMEM] * 2,
+            out_specs=[VMEM] * (half - 1),
+            compiler_params=params(),
+            cost_estimate=LIGHT,
+        )(own_gates, swapped)
 
     state_type = BF16 if outer == 2 else F32
     with jax.named_scope("factors"):
@@ -410,38 +418,36 @@
             shape((blocks, ratio, SPAN, width), BF16),
             shape((blocks, ratio, SPAN, width), F32),
         ] + tree
-        state, w, u, *tree = pl.pallas_call(
-            functools.partial(factor_kernel, tokens, ratio, sub, outer > 2),
-            out_shape=out_shape,
-            in_specs=[VMEM, ANY],
-            out_specs=[VMEM] * len(out_shape),
+        state, w, u, *rest = pl.pallas_call(
+            functools.partial(factor_kernel, tokens, ratio, sub, half - 1, outer > 2),
+            out_shape=out_shape + [shape((2,) + group, BF16)] * (half - 1),
+            in_specs=[VMEM] + [ANY] * (half - 1),
+            out_specs=[VMEM] * len(out_shape) + [ANY] * (half - 1),
+            input_output_aliases={1 + number: len(out_shape) + number for number in range(half - 1)},
             compiler_params=params(),
             cost_estimate=LIGHT,
-        )(got, other_gates)
+        )(got, *pairs)
+        tree, pairs = rest[: len(rest) - half + 1], rest[len(rest) - half + 1 :]
 
     onward = [(here, (here + 1) % outer) for here in range(outer)]
     incoming = lax.ppermute(state, "outer", onward)
     with jax.named_scope("spread"):
-        passing = len(pair_gates)
-        first = 3 + 2 * len(depths)
-        local, reach, *pair_gates = pl.pallas_call(
-            functools.partial(spread_kernel, tokens, ratio, sub, passing),
+        local, reach = pl.pallas_call(
+            functools.partial(spread_kernel, tokens, ratio, sub),
             out_shape=[
                 shape((ratio, blocks, SPAN, width), F32),
                 shape((ratio, blocks, SPAN, width), BF16),
-            ]
-            + [shape((2,) + group, BF16)] * passing,
-            in_specs=[VMEM] * first + [ANY] * passing,
-            out_specs=[VMEM] * 2 + [ANY] * passing,
-            input_output_aliases={first + number: 2 + number for number in range(passing)},
+            ],
+            in_specs=[VMEM] * (3 + 2 * len(depths)),
+            out_specs=[VMEM] * 2,
             compiler_params=params(),
             cost_estimate=LIGHT,
-        )(got, w, u, *tree[: 2 * len(depths)], *pair_gates)
-    gates = [own_gates, other_gates]
-    for number, pair in enumerate(pair_gates):
+        )(got, w, u, *tree[: 2 * len(depths)])
+    gates = [(own_gates, 0), (swapped, 0)]
+    for number, pair in enumerate(pairs):
         distance = 2 * number + 2
         pair = lax.ppermute(pair, along_head, [(here, here ^ distance) for here in range(n_head)])
-        gates += [pair, lax.ppermute(pair[1:], along_head, by_core)]
+        gates += [(pair, 0), (pair, 1)]
     for hop in range(outer - 2):
         incoming = jnp.where(lax.axis_index("outer") == 0, 0.0, incoming)
         turned_by = jnp.einsum("hde,hef->hdf", tree[-1], incoming, precision=lax.Precision.HIGHEST)
@@ -467,13 +473,14 @@
     ]
     for kept in range(2):
         cuts = 1 + kept
-        operands = [*normed, *gates[half * (1 - kept) :], *gates[: half * (1 - kept)], output_weight]
+        used, others = gates[half * (1 - kept) : half * (2 - kept)], gates[half * kept : half * (1 + kept)]
+        operands = [*normed, *[array for array, unused in used + others], output_weight]
         results = []
         for mine in range(2):
             pieces_of = 1 if mine else cuts
             with jax.named_scope("project"):
                 results += pl.pallas_call(
-                    functools.partial(project_kernel, order, half, kept, mine),
+                    functools.partial(project_kernel, order, [place for unused, place in used], kept, mine),
                     out_shape=[shape(quarter[:-1] + (columns // pieces_of,), F32 if mine else BF16)] * pieces_of,
                     in_specs=[VMEM] * (sub + half) + [ANY] * half + [VMEM],
                     out_specs=[VMEM] * pieces_of,

time: 56.9 us -> 55.8 us (0.981)
  waiting for transfers between devices: 26.8 us -> 25.8 us
    ppermute x1, waiting for transfers between devices: 2.62 us -> 1.53 us  [per_device(): incoming = lax.ppermute(state, 'outer', onward)]
    ppermute x2 -> x1, waiting for transfers between devices: 0.99 us -> 1.16 us  [per_device(): swapped = lax.ppermute(swap, along_head, by_core)]
    pallas_call x6 -> x7, Pallas kernels: 7.95 us -> 7.95 us  [the longest x4 3.48 us: per_device(): pl.pallas_call(functools.partial(project_kernel, order, [place for unused...]
  transfers between devices with their start and end apart: 12 -> 11, of which waited for: 9 -> 9; matrix products, arithmetic and copies ran while one was open for 0% -> 0% of each run, Pallas kernels for 7% -> 9%
where the time goes in v7:
time: 55.8 us; the launch traced here: 55.6 us
  waiting for transfers between devices  25.8 us (46%)
  starting transfers between devices  17.5 us (31%)
  Pallas kernels  12.1 us (22%)
    all_to_all x1, waiting for transfers between devices, per_device(): lax.all_to_all(packed, partner_order(sub, n_head), split_axis=0, concat_a...  13.2 us
    all_to_all x1, starting transfers between devices, per_device(): lax.all_to_all(packed, partner_order(sub, n_head), split_axis=0, concat_a...  6.43 us
    ppermute x3, waiting for transfers between devices, per_device(): lax.ppermute(part, along_sub, [(here, here ^ distance) for here in range(...  4.96 us
    ppermute x1, waiting for transfers between devices, per_device(): lax.ppermute(summed, along_head, [(here, here ^ half) for here in range(n...  4.12 us
    ppermute x3, starting transfers between devices, per_device(): lax.ppermute(part, along_sub, [(here, here ^ distance) for here in range(...  3.64 us
    pallas_call x4, Pallas kernels, per_device(): pl.pallas_call(functools.partial(project_kernel, order, [place for unused...  3.48 us
    pallas_call x1, Pallas kernels, per_device(): pl.pallas_call(functools.partial(factor_kernel, tokens, ratio, sub, half...  3.38 us
    ppermute x1, starting transfers between devices, per_device(): incoming = lax.ppermute(state, 'outer', onward)  2.6 us
  transfers between devices with their start and end apart: 11, of which 9 were waited for; matrix products, arithmetic and copies ran while one was open for 0% of the time, Pallas kernels for 9%

profile of v7, /device:TPU:0, one launch (start us, length us, event | category | flops | bytes accessed | tf_op | source)
XLA Modules:
  0.0 55.6 jit_solution(3001312838150837039)
XLA Ops:
  0.0 2.2 %pack.1 = bf16[16,272,128]{2,1,0:T(8,128)(2,1)} custom-call(bf16[64,16,128]{2,1,0:T(8,128)(2,1)} %q_hbm.1, bf16[64,16,128]{2,1,0:T(8,128)(2,1)} %k_hbm.1, bf16[64,32,128]{2,1,0:T(8,128)(2,1)} %v_hbm.1, bf16[32,64]{1,0:T(8,128)(2,1)} %bitcast.4), custom_call_target="tpu_custom_call" | custom-call | tf_op jit(solution)/shard_map/pack/pallas_call | solution.py:363
  2.3 0.0 copy-start.1
  2.3 0.0 copy-start.2
  2.3 6.4 %all-to-all-start = ((bf16[16,272,128]{2,1,0:T(8,128)(2,1)}), bf16[16,272,128]{2,1,0:T(8,128)(2,1)S(1)}, u32[]{:S(2)}, u32[]{:S(2)}) async-start(bf16[16,272,128]{2,1,0:T(8,128)(2,1)} %pack.1), calls=%async_computation | async-start | bytes 2228224 | tf_op jit(solution)/shard_map/all_to_all | solution.py:379
  8.7 0.6 %gates.1 = (bf16[2,8,64,128]{3,2,1,0:T(8,128)(2,1)S(1)}, bf16[2,8,64,128]{3,2,1,0:T(8,128)(2,1)S(1)}) custom-call(bf16[64,32,128]{2,1,0:T(8,128)(2,1)S(1)} %copy-done.1, bf16[1,128]{1,0:T(2,128)(2,1)S(1)} %bitcast.3), custom_call_target="tpu_custom_call" | custom-call | flops 1 | bytes 1 | tf_op jit(solution)/shard_map/gates/pallas_call | solution.py:386
  9.3 0.5 collective-permute-start
  9.8 1.2 %collective-permute-done.swapped_ref.refs_5_.refs_7_ = bf16[2,8,64,128]{3,2,1,0:T(8,128)(2,1)S(1)} collective-permute-done((bf16[2,8,64,128]{3,2,1,0:T(8,128)(2,1)S(1)}, bf16[2,8,64,128]{3,2,1,0:T(8,128)(2,1)S(1)}, u32[]{:S(2)}, u32[]{:S(2)}) %collective-permute-start) | collective-permute-done | bytes 262176 | tf_op jit(solution)/shard_map/ppermute | solution.py:395
  11.0 13.2 %all-to-all-done.got_ref = bf16[16,272,128]{2,1,0:T(8,128)(2,1)S(1)} async-done(((bf16[16,272,128]{2,1,0:T(8,128)(2,1)}), bf16[16,272,128]{2,1,0:T(8,128)(2,1)S(1)}, u32[]{:S(2)}, u32[]{:S(2)}) %all-to-all-start) | async-done | bytes 1114144 | tf_op jit(solution)/shard_map/all_to_all | solution.py:379
  24.2 3.4 %factors.1 = (bf16[2,128,128]{2,1,0:T(8,128)(2,1)S(1)}, bf16[8,2,128,128]{3,2,1,0:T(8,128)(2,1)S(1)}, f32[8,2,128,128]{3,2,1,0:T(8,128)S(1)}, bf16[8,2,128,128]{...) custom-call(bf16[16,272,128]{2,1,0:T(8,128)(2,1)S(1)} %all-to-all-do, ...), custom_call_target="tpu_custom_call", output_to_operand_aliasing={{9}: (1, {})} | custom-call | flops 1 | bytes 1 | tf_op jit(solution)/shard_map/factors/pallas_call | solution.py:421
  27.6 1.2 %collective-permute-start.5 = (bf16[2,8,64,128]{3,2,1,0:T(8,128)(2,1)S(1)}, bf16[2,8,64,128]{3,2,1,0:T(8,128)(2,1)S(1)}, u32[]{:S(2)}, u32[]{:S(2)}) collective-permute-start(bf16[2,8,64,128]{3,2,1,0:T(8,128)(2,1)S(1)} %get-tuple-element.42), channel_id=1, source_target_pairs={{0,2},{1,3},{2,0},{3,1},{4,6},{5,7},{6,4},{7,5},{8,10},{9,11},{10,... | collective-permute-start | bytes 786440 | tf_op jit(solution)/shard_map/ppermute | solution.py:449
  28.7 2.6 %collective-permute-start.1 = (bf16[2,128,128]{2,1,0:T(8,128)(2,1)S(1)}, bf16[2,128,128]{2,1,0:T(8,128)(2,1)S(1)}, u32[]{:S(2)}, u32[]{:S(2)}) collective-permute-start(bf16[2,128,128]{2,1,0:T(8,128)(2,1)S(1)} %get-tuple-element.27), channel_id=1, source_target_pairs={{0,16},{16,0},{1,17},{17,1},{2,18},{18,2},{3,19},{19,3},{4,20},{20... | collective-permute-start | bytes 196616 | tf_op jit(solution)/shard_map/ppermute | solution.py:433
  31.4 1.1 %spread.1 = (f32[2,8,128,128]{3,2,1,0:T(8,128)S(1)}, bf16[2,8,128,128]{3,2,1,0:T(8,128)(2,1)S(1)}) custom-call(bf16[16,272,128]{2,1,0:T(8,128)(2,1)S(1)} %all-to-all-done.got_ref, bf16[8,2,128,128]{3,2,1,0:T(8,128)(2,1)S(1)} %get-tuple-element.28.w_ref, f32[8,2,128,128]{3,2,1,0:T(8,128)S(1)} %get-tuple-element.29.u_ref, ...), custom_call_target="tpu_custom_call" | custom-call | flops 1 | bytes 1 | tf_op jit(solution)/shard_map/spread/pallas_call | solution.py:435
  32.4 1.5 %collective-permute-done.1.state_ref = bf16[2,128,128]{2,1,0:T(8,128)(2,1)S(1)} collective-permute-done((bf16[2,128,128]{2,1,0:T(8,128)(2,1)S(1)}, bf16[2,128,128]{2,1,0:T(8,128)(2,1)S(1)}, u32[]{:S(2)}, u32[]{:S(2)}) %collective-permute-start.1) | collective-permute-done | bytes 65568 | tf_op jit(solution)/shard_map/ppermute | solution.py:433
  34.0 0.5 join.1
  34.5 1.5 %collective-permute-start.2 = (bf16[2,1,2,128,128]{4,3,2,1,0:T(8,128)(2,1)S(1)}, bf16[2,1,2,128,128]{4,3,2,1,0:T(8,128)(2,1)S(1)}, u32[]{:S(2)}, u32[]{:S(2)}) collective-permute-start(bf16[2,1,2,128,128]{4,3,2,1,0:T(8,128)(2,1)S(1)} %get-tuple-element.39), channel_id=1, source_target_pairs={{0,12},{4,8},{8,4},{12,0},{1,13},{5,9},{9,5},{13,1},{2,14},{6,10},... | collective-permute-start | bytes 393224 | tf_op jit(solution)/shard_map/ppermute | solution.py:471
  36.0 2.1 %collective-permute-start.3 = (bf16[2,1,2,128,128]{4,3,2,1,0:T(8,128)(2,1)S(1)}, bf16[2,1,2,128,128]{4,3,2,1,0:T(8,128)(2,1)S(1)}, u32[]{:S(2)}, u32[]{:S(2)}) collective-permute-start(bf16[2,1,2,128,128]{4,3,2,1,0:T(8,128)(2,1)S(1)} %get-tuple-element.40), channel_id=1, source_target_pairs={{0,8},{4,12},{8,0},{12,4},{1,9},{5,13},{9,1},{13,5},{2,10},{6,14},... | collective-permute-start | bytes 393224 | tf_op jit(solution)/shard_map/ppermute | solution.py:471
  38.1 0.0 collective-permute-start.4
  38.1 2.4 %collective-permute-done.2.refs_1_ = bf16[2,1,2,128,128]{4,3,2,1,0:T(8,128)(2,1)S(1)} collective-permute-done((bf16[2,1,2,128,128]{4,3,2,1,0:T(8,128)(2,1)S(1)}, bf16[2,1,2,128,128]{4,3,2,1,0:T(8,128)(2,1)S(1)}, u32[]{:S(2)}, u32[]{:S(2)}) %collective-permute-start.2) | collective-permute-done | bytes 131104 | tf_op jit(solution)/shard_map/ppermute | solution.py:471
  40.5 2.1 %collective-permute-done.3.refs_2_ = bf16[2,1,2,128,128]{4,3,2,1,0:T(8,128)(2,1)S(1)} collective-permute-done((bf16[2,1,2,128,128]{4,3,2,1,0:T(8,128)(2,1)S(1)}, bf16[2,1,2,128,128]{4,3,2,1,0:T(8,128)(2,1)S(1)}, u32[]{:S(2)}, u32[]{:S(2)}) %collective-permute-start.3) | collective-permute-done | bytes 131104 | tf_op jit(solution)/shard_map/ppermute | solution.py:471
  42.6 0.5 collective-permute-done.4.refs_3_
  43.1 0.9 %project.7 = bf16[1,64,2048]{2,1,0:T(8,128)(2,1)S(1)} custom-call(bf16[2,1,2,128,128]{4,3,2,1,0:T(8,128)(2,1)S(1)} %get-tuple-element.38.refs_0_, bf16[2,1,2,128,128]{4,3,2,1,0:T(8,128)(2,1)S(1)} %collective-permute-done.2.refs_1_, bf16[2,1,2,128,128]{4,3,2,1,0:T(8,128)(2,1)S(1)} %collective-permute-done.3.refs_2_, ...), custom_call_target="tpu_custom_call" | custom-call | flops 1 | bytes 1 | tf_op jit(solution)/shard_map/project/pallas_call | solution.py:482
  44.0 0.1 collective-permute-start.8
  44.0 0.9 %project.6.keep_ref = f32[1,64,2048]{2,1,0:T(8,128)S(1)} custom-call(bf16[2,1,2,128,128]{4,3,2,1,0:T(8,128)(2,1)S(1)} %get-tuple-element.38.refs_0_, bf16[2,1,2,128,128]{4,3,2,1,0:T(8,128)(2,1)S(1)} %collective-permute-done.2.refs_1_, bf16[2,1,2,128,128]{4,3,2,1,0:T(8,128)(2,1)S(1)} %collective-permute-done.3.refs_2_, ...), custom_call_target="tpu_custom_call" | custom-call | flops 1 | bytes 1 | tf_op jit(solution)/shard_map/project/pallas_call | solution.py:482
  44.9 0.6 %collective-permute-done.8.refs_0_ = bf16[1,64,2048]{2,1,0:T(8,128)(2,1)S(1)} collective-permute-done((bf16[1,64,2048]{2,1,0:T(8,128)(2,1)S(1)}, bf16[1,64,2048]{2,1,0:T(8,128)(2,1)S(1)}, u32[]{:S(2)}, u32[]{:S(2)}) %collective-permute-start.8) | collective-permute-done | bytes 262176 | tf_op jit(solution)/shard_map/ppermute | solution.py:492
  45.6 2.5 %collective-permute-start.9 = (bf16[1,64,2048]{2,1,0:T(8,128)(2,1)S(1)}, bf16[1,64,2048]{2,1,0:T(8,128)(2,1)S(1)}, u32[]{:S(2)}, u32[]{:S(2)}) collective-permute-start(bf16[1,64,2048]{2,1,0:T(8,128)(2,1)S(1)} %sum.2), channel_id=1, source_target_pairs={{0,2},{1,3},{2,0},{3,1},{4,6},{5,7},{6,4},{7,5},{8,10},{9,11},{10,... | collective-permute-start | bytes 786440 | tf_op jit(solution)/shard_map/ppermute | solution.py:504
  48.2 0.9 %project.5 = (bf16[1,64,1024]{2,1,0:T(8,128)(2,1)S(1)}, bf16[1,64,1024]{2,1,0:T(8,128)(2,1)S(1)}) custom-call(bf16[2,1,2,128,128]{4,3,2,1,0:T(8,128)(2,1)S(1)} %get-tuple-element.38.refs_0_, bf16[2,1,2,128,128]{4,3,2,1,0:T(8,128)(2,1)S(1)} %collective-permute-done.2.refs_1_, bf16[2,1,2,128,128]{4,3,2,1,0:T(8,128)(2,1)S(1)} %collective-permute-done.3.refs_2_, ...), custom_call_target="tpu_custom_call" | custom-call | flops 1 | bytes 1 | tf_op jit(solution)/shard_map/project/pallas_call | solution.py:482
  49.0 0.1 collective-permute-start.6
  49.1 0.5 collective-permute-start.7
  49.6 0.9 %project.4.keep_ref = f32[1,64,2048]{2,1,0:T(8,128)S(1)} custom-call(bf16[2,1,2,128,128]{4,3,2,1,0:T(8,128)(2,1)S(1)} %get-tuple-element.38.refs_0_, bf16[2,1,2,128,128]{4,3,2,1,0:T(8,128)(2,1)S(1)} %collective-permute-done.2.refs_1_, bf16[2,1,2,128,128]{4,3,2,1,0:T(8,128)(2,1)S(1)} %collective-permute-done.3.refs_2_, ...), custom_call_target="tpu_custom_call" | custom-call | flops 1 | bytes 1 | tf_op jit(solution)/shard_map/project/pallas_call | solution.py:482
  50.5 0.1 collective-permute-done.7.refs_1_
  50.6 4.1 %collective-permute-done.9.refs_2_ = bf16[1,64,2048]{2,1,0:T(8,128)(2,1)S(1)} collective-permute-done((bf16[1,64,2048]{2,1,0:T(8,128)(2,1)S(1)}, bf16[1,64,2048]{2,1,0:T(8,128)(2,1)S(1)}, u32[]{:S(2)}, u32[]{:S(2)}) %collective-permute-start.9) | collective-permute-done | bytes 262176 | tf_op jit(solution)/shard_map/ppermute | solution.py:504
  54.8 0.8 %sum.3 = bf16[1,64,2048]{2,1,0:T(8,128)(2,1)} custom-call(f32[1,64,2048]{2,1,0:T(8,128)S(1)} %project.4.keep_ref, bf16[1,64,1024]{2,1,0:T(8,128)(2,1)S(1)} %collective-permute-done.6.refs_0_, bf16[1,64,1024]{2,1,0:T(8,128)(2,1)S(1)} %collective-permute-done.7.refs_1_, bf16[1,64,2048]{2,1,0:T(8,128)(2,1)S(1)} %collective-permute-done.9.refs_2_), custom_call_target="tpu_custom_call" | custom-call | flops 1 | bytes 1 | tf_op jit(solution)/shard_map/sum/pallas_call | solution.py:495
  (8 shorter events, 0.1 us)
Async XLA Ops:
  2.3 6.5 %copy-start.1 = (bf16[64,32,128]{2,1,0:T(8,128)(2,1)S(1)}, bf16[64,32,128]{2,1,0:T(8,128)(2,1)}, u32[]{:S(2)}) copy-start(bf16[64,32,128]{2,1,0:T(8,128)(2,1)} %gate_ref.1) | copy-start | bytes 1572868
  2.3 6.5 %copy-start.2 = (bf16[128]{0:T(256)(128)(2,1)S(1)}, bf16[128]{0:T(256)(128)(2,1)}, u32[]{:S(2)}) copy-start(bf16[128]{0:T(256)(128)(2,1)} %param.12) | copy-start | bytes 772
  2.3 21.9 %all-to-all-start = ((bf16[16,272,128]{2,1,0:T(8,128)(2,1)}), bf16[16,272,128]{2,1,0:T(8,128)(2,1)S(1)}, u32[]{:S(2)}, u32[]{:S(2)}) async-start(bf16[16,272,128]{2,1,0:T(8,128)(2,1)} %pack.1), calls=%async_computation | async-start | bytes 2228224 | tf_op jit(solution)/shard_map/all_to_all | solution.py:379
  9.3 1.6 %collective-permute-start = (bf16[2,8,64,128]{3,2,1,0:T(8,128)(2,1)S(1)}, bf16[2,8,64,128]{3,2,1,0:T(8,128)(2,1)S(1)}, u32[]{:S(2)}, u32[]{:S(2)}) collective-permute-start(bf16[2,8,64,128]{3,2,1,0:T(8,128)(2,1)S(1)} %get-tuple-element.26), channel_id=1, source_target_pairs={{0,1},{1,0},{2,3},{3,2},{4,5},{5,4},{6,7},{7,6},{8,9},{9,8},{10,11... | collective-permute-start | bytes 786440 | tf_op jit(solution)/shard_map/ppermute | solution.py:395
  27.6 15.5 %collective-permute-start.5 = (bf16[2,8,64,128]{3,2,1,0:T(8,128)(2,1)S(1)}, bf16[2,8,64,128]{3,2,1,0:T(8,128)(2,1)S(1)}, u32[]{:S(2)}, u32[]{:S(2)}) collective-permute-start(bf16[2,8,64,128]{3,2,1,0:T(8,128)(2,1)S(1)} %get-tuple-element.42), channel_id=1, source_target_pairs={{0,2},{1,3},{2,0},{3,1},{4,6},{5,7},{6,4},{7,5},{8,10},{9,11},{10,... | collective-permute-start | bytes 786440 | tf_op jit(solution)/shard_map/ppermute | solution.py:449
  28.7 5.2 %collective-permute-start.1 = (bf16[2,128,128]{2,1,0:T(8,128)(2,1)S(1)}, bf16[2,128,128]{2,1,0:T(8,128)(2,1)S(1)}, u32[]{:S(2)}, u32[]{:S(2)}) collective-permute-start(bf16[2,128,128]{2,1,0:T(8,128)(2,1)S(1)} %get-tuple-element.27), channel_id=1, source_target_pairs={{0,16},{16,0},{1,17},{17,1},{2,18},{18,2},{3,19},{19,3},{4,20},{20... | collective-permute-start | bytes 196616 | tf_op jit(solution)/shard_map/ppermute | solution.py:433
  31.3 11.7 %copy-start = (bf16[1024,2048]{1,0:T(8,128)(2,1)S(1)}, bf16[1024,2048]{1,0:T(8,128)(2,1)}, u32[]{:S(2)}) copy-start(bf16[1024,2048]{1,0:T(8,128)(2,1)} %refs_8_.7) | copy-start | bytes 12582916
  34.5 6.0 %collective-permute-start.2 = (bf16[2,1,2,128,128]{4,3,2,1,0:T(8,128)(2,1)S(1)}, bf16[2,1,2,128,128]{4,3,2,1,0:T(8,128)(2,1)S(1)}, u32[]{:S(2)}, u32[]{:S(2)}) collective-permute-start(bf16[2,1,2,128,128]{4,3,2,1,0:T(8,128)(2,1)S(1)} %get-tuple-element.39), channel_id=1, source_target_pairs={{0,12},{4,8},{8,4},{12,0},{1,13},{5,9},{9,5},{13,1},{2,14},{6,10},... | collective-permute-start | bytes 393224 | tf_op jit(solution)/shard_map/ppermute | solution.py:471
  36.0 6.6 %collective-permute-start.3 = (bf16[2,1,2,128,128]{4,3,2,1,0:T(8,128)(2,1)S(1)}, bf16[2,1,2,128,128]{4,3,2,1,0:T(8,128)(2,1)S(1)}, u32[]{:S(2)}, u32[]{:S(2)}) collective-permute-start(bf16[2,1,2,128,128]{4,3,2,1,0:T(8,128)(2,1)S(1)} %get-tuple-element.40), channel_id=1, source_target_pairs={{0,8},{4,12},{8,0},{12,4},{1,9},{5,13},{9,1},{13,5},{2,10},{6,14},... | collective-permute-start | bytes 393224 | tf_op jit(solution)/shard_map/ppermute | solution.py:471
  38.1 5.0 %collective-permute-start.4 = (bf16[2,1,2,128,128]{4,3,2,1,0:T(8,128)(2,1)S(1)}, bf16[2,1,2,128,128]{4,3,2,1,0:T(8,128)(2,1)S(1)}, u32[]{:S(2)}, u32[]{:S(2)}) collective-permute-start(bf16[2,1,2,128,128]{4,3,2,1,0:T(8,128)(2,1)S(1)} %get-tuple-element.41), channel_id=1, source_target_pairs={{0,4},{4,0},{8,12},{12,8},{1,5},{5,1},{9,13},{13,9},{2,6},{6,2},{1... | collective-permute-start | bytes 393224 | tf_op jit(solution)/shard_map/ppermute | solution.py:471
  44.0 1.6 %collective-permute-start.8 = (bf16[1,64,2048]{2,1,0:T(8,128)(2,1)S(1)}, bf16[1,64,2048]{2,1,0:T(8,128)(2,1)S(1)}, u32[]{:S(2)}, u32[]{:S(2)}) collective-permute-start(bf16[1,64,2048]{2,1,0:T(8,128)(2,1)S(1)} %project.7), channel_id=1, source_target_pairs={{0,1},{1,0},{2,3},{3,2},{4,5},{5,4},{6,7},{7,6},{8,9},{9,8},{10,11... | collective-permute-start | bytes 786440 | tf_op jit(solution)/shard_map/ppermute | solution.py:492
  45.6 9.1 %collective-permute-start.9 = (bf16[1,64,2048]{2,1,0:T(8,128)(2,1)S(1)}, bf16[1,64,2048]{2,1,0:T(8,128)(2,1)S(1)}, u32[]{:S(2)}, u32[]{:S(2)}) collective-permute-start(bf16[1,64,2048]{2,1,0:T(8,128)(2,1)S(1)} %sum.2), channel_id=1, source_target_pairs={{0,2},{1,3},{2,0},{3,1},{4,6},{5,7},{6,4},{7,5},{8,10},{9,11},{10,... | collective-permute-start | bytes 786440 | tf_op jit(solution)/shard_map/ppermute | solution.py:504
  49.0 1.5 %collective-permute-start.6 = (bf16[1,64,1024]{2,1,0:T(8,128)(2,1)S(1)}, bf16[1,64,1024]{2,1,0:T(8,128)(2,1)S(1)}, u32[]{:S(2)}, u32[]{:S(2)}) collective-permute-start(bf16[1,64,1024]{2,1,0:T(8,128)(2,1)S(1)} %get-tuple-element.43), channel_id=1, source_target_pairs={{0,1},{1,0},{2,3},{3,2},{4,5},{5,4},{6,7},{7,6},{8,9},{9,8},{10,11... | collective-permute-start | bytes 393224 | tf_op jit(solution)/shard_map/ppermute | solution.py:492
  49.1 1.5 %collective-permute-start.7 = (bf16[1,64,1024]{2,1,0:T(8,128)(2,1)S(1)}, bf16[1,64,1024]{2,1,0:T(8,128)(2,1)S(1)}, u32[]{:S(2)}, u32[]{:S(2)}) collective-permute-start(bf16[1,64,1024]{2,1,0:T(8,128)(2,1)S(1)} %get-tuple-element.44), channel_id=1, source_target_pairs={{0,1},{1,0},{2,3},{3,2},{4,5},{5,4},{6,7},{7,6},{8,9},{9,8},{10,11... | collective-permute-start | bytes 393224 | tf_op jit(solution)/shard_map/ppermute | solution.py:492

commit v8 on v7

--- a/solution.py
+++ b/solution.py
@@ -118,6 +118,10 @@
         pair_ref[1] = swapped_ref[number + 1]
 
 
+def release_kernel(*refs):
+    pass
+
+
 def block_slabs(blocks, sub, sources):
     places = [partner(source, sub, sources // sub) for source in range(sources)]
     per = sources // blocks
@@ -159,7 +163,7 @@
 
 
 def factor_kernel(tokens, ratio, sub, passing, total_too, got_ref, *refs):
-    state_ref, w_ref, u_ref, *tree_refs = refs[passing : len(refs) - passing]
+    state_ref, w_ref, u_ref, *tree_refs = refs[passing:]
     width = got_ref.shape[-1]
     per = SPAN // tokens
     blocks = got_ref.shape[0] // per
@@ -303,31 +307,33 @@
                     out_ref[kept, piece, r] = (core * lax.rsqrt(mean_square + EPSILON)).astype(BF16)
 
 
-def project_kernel(order, gate_places, kept, mine, *refs):
+def project_kernel(order, gate_places, kept, *refs):
     parts, shares = len(order), len(gate_places)
     normed_refs, gate_refs = refs[:parts], refs[parts : parts + shares]
-    weight_ref, *out_refs, rows_ref = refs[parts + 2 * shares :]
+    weight_ref, *send_refs, keep_ref, rows_ref = refs[parts + 2 * shares :]
     unused, pieces, ratio, span, width = normed_refs[0].shape
     tokens = gate_refs[0].shape[2]
     per = span // tokens
     along_sub, along_head = position(parts, 2 * shares)
     for distance, normed_ref in zip(order, normed_refs):
         source = along_sub ^ distance
-        for apart in range(1 - mine, shares, 2):
+        for apart, gate_ref in enumerate(gate_refs):
             share = (along_head ^ apart) & (shares - 1)
-            place = pl.ds(pl.multiple_of(share // 2 * tokens, tokens), tokens)
+            first = ((1 - apart % 2) * (shares // 2) + share // 2) * tokens
+            place = pl.ds(pl.multiple_of(first, tokens), tokens)
             from_rows = pl.ds(pl.multiple_of(share % per * tokens, tokens), tokens)
             for r in range(ratio):
                 lanes = pl.ds(pl.multiple_of((source * ratio + r) * width, width), width)
                 normed = normed_ref[kept, share // per, r, from_rows].astype(F32)
-                gate = gate_refs[apart][gate_places[apart], source * ratio + r].astype(F32)
+                gate = gate_ref[gate_places[apart], source * ratio + r].astype(F32)
                 rows_ref[place, lanes] = (normed * gate).astype(BF16)
+    out = dot(rows_ref[...], weight_ref[...]).reshape((2,) + keep_ref.shape)
     first = 0
-    for out_ref in out_refs:
-        columns = out_ref.shape[-1]
-        out = dot(rows_ref[...], weight_ref[:, first : first + columns])
-        out_ref[...] = out.reshape(out_ref.shape).astype(out_ref.dtype)
+    for send_ref in send_refs:
+        columns = send_ref.shape[-1]
+        send_ref[...] = out[0, :, :, first : first + columns].astype(BF16)
         first += columns
+    keep_ref[...] = out[1]
 
 
 def sum_kernel(keep_ref, *refs):
@@ -418,16 +424,14 @@
             shape((blocks, ratio, SPAN, width), BF16),
             shape((blocks, ratio, SPAN, width), F32),
         ] + tree
-        state, w, u, *rest = pl.pallas_call(
+        state, w, u, *tree = pl.pallas_call(
             functools.partial(factor_kernel, tokens, ratio, sub, half - 1, outer > 2),
-            out_shape=out_shape + [shape((2,) + group, BF16)] * (half - 1),
+            out_shape=out_shape,
             in_specs=[VMEM] + [ANY] * (half - 1),
-            out_specs=[VMEM] * len(out_shape) + [ANY] * (half - 1),
-            input_output_aliases={1 + number: len(out_shape) + number for number in range(half - 1)},
+            out_specs=[VMEM] * len(out_shape),
             compiler_params=params(),
             cost_estimate=LIGHT,
         )(got, *pairs)
-        tree, pairs = rest[: len(rest) - half + 1], rest[len(rest) - half + 1 :]
 
     onward = [(here, (here + 1) % outer) for here in range(outer)]
     incoming = lax.ppermute(state, "outer", onward)
@@ -443,6 +447,16 @@
             compiler_params=params(),
             cost_estimate=LIGHT,
         )(got, w, u, *tree[: 2 * len(depths)])
+    with jax.named_scope("release"):
+        pairs = pl.pallas_call(
+            release_kernel,
+            out_shape=[shape((2,) + group, BF16)] * (half - 1),
+            in_specs=[ANY] * half,
+            out_specs=[ANY] * (half - 1),
+            input_output_aliases={1 + number: number for number in range(half - 1)},
+            compiler_params=params(),
+            cost_estimate=LIGHT,
+        )(state, *pairs)
     gates = [(own_gates, 0), (swapped, 0)]
     for number, pair in enumerate(pairs):
         distance = 2 * number + 2
@@ -465,7 +479,7 @@
             in_specs=[VMEM] * 3,
             out_specs=[VMEM] * sub,
             compiler_params=params(),
-            cost_estimate=LIGHT,
+            cost_estimate=pl.CostEstimate(flops=2 * 10**9, bytes_accessed=1, transcendentals=0),
         )(incoming, local, reach)
     normed = [
         lax.ppermute(part, along_sub, [(here, here ^ distance) for here in range(sub)]) if distance else part
@@ -475,20 +489,16 @@
         cuts = 1 + kept
         used, others = gates[half * (1 - kept) : half * (2 - kept)], gates[half * kept : half * (1 + kept)]
         operands = [*normed, *[array for array, unused in used + others], output_weight]
-        results = []
-        for mine in range(2):
-            pieces_of = 1 if mine else cuts
-            with jax.named_scope("project"):
-                results += pl.pallas_call(
-                    functools.partial(project_kernel, order, [place for unused, place in used], kept, mine),
-                    out_shape=[shape(quarter[:-1] + (columns // pieces_of,), F32 if mine else BF16)] * pieces_of,
-                    in_specs=[VMEM] * (sub + half) + [ANY] * half + [VMEM],
-                    out_specs=[VMEM] * pieces_of,
-                    scratch_shapes=[pltpu.VMEM((shard_tokens // 4, heads * width), BF16)],
-                    compiler_params=params(),
-                    cost_estimate=LIGHT,
-                )(*operands)
-        *sends, keep = results
+        with jax.named_scope("project"):
+            *sends, keep = pl.pallas_call(
+                functools.partial(project_kernel, order, [place for unused, place in used], kept),
+                out_shape=[shape(quarter[:-1] + (columns // cuts,), BF16)] * cuts + [shape(quarter, F32)],
+                in_specs=[VMEM] * (sub + half) + [ANY] * half + [VMEM],
+                out_specs=[VMEM] * (cuts + 1),
+                scratch_shapes=[pltpu.VMEM((shard_tokens // 2, heads * width), BF16)],
+                compiler_params=params(),
+                cost_estimate=LIGHT,
+            )(*operands)
         arrived = [lax.ppermute(send, along_head, by_core) for send in sends]
         last = n_head == 4 and kept == 1
         with jax.named_scope("sum"):

time: 55.8 us -> 55.7 us (level)
  waiting for transfers between devices: 25.8 us -> 30.1 us
  starting transfers between devices: 17.5 us -> 15 us
  Pallas kernels: 12.1 us -> 10.2 us
    ppermute x1, starting transfers between devices: 2.54 us -> 0.11 us  [per_device(): lax.ppermute(summed, along_head, [(here, here ^ half) for here in range(n...]
    pallas_call x4 -> x2, Pallas kernels: 3.48 us -> 1.58 us  [per_device(): pl.pallas_call(functools.partial(project_kernel, order, [place for unused...]
    ppermute x1, waiting for transfers between devices: 4.12 us -> 5.91 us  [per_device(): lax.ppermute(summed, along_head, [(here, here ^ half) for here in range(n...]
    ppermute x3, waiting for transfers between devices: 0.79 us -> 2.55 us  [per_device(): arrived = [lax.ppermute(send, along_head, by_core) for send in sends]]
  transfers between devices with their start and end apart: 11 -> 11, of which waited for: 9 -> 10; matrix products, arithmetic and copies ran while one was open for 0% -> 0% of each run, Pallas kernels for 9% -> 5%
where the time goes in v8:
time: 55.7 us; the launch traced here: 55.4 us
  waiting for transfers between devices  30.1 us (54%)
  starting transfers between devices  15 us (27%)
  Pallas kernels  10.2 us (18%)
    all_to_all x1, waiting for transfers between devices, per_device(): lax.all_to_all(packed, partner_order(sub, n_head), split_axis=0, concat_a...  13.2 us
    all_to_all x1, starting transfers between devices, per_device(): lax.all_to_all(packed, partner_order(sub, n_head), split_axis=0, concat_a...  6.43 us
    ppermute x1, waiting for transfers between devices, per_device(): lax.ppermute(summed, along_head, [(here, here ^ half) for here in range(n...  5.91 us
    ppermute x3, waiting for transfers between devices, per_device(): lax.ppermute(part, along_sub, [(here, here ^ distance) for here in range(...  5.46 us
    ppermute x3, starting transfers between devices, per_device(): lax.ppermute(part, along_sub, [(here, here ^ distance) for here in range(...  3.55 us
    pallas_call x1, Pallas kernels, per_device(): pl.pallas_call(functools.partial(factor_kernel, tokens, ratio, sub, half...  3.39 us
    ppermute x1, starting transfers between devices, per_device(): incoming = lax.ppermute(state, 'outer', onward)  2.65 us
    ppermute x3, waiting for transfers between devices, per_device(): arrived = [lax.ppermute(send, along_head, by_core) for send in sends]  2.55 us
  transfers between devices with their start and end apart: 11, of which 10 were waited for; matrix products, arithmetic and copies ran while one was open for 0% of the time, Pallas kernels for 5%

profile of v8, /device:TPU:0, one launch (start us, length us, event | category | flops | bytes accessed | tf_op | source)
XLA Modules:
  0.0 55.4 jit_solution(6702519739654257291)
XLA Ops:
  0.0 2.2 %pack.1 = bf16[16,272,128]{2,1,0:T(8,128)(2,1)} custom-call(bf16[64,16,128]{2,1,0:T(8,128)(2,1)} %q_hbm.1, bf16[64,16,128]{2,1,0:T(8,128)(2,1)} %k_hbm.1, bf16[64,32,128]{2,1,0:T(8,128)(2,1)} %v_hbm.1, bf16[32,64]{1,0:T(8,128)(2,1)} %bitcast.4), custom_call_target="tpu_custom_call" | custom-call | tf_op jit(solution)/shard_map/pack/pallas_call | solution.py:369
  2.2 0.0 copy-start.1
  2.3 0.0 copy-start.2
  2.3 6.4 %all-to-all-start = ((bf16[16,272,128]{2,1,0:T(8,128)(2,1)}), bf16[16,272,128]{2,1,0:T(8,128)(2,1)S(1)}, u32[]{:S(2)}, u32[]{:S(2)}) async-start(bf16[16,272,128]{2,1,0:T(8,128)(2,1)} %pack.1), calls=%async_computation | async-start | bytes 2228224 | tf_op jit(solution)/shard_map/all_to_all | solution.py:385
  8.7 0.6 %gates.1 = (bf16[2,8,64,128]{3,2,1,0:T(8,128)(2,1)S(1)}, bf16[2,8,64,128]{3,2,1,0:T(8,128)(2,1)S(1)}) custom-call(bf16[64,32,128]{2,1,0:T(8,128)(2,1)S(1)} %copy-done.1, bf16[1,128]{1,0:T(2,128)(2,1)S(1)} %bitcast.3), custom_call_target="tpu_custom_call" | custom-call | flops 1 | bytes 1 | tf_op jit(solution)/shard_map/gates/pallas_call | solution.py:392
  9.3 0.5 collective-permute-start
  9.8 1.2 %collective-permute-done.swapped_ref.refs_5_.refs_7_ = bf16[2,8,64,128]{3,2,1,0:T(8,128)(2,1)S(1)} collective-permute-done((bf16[2,8,64,128]{3,2,1,0:T(8,128)(2,1)S(1)}, bf16[2,8,64,128]{3,2,1,0:T(8,128)(2,1)S(1)}, u32[]{:S(2)}, u32[]{:S(2)}) %collective-permute-start) | collective-permute-done | bytes 262176 | tf_op jit(solution)/shard_map/ppermute | solution.py:401
  11.0 13.2 %all-to-all-done.got_ref = bf16[16,272,128]{2,1,0:T(8,128)(2,1)S(1)} async-done(((bf16[16,272,128]{2,1,0:T(8,128)(2,1)}), bf16[16,272,128]{2,1,0:T(8,128)(2,1)S(1)}, u32[]{:S(2)}, u32[]{:S(2)}) %all-to-all-start) | async-done | bytes 1114144 | tf_op jit(solution)/shard_map/all_to_all | solution.py:385
  24.2 3.4 %factors.1 = (bf16[2,128,128]{2,1,0:T(8,128)(2,1)S(1)}, bf16[8,2,128,128]{3,2,1,0:T(8,128)(2,1)S(1)}, f32[8,2,128,128]{3,2,1,0:T(8,128)S(1)}, bf16[8,2,128,128]{...) custom-call(bf16[16,272,128]{2,1,0:T(8,128)(2,1)S(1)} %all-to-all-do, ...), custom_call_target="tpu_custom_call" | custom-call | flops 1 | bytes 1 | tf_op jit(solution)/shard_map/factors/pallas_call | solution.py:427
  27.6 2.7 %collective-permute-start.1 = (bf16[2,128,128]{2,1,0:T(8,128)(2,1)S(1)}, bf16[2,128,128]{2,1,0:T(8,128)(2,1)S(1)}, u32[]{:S(2)}, u32[]{:S(2)}) collective-permute-start(bf16[2,128,128]{2,1,0:T(8,128)(2,1)S(1)} %get-tuple-element.29.refs_0_), channel_id=1, source_target_pairs={{0,16},{16,0},{1,17},{17,1},{2,18},{18,2},{3,19},{19,3},{4,20},{20... | collective-permute-start | bytes 196616 | tf_op jit(solution)/shard_map/ppermute | solution.py:437
  30.2 1.1 %collective-permute-start.5 = (bf16[2,8,64,128]{3,2,1,0:T(8,128)(2,1)S(1)}, bf16[2,8,64,128]{3,2,1,0:T(8,128)(2,1)S(1)}, u32[]{:S(2)}, u32[]{:S(2)}) collective-permute-start(bf16[2,8,64,128]{3,2,1,0:T(8,128)(2,1)S(1)} %release.1), channel_id=1, source_target_pairs={{0,2},{1,3},{2,0},{3,1},{4,6},{5,7},{6,4},{7,5},{8,10},{9,11},{10,... | collective-permute-start | bytes 786440 | tf_op jit(solution)/shard_map/ppermute | solution.py:463
  31.3 1.1 %spread.1 = (f32[2,8,128,128]{3,2,1,0:T(8,128)S(1)}, bf16[2,8,128,128]{3,2,1,0:T(8,128)(2,1)S(1)}) custom-call(bf16[16,272,128]{2,1,0:T(8,128)(2,1)S(1)} %all-to-all-done.got_ref, bf16[8,2,128,128]{3,2,1,0:T(8,128)(2,1)S(1)} %get-tuple-element.30.w_ref, f32[8,2,128,128]{3,2,1,0:T(8,128)S(1)} %get-tuple-element.31.u_ref, ...), custom_call_target="tpu_custom_call" | custom-call | flops 1 | bytes 1 | tf_op jit(solution)/shard_map/spread/pallas_call | solution.py:439
  32.4 1.8 %collective-permute-done.1.state_ref = bf16[2,128,128]{2,1,0:T(8,128)(2,1)S(1)} collective-permute-done((bf16[2,128,128]{2,1,0:T(8,128)(2,1)S(1)}, bf16[2,128,128]{2,1,0:T(8,128)(2,1)S(1)}, u32[]{:S(2)}, u32[]{:S(2)}) %collective-permute-start.1) | collective-permute-done | bytes 65568 | tf_op jit(solution)/shard_map/ppermute | solution.py:437
  34.3 0.5 join.1
  34.8 1.1 %collective-permute-start.2 = (bf16[2,1,2,128,128]{4,3,2,1,0:T(8,128)(2,1)S(1)}, bf16[2,1,2,128,128]{4,3,2,1,0:T(8,128)(2,1)S(1)}, u32[]{:S(2)}, u32[]{:S(2)}) collective-permute-start(bf16[2,1,2,128,128]{4,3,2,1,0:T(8,128)(2,1)S(1)} %get-tuple-element.41), channel_id=1, source_target_pairs={{0,12},{4,8},{8,4},{12,0},{1,13},{5,9},{9,5},{13,1},{2,14},{6,10},... | collective-permute-start | bytes 393224 | tf_op jit(solution)/shard_map/ppermute | solution.py:485
  35.9 1.7 %collective-permute-start.3 = (bf16[2,1,2,128,128]{4,3,2,1,0:T(8,128)(2,1)S(1)}, bf16[2,1,2,128,128]{4,3,2,1,0:T(8,128)(2,1)S(1)}, u32[]{:S(2)}, u32[]{:S(2)}) collective-permute-start(bf16[2,1,2,128,128]{4,3,2,1,0:T(8,128)(2,1)S(1)} %get-tuple-element.42), channel_id=1, source_target_pairs={{0,8},{4,12},{8,0},{12,4},{1,9},{5,13},{9,1},{13,5},{2,10},{6,14},... | collective-permute-start | bytes 393224 | tf_op jit(solution)/shard_map/ppermute | solution.py:485
  37.6 0.7 %collective-permute-start.4 = (bf16[2,1,2,128,128]{4,3,2,1,0:T(8,128)(2,1)S(1)}, bf16[2,1,2,128,128]{4,3,2,1,0:T(8,128)(2,1)S(1)}, u32[]{:S(2)}, u32[]{:S(2)}) collective-permute-start(bf16[2,1,2,128,128]{4,3,2,1,0:T(8,128)(2,1)S(1)} %get-tuple-element.43), channel_id=1, source_target_pairs={{0,4},{4,0},{8,12},{12,8},{1,5},{5,1},{9,13},{13,9},{2,6},{6,2},{1... | collective-permute-start | bytes 393224 | tf_op jit(solution)/shard_map/ppermute | solution.py:485
  38.3 3.8 %collective-permute-done.2.refs_1_ = bf16[2,1,2,128,128]{4,3,2,1,0:T(8,128)(2,1)S(1)} collective-permute-done((bf16[2,1,2,128,128]{4,3,2,1,0:T(8,128)(2,1)S(1)}, bf16[2,1,2,128,128]{4,3,2,1,0:T(8,128)(2,1)S(1)}, u32[]{:S(2)}, u32[]{:S(2)}) %collective-permute-start.2) | collective-permute-done | bytes 131104 | tf_op jit(solution)/shard_map/ppermute | solution.py:485
  42.1 1.4 %collective-permute-done.3.refs_2_ = bf16[2,1,2,128,128]{4,3,2,1,0:T(8,128)(2,1)S(1)} collective-permute-done((bf16[2,1,2,128,128]{4,3,2,1,0:T(8,128)(2,1)S(1)}, bf16[2,1,2,128,128]{4,3,2,1,0:T(8,128)(2,1)S(1)}, u32[]{:S(2)}, u32[]{:S(2)}) %collective-permute-start.3) | collective-permute-done | bytes 131104 | tf_op jit(solution)/shard_map/ppermute | solution.py:485
  43.6 0.2 collective-permute-done.4.refs_3_
  43.8 0.0 collective-permute-done.5.refs_6_.refs_7_.refs_4_.refs_5_
  43.8 0.8 %project.3 = (bf16[1,64,2048]{2,1,0:T(8,128)(2,1)S(1)}, f32[1,64,2048]{2,1,0:T(8,128)S(1)}) custom-call(bf16[2,1,2,128,128]{4,3,2,1,0:T(8,128)(2,1)S(1)} %get-tuple-element.40.refs_0_, bf16[2,1,2,128,128]{4,3,2,1,0:T(8,128)(2,1)S(1)} %collective-permute-done.2.refs_1_, bf16[2,1,2,128,128]{4,3,2,1,0:T(8,128)(2,1)S(1)} %collective-permute-done.3.refs_2_, ...), custom_call_target="tpu_custom_call" | custom-call | flops 1 | bytes 1 | tf_op jit(solution)/shard_map/project/pallas_call | solution.py:493
  44.6 0.1 collective-permute-start.8
  44.7 1.5 %collective-permute-done.8.refs_0_ = bf16[1,64,2048]{2,1,0:T(8,128)(2,1)S(1)} collective-permute-done((bf16[1,64,2048]{2,1,0:T(8,128)(2,1)S(1)}, bf16[1,64,2048]{2,1,0:T(8,128)(2,1)S(1)}, u32[]{:S(2)}, u32[]{:S(2)}) %collective-permute-start.8) | collective-permute-done | bytes 262176 | tf_op jit(solution)/shard_map/ppermute | solution.py:502
  46.2 0.1 collective-permute-start.9
  46.4 0.8 %project.2 = (bf16[1,64,1024]{2,1,0:T(8,128)(2,1)S(1)}, bf16[1,64,1024]{2,1,0:T(8,128)(2,1)S(1)}, f32[1,64,2048]{2,1,0:T(8,128)S(1)}) custom-call(bf16[2,1,2,128,128]{4,3,2,1,0:T(8,128)(2,1)S(1)} %get-tuple-element.40.refs_0_, bf16[2,1,2,128,128]{4,3,2,1,0:T(8,128)(2,1)S(1)} %collective-permute-done.2.refs_1_, ...), custom_call_target="tpu_custom_call" | custom-call | flops 1 | bytes 1 | tf_op jit(solution)/shard_map/project/pallas_call | solution.py:493
  47.1 0.2 collective-permute-start.6
  47.3 0.4 collective-permute-start.7
  47.7 0.8 %collective-permute-done.6.refs_0_ = bf16[1,64,1024]{2,1,0:T(8,128)(2,1)S(1)} collective-permute-done((bf16[1,64,1024]{2,1,0:T(8,128)(2,1)S(1)}, bf16[1,64,1024]{2,1,0:T(8,128)(2,1)S(1)}, u32[]{:S(2)}, u32[]{:S(2)}) %collective-permute-start.6) | collective-permute-done | bytes 131104 | tf_op jit(solution)/shard_map/ppermute | solution.py:502
  48.6 0.2 collective-permute-done.7.refs_1_
  48.7 5.9 %collective-permute-done.9.refs_2_ = bf16[1,64,2048]{2,1,0:T(8,128)(2,1)S(1)} collective-permute-done((bf16[1,64,2048]{2,1,0:T(8,128)(2,1)S(1)}, bf16[1,64,2048]{2,1,0:T(8,128)(2,1)S(1)}, u32[]{:S(2)}, u32[]{:S(2)}) %collective-permute-start.9) | collective-permute-done | bytes 262176 | tf_op jit(solution)/shard_map/ppermute | solution.py:514
  54.7 0.8 %sum.3 = bf16[1,64,2048]{2,1,0:T(8,128)(2,1)} custom-call(f32[1,64,2048]{2,1,0:T(8,128)S(1)} %get-tuple-element.44.keep_ref, bf16[1,64,1024]{2,1,0:T(8,128)(2,1)S(1)} %collective-permute-done.6.refs_0_, bf16[1,64,1024]{2,1,0:T(8,128)(2,1)S(1)} %collective-permute-done.7.refs_1_, bf16[1,64,2048]{2,1,0:T(8,128)(2,1)S(1)} %collective-permute-done.9.refs_2_), custom_call_target="tpu_custom_call" | custom-call | flops 1 | bytes 1 | tf_op jit(solution)/shard_map/sum/pallas_call | solution.py:505
  (7 shorter events, 0.1 us)
Async XLA Ops:
  2.2 6.5 %copy-start.1 = (bf16[64,32,128]{2,1,0:T(8,128)(2,1)S(1)}, bf16[64,32,128]{2,1,0:T(8,128)(2,1)}, u32[]{:S(2)}) copy-start(bf16[64,32,128]{2,1,0:T(8,128)(2,1)} %gate_ref.1) | copy-start | bytes 1572868
  2.3 6.5 %copy-start.2 = (bf16[128]{0:T(256)(128)(2,1)S(1)}, bf16[128]{0:T(256)(128)(2,1)}, u32[]{:S(2)}) copy-start(bf16[128]{0:T(256)(128)(2,1)} %param.12) | copy-start | bytes 772
  2.3 21.9 %all-to-all-start = ((bf16[16,272,128]{2,1,0:T(8,128)(2,1)}), bf16[16,272,128]{2,1,0:T(8,128)(2,1)S(1)}, u32[]{:S(2)}, u32[]{:S(2)}) async-start(bf16[16,272,128]{2,1,0:T(8,128)(2,1)} %pack.1), calls=%async_computation | async-start | bytes 2228224 | tf_op jit(solution)/shard_map/all_to_all | solution.py:385
  9.3 1.6 %collective-permute-start = (bf16[2,8,64,128]{3,2,1,0:T(8,128)(2,1)S(1)}, bf16[2,8,64,128]{3,2,1,0:T(8,128)(2,1)S(1)}, u32[]{:S(2)}, u32[]{:S(2)}) collective-permute-start(bf16[2,8,64,128]{3,2,1,0:T(8,128)(2,1)S(1)} %get-tuple-element.28), channel_id=1, source_target_pairs={{0,1},{1,0},{2,3},{3,2},{4,5},{5,4},{6,7},{7,6},{8,9},{9,8},{10,11... | collective-permute-start | bytes 786440 | tf_op jit(solution)/shard_map/ppermute | solution.py:401
  27.6 6.7 %collective-permute-start.1 = (bf16[2,128,128]{2,1,0:T(8,128)(2,1)S(1)}, bf16[2,128,128]{2,1,0:T(8,128)(2,1)S(1)}, u32[]{:S(2)}, u32[]{:S(2)}) collective-permute-start(bf16[2,128,128]{2,1,0:T(8,128)(2,1)S(1)} %get-tuple-element.29.refs_0_), channel_id=1, source_target_pairs={{0,16},{16,0},{1,17},{17,1},{2,18},{18,2},{3,19},{19,3},{4,20},{20... | collective-permute-start | bytes 196616 | tf_op jit(solution)/shard_map/ppermute | solution.py:437
  30.2 13.5 %collective-permute-start.5 = (bf16[2,8,64,128]{3,2,1,0:T(8,128)(2,1)S(1)}, bf16[2,8,64,128]{3,2,1,0:T(8,128)(2,1)S(1)}, u32[]{:S(2)}, u32[]{:S(2)}) collective-permute-start(bf16[2,8,64,128]{3,2,1,0:T(8,128)(2,1)S(1)} %release.1), channel_id=1, source_target_pairs={{0,2},{1,3},{2,0},{3,1},{4,6},{5,7},{6,4},{7,5},{8,10},{9,11},{10,... | collective-permute-start | bytes 786440 | tf_op jit(solution)/shard_map/ppermute | solution.py:463
  34.3 9.5 %copy-start = (bf16[1024,2048]{1,0:T(8,128)(2,1)S(1)}, bf16[1024,2048]{1,0:T(8,128)(2,1)}, u32[]{:S(2)}) copy-start(bf16[1024,2048]{1,0:T(8,128)(2,1)} %refs_8_.3) | copy-start | bytes 12582916
  34.8 7.3 %collective-permute-start.2 = (bf16[2,1,2,128,128]{4,3,2,1,0:T(8,128)(2,1)S(1)}, bf16[2,1,2,128,128]{4,3,2,1,0:T(8,128)(2,1)S(1)}, u32[]{:S(2)}, u32[]{:S(2)}) collective-permute-start(bf16[2,1,2,128,128]{4,3,2,1,0:T(8,128)(2,1)S(1)} %get-tuple-element.41), channel_id=1, source_target_pairs={{0,12},{4,8},{8,4},{12,0},{1,13},{5,9},{9,5},{13,1},{2,14},{6,10},... | collective-permute-start | bytes 393224 | tf_op jit(solution)/shard_map/ppermute | solution.py:485
  35.9 7.7 %collective-permute-start.3 = (bf16[2,1,2,128,128]{4,3,2,1,0:T(8,128)(2,1)S(1)}, bf16[2,1,2,128,128]{4,3,2,1,0:T(8,128)(2,1)S(1)}, u32[]{:S(2)}, u32[]{:S(2)}) collective-permute-start(bf16[2,1,2,128,128]{4,3,2,1,0:T(8,128)(2,1)S(1)} %get-tuple-element.42), channel_id=1, source_target_pairs={{0,8},{4,12},{8,0},{12,4},{1,9},{5,13},{9,1},{13,5},{2,10},{6,14},... | collective-permute-start | bytes 393224 | tf_op jit(solution)/shard_map/ppermute | solution.py:485
  37.6 6.2 %collective-permute-start.4 = (bf16[2,1,2,128,128]{4,3,2,1,0:T(8,128)(2,1)S(1)}, bf16[2,1,2,128,128]{4,3,2,1,0:T(8,128)(2,1)S(1)}, u32[]{:S(2)}, u32[]{:S(2)}) collective-permute-start(bf16[2,1,2,128,128]{4,3,2,1,0:T(8,128)(2,1)S(1)} %get-tuple-element.43), channel_id=1, source_target_pairs={{0,4},{4,0},{8,12},{12,8},{1,5},{5,1},{9,13},{13,9},{2,6},{6,2},{1... | collective-permute-start | bytes 393224 | tf_op jit(solution)/shard_map/ppermute | solution.py:485
  44.6 1.6 %collective-permute-start.8 = (bf16[1,64,2048]{2,1,0:T(8,128)(2,1)S(1)}, bf16[1,64,2048]{2,1,0:T(8,128)(2,1)S(1)}, u32[]{:S(2)}, u32[]{:S(2)}) collective-permute-start(bf16[1,64,2048]{2,1,0:T(8,128)(2,1)S(1)} %get-tuple-element.48), channel_id=1, source_target_pairs={{0,1},{1,0},{2,3},{3,2},{4,5},{5,4},{6,7},{7,6},{8,9},{9,8},{10,11... | collective-permute-start | bytes 786440 | tf_op jit(solution)/shard_map/ppermute | solution.py:502
  46.2 8.4 %collective-permute-start.9 = (bf16[1,64,2048]{2,1,0:T(8,128)(2,1)S(1)}, bf16[1,64,2048]{2,1,0:T(8,128)(2,1)S(1)}, u32[]{:S(2)}, u32[]{:S(2)}) collective-permute-start(bf16[1,64,2048]{2,1,0:T(8,128)(2,1)S(1)} %sum.2), channel_id=1, source_target_pairs={{0,2},{1,3},{2,0},{3,1},{4,6},{5,7},{6,4},{7,5},{8,10},{9,11},{10,... | collective-permute-start | bytes 786440 | tf_op jit(solution)/shard_map/ppermute | solution.py:514
  47.1 1.4 %collective-permute-start.6 = (bf16[1,64,1024]{2,1,0:T(8,128)(2,1)S(1)}, bf16[1,64,1024]{2,1,0:T(8,128)(2,1)S(1)}, u32[]{:S(2)}, u32[]{:S(2)}) collective-permute-start(bf16[1,64,1024]{2,1,0:T(8,128)(2,1)S(1)} %get-tuple-element.45), channel_id=1, source_target_pairs={{0,1},{1,0},{2,3},{3,2},{4,5},{5,4},{6,7},{7,6},{8,9},{9,8},{10,11... | collective-permute-start | bytes 393224 | tf_op jit(solution)/shard_map/ppermute | solution.py:502
  47.3 1.4 %collective-permute-start.7 = (bf16[1,64,1024]{2,1,0:T(8,128)(2,1)S(1)}, bf16[1,64,1024]{2,1,0:T(8,128)(2,1)S(1)}, u32[]{:S(2)}, u32[]{:S(2)}) collective-permute-start(bf16[1,64,1024]{2,1,0:T(8,128)(2,1)S(1)} %get-tuple-element.46), channel_id=1, source_target_pairs={{0,1},{1,0},{2,3},{3,2},{4,5},{5,4},{6,7},{7,6},{8,9},{9,8},{10,11... | collective-permute-start | bytes 393224 | tf_op jit(solution)/shard_map/ppermute | solution.py:502

commit v9 on v8

--- a/solution.py
+++ b/solution.py
@@ -116,10 +116,6 @@
     for number, pair_ref in enumerate(pair_refs):
         pair_ref[0] = own_ref[number + 1]
         pair_ref[1] = swapped_ref[number + 1]
-
-
-def release_kernel(*refs):
-    pass
 
 
 def block_slabs(blocks, sub, sources):
@@ -259,8 +255,9 @@
     return [neutral if start is None else start for start in starts]
 
 
-def spread_kernel(tokens, ratio, sub, got_ref, w_ref, u_ref, *refs):
-    tree_refs, (local_ref, reach_ref) = refs[:-2], refs[-2:]
+def spread_kernel(tokens, ratio, sub, passing, got_ref, w_ref, u_ref, *refs):
+    refs = refs[: len(refs) - passing]
+    tree_refs, (local_ref, reach_ref) = refs[: len(refs) - passing - 2], refs[-2:]
     width = got_ref.shape[-1]
     per = SPAN // tokens
     blocks = got_ref.shape[0] // per
@@ -310,7 +307,7 @@
 def project_kernel(order, gate_places, kept, *refs):
     parts, shares = len(order), len(gate_places)
     normed_refs, gate_refs = refs[:parts], refs[parts : parts + shares]
-    weight_ref, *send_refs, keep_ref, rows_ref = refs[parts + 2 * shares :]
+    weight_ref, *out_refs, rows_ref = refs[parts + 2 * shares :]
     unused, pieces, ratio, span, width = normed_refs[0].shape
     tokens = gate_refs[0].shape[2]
     per = span // tokens
@@ -327,28 +324,39 @@
                 normed = normed_ref[kept, share // per, r, from_rows].astype(F32)
                 gate = gate_ref[gate_places[apart], source * ratio + r].astype(F32)
                 rows_ref[place, lanes] = (normed * gate).astype(BF16)
-    out = dot(rows_ref[...], weight_ref[...]).reshape((2,) + keep_ref.shape)
-    first = 0
+    multiply(0, rows_ref[...], weight_ref, out_refs)
+
+
+def multiply(first, rows, weight_ref, out_refs):
+    *send_refs, keep_ref = out_refs
+    every = keep_ref.shape[-1]
+    out = dot(rows, weight_ref[:, first : first + every]).reshape((2,) + keep_ref.shape)
+    start = 0
     for send_ref in send_refs:
         columns = send_ref.shape[-1]
-        send_ref[...] = out[0, :, :, first : first + columns].astype(BF16)
-        first += columns
+        send_ref[...] = out[0, :, :, start : start + columns].astype(BF16)
+        start += columns
     keep_ref[...] = out[1]
 
 
+def more_kernel(first, rows_ref, weight_ref, *out_refs):
+    multiply(first, rows_ref[...], weight_ref, out_refs)
+
+
 def sum_kernel(keep_ref, *refs):
-    out_ref = refs[-1]
-    first = 0
-    for number, got_ref in enumerate(refs[:-1]):
-        columns = got_ref.shape[-1]
-        if first == keep_ref.shape[-1]:
-            break
-        total = keep_ref[:, :, first : first + columns] + got_ref[...].astype(F32)
-        for more_ref in refs[:-1]:
-            if more_ref.shape[-1] == keep_ref.shape[-1] and more_ref is not got_ref:
-                total = total + more_ref[:, :, first : first + columns].astype(F32)
-        out_ref[:, :, first : first + columns] = total.astype(out_ref.dtype)
-        first += columns
+    *got_refs, out_ref = refs
+    every = keep_ref.shape[-1]
+    placed, start = [], 0
+    for got_ref in got_refs:
+        placed.append((start, got_ref))
+        start = (start + got_ref.shape[-1]) % every
+    cuts = sorted({first for first, unused in placed} | {every})
+    for first, last in zip(cuts, cuts[1:]):
+        total = keep_ref[:, :, first:last]
+        for start, got_ref in placed:
+            if start <= first and last <= start + got_ref.shape[-1]:
+                total = total + got_ref[:, :, first - start : last - start].astype(F32)
+        out_ref[:, :, first:last] = total.astype(out_ref.dtype)
 
 
 def per_device(
@@ -436,27 +444,20 @@
     onward = [(here, (here + 1) % outer) for here in range(outer)]
     incoming = lax.ppermute(state, "outer", onward)
     with jax.named_scope("spread"):
-        local, reach = pl.pallas_call(
-            functools.partial(spread_kernel, tokens, ratio, sub),
+        read = 3 + 2 * len(depths)
+        local, reach, *pairs = pl.pallas_call(
+            functools.partial(spread_kernel, tokens, ratio, sub, half - 1),
             out_shape=[
                 shape((ratio, blocks, SPAN, width), F32),
                 shape((ratio, blocks, SPAN, width), BF16),
-            ],
-            in_specs=[VMEM] * (3 + 2 * len(depths)),
-            out_specs=[VMEM] * 2,
+            ]
+            + [shape((2,) + group, BF16)] * (half - 1),
+            in_specs=[VMEM] * read + [ANY] * (half - 1),
+            out_specs=[VMEM] * 2 + [ANY] * (half - 1),
+            input_output_aliases={read + number: 2 + number for number in range(half - 1)},
             compiler_params=params(),
             cost_estimate=LIGHT,
-        )(got, w, u, *tree[: 2 * len(depths)])
-    with jax.named_scope("release"):
-        pairs = pl.pallas_call(
-            release_kernel,
-            out_shape=[shape((2,) + group, BF16)] * (half - 1),
-            in_specs=[ANY] * half,
-            out_specs=[ANY] * (half - 1),
-            input_output_aliases={1 + number: number for number in range(half - 1)},
-            compiler_params=params(),
-            cost_estimate=LIGHT,
-        )(state, *pairs)
+        )(got, w, u, *tree[: 2 * len(depths)], *pairs)
     gates = [(own_gates, 0), (swapped, 0)]
     for number, pair in enumerate(pairs):
         distance = 2 * number + 2
@@ -485,33 +486,57 @@
         lax.ppermute(part, along_sub, [(here, here ^ distance) for here in range(sub)]) if distance else part
         for distance, part in zip(order, normed)
     ]
-    for kept in range(2):
-        cuts = 1 + kept
+    across = [(here, here ^ half) for here in range(n_head)]
+
+    def project(kept, pieces, every, rows_too):
         used, others = gates[half * (1 - kept) : half * (2 - kept)], gates[half * kept : half * (1 + kept)]
-        operands = [*normed, *[array for array, unused in used + others], output_weight]
+        rows = pltpu.VMEM((shard_tokens // 2, heads * width), BF16)
         with jax.named_scope("project"):
-            *sends, keep = pl.pallas_call(
+            return pl.pallas_call(
                 functools.partial(project_kernel, order, [place for unused, place in used], kept),
-                out_shape=[shape(quarter[:-1] + (columns // cuts,), BF16)] * cuts + [shape(quarter, F32)],
+                out_shape=[shape(quarter[:-1] + (piece,), BF16) for piece in pieces]
+                + [shape(quarter[:-1] + (every,), F32)]
+                + [shape(rows.shape, BF16)] * rows_too,
                 in_specs=[VMEM] * (sub + half) + [ANY] * half + [VMEM],
-                out_specs=[VMEM] * (cuts + 1),
-                scratch_shapes=[pltpu.VMEM((shard_tokens // 2, heads * width), BF16)],
+                out_specs=[VMEM] * (len(pieces) + 1 + rows_too),
+                scratch_shapes=[rows] * (1 - rows_too),
                 compiler_params=params(),
                 cost_estimate=LIGHT,
-            )(*operands)
-        arrived = [lax.ppermute(send, along_head, by_core) for send in sends]
-        last = n_head == 4 and kept == 1
+            )(*normed, *[array for array, unused in used + others], output_weight)
+
+    def add(keep, arrived, kind):
         with jax.named_scope("sum"):
-            summed = pl.pallas_call(
+            return pl.pallas_call(
                 sum_kernel,
-                out_shape=shape(quarter, F32 if kept and not last else BF16),
-                in_specs=[VMEM] * (1 + cuts + kept),
+                out_shape=shape(keep.shape, kind),
+                in_specs=[VMEM] * (1 + len(arrived)),
                 out_specs=VMEM,
                 compiler_params=params(),
                 cost_estimate=LIGHT,
-            )(keep, *arrived, *([passed_on] if kept else []))
-        if not kept:
-            passed_on = lax.ppermute(summed, along_head, [(here, here ^ half) for here in range(n_head)])
+            )(keep, *arrived)
+
+    cuts = 2
+    every = columns // cuts
+    passed_on = []
+    for cut in range(cuts):
+        if cut == 0:
+            send, keep, rows = project(0, [every], every, 1)
+        else:
+            with jax.named_scope("project_more"):
+                send, keep = pl.pallas_call(
+                    functools.partial(more_kernel, cut * every),
+                    out_shape=[shape(quarter[:-1] + (every,), BF16), shape(quarter[:-1] + (every,), F32)],
+                    in_specs=[VMEM] * 2,
+                    out_specs=[VMEM] * 2,
+                    compiler_params=params(),
+                    cost_estimate=LIGHT,
+                )(rows, output_weight)
+        summed = add(keep, [lax.ppermute(send, along_head, by_core)], BF16)
+        passed_on.append(lax.ppermute(summed, along_head, across))
+    third = columns // 3 // width * width
+    *sends, keep = project(1, [columns - 2 * third, third, third], columns, 0)
+    arrived = [lax.ppermute(send, along_head, by_core) for send in sends]
+    summed = add(keep, arrived + passed_on, BF16 if n_head == 4 else F32)
     bit = 2
     while bit < half:
         mine = (lax.axis_index(along_head) // bit) % 2

time: 55.7 us -> 55.2 us (level)
  waiting for transfers between devices: 30.1 us -> 27.2 us
  starting transfers between devices: 15 us -> 17.2 us
    ppermute x1 -> x4, starting transfers between devices: 0.11 us -> 2.26 us  [the longest x2 1.63 us: per_device(): passed_on.append(lax.ppermute(summed, along_head, across))]
    ppermute x1 -> x4, waiting for transfers between devices: 5.91 us -> 4.43 us  [the longest x2 3.58 us: per_device(): passed_on.append(lax.ppermute(summed, along_head, across))]
    ppermute x3, waiting for transfers between devices: 2.55 us -> 1.2 us  [per_device(): arrived = [lax.ppermute(send, along_head, by_core) for send in sends]]
    pallas_call x6 -> x7, Pallas kernels: 3.48 us -> 3.66 us  [the longest x2 1.3 us: project(): pl.pallas_call(functools.partial(project_kernel, order, [place for unused...]
  transfers between devices with their start and end apart: 11 -> 14, of which waited for: 10 -> 12; matrix products, arithmetic and copies ran while one was open for 0% -> 0% of each run, Pallas kernels for 5% -> 6%
where the time goes in v9:
time: 55.2 us; the launch traced here: 55 us
  waiting for transfers between devices  27.2 us (49%)
  starting transfers between devices  17.2 us (31%)
  Pallas kernels  10.5 us (19%)
    all_to_all x1, waiting for transfers between devices, per_device(): lax.all_to_all(packed, partner_order(sub, n_head), split_axis=0, concat_a...  13.2 us
    all_to_all x1, starting transfers between devices, per_device(): lax.all_to_all(packed, partner_order(sub, n_head), split_axis=0, concat_a...  6.43 us
    ppermute x3, waiting for transfers between devices, per_device(): lax.ppermute(part, along_sub, [(here, here ^ distance) for here in range(...  5.46 us
    ppermute x2, waiting for transfers between devices, per_device(): passed_on.append(lax.ppermute(summed, along_head, across))  3.58 us
    ppermute x3, starting transfers between devices, per_device(): lax.ppermute(part, along_sub, [(here, here ^ distance) for here in range(...  3.55 us
    pallas_call x1, Pallas kernels, per_device(): pl.pallas_call(functools.partial(factor_kernel, tokens, ratio, sub, half...  3.39 us
    ppermute x1, starting transfers between devices, per_device(): incoming = lax.ppermute(state, 'outer', onward)  2.65 us
    pallas_call x1, Pallas kernels, per_device(): pl.pallas_call(functools.partial(pack_kernel, sub), out_shape=shape((sour...  2.29 us
  transfers between devices with their start and end apart: 14, of which 12 were waited for; matrix products, arithmetic and copies ran while one was open for 0% of the time, Pallas kernels for 6%

profile of v9, /device:TPU:0, one launch (start us, length us, event | category | flops | bytes accessed | tf_op | source)
XLA Modules:
  0.0 55.0 jit_solution(2342747746808165726)
XLA Ops:
  0.0 2.3 %pack.1 = bf16[16,272,128]{2,1,0:T(8,128)(2,1)} custom-call(bf16[64,16,128]{2,1,0:T(8,128)(2,1)} %q_hbm.1, bf16[64,16,128]{2,1,0:T(8,128)(2,1)} %k_hbm.1, bf16[64,32,128]{2,1,0:T(8,128)(2,1)} %v_hbm.1, bf16[32,64]{1,0:T(8,128)(2,1)} %bitcast.4), custom_call_target="tpu_custom_call" | custom-call | tf_op jit(solution)/shard_map/pack/pallas_call | solution.py:377
  2.3 6.4 %all-to-all-start = ((bf16[16,272,128]{2,1,0:T(8,128)(2,1)}), bf16[16,272,128]{2,1,0:T(8,128)(2,1)S(1)}, u32[]{:S(2)}, u32[]{:S(2)}) async-start(bf16[16,272,128]{2,1,0:T(8,128)(2,1)} %pack.1), calls=%async_computation | async-start | bytes 2228224 | tf_op jit(solution)/shard_map/all_to_all | solution.py:393
  8.8 0.6 %gates.1 = (bf16[2,8,64,128]{3,2,1,0:T(8,128)(2,1)S(1)}, bf16[2,8,64,128]{3,2,1,0:T(8,128)(2,1)S(1)}) custom-call(bf16[64,32,128]{2,1,0:T(8,128)(2,1)S(1)} %copy-done.1, bf16[1,128]{1,0:T(2,128)(2,1)S(1)} %bitcast.3), custom_call_target="tpu_custom_call" | custom-call | flops 1 | bytes 1 | tf_op jit(solution)/shard_map/gates/pallas_call | solution.py:400
  9.4 0.5 collective-permute-start
  9.9 1.2 %collective-permute-done.swapped_ref.refs_5_.refs_7_ = bf16[2,8,64,128]{3,2,1,0:T(8,128)(2,1)S(1)} collective-permute-done((bf16[2,8,64,128]{3,2,1,0:T(8,128)(2,1)S(1)}, bf16[2,8,64,128]{3,2,1,0:T(8,128)(2,1)S(1)}, u32[]{:S(2)}, u32[]{:S(2)}) %collective-permute-start) | collective-permute-done | bytes 262176 | tf_op jit(solution)/shard_map/ppermute | solution.py:409
  11.0 13.2 %all-to-all-done.got_ref = bf16[16,272,128]{2,1,0:T(8,128)(2,1)S(1)} async-done(((bf16[16,272,128]{2,1,0:T(8,128)(2,1)}), bf16[16,272,128]{2,1,0:T(8,128)(2,1)S(1)}, u32[]{:S(2)}, u32[]{:S(2)}) %all-to-all-start) | async-done | bytes 1114144 | tf_op jit(solution)/shard_map/all_to_all | solution.py:393
  24.2 3.4 %factors.1 = (bf16[2,128,128]{2,1,0:T(8,128)(2,1)S(1)}, bf16[8,2,128,128]{3,2,1,0:T(8,128)(2,1)S(1)}, f32[8,2,128,128]{3,2,1,0:T(8,128)S(1)}, bf16[8,2,128,128]{...) custom-call(bf16[16,272,128]{2,1,0:T(8,128)(2,1)S(1)} %all-to-all-do, ...), custom_call_target="tpu_custom_call" | custom-call | flops 1 | bytes 1 | tf_op jit(solution)/shard_map/factors/pallas_call | solution.py:435
  27.6 2.7 %collective-permute-start.1 = (bf16[2,128,128]{2,1,0:T(8,128)(2,1)S(1)}, bf16[2,128,128]{2,1,0:T(8,128)(2,1)S(1)}, u32[]{:S(2)}, u32[]{:S(2)}) collective-permute-start(bf16[2,128,128]{2,1,0:T(8,128)(2,1)S(1)} %get-tuple-element.34), channel_id=1, source_target_pairs={{0,16},{16,0},{1,17},{17,1},{2,18},{18,2},{3,19},{19,3},{4,20},{20... | collective-permute-start | bytes 196616 | tf_op jit(solution)/shard_map/ppermute | solution.py:445
  30.3 1.1 %spread.1 = (f32[2,8,128,128]{3,2,1,0:T(8,128)S(1)}, bf16[2,8,128,128]{3,2,1,0:T(8,128)(2,1)S(1)}, bf16[2,8,64,128]{3,2,1,0:T(8,128)(2,1)S(1)}) custom-call(bf16[16,272,128]{2,1,0:T(8,128)(2,1)S(1)} %all-to-all-done.got_ref, bf16[8,2,128,128]{3,2,1,0:T(8,128)(2,1)S(1)} %get-tuple-element.35.w_ref, ...), custom_call_target="tpu_custom_call", output_to_operand_aliasing={{2}: (9, {})} | custom-call | flops 1 | bytes 1 | tf_op jit(solution)/shard_map/spread/pallas_call | solution.py:448
  31.4 1.2 %collective-permute-start.5 = (bf16[2,8,64,128]{3,2,1,0:T(8,128)(2,1)S(1)}, bf16[2,8,64,128]{3,2,1,0:T(8,128)(2,1)S(1)}, u32[]{:S(2)}, u32[]{:S(2)}) collective-permute-start(bf16[2,8,64,128]{3,2,1,0:T(8,128)(2,1)S(1)} %get-tuple-element.49), channel_id=1, source_target_pairs={{0,2},{1,3},{2,0},{3,1},{4,6},{5,7},{6,4},{7,5},{8,10},{9,11},{10,... | collective-permute-start | bytes 786440 | tf_op jit(solution)/shard_map/ppermute | solution.py:464
  32.5 1.8 %collective-permute-done.1.state_ref = bf16[2,128,128]{2,1,0:T(8,128)(2,1)S(1)} collective-permute-done((bf16[2,128,128]{2,1,0:T(8,128)(2,1)S(1)}, bf16[2,128,128]{2,1,0:T(8,128)(2,1)S(1)}, u32[]{:S(2)}, u32[]{:S(2)}) %collective-permute-start.1) | collective-permute-done | bytes 65568 | tf_op jit(solution)/shard_map/ppermute | solution.py:445
  34.3 0.5 join.1
  34.8 1.1 %collective-permute-start.2 = (bf16[2,1,2,128,128]{4,3,2,1,0:T(8,128)(2,1)S(1)}, bf16[2,1,2,128,128]{4,3,2,1,0:T(8,128)(2,1)S(1)}, u32[]{:S(2)}, u32[]{:S(2)}) collective-permute-start(bf16[2,1,2,128,128]{4,3,2,1,0:T(8,128)(2,1)S(1)} %get-tuple-element.46), channel_id=1, source_target_pairs={{0,12},{4,8},{8,4},{12,0},{1,13},{5,9},{9,5},{13,1},{2,14},{6,10},... | collective-permute-start | bytes 393224 | tf_op jit(solution)/shard_map/ppermute | solution.py:486
  36.0 1.7 %collective-permute-start.3 = (bf16[2,1,2,128,128]{4,3,2,1,0:T(8,128)(2,1)S(1)}, bf16[2,1,2,128,128]{4,3,2,1,0:T(8,128)(2,1)S(1)}, u32[]{:S(2)}, u32[]{:S(2)}) collective-permute-start(bf16[2,1,2,128,128]{4,3,2,1,0:T(8,128)(2,1)S(1)} %get-tuple-element.47), channel_id=1, source_target_pairs={{0,8},{4,12},{8,0},{12,4},{1,9},{5,13},{9,1},{13,5},{2,10},{6,14},... | collective-permute-start | bytes 393224 | tf_op jit(solution)/shard_map/ppermute | solution.py:486
  37.6 0.7 %collective-permute-start.4 = (bf16[2,1,2,128,128]{4,3,2,1,0:T(8,128)(2,1)S(1)}, bf16[2,1,2,128,128]{4,3,2,1,0:T(8,128)(2,1)S(1)}, u32[]{:S(2)}, u32[]{:S(2)}) collective-permute-start(bf16[2,1,2,128,128]{4,3,2,1,0:T(8,128)(2,1)S(1)} %get-tuple-element.48), channel_id=1, source_target_pairs={{0,4},{4,0},{8,12},{12,8},{1,5},{5,1},{9,13},{13,9},{2,6},{6,2},{1... | collective-permute-start | bytes 393224 | tf_op jit(solution)/shard_map/ppermute | solution.py:486
  38.4 3.8 %collective-permute-done.2.refs_1_ = bf16[2,1,2,128,128]{4,3,2,1,0:T(8,128)(2,1)S(1)} collective-permute-done((bf16[2,1,2,128,128]{4,3,2,1,0:T(8,128)(2,1)S(1)}, bf16[2,1,2,128,128]{4,3,2,1,0:T(8,128)(2,1)S(1)}, u32[]{:S(2)}, u32[]{:S(2)}) %collective-permute-start.2) | collective-permute-done | bytes 131104 | tf_op jit(solution)/shard_map/ppermute | solution.py:486
  42.2 1.4 %collective-permute-done.3.refs_2_ = bf16[2,1,2,128,128]{4,3,2,1,0:T(8,128)(2,1)S(1)} collective-permute-done((bf16[2,1,2,128,128]{4,3,2,1,0:T(8,128)(2,1)S(1)}, bf16[2,1,2,128,128]{4,3,2,1,0:T(8,128)(2,1)S(1)}, u32[]{:S(2)}, u32[]{:S(2)}) %collective-permute-start.3) | collective-permute-done | bytes 131104 | tf_op jit(solution)/shard_map/ppermute | solution.py:486
  43.6 0.2 collective-permute-done.4.refs_3_
  43.8 0.5 project.3
  44.4 0.4 project_more.1
  44.9 0.6 %collective-permute-start.11 = (bf16[1,64,1024]{2,1,0:T(8,128)(2,1)S(1)}, bf16[1,64,1024]{2,1,0:T(8,128)(2,1)S(1)}, u32[]{:S(2)}, u32[]{:S(2)}) collective-permute-start(bf16[1,64,1024]{2,1,0:T(8,128)(2,1)S(1)} %get-tuple-element.58), channel_id=1, source_target_pairs={{0,1},{1,0},{2,3},{3,2},{4,5},{5,4},{6,7},{7,6},{8,9},{9,8},{10,11... | collective-permute-start | bytes 393224 | tf_op jit(solution)/shard_map/ppermute | solution.py:534
  45.5 0.3 collective-permute-done.9.refs_0_
  45.8 0.1 collective-permute-start.10
  45.9 0.5 collective-permute-done.11.refs_0_
  46.5 1.5 %collective-permute-start.12 = (bf16[1,64,1024]{2,1,0:T(8,128)(2,1)S(1)}, bf16[1,64,1024]{2,1,0:T(8,128)(2,1)S(1)}, u32[]{:S(2)}, u32[]{:S(2)}) collective-permute-start(bf16[1,64,1024]{2,1,0:T(8,128)(2,1)S(1)} %sum.4), channel_id=1, source_target_pairs={{0,2},{1,3},{2,0},{3,1},{4,6},{5,7},{6,4},{7,5},{8,10},{9,11},{10,... | collective-permute-start | bytes 393224 | tf_op jit(solution)/shard_map/ppermute | solution.py:535
  48.0 0.8 %project.2 = (bf16[1,64,768]{2,1,0:T(8,128)(2,1)S(1)}, bf16[1,64,640]{2,1,0:T(8,128)(2,1)S(1)}, bf16[1,64,640]{2,1,0:T(8,128)(2,1)S(1)}, f32[1,64,2048]{2,1,0:T(8,128)S(1)}) custom-call(bf16[2,1,2,128,128]{4,3,2,1,0:T(8,128)(2,1)S(1)} %get-tuple-element.45.refs_0_, bf16[2,1,2,128,128]{4,3,2,1,0:T(8,128)(2,1)S(1)} %collective-permute-done.2.refs_1_, ...), custom_call_target="tpu_custom_call" | custom-call | flops 1 | bytes 1 | tf_op jit(solution)/shard_map/project/pallas_call | solution.py:495
  48.9 0.5 collective-permute-start.7
  49.5 0.8 %collective-permute-done.7.refs_1_ = bf16[1,64,640]{2,1,0:T(8,128)(2,1)S(1)} collective-permute-done((bf16[1,64,640]{2,1,0:T(8,128)(2,1)S(1)}, bf16[1,64,640]{2,1,0:T(8,128)(2,1)S(1)}, u32[]{:S(2)}, u32[]{:S(2)}) %collective-permute-start.7) | collective-permute-done | bytes 81952 | tf_op jit(solution)/shard_map/ppermute | solution.py:538
  50.3 0.4 collective-permute-done.8.refs_2_
  50.7 1.6 %collective-permute-done.10.refs_3_ = bf16[1,64,1024]{2,1,0:T(8,128)(2,1)S(1)} collective-permute-done((bf16[1,64,1024]{2,1,0:T(8,128)(2,1)S(1)}, bf16[1,64,1024]{2,1,0:T(8,128)(2,1)S(1)}, u32[]{:S(2)}, u32[]{:S(2)}) %collective-permute-start.10) | collective-permute-done | bytes 131104 | tf_op jit(solution)/shard_map/ppermute | solution.py:535
  52.2 2.0 %collective-permute-done.12.refs_4_ = bf16[1,64,1024]{2,1,0:T(8,128)(2,1)S(1)} collective-permute-done((bf16[1,64,1024]{2,1,0:T(8,128)(2,1)S(1)}, bf16[1,64,1024]{2,1,0:T(8,128)(2,1)S(1)}, u32[]{:S(2)}, u32[]{:S(2)}) %collective-permute-start.12) | collective-permute-done | bytes 131104 | tf_op jit(solution)/shard_map/ppermute | solution.py:535
  54.2 0.8 %sum.5 = bf16[1,64,2048]{2,1,0:T(8,128)(2,1)} custom-call(f32[1,64,2048]{2,1,0:T(8,128)S(1)} %get-tuple-element.50.keep_ref, bf16[1,64,768]{2,1,0:T(8,128)(2,1)S(1)} %collective-permute-done.6.refs_0_, bf16[1,64,640]{2,1,0:T(8,128)(2,1)S(1)} %collective-permute-done.7.refs_1_, bf16[1,64,640]{2,1,0:T(8,128)(2,1)S(1)} %collective-permute-done.8.refs_2_, ...), custom_call_target="tpu_custom_call" | custom-call | flops 1 | bytes 1 | tf_op jit(solution)/shard_map/sum/pallas_call | solution.py:509
  (14 shorter events, 0.3 us)
Async XLA Ops:
  2.3 6.5 %copy-start.1 = (bf16[64,32,128]{2,1,0:T(8,128)(2,1)S(1)}, bf16[64,32,128]{2,1,0:T(8,128)(2,1)}, u32[]{:S(2)}) copy-start(bf16[64,32,128]{2,1,0:T(8,128)(2,1)} %gate_ref.1) | copy-start | bytes 1572868
  2.3 6.5 %copy-start.2 = (bf16[128]{0:T(256)(128)(2,1)S(1)}, bf16[128]{0:T(256)(128)(2,1)}, u32[]{:S(2)}) copy-start(bf16[128]{0:T(256)(128)(2,1)} %param.12) | copy-start | bytes 772
  2.3 21.9 %all-to-all-start = ((bf16[16,272,128]{2,1,0:T(8,128)(2,1)}), bf16[16,272,128]{2,1,0:T(8,128)(2,1)S(1)}, u32[]{:S(2)}, u32[]{:S(2)}) async-start(bf16[16,272,128]{2,1,0:T(8,128)(2,1)} %pack.1), calls=%async_computation | async-start | bytes 2228224 | tf_op jit(solution)/shard_map/all_to_all | solution.py:393
  9.4 1.6 %collective-permute-start = (bf16[2,8,64,128]{3,2,1,0:T(8,128)(2,1)S(1)}, bf16[2,8,64,128]{3,2,1,0:T(8,128)(2,1)S(1)}, u32[]{:S(2)}, u32[]{:S(2)}) collective-permute-start(bf16[2,8,64,128]{3,2,1,0:T(8,128)(2,1)S(1)} %get-tuple-element.33), channel_id=1, source_target_pairs={{0,1},{1,0},{2,3},{3,2},{4,5},{5,4},{6,7},{7,6},{8,9},{9,8},{10,11... | collective-permute-start | bytes 786440 | tf_op jit(solution)/shard_map/ppermute | solution.py:409
  27.6 6.7 %collective-permute-start.1 = (bf16[2,128,128]{2,1,0:T(8,128)(2,1)S(1)}, bf16[2,128,128]{2,1,0:T(8,128)(2,1)S(1)}, u32[]{:S(2)}, u32[]{:S(2)}) collective-permute-start(bf16[2,128,128]{2,1,0:T(8,128)(2,1)S(1)} %get-tuple-element.34), channel_id=1, source_target_pairs={{0,16},{16,0},{1,17},{17,1},{2,18},{18,2},{3,19},{19,3},{4,20},{20... | collective-permute-start | bytes 196616 | tf_op jit(solution)/shard_map/ppermute | solution.py:445
  31.4 12.5 %collective-permute-start.5 = (bf16[2,8,64,128]{3,2,1,0:T(8,128)(2,1)S(1)}, bf16[2,8,64,128]{3,2,1,0:T(8,128)(2,1)S(1)}, u32[]{:S(2)}, u32[]{:S(2)}) collective-permute-start(bf16[2,8,64,128]{3,2,1,0:T(8,128)(2,1)S(1)} %get-tuple-element.49), channel_id=1, source_target_pairs={{0,2},{1,3},{2,0},{3,1},{4,6},{5,7},{6,4},{7,5},{8,10},{9,11},{10,... | collective-permute-start | bytes 786440 | tf_op jit(solution)/shard_map/ppermute | solution.py:464
  34.3 9.5 %copy-start = (bf16[1024,2048]{1,0:T(8,128)(2,1)S(1)}, bf16[1024,2048]{1,0:T(8,128)(2,1)}, u32[]{:S(2)}) copy-start(bf16[1024,2048]{1,0:T(8,128)(2,1)} %weight_ref.1) | copy-start | bytes 12582916
  34.8 7.3 %collective-permute-start.2 = (bf16[2,1,2,128,128]{4,3,2,1,0:T(8,128)(2,1)S(1)}, bf16[2,1,2,128,128]{4,3,2,1,0:T(8,128)(2,1)S(1)}, u32[]{:S(2)}, u32[]{:S(2)}) collective-permute-start(bf16[2,1,2,128,128]{4,3,2,1,0:T(8,128)(2,1)S(1)} %get-tuple-element.46), channel_id=1, source_target_pairs={{0,12},{4,8},{8,4},{12,0},{1,13},{5,9},{9,5},{13,1},{2,14},{6,10},... | collective-permute-start | bytes 393224 | tf_op jit(solution)/shard_map/ppermute | solution.py:486
  36.0 7.7 %collective-permute-start.3 = (bf16[2,1,2,128,128]{4,3,2,1,0:T(8,128)(2,1)S(1)}, bf16[2,1,2,128,128]{4,3,2,1,0:T(8,128)(2,1)S(1)}, u32[]{:S(2)}, u32[]{:S(2)}) collective-permute-start(bf16[2,1,2,128,128]{4,3,2,1,0:T(8,128)(2,1)S(1)} %get-tuple-element.47), channel_id=1, source_target_pairs={{0,8},{4,12},{8,0},{12,4},{1,9},{5,13},{9,1},{13,5},{2,10},{6,14},... | collective-permute-start | bytes 393224 | tf_op jit(solution)/shard_map/ppermute | solution.py:486
  37.6 6.2 %collective-permute-start.4 = (bf16[2,1,2,128,128]{4,3,2,1,0:T(8,128)(2,1)S(1)}, bf16[2,1,2,128,128]{4,3,2,1,0:T(8,128)(2,1)S(1)}, u32[]{:S(2)}, u32[]{:S(2)}) collective-permute-start(bf16[2,1,2,128,128]{4,3,2,1,0:T(8,128)(2,1)S(1)} %get-tuple-element.48), channel_id=1, source_target_pairs={{0,4},{4,0},{8,12},{12,8},{1,5},{5,1},{9,13},{13,9},{2,6},{6,2},{1... | collective-permute-start | bytes 393224 | tf_op jit(solution)/shard_map/ppermute | solution.py:486
  44.4 1.4 %collective-permute-start.9 = (bf16[1,64,1024]{2,1,0:T(8,128)(2,1)S(1)}, bf16[1,64,1024]{2,1,0:T(8,128)(2,1)S(1)}, u32[]{:S(2)}, u32[]{:S(2)}) collective-permute-start(bf16[1,64,1024]{2,1,0:T(8,128)(2,1)S(1)} %get-tuple-element.55), channel_id=1, source_target_pairs={{0,1},{1,0},{2,3},{3,2},{4,5},{5,4},{6,7},{7,6},{8,9},{9,8},{10,11... | collective-permute-start | bytes 393224 | tf_op jit(solution)/shard_map/ppermute | solution.py:534
  44.9 1.6 %collective-permute-start.11 = (bf16[1,64,1024]{2,1,0:T(8,128)(2,1)S(1)}, bf16[1,64,1024]{2,1,0:T(8,128)(2,1)S(1)}, u32[]{:S(2)}, u32[]{:S(2)}) collective-permute-start(bf16[1,64,1024]{2,1,0:T(8,128)(2,1)S(1)} %get-tuple-element.58), channel_id=1, source_target_pairs={{0,1},{1,0},{2,3},{3,2},{4,5},{5,4},{6,7},{7,6},{8,9},{9,8},{10,11... | collective-permute-start | bytes 393224 | tf_op jit(solution)/shard_map/ppermute | solution.py:534
  45.8 6.4 %collective-permute-start.10 = (bf16[1,64,1024]{2,1,0:T(8,128)(2,1)S(1)}, bf16[1,64,1024]{2,1,0:T(8,128)(2,1)S(1)}, u32[]{:S(2)}, u32[]{:S(2)}) collective-permute-start(bf16[1,64,1024]{2,1,0:T(8,128)(2,1)S(1)} %sum.3), channel_id=1, source_target_pairs={{0,2},{1,3},{2,0},{3,1},{4,6},{5,7},{6,4},{7,5},{8,10},{9,11},{10,... | collective-permute-start | bytes 393224 | tf_op jit(solution)/shard_map/ppermute | solution.py:535
  46.5 7.8 %collective-permute-start.12 = (bf16[1,64,1024]{2,1,0:T(8,128)(2,1)S(1)}, bf16[1,64,1024]{2,1,0:T(8,128)(2,1)S(1)}, u32[]{:S(2)}, u32[]{:S(2)}) collective-permute-start(bf16[1,64,1024]{2,1,0:T(8,128)(2,1)S(1)} %sum.4), channel_id=1, source_target_pairs={{0,2},{1,3},{2,0},{3,1},{4,6},{5,7},{6,4},{7,5},{8,10},{9,11},{10,... | collective-permute-start | bytes 393224 | tf_op jit(solution)/shard_map/ppermute | solution.py:535
  48.8 1.9 %collective-permute-start.6 = (bf16[1,64,768]{2,1,0:T(8,128)(2,1)S(1)}, bf16[1,64,768]{2,1,0:T(8,128)(2,1)S(1)}, u32[]{:S(2)}, u32[]{:S(2)}) collective-permute-start(bf16[1,64,768]{2,1,0:T(8,128)(2,1)S(1)} %get-tuple-element.51), channel_id=1, source_target_pairs={{0,1},{1,0},{2,3},{3,2},{4,5},{5,4},{6,7},{7,6},{8,9},{9,8},{10,11... | collective-permute-start | bytes 294920 | tf_op jit(solution)/shard_map/ppermute | solution.py:538
  48.9 1.4 %collective-permute-start.7 = (bf16[1,64,640]{2,1,0:T(8,128)(2,1)S(1)}, bf16[1,64,640]{2,1,0:T(8,128)(2,1)S(1)}, u32[]{:S(2)}, u32[]{:S(2)}) collective-permute-start(bf16[1,64,640]{2,1,0:T(8,128)(2,1)S(1)} %get-tuple-element.52), channel_id=1, source_target_pairs={{0,1},{1,0},{2,3},{3,2},{4,5},{5,4},{6,7},{7,6},{8,9},{9,8},{10,11... | collective-permute-start | bytes 245768 | tf_op jit(solution)/shard_map/ppermute | solution.py:538
  49.4 1.3 %collective-permute-start.8 = (bf16[1,64,640]{2,1,0:T(8,128)(2,1)S(1)}, bf16[1,64,640]{2,1,0:T(8,128)(2,1)S(1)}, u32[]{:S(2)}, u32[]{:S(2)}) collective-permute-start(bf16[1,64,640]{2,1,0:T(8,128)(2,1)S(1)} %get-tuple-element.53), channel_id=1, source_target_pairs={{0,1},{1,0},{2,3},{3,2},{4,5},{5,4},{6,7},{7,6},{8,9},{9,8},{10,11... | collective-permute-start | bytes 245768 | tf_op jit(solution)/shard_map/ppermute | solution.py:538

commit v10 on v9

--- a/solution.py
+++ b/solution.py
@@ -137,23 +137,41 @@
     return [wide[:, part * width : (part + 1) * width] for part in range(count)]
 
 
+def odd_rows(matrix, step):
+    return jnp.concatenate([matrix[first : first + step] for first in range(step, matrix.shape[0], 2 * step)], axis=0)
+
+
+def between_zeros(rows, step):
+    zero = jnp.zeros((step, rows.shape[1]), rows.dtype)
+    groups = []
+    for first in range(0, rows.shape[0], step):
+        groups += [zero, rows[first : first + step]]
+    return jnp.concatenate(groups, axis=0)
+
+
 def block_inverse(below):
     size = below[0].shape[0]
     rows = lax.broadcasted_iota(jnp.int32, (size, size), 0)
     cols = lax.broadcasted_iota(jnp.int32, (size, size), 1)
-    zero = jnp.zeros((size, size), F32)
     step = 1
     solved = None
     while step < size:
         joins = (rows // (2 * step) == cols // (2 * step)) & (rows // step > cols // step)
-        parts = [jnp.where(joins, matrix, zero) for matrix in below]
         if step == 1:
             solved = [
-                jnp.where(rows == cols, jnp.ones_like(zero), -part).astype(BF16) for part in parts
+                jnp.where(rows == cols, 1.0, -jnp.where(joins, matrix, 0.0)).astype(BF16) for matrix in below
             ]
+        elif step < ROW_TILE:
+            parts = [jnp.where(joins, matrix, 0.0).astype(BF16) for matrix in below]
+            inner = [dot(part, now).astype(BF16) for part, now in zip(parts, solved)]
+            solved = [now - dot(now, mid).astype(BF16) for now, mid in zip(solved, inner)]
         else:
-            inner = [dot(part.astype(BF16), now).astype(BF16) for part, now in zip(parts, solved)]
-            solved = [now - dot(now, mid).astype(BF16) for now, mid in zip(solved, inner)]
+            joins = odd_rows(jnp.where(joins, 1, 0), step) > 0
+            parts = [jnp.where(joins, odd_rows(matrix, step), 0.0).astype(BF16) for matrix in below]
+            inner = [dot(part, now).astype(BF16) for part, now in zip(parts, solved)]
+            inner = [between_zeros(mid, step) for mid in inner]
+            outer = [dot(odd_rows(now, step), mid).astype(BF16) for now, mid in zip(solved, inner)]
+            solved = [now - between_zeros(part, step) for now, part in zip(solved, outer)]
         step *= 2
     return solved
 

time: 55.2 us -> 55.2 us (level)
  no operation moved by 1% of the time
where the time goes in v10:
time: 55.2 us; the launch traced here: 55 us
  waiting for transfers between devices  27.2 us (49%)
  starting transfers between devices  17.2 us (31%)
  Pallas kernels  10.4 us (19%)
    all_to_all x1, waiting for transfers between devices, per_device(): lax.all_to_all(packed, partner_order(sub, n_head), split_axis=0, concat_a...  13.2 us
    all_to_all x1, starting transfers between devices, per_device(): lax.all_to_all(packed, partner_order(sub, n_head), split_axis=0, concat_a...  6.43 us
    ppermute x3, waiting for transfers between devices, per_device(): lax.ppermute(part, along_sub, [(here, here ^ distance) for here in range(...  5.45 us
    ppermute x2, waiting for transfers between devices, per_device(): passed_on.append(lax.ppermute(summed, along_head, across))  3.58 us
    ppermute x3, starting transfers between devices, per_device(): lax.ppermute(part, along_sub, [(here, here ^ distance) for here in range(...  3.55 us
    pallas_call x1, Pallas kernels, per_device(): pl.pallas_call(functools.partial(factor_kernel, tokens, ratio, sub, half...  3.33 us
    ppermute x1, starting transfers between devices, per_device(): incoming = lax.ppermute(state, 'outer', onward)  2.65 us
    pallas_call x1, Pallas kernels, per_device(): pl.pallas_call(functools.partial(pack_kernel, sub), out_shape=shape((sour...  2.29 us
  transfers between devices with their start and end apart: 14, of which 12 were waited for; matrix products, arithmetic and copies ran while one was open for 0% of the time, Pallas kernels for 6%

profile of v10, /device:TPU:0, one launch (start us, length us, event | category | flops | bytes accessed | tf_op | source)
XLA Modules:
  0.0 55.0 jit_solution(8218988382027736662)
XLA Ops:
  0.0 2.3 %pack.1 = bf16[16,272,128]{2,1,0:T(8,128)(2,1)} custom-call(bf16[64,16,128]{2,1,0:T(8,128)(2,1)} %q_hbm.1, bf16[64,16,128]{2,1,0:T(8,128)(2,1)} %k_hbm.1, bf16[64,32,128]{2,1,0:T(8,128)(2,1)} %v_hbm.1, bf16[32,64]{1,0:T(8,128)(2,1)} %bitcast.4), custom_call_target="tpu_custom_call" | custom-call | tf_op jit(solution)/shard_map/pack/pallas_call | solution.py:395
  2.3 6.4 %all-to-all-start = ((bf16[16,272,128]{2,1,0:T(8,128)(2,1)}), bf16[16,272,128]{2,1,0:T(8,128)(2,1)S(1)}, u32[]{:S(2)}, u32[]{:S(2)}) async-start(bf16[16,272,128]{2,1,0:T(8,128)(2,1)} %pack.1), calls=%async_computation | async-start | bytes 2228224 | tf_op jit(solution)/shard_map/all_to_all | solution.py:411
  8.8 0.6 %gates.1 = (bf16[2,8,64,128]{3,2,1,0:T(8,128)(2,1)S(1)}, bf16[2,8,64,128]{3,2,1,0:T(8,128)(2,1)S(1)}) custom-call(bf16[64,32,128]{2,1,0:T(8,128)(2,1)S(1)} %copy-done.1, bf16[1,128]{1,0:T(2,128)(2,1)S(1)} %bitcast.3), custom_call_target="tpu_custom_call" | custom-call | flops 1 | bytes 1 | tf_op jit(solution)/shard_map/gates/pallas_call | solution.py:418
  9.4 0.5 collective-permute-start
  9.9 1.2 %collective-permute-done.swapped_ref.refs_5_.refs_7_ = bf16[2,8,64,128]{3,2,1,0:T(8,128)(2,1)S(1)} collective-permute-done((bf16[2,8,64,128]{3,2,1,0:T(8,128)(2,1)S(1)}, bf16[2,8,64,128]{3,2,1,0:T(8,128)(2,1)S(1)}, u32[]{:S(2)}, u32[]{:S(2)}) %collective-permute-start) | collective-permute-done | bytes 262176 | tf_op jit(solution)/shard_map/ppermute | solution.py:427
  11.0 13.2 %all-to-all-done.got_ref = bf16[16,272,128]{2,1,0:T(8,128)(2,1)S(1)} async-done(((bf16[16,272,128]{2,1,0:T(8,128)(2,1)}), bf16[16,272,128]{2,1,0:T(8,128)(2,1)S(1)}, u32[]{:S(2)}, u32[]{:S(2)}) %all-to-all-start) | async-done | bytes 1114144 | tf_op jit(solution)/shard_map/all_to_all | solution.py:411
  24.2 3.3 %factors.1 = (bf16[2,128,128]{2,1,0:T(8,128)(2,1)S(1)}, bf16[8,2,128,128]{3,2,1,0:T(8,128)(2,1)S(1)}, f32[8,2,128,128]{3,2,1,0:T(8,128)S(1)}, bf16[8,2,128,128]{...) custom-call(bf16[16,272,128]{2,1,0:T(8,128)(2,1)S(1)} %all-to-all-do, ...), custom_call_target="tpu_custom_call" | custom-call | flops 1 | bytes 1 | tf_op jit(solution)/shard_map/factors/pallas_call | solution.py:453
  27.6 2.6 %collective-permute-start.1 = (bf16[2,128,128]{2,1,0:T(8,128)(2,1)S(1)}, bf16[2,128,128]{2,1,0:T(8,128)(2,1)S(1)}, u32[]{:S(2)}, u32[]{:S(2)}) collective-permute-start(bf16[2,128,128]{2,1,0:T(8,128)(2,1)S(1)} %get-tuple-element.34), channel_id=1, source_target_pairs={{0,16},{16,0},{1,17},{17,1},{2,18},{18,2},{3,19},{19,3},{4,20},{20... | collective-permute-start | bytes 196616 | tf_op jit(solution)/shard_map/ppermute | solution.py:463
  30.2 1.1 %spread.1 = (f32[2,8,128,128]{3,2,1,0:T(8,128)S(1)}, bf16[2,8,128,128]{3,2,1,0:T(8,128)(2,1)S(1)}, bf16[2,8,64,128]{3,2,1,0:T(8,128)(2,1)S(1)}) custom-call(bf16[16,272,128]{2,1,0:T(8,128)(2,1)S(1)} %all-to-all-done.got_ref, bf16[8,2,128,128]{3,2,1,0:T(8,128)(2,1)S(1)} %get-tuple-element.35.w_ref, ...), custom_call_target="tpu_custom_call", output_to_operand_aliasing={{2}: (9, {})} | custom-call | flops 1 | bytes 1 | tf_op jit(solution)/shard_map/spread/pallas_call | solution.py:466
  31.3 1.2 %collective-permute-start.5 = (bf16[2,8,64,128]{3,2,1,0:T(8,128)(2,1)S(1)}, bf16[2,8,64,128]{3,2,1,0:T(8,128)(2,1)S(1)}, u32[]{:S(2)}, u32[]{:S(2)}) collective-permute-start(bf16[2,8,64,128]{3,2,1,0:T(8,128)(2,1)S(1)} %get-tuple-element.49), channel_id=1, source_target_pairs={{0,2},{1,3},{2,0},{3,1},{4,6},{5,7},{6,4},{7,5},{8,10},{9,11},{10,... | collective-permute-start | bytes 786440 | tf_op jit(solution)/shard_map/ppermute | solution.py:482
  32.5 1.8 %collective-permute-done.1.state_ref = bf16[2,128,128]{2,1,0:T(8,128)(2,1)S(1)} collective-permute-done((bf16[2,128,128]{2,1,0:T(8,128)(2,1)S(1)}, bf16[2,128,128]{2,1,0:T(8,128)(2,1)S(1)}, u32[]{:S(2)}, u32[]{:S(2)}) %collective-permute-start.1) | collective-permute-done | bytes 65568 | tf_op jit(solution)/shard_map/ppermute | solution.py:463
  34.2 0.5 join.1
  34.8 1.1 %collective-permute-start.2 = (bf16[2,1,2,128,128]{4,3,2,1,0:T(8,128)(2,1)S(1)}, bf16[2,1,2,128,128]{4,3,2,1,0:T(8,128)(2,1)S(1)}, u32[]{:S(2)}, u32[]{:S(2)}) collective-permute-start(bf16[2,1,2,128,128]{4,3,2,1,0:T(8,128)(2,1)S(1)} %get-tuple-element.46), channel_id=1, source_target_pairs={{0,12},{4,8},{8,4},{12,0},{1,13},{5,9},{9,5},{13,1},{2,14},{6,10},... | collective-permute-start | bytes 393224 | tf_op jit(solution)/shard_map/ppermute | solution.py:504
  35.9 1.7 %collective-permute-start.3 = (bf16[2,1,2,128,128]{4,3,2,1,0:T(8,128)(2,1)S(1)}, bf16[2,1,2,128,128]{4,3,2,1,0:T(8,128)(2,1)S(1)}, u32[]{:S(2)}, u32[]{:S(2)}) collective-permute-start(bf16[2,1,2,128,128]{4,3,2,1,0:T(8,128)(2,1)S(1)} %get-tuple-element.47), channel_id=1, source_target_pairs={{0,8},{4,12},{8,0},{12,4},{1,9},{5,13},{9,1},{13,5},{2,10},{6,14},... | collective-permute-start | bytes 393224 | tf_op jit(solution)/shard_map/ppermute | solution.py:504
  37.6 0.7 %collective-permute-start.4 = (bf16[2,1,2,128,128]{4,3,2,1,0:T(8,128)(2,1)S(1)}, bf16[2,1,2,128,128]{4,3,2,1,0:T(8,128)(2,1)S(1)}, u32[]{:S(2)}, u32[]{:S(2)}) collective-permute-start(bf16[2,1,2,128,128]{4,3,2,1,0:T(8,128)(2,1)S(1)} %get-tuple-element.48), channel_id=1, source_target_pairs={{0,4},{4,0},{8,12},{12,8},{1,5},{5,1},{9,13},{13,9},{2,6},{6,2},{1... | collective-permute-start | bytes 393224 | tf_op jit(solution)/shard_map/ppermute | solution.py:504
  38.3 3.8 %collective-permute-done.2.refs_1_ = bf16[2,1,2,128,128]{4,3,2,1,0:T(8,128)(2,1)S(1)} collective-permute-done((bf16[2,1,2,128,128]{4,3,2,1,0:T(8,128)(2,1)S(1)}, bf16[2,1,2,128,128]{4,3,2,1,0:T(8,128)(2,1)S(1)}, u32[]{:S(2)}, u32[]{:S(2)}) %collective-permute-start.2) | collective-permute-done | bytes 131104 | tf_op jit(solution)/shard_map/ppermute | solution.py:504
  42.1 1.4 %collective-permute-done.3.refs_2_ = bf16[2,1,2,128,128]{4,3,2,1,0:T(8,128)(2,1)S(1)} collective-permute-done((bf16[2,1,2,128,128]{4,3,2,1,0:T(8,128)(2,1)S(1)}, bf16[2,1,2,128,128]{4,3,2,1,0:T(8,128)(2,1)S(1)}, u32[]{:S(2)}, u32[]{:S(2)}) %collective-permute-start.3) | collective-permute-done | bytes 131104 | tf_op jit(solution)/shard_map/ppermute | solution.py:504
  43.6 0.2 collective-permute-done.4.refs_3_
  43.8 0.5 project.3
  44.4 0.4 project_more.1
  44.8 0.6 %collective-permute-start.11 = (bf16[1,64,1024]{2,1,0:T(8,128)(2,1)S(1)}, bf16[1,64,1024]{2,1,0:T(8,128)(2,1)S(1)}, u32[]{:S(2)}, u32[]{:S(2)}) collective-permute-start(bf16[1,64,1024]{2,1,0:T(8,128)(2,1)S(1)} %get-tuple-element.58), channel_id=1, source_target_pairs={{0,1},{1,0},{2,3},{3,2},{4,5},{5,4},{6,7},{7,6},{8,9},{9,8},{10,11... | collective-permute-start | bytes 393224 | tf_op jit(solution)/shard_map/ppermute | solution.py:552
  45.4 0.3 collective-permute-done.9.refs_0_
  45.8 0.1 collective-permute-start.10
  45.9 0.5 collective-permute-done.11.refs_0_
  46.4 1.5 %collective-permute-start.12 = (bf16[1,64,1024]{2,1,0:T(8,128)(2,1)S(1)}, bf16[1,64,1024]{2,1,0:T(8,128)(2,1)S(1)}, u32[]{:S(2)}, u32[]{:S(2)}) collective-permute-start(bf16[1,64,1024]{2,1,0:T(8,128)(2,1)S(1)} %sum.4), channel_id=1, source_target_pairs={{0,2},{1,3},{2,0},{3,1},{4,6},{5,7},{6,4},{7,5},{8,10},{9,11},{10,... | collective-permute-start | bytes 393224 | tf_op jit(solution)/shard_map/ppermute | solution.py:553
  47.9 0.8 %project.2 = (bf16[1,64,768]{2,1,0:T(8,128)(2,1)S(1)}, bf16[1,64,640]{2,1,0:T(8,128)(2,1)S(1)}, bf16[1,64,640]{2,1,0:T(8,128)(2,1)S(1)}, f32[1,64,2048]{2,1,0:T(8,128)S(1)}) custom-call(bf16[2,1,2,128,128]{4,3,2,1,0:T(8,128)(2,1)S(1)} %get-tuple-element.45.refs_0_, bf16[2,1,2,128,128]{4,3,2,1,0:T(8,128)(2,1)S(1)} %collective-permute-done.2.refs_1_, ...), custom_call_target="tpu_custom_call" | custom-call | flops 1 | bytes 1 | tf_op jit(solution)/shard_map/project/pallas_call | solution.py:513
  48.8 0.5 collective-permute-start.7
  49.4 0.8 %collective-permute-done.7.refs_1_ = bf16[1,64,640]{2,1,0:T(8,128)(2,1)S(1)} collective-permute-done((bf16[1,64,640]{2,1,0:T(8,128)(2,1)S(1)}, bf16[1,64,640]{2,1,0:T(8,128)(2,1)S(1)}, u32[]{:S(2)}, u32[]{:S(2)}) %collective-permute-start.7) | collective-permute-done | bytes 81952 | tf_op jit(solution)/shard_map/ppermute | solution.py:556
  50.2 0.4 collective-permute-done.8.refs_2_
  50.6 1.6 %collective-permute-done.10.refs_3_ = bf16[1,64,1024]{2,1,0:T(8,128)(2,1)S(1)} collective-permute-done((bf16[1,64,1024]{2,1,0:T(8,128)(2,1)S(1)}, bf16[1,64,1024]{2,1,0:T(8,128)(2,1)S(1)}, u32[]{:S(2)}, u32[]{:S(2)}) %collective-permute-start.10) | collective-permute-done | bytes 131104 | tf_op jit(solution)/shard_map/ppermute | solution.py:553
  52.2 2.0 %collective-permute-done.12.refs_4_ = bf16[1,64,1024]{2,1,0:T(8,128)(2,1)S(1)} collective-permute-done((bf16[1,64,1024]{2,1,0:T(8,128)(2,1)S(1)}, bf16[1,64,1024]{2,1,0:T(8,128)(2,1)S(1)}, u32[]{:S(2)}, u32[]{:S(2)}) %collective-permute-start.12) | collective-permute-done | bytes 131104 | tf_op jit(solution)/shard_map/ppermute | solution.py:553
  54.2 0.8 %sum.5 = bf16[1,64,2048]{2,1,0:T(8,128)(2,1)} custom-call(f32[1,64,2048]{2,1,0:T(8,128)S(1)} %get-tuple-element.50.keep_ref, bf16[1,64,768]{2,1,0:T(8,128)(2,1)S(1)} %collective-permute-done.6.refs_0_, bf16[1,64,640]{2,1,0:T(8,128)(2,1)S(1)} %collective-permute-done.7.refs_1_, bf16[1,64,640]{2,1,0:T(8,128)(2,1)S(1)} %collective-permute-done.8.refs_2_, ...), custom_call_target="tpu_custom_call" | custom-call | flops 1 | bytes 1 | tf_op jit(solution)/shard_map/sum/pallas_call | solution.py:527
  (14 shorter events, 0.3 us)
Async XLA Ops:
  2.3 6.5 %copy-start.1 = (bf16[64,32,128]{2,1,0:T(8,128)(2,1)S(1)}, bf16[64,32,128]{2,1,0:T(8,128)(2,1)}, u32[]{:S(2)}) copy-start(bf16[64,32,128]{2,1,0:T(8,128)(2,1)} %gate_ref.1) | copy-start | bytes 1572868
  2.3 6.5 %copy-start.2 = (bf16[128]{0:T(256)(128)(2,1)S(1)}, bf16[128]{0:T(256)(128)(2,1)}, u32[]{:S(2)}) copy-start(bf16[128]{0:T(256)(128)(2,1)} %param.12) | copy-start | bytes 772
  2.3 21.9 %all-to-all-start = ((bf16[16,272,128]{2,1,0:T(8,128)(2,1)}), bf16[16,272,128]{2,1,0:T(8,128)(2,1)S(1)}, u32[]{:S(2)}, u32[]{:S(2)}) async-start(bf16[16,272,128]{2,1,0:T(8,128)(2,1)} %pack.1), calls=%async_computation | async-start | bytes 2228224 | tf_op jit(solution)/shard_map/all_to_all | solution.py:411
  9.4 1.6 %collective-permute-start = (bf16[2,8,64,128]{3,2,1,0:T(8,128)(2,1)S(1)}, bf16[2,8,64,128]{3,2,1,0:T(8,128)(2,1)S(1)}, u32[]{:S(2)}, u32[]{:S(2)}) collective-permute-start(bf16[2,8,64,128]{3,2,1,0:T(8,128)(2,1)S(1)} %get-tuple-element.33), channel_id=1, source_target_pairs={{0,1},{1,0},{2,3},{3,2},{4,5},{5,4},{6,7},{7,6},{8,9},{9,8},{10,11... | collective-permute-start | bytes 786440 | tf_op jit(solution)/shard_map/ppermute | solution.py:427
  27.6 6.7 %collective-permute-start.1 = (bf16[2,128,128]{2,1,0:T(8,128)(2,1)S(1)}, bf16[2,128,128]{2,1,0:T(8,128)(2,1)S(1)}, u32[]{:S(2)}, u32[]{:S(2)}) collective-permute-start(bf16[2,128,128]{2,1,0:T(8,128)(2,1)S(1)} %get-tuple-element.34), channel_id=1, source_target_pairs={{0,16},{16,0},{1,17},{17,1},{2,18},{18,2},{3,19},{19,3},{4,20},{20... | collective-permute-start | bytes 196616 | tf_op jit(solution)/shard_map/ppermute | solution.py:463
  31.3 12.5 %collective-permute-start.5 = (bf16[2,8,64,128]{3,2,1,0:T(8,128)(2,1)S(1)}, bf16[2,8,64,128]{3,2,1,0:T(8,128)(2,1)S(1)}, u32[]{:S(2)}, u32[]{:S(2)}) collective-permute-start(bf16[2,8,64,128]{3,2,1,0:T(8,128)(2,1)S(1)} %get-tuple-element.49), channel_id=1, source_target_pairs={{0,2},{1,3},{2,0},{3,1},{4,6},{5,7},{6,4},{7,5},{8,10},{9,11},{10,... | collective-permute-start | bytes 786440 | tf_op jit(solution)/shard_map/ppermute | solution.py:482
  34.2 9.5 %copy-start = (bf16[1024,2048]{1,0:T(8,128)(2,1)S(1)}, bf16[1024,2048]{1,0:T(8,128)(2,1)}, u32[]{:S(2)}) copy-start(bf16[1024,2048]{1,0:T(8,128)(2,1)} %weight_ref.1) | copy-start | bytes 12582916
  34.8 7.3 %collective-permute-start.2 = (bf16[2,1,2,128,128]{4,3,2,1,0:T(8,128)(2,1)S(1)}, bf16[2,1,2,128,128]{4,3,2,1,0:T(8,128)(2,1)S(1)}, u32[]{:S(2)}, u32[]{:S(2)}) collective-permute-start(bf16[2,1,2,128,128]{4,3,2,1,0:T(8,128)(2,1)S(1)} %get-tuple-element.46), channel_id=1, source_target_pairs={{0,12},{4,8},{8,4},{12,0},{1,13},{5,9},{9,5},{13,1},{2,14},{6,10},... | collective-permute-start | bytes 393224 | tf_op jit(solution)/shard_map/ppermute | solution.py:504
  35.9 7.6 %collective-permute-start.3 = (bf16[2,1,2,128,128]{4,3,2,1,0:T(8,128)(2,1)S(1)}, bf16[2,1,2,128,128]{4,3,2,1,0:T(8,128)(2,1)S(1)}, u32[]{:S(2)}, u32[]{:S(2)}) collective-permute-start(bf16[2,1,2,128,128]{4,3,2,1,0:T(8,128)(2,1)S(1)} %get-tuple-element.47), channel_id=1, source_target_pairs={{0,8},{4,12},{8,0},{12,4},{1,9},{5,13},{9,1},{13,5},{2,10},{6,14},... | collective-permute-start | bytes 393224 | tf_op jit(solution)/shard_map/ppermute | solution.py:504
  37.6 6.2 %collective-permute-start.4 = (bf16[2,1,2,128,128]{4,3,2,1,0:T(8,128)(2,1)S(1)}, bf16[2,1,2,128,128]{4,3,2,1,0:T(8,128)(2,1)S(1)}, u32[]{:S(2)}, u32[]{:S(2)}) collective-permute-start(bf16[2,1,2,128,128]{4,3,2,1,0:T(8,128)(2,1)S(1)} %get-tuple-element.48), channel_id=1, source_target_pairs={{0,4},{4,0},{8,12},{12,8},{1,5},{5,1},{9,13},{13,9},{2,6},{6,2},{1... | collective-permute-start | bytes 393224 | tf_op jit(solution)/shard_map/ppermute | solution.py:504
  44.3 1.4 %collective-permute-start.9 = (bf16[1,64,1024]{2,1,0:T(8,128)(2,1)S(1)}, bf16[1,64,1024]{2,1,0:T(8,128)(2,1)S(1)}, u32[]{:S(2)}, u32[]{:S(2)}) collective-permute-start(bf16[1,64,1024]{2,1,0:T(8,128)(2,1)S(1)} %get-tuple-element.55), channel_id=1, source_target_pairs={{0,1},{1,0},{2,3},{3,2},{4,5},{5,4},{6,7},{7,6},{8,9},{9,8},{10,11... | collective-permute-start | bytes 393224 | tf_op jit(solution)/shard_map/ppermute | solution.py:552
  44.8 1.5 %collective-permute-start.11 = (bf16[1,64,1024]{2,1,0:T(8,128)(2,1)S(1)}, bf16[1,64,1024]{2,1,0:T(8,128)(2,1)S(1)}, u32[]{:S(2)}, u32[]{:S(2)}) collective-permute-start(bf16[1,64,1024]{2,1,0:T(8,128)(2,1)S(1)} %get-tuple-element.58), channel_id=1, source_target_pairs={{0,1},{1,0},{2,3},{3,2},{4,5},{5,4},{6,7},{7,6},{8,9},{9,8},{10,11... | collective-permute-start | bytes 393224 | tf_op jit(solution)/shard_map/ppermute | solution.py:552
  45.8 6.4 %collective-permute-start.10 = (bf16[1,64,1024]{2,1,0:T(8,128)(2,1)S(1)}, bf16[1,64,1024]{2,1,0:T(8,128)(2,1)S(1)}, u32[]{:S(2)}, u32[]{:S(2)}) collective-permute-start(bf16[1,64,1024]{2,1,0:T(8,128)(2,1)S(1)} %sum.3), channel_id=1, source_target_pairs={{0,2},{1,3},{2,0},{3,1},{4,6},{5,7},{6,4},{7,5},{8,10},{9,11},{10,... | collective-permute-start | bytes 393224 | tf_op jit(solution)/shard_map/ppermute | solution.py:553
  46.4 7.8 %collective-permute-start.12 = (bf16[1,64,1024]{2,1,0:T(8,128)(2,1)S(1)}, bf16[1,64,1024]{2,1,0:T(8,128)(2,1)S(1)}, u32[]{:S(2)}, u32[]{:S(2)}) collective-permute-start(bf16[1,64,1024]{2,1,0:T(8,128)(2,1)S(1)} %sum.4), channel_id=1, source_target_pairs={{0,2},{1,3},{2,0},{3,1},{4,6},{5,7},{6,4},{7,5},{8,10},{9,11},{10,... | collective-permute-start | bytes 393224 | tf_op jit(solution)/shard_map/ppermute | solution.py:553
  48.7 1.9 %collective-permute-start.6 = (bf16[1,64,768]{2,1,0:T(8,128)(2,1)S(1)}, bf16[1,64,768]{2,1,0:T(8,128)(2,1)S(1)}, u32[]{:S(2)}, u32[]{:S(2)}) collective-permute-start(bf16[1,64,768]{2,1,0:T(8,128)(2,1)S(1)} %get-tuple-element.51), channel_id=1, source_target_pairs={{0,1},{1,0},{2,3},{3,2},{4,5},{5,4},{6,7},{7,6},{8,9},{9,8},{10,11... | collective-permute-start | bytes 294920 | tf_op jit(solution)/shard_map/ppermute | solution.py:556
  48.8 1.4 %collective-permute-start.7 = (bf16[1,64,640]{2,1,0:T(8,128)(2,1)S(1)}, bf16[1,64,640]{2,1,0:T(8,128)(2,1)S(1)}, u32[]{:S(2)}, u32[]{:S(2)}) collective-permute-start(bf16[1,64,640]{2,1,0:T(8,128)(2,1)S(1)} %get-tuple-element.52), channel_id=1, source_target_pairs={{0,1},{1,0},{2,3},{3,2},{4,5},{5,4},{6,7},{7,6},{8,9},{9,8},{10,11... | collective-permute-start | bytes 245768 | tf_op jit(solution)/shard_map/ppermute | solution.py:556
  49.3 1.3 %collective-permute-start.8 = (bf16[1,64,640]{2,1,0:T(8,128)(2,1)S(1)}, bf16[1,64,640]{2,1,0:T(8,128)(2,1)S(1)}, u32[]{:S(2)}, u32[]{:S(2)}) collective-permute-start(bf16[1,64,640]{2,1,0:T(8,128)(2,1)S(1)} %get-tuple-element.53), channel_id=1, source_target_pairs={{0,1},{1,0},{2,3},{3,2},{4,5},{5,4},{6,7},{7,6},{8,9},{9,8},{10,11... | collective-permute-start | bytes 245768 | tf_op jit(solution)/shard_map/ppermute | solution.py:556

commit v11 on v9

--- a/solution.py
+++ b/solution.py
@@ -156,6 +156,24 @@
             solved = [now - dot(now, mid).astype(BF16) for now, mid in zip(solved, inner)]
         step *= 2
     return solved
+
+
+def dot_two(left, right):
+    high = left.astype(BF16)
+    low = (left - high.astype(F32)).astype(BF16)
+    both = dot(jnp.concatenate([high, low], axis=0), right)
+    return both[: left.shape[0]] + both[left.shape[0] :]
+
+
+def refined(below, solved):
+    size = below[0].shape[0]
+    rows = lax.broadcasted_iota(jnp.int32, (size, size), 0)
+    cols = lax.broadcasted_iota(jnp.int32, (size, size), 1)
+    identity = jnp.where(rows == cols, 1.0, 0.0)
+    left_over = [
+        (identity - now.astype(F32) - dot_two(matrix, now)).astype(BF16) for matrix, now in zip(below, solved)
+    ]
+    return [now.astype(F32) + dot(now, rest) for now, rest in zip(solved, left_over)]
 
 
 def factor_kernel(tokens, ratio, sub, passing, total_too, got_ref, *refs):
@@ -186,18 +204,18 @@
             below.append(lower * scaled_col)
             strengths.append(strength)
         held.append((block, key, key_col, key_row, strengths))
-    solved = block_inverse(below)
+    solved = refined(below, block_inverse(below))
     flat = [(block, r) for block in range(blocks) for r in range(ratio)]
     weighted = []
     for inverse, (block, r) in zip(solved, flat):
         unused, key, key_col, key_row, strengths = held[block]
-        weighted.append(inverse.astype(F32) * key_col * strengths[r])
+        weighted.append(inverse * key_col * strengths[r])
     for part, (block, r) in zip(weighted, flat):
         value = block_rows(got_ref, slabs[block], tokens, 2 + r)
-        u_ref[block, r] = dot(part.astype(BF16), value)
+        u_ref[block, r] = dot_two(part, value)
     for part, (block, r) in zip(weighted, flat):
         unused, key, key_col, key_row, strengths = held[block]
-        w_ref[block, r] = dot((part * key_row).astype(BF16), key).astype(BF16)
+        w_ref[block, r] = dot_two(part * key_row, key).astype(BF16)
     turns, adds = [], []
     for block in range(blocks):
         key_t = held[block][1].T

time: 55.2 us -> 56 us (1.014)
  Pallas kernels: 10.5 us -> 11.2 us
    pallas_call x1, Pallas kernels: 3.39 us -> 4.13 us  [per_device(): pl.pallas_call(functools.partial(factor_kernel, tokens, ratio, sub, half...]
where the time goes in v11:
time: 56 us; the launch traced here: 55.8 us
  waiting for transfers between devices  27.2 us (49%)
  starting transfers between devices  17.2 us (31%)
  Pallas kernels  11.2 us (20%)
    all_to_all x1, waiting for transfers between devices, per_device(): lax.all_to_all(packed, partner_order(sub, n_head), split_axis=0, concat_a...  13.2 us
    all_to_all x1, starting transfers between devices, per_device(): lax.all_to_all(packed, partner_order(sub, n_head), split_axis=0, concat_a...  6.43 us
    ppermute x3, waiting for transfers between devices, per_device(): lax.ppermute(part, along_sub, [(here, here ^ distance) for here in range(...  5.46 us
    pallas_call x1, Pallas kernels, per_device(): pl.pallas_call(functools.partial(factor_kernel, tokens, ratio, sub, half...  4.13 us
    ppermute x2, waiting for transfers between devices, per_device(): passed_on.append(lax.ppermute(summed, along_head, across))  3.58 us
    ppermute x3, starting transfers between devices, per_device(): lax.ppermute(part, along_sub, [(here, here ^ distance) for here in range(...  3.55 us
    ppermute x1, starting transfers between devices, per_device(): incoming = lax.ppermute(state, 'outer', onward)  2.65 us
    pallas_call x1, Pallas kernels, per_device(): pl.pallas_call(functools.partial(pack_kernel, sub), out_shape=shape((sour...  2.29 us
  transfers between devices with their start and end apart: 14, of which 12 were waited for; matrix products, arithmetic and copies ran while one was open for 0% of the time, Pallas kernels for 6%

profile of v11, /device:TPU:0, one launch (start us, length us, event | category | flops | bytes accessed | tf_op | source)
XLA Modules:
  0.0 55.8 jit_solution(13949448302748612762)
XLA Ops:
  0.0 2.3 %pack.1 = bf16[16,272,128]{2,1,0:T(8,128)(2,1)} custom-call(bf16[64,16,128]{2,1,0:T(8,128)(2,1)} %q_hbm.1, bf16[64,16,128]{2,1,0:T(8,128)(2,1)} %k_hbm.1, bf16[64,32,128]{2,1,0:T(8,128)(2,1)} %v_hbm.1, bf16[32,64]{1,0:T(8,128)(2,1)} %bitcast.4), custom_call_target="tpu_custom_call" | custom-call | tf_op jit(solution)/shard_map/pack/pallas_call | solution.py:395
  2.3 6.4 %all-to-all-start = ((bf16[16,272,128]{2,1,0:T(8,128)(2,1)}), bf16[16,272,128]{2,1,0:T(8,128)(2,1)S(1)}, u32[]{:S(2)}, u32[]{:S(2)}) async-start(bf16[16,272,128]{2,1,0:T(8,128)(2,1)} %pack.1), calls=%async_computation | async-start | bytes 2228224 | tf_op jit(solution)/shard_map/all_to_all | solution.py:411
  8.8 0.6 %gates.1 = (bf16[2,8,64,128]{3,2,1,0:T(8,128)(2,1)S(1)}, bf16[2,8,64,128]{3,2,1,0:T(8,128)(2,1)S(1)}) custom-call(bf16[64,32,128]{2,1,0:T(8,128)(2,1)S(1)} %copy-done.1, bf16[1,128]{1,0:T(2,128)(2,1)S(1)} %bitcast.3), custom_call_target="tpu_custom_call" | custom-call | flops 1 | bytes 1 | tf_op jit(solution)/shard_map/gates/pallas_call | solution.py:418
  9.4 0.5 collective-permute-start
  9.9 1.2 %collective-permute-done.swapped_ref.refs_5_.refs_7_ = bf16[2,8,64,128]{3,2,1,0:T(8,128)(2,1)S(1)} collective-permute-done((bf16[2,8,64,128]{3,2,1,0:T(8,128)(2,1)S(1)}, bf16[2,8,64,128]{3,2,1,0:T(8,128)(2,1)S(1)}, u32[]{:S(2)}, u32[]{:S(2)}) %collective-permute-start) | collective-permute-done | bytes 262176 | tf_op jit(solution)/shard_map/ppermute | solution.py:427
  11.0 13.2 %all-to-all-done.got_ref = bf16[16,272,128]{2,1,0:T(8,128)(2,1)S(1)} async-done(((bf16[16,272,128]{2,1,0:T(8,128)(2,1)}), bf16[16,272,128]{2,1,0:T(8,128)(2,1)S(1)}, u32[]{:S(2)}, u32[]{:S(2)}) %all-to-all-start) | async-done | bytes 1114144 | tf_op jit(solution)/shard_map/all_to_all | solution.py:411
  24.2 4.1 %factors.1 = (bf16[2,128,128]{2,1,0:T(8,128)(2,1)S(1)}, bf16[8,2,128,128]{3,2,1,0:T(8,128)(2,1)S(1)}, f32[8,2,128,128]{3,2,1,0:T(8,128)S(1)}, bf16[8,2,128,128]{...) custom-call(bf16[16,272,128]{2,1,0:T(8,128)(2,1)S(1)} %all-to-all-do, ...), custom_call_target="tpu_custom_call" | custom-call | flops 1 | bytes 1 | tf_op jit(solution)/shard_map/factors/pallas_call | solution.py:453
  28.4 2.7 %collective-permute-start.1 = (bf16[2,128,128]{2,1,0:T(8,128)(2,1)S(1)}, bf16[2,128,128]{2,1,0:T(8,128)(2,1)S(1)}, u32[]{:S(2)}, u32[]{:S(2)}) collective-permute-start(bf16[2,128,128]{2,1,0:T(8,128)(2,1)S(1)} %get-tuple-element.34), channel_id=1, source_target_pairs={{0,16},{16,0},{1,17},{17,1},{2,18},{18,2},{3,19},{19,3},{4,20},{20... | collective-permute-start | bytes 196616 | tf_op jit(solution)/shard_map/ppermute | solution.py:463
  31.0 1.1 %spread.1 = (f32[2,8,128,128]{3,2,1,0:T(8,128)S(1)}, bf16[2,8,128,128]{3,2,1,0:T(8,128)(2,1)S(1)}, bf16[2,8,64,128]{3,2,1,0:T(8,128)(2,1)S(1)}) custom-call(bf16[16,272,128]{2,1,0:T(8,128)(2,1)S(1)} %all-to-all-done.got_ref, bf16[8,2,128,128]{3,2,1,0:T(8,128)(2,1)S(1)} %get-tuple-element.35.w_ref, ...), custom_call_target="tpu_custom_call", output_to_operand_aliasing={{2}: (9, {})} | custom-call | flops 1 | bytes 1 | tf_op jit(solution)/shard_map/spread/pallas_call | solution.py:466
  32.1 1.2 %collective-permute-start.5 = (bf16[2,8,64,128]{3,2,1,0:T(8,128)(2,1)S(1)}, bf16[2,8,64,128]{3,2,1,0:T(8,128)(2,1)S(1)}, u32[]{:S(2)}, u32[]{:S(2)}) collective-permute-start(bf16[2,8,64,128]{3,2,1,0:T(8,128)(2,1)S(1)} %get-tuple-element.49), channel_id=1, source_target_pairs={{0,2},{1,3},{2,0},{3,1},{4,6},{5,7},{6,4},{7,5},{8,10},{9,11},{10,... | collective-permute-start | bytes 786440 | tf_op jit(solution)/shard_map/ppermute | solution.py:482
  33.3 1.8 %collective-permute-done.1.state_ref = bf16[2,128,128]{2,1,0:T(8,128)(2,1)S(1)} collective-permute-done((bf16[2,128,128]{2,1,0:T(8,128)(2,1)S(1)}, bf16[2,128,128]{2,1,0:T(8,128)(2,1)S(1)}, u32[]{:S(2)}, u32[]{:S(2)}) %collective-permute-start.1) | collective-permute-done | bytes 65568 | tf_op jit(solution)/shard_map/ppermute | solution.py:463
  35.0 0.5 join.1
  35.6 1.1 %collective-permute-start.2 = (bf16[2,1,2,128,128]{4,3,2,1,0:T(8,128)(2,1)S(1)}, bf16[2,1,2,128,128]{4,3,2,1,0:T(8,128)(2,1)S(1)}, u32[]{:S(2)}, u32[]{:S(2)}) collective-permute-start(bf16[2,1,2,128,128]{4,3,2,1,0:T(8,128)(2,1)S(1)} %get-tuple-element.46), channel_id=1, source_target_pairs={{0,12},{4,8},{8,4},{12,0},{1,13},{5,9},{9,5},{13,1},{2,14},{6,10},... | collective-permute-start | bytes 393224 | tf_op jit(solution)/shard_map/ppermute | solution.py:504
  36.7 1.7 %collective-permute-start.3 = (bf16[2,1,2,128,128]{4,3,2,1,0:T(8,128)(2,1)S(1)}, bf16[2,1,2,128,128]{4,3,2,1,0:T(8,128)(2,1)S(1)}, u32[]{:S(2)}, u32[]{:S(2)}) collective-permute-start(bf16[2,1,2,128,128]{4,3,2,1,0:T(8,128)(2,1)S(1)} %get-tuple-element.47), channel_id=1, source_target_pairs={{0,8},{4,12},{8,0},{12,4},{1,9},{5,13},{9,1},{13,5},{2,10},{6,14},... | collective-permute-start | bytes 393224 | tf_op jit(solution)/shard_map/ppermute | solution.py:504
  38.4 0.7 %collective-permute-start.4 = (bf16[2,1,2,128,128]{4,3,2,1,0:T(8,128)(2,1)S(1)}, bf16[2,1,2,128,128]{4,3,2,1,0:T(8,128)(2,1)S(1)}, u32[]{:S(2)}, u32[]{:S(2)}) collective-permute-start(bf16[2,1,2,128,128]{4,3,2,1,0:T(8,128)(2,1)S(1)} %get-tuple-element.48), channel_id=1, source_target_pairs={{0,4},{4,0},{8,12},{12,8},{1,5},{5,1},{9,13},{13,9},{2,6},{6,2},{1... | collective-permute-start | bytes 393224 | tf_op jit(solution)/shard_map/ppermute | solution.py:504
  39.1 3.8 %collective-permute-done.2.refs_1_ = bf16[2,1,2,128,128]{4,3,2,1,0:T(8,128)(2,1)S(1)} collective-permute-done((bf16[2,1,2,128,128]{4,3,2,1,0:T(8,128)(2,1)S(1)}, bf16[2,1,2,128,128]{4,3,2,1,0:T(8,128)(2,1)S(1)}, u32[]{:S(2)}, u32[]{:S(2)}) %collective-permute-start.2) | collective-permute-done | bytes 131104 | tf_op jit(solution)/shard_map/ppermute | solution.py:504
  42.9 1.4 %collective-permute-done.3.refs_2_ = bf16[2,1,2,128,128]{4,3,2,1,0:T(8,128)(2,1)S(1)} collective-permute-done((bf16[2,1,2,128,128]{4,3,2,1,0:T(8,128)(2,1)S(1)}, bf16[2,1,2,128,128]{4,3,2,1,0:T(8,128)(2,1)S(1)}, u32[]{:S(2)}, u32[]{:S(2)}) %collective-permute-start.3) | collective-permute-done | bytes 131104 | tf_op jit(solution)/shard_map/ppermute | solution.py:504
  44.3 0.2 collective-permute-done.4.refs_3_
  44.6 0.5 project.3
  45.2 0.4 project_more.1
  45.6 0.6 %collective-permute-start.11 = (bf16[1,64,1024]{2,1,0:T(8,128)(2,1)S(1)}, bf16[1,64,1024]{2,1,0:T(8,128)(2,1)S(1)}, u32[]{:S(2)}, u32[]{:S(2)}) collective-permute-start(bf16[1,64,1024]{2,1,0:T(8,128)(2,1)S(1)} %get-tuple-element.58), channel_id=1, source_target_pairs={{0,1},{1,0},{2,3},{3,2},{4,5},{5,4},{6,7},{7,6},{8,9},{9,8},{10,11... | collective-permute-start | bytes 393224 | tf_op jit(solution)/shard_map/ppermute | solution.py:552
  46.2 0.3 collective-permute-done.9.refs_0_
  46.5 0.1 collective-permute-start.10
  46.7 0.5 collective-permute-done.11.refs_0_
  47.2 1.5 %collective-permute-start.12 = (bf16[1,64,1024]{2,1,0:T(8,128)(2,1)S(1)}, bf16[1,64,1024]{2,1,0:T(8,128)(2,1)S(1)}, u32[]{:S(2)}, u32[]{:S(2)}) collective-permute-start(bf16[1,64,1024]{2,1,0:T(8,128)(2,1)S(1)} %sum.4), channel_id=1, source_target_pairs={{0,2},{1,3},{2,0},{3,1},{4,6},{5,7},{6,4},{7,5},{8,10},{9,11},{10,... | collective-permute-start | bytes 393224 | tf_op jit(solution)/shard_map/ppermute | solution.py:553
  48.7 0.8 %project.2 = (bf16[1,64,768]{2,1,0:T(8,128)(2,1)S(1)}, bf16[1,64,640]{2,1,0:T(8,128)(2,1)S(1)}, bf16[1,64,640]{2,1,0:T(8,128)(2,1)S(1)}, f32[1,64,2048]{2,1,0:T(8,128)S(1)}) custom-call(bf16[2,1,2,128,128]{4,3,2,1,0:T(8,128)(2,1)S(1)} %get-tuple-element.45.refs_0_, bf16[2,1,2,128,128]{4,3,2,1,0:T(8,128)(2,1)S(1)} %collective-permute-done.2.refs_1_, ...), custom_call_target="tpu_custom_call" | custom-call | flops 1 | bytes 1 | tf_op jit(solution)/shard_map/project/pallas_call | solution.py:513
  49.6 0.5 collective-permute-start.7
  50.2 0.8 %collective-permute-done.7.refs_1_ = bf16[1,64,640]{2,1,0:T(8,128)(2,1)S(1)} collective-permute-done((bf16[1,64,640]{2,1,0:T(8,128)(2,1)S(1)}, bf16[1,64,640]{2,1,0:T(8,128)(2,1)S(1)}, u32[]{:S(2)}, u32[]{:S(2)}) %collective-permute-start.7) | collective-permute-done | bytes 81952 | tf_op jit(solution)/shard_map/ppermute | solution.py:556
  51.0 0.4 collective-permute-done.8.refs_2_
  51.4 1.6 %collective-permute-done.10.refs_3_ = bf16[1,64,1024]{2,1,0:T(8,128)(2,1)S(1)} collective-permute-done((bf16[1,64,1024]{2,1,0:T(8,128)(2,1)S(1)}, bf16[1,64,1024]{2,1,0:T(8,128)(2,1)S(1)}, u32[]{:S(2)}, u32[]{:S(2)}) %collective-permute-start.10) | collective-permute-done | bytes 131104 | tf_op jit(solution)/shard_map/ppermute | solution.py:553
  52.9 2.0 %collective-permute-done.12.refs_4_ = bf16[1,64,1024]{2,1,0:T(8,128)(2,1)S(1)} collective-permute-done((bf16[1,64,1024]{2,1,0:T(8,128)(2,1)S(1)}, bf16[1,64,1024]{2,1,0:T(8,128)(2,1)S(1)}, u32[]{:S(2)}, u32[]{:S(2)}) %collective-permute-start.12) | collective-permute-done | bytes 131104 | tf_op jit(solution)/shard_map/ppermute | solution.py:553
  55.0 0.8 %sum.5 = bf16[1,64,2048]{2,1,0:T(8,128)(2,1)} custom-call(f32[1,64,2048]{2,1,0:T(8,128)S(1)} %get-tuple-element.50.keep_ref, bf16[1,64,768]{2,1,0:T(8,128)(2,1)S(1)} %collective-permute-done.6.refs_0_, bf16[1,64,640]{2,1,0:T(8,128)(2,1)S(1)} %collective-permute-done.7.refs_1_, bf16[1,64,640]{2,1,0:T(8,128)(2,1)S(1)} %collective-permute-done.8.refs_2_, ...), custom_call_target="tpu_custom_call" | custom-call | flops 1 | bytes 1 | tf_op jit(solution)/shard_map/sum/pallas_call | solution.py:527
  (14 shorter events, 0.3 us)
Async XLA Ops:
  2.3 6.5 %copy-start.1 = (bf16[64,32,128]{2,1,0:T(8,128)(2,1)S(1)}, bf16[64,32,128]{2,1,0:T(8,128)(2,1)}, u32[]{:S(2)}) copy-start(bf16[64,32,128]{2,1,0:T(8,128)(2,1)} %gate_ref.1) | copy-start | bytes 1572868
  2.3 6.5 %copy-start.2 = (bf16[128]{0:T(256)(128)(2,1)S(1)}, bf16[128]{0:T(256)(128)(2,1)}, u32[]{:S(2)}) copy-start(bf16[128]{0:T(256)(128)(2,1)} %param.12) | copy-start | bytes 772
  2.3 21.9 %all-to-all-start = ((bf16[16,272,128]{2,1,0:T(8,128)(2,1)}), bf16[16,272,128]{2,1,0:T(8,128)(2,1)S(1)}, u32[]{:S(2)}, u32[]{:S(2)}) async-start(bf16[16,272,128]{2,1,0:T(8,128)(2,1)} %pack.1), calls=%async_computation | async-start | bytes 2228224 | tf_op jit(solution)/shard_map/all_to_all | solution.py:411
  9.4 1.6 %collective-permute-start = (bf16[2,8,64,128]{3,2,1,0:T(8,128)(2,1)S(1)}, bf16[2,8,64,128]{3,2,1,0:T(8,128)(2,1)S(1)}, u32[]{:S(2)}, u32[]{:S(2)}) collective-permute-start(bf16[2,8,64,128]{3,2,1,0:T(8,128)(2,1)S(1)} %get-tuple-element.33), channel_id=1, source_target_pairs={{0,1},{1,0},{2,3},{3,2},{4,5},{5,4},{6,7},{7,6},{8,9},{9,8},{10,11... | collective-permute-start | bytes 786440 | tf_op jit(solution)/shard_map/ppermute | solution.py:427
  28.4 6.7 %collective-permute-start.1 = (bf16[2,128,128]{2,1,0:T(8,128)(2,1)S(1)}, bf16[2,128,128]{2,1,0:T(8,128)(2,1)S(1)}, u32[]{:S(2)}, u32[]{:S(2)}) collective-permute-start(bf16[2,128,128]{2,1,0:T(8,128)(2,1)S(1)} %get-tuple-element.34), channel_id=1, source_target_pairs={{0,16},{16,0},{1,17},{17,1},{2,18},{18,2},{3,19},{19,3},{4,20},{20... | collective-permute-start | bytes 196616 | tf_op jit(solution)/shard_map/ppermute | solution.py:463
  32.1 12.4 %collective-permute-start.5 = (bf16[2,8,64,128]{3,2,1,0:T(8,128)(2,1)S(1)}, bf16[2,8,64,128]{3,2,1,0:T(8,128)(2,1)S(1)}, u32[]{:S(2)}, u32[]{:S(2)}) collective-permute-start(bf16[2,8,64,128]{3,2,1,0:T(8,128)(2,1)S(1)} %get-tuple-element.49), channel_id=1, source_target_pairs={{0,2},{1,3},{2,0},{3,1},{4,6},{5,7},{6,4},{7,5},{8,10},{9,11},{10,... | collective-permute-start | bytes 786440 | tf_op jit(solution)/shard_map/ppermute | solution.py:482
  35.0 9.5 %copy-start = (bf16[1024,2048]{1,0:T(8,128)(2,1)S(1)}, bf16[1024,2048]{1,0:T(8,128)(2,1)}, u32[]{:S(2)}) copy-start(bf16[1024,2048]{1,0:T(8,128)(2,1)} %weight_ref.1) | copy-start | bytes 12582916
  35.6 7.3 %collective-permute-start.2 = (bf16[2,1,2,128,128]{4,3,2,1,0:T(8,128)(2,1)S(1)}, bf16[2,1,2,128,128]{4,3,2,1,0:T(8,128)(2,1)S(1)}, u32[]{:S(2)}, u32[]{:S(2)}) collective-permute-start(bf16[2,1,2,128,128]{4,3,2,1,0:T(8,128)(2,1)S(1)} %get-tuple-element.46), channel_id=1, source_target_pairs={{0,12},{4,8},{8,4},{12,0},{1,13},{5,9},{9,5},{13,1},{2,14},{6,10},... | collective-permute-start | bytes 393224 | tf_op jit(solution)/shard_map/ppermute | solution.py:504
  36.7 7.6 %collective-permute-start.3 = (bf16[2,1,2,128,128]{4,3,2,1,0:T(8,128)(2,1)S(1)}, bf16[2,1,2,128,128]{4,3,2,1,0:T(8,128)(2,1)S(1)}, u32[]{:S(2)}, u32[]{:S(2)}) collective-permute-start(bf16[2,1,2,128,128]{4,3,2,1,0:T(8,128)(2,1)S(1)} %get-tuple-element.47), channel_id=1, source_target_pairs={{0,8},{4,12},{8,0},{12,4},{1,9},{5,13},{9,1},{13,5},{2,10},{6,14},... | collective-permute-start | bytes 393224 | tf_op jit(solution)/shard_map/ppermute | solution.py:504
  38.4 6.2 %collective-permute-start.4 = (bf16[2,1,2,128,128]{4,3,2,1,0:T(8,128)(2,1)S(1)}, bf16[2,1,2,128,128]{4,3,2,1,0:T(8,128)(2,1)S(1)}, u32[]{:S(2)}, u32[]{:S(2)}) collective-permute-start(bf16[2,1,2,128,128]{4,3,2,1,0:T(8,128)(2,1)S(1)} %get-tuple-element.48), channel_id=1, source_target_pairs={{0,4},{4,0},{8,12},{12,8},{1,5},{5,1},{9,13},{13,9},{2,6},{6,2},{1... | collective-permute-start | bytes 393224 | tf_op jit(solution)/shard_map/ppermute | solution.py:504
  45.1 1.4 %collective-permute-start.9 = (bf16[1,64,1024]{2,1,0:T(8,128)(2,1)S(1)}, bf16[1,64,1024]{2,1,0:T(8,128)(2,1)S(1)}, u32[]{:S(2)}, u32[]{:S(2)}) collective-permute-start(bf16[1,64,1024]{2,1,0:T(8,128)(2,1)S(1)} %get-tuple-element.55), channel_id=1, source_target_pairs={{0,1},{1,0},{2,3},{3,2},{4,5},{5,4},{6,7},{7,6},{8,9},{9,8},{10,11... | collective-permute-start | bytes 393224 | tf_op jit(solution)/shard_map/ppermute | solution.py:552
  45.6 1.5 %collective-permute-start.11 = (bf16[1,64,1024]{2,1,0:T(8,128)(2,1)S(1)}, bf16[1,64,1024]{2,1,0:T(8,128)(2,1)S(1)}, u32[]{:S(2)}, u32[]{:S(2)}) collective-permute-start(bf16[1,64,1024]{2,1,0:T(8,128)(2,1)S(1)} %get-tuple-element.58), channel_id=1, source_target_pairs={{0,1},{1,0},{2,3},{3,2},{4,5},{5,4},{6,7},{7,6},{8,9},{9,8},{10,11... | collective-permute-start | bytes 393224 | tf_op jit(solution)/shard_map/ppermute | solution.py:552
  46.5 6.4 %collective-permute-start.10 = (bf16[1,64,1024]{2,1,0:T(8,128)(2,1)S(1)}, bf16[1,64,1024]{2,1,0:T(8,128)(2,1)S(1)}, u32[]{:S(2)}, u32[]{:S(2)}) collective-permute-start(bf16[1,64,1024]{2,1,0:T(8,128)(2,1)S(1)} %sum.3), channel_id=1, source_target_pairs={{0,2},{1,3},{2,0},{3,1},{4,6},{5,7},{6,4},{7,5},{8,10},{9,11},{10,... | collective-permute-start | bytes 393224 | tf_op jit(solution)/shard_map/ppermute | solution.py:553
  47.2 7.8 %collective-permute-start.12 = (bf16[1,64,1024]{2,1,0:T(8,128)(2,1)S(1)}, bf16[1,64,1024]{2,1,0:T(8,128)(2,1)S(1)}, u32[]{:S(2)}, u32[]{:S(2)}) collective-permute-start(bf16[1,64,1024]{2,1,0:T(8,128)(2,1)S(1)} %sum.4), channel_id=1, source_target_pairs={{0,2},{1,3},{2,0},{3,1},{4,6},{5,7},{6,4},{7,5},{8,10},{9,11},{10,... | collective-permute-start | bytes 393224 | tf_op jit(solution)/shard_map/ppermute | solution.py:553
  49.5 1.9 %collective-permute-start.6 = (bf16[1,64,768]{2,1,0:T(8,128)(2,1)S(1)}, bf16[1,64,768]{2,1,0:T(8,128)(2,1)S(1)}, u32[]{:S(2)}, u32[]{:S(2)}) collective-permute-start(bf16[1,64,768]{2,1,0:T(8,128)(2,1)S(1)} %get-tuple-element.51), channel_id=1, source_target_pairs={{0,1},{1,0},{2,3},{3,2},{4,5},{5,4},{6,7},{7,6},{8,9},{9,8},{10,11... | collective-permute-start | bytes 294920 | tf_op jit(solution)/shard_map/ppermute | solution.py:556
  49.6 1.4 %collective-permute-start.7 = (bf16[1,64,640]{2,1,0:T(8,128)(2,1)S(1)}, bf16[1,64,640]{2,1,0:T(8,128)(2,1)S(1)}, u32[]{:S(2)}, u32[]{:S(2)}) collective-permute-start(bf16[1,64,640]{2,1,0:T(8,128)(2,1)S(1)} %get-tuple-element.52), channel_id=1, source_target_pairs={{0,1},{1,0},{2,3},{3,2},{4,5},{5,4},{6,7},{7,6},{8,9},{9,8},{10,11... | collective-permute-start | bytes 245768 | tf_op jit(solution)/shard_map/ppermute | solution.py:556
  50.1 1.3 %collective-permute-start.8 = (bf16[1,64,640]{2,1,0:T(8,128)(2,1)S(1)}, bf16[1,64,640]{2,1,0:T(8,128)(2,1)S(1)}, u32[]{:S(2)}, u32[]{:S(2)}) collective-permute-start(bf16[1,64,640]{2,1,0:T(8,128)(2,1)S(1)} %get-tuple-element.53), channel_id=1, source_target_pairs={{0,1},{1,0},{2,3},{3,2},{4,5},{5,4},{6,7},{7,6},{8,9},{9,8},{10,11... | collective-permute-start | bytes 245768 | tf_op jit(solution)/shard_map/ppermute | solution.py:556

commit v12 on v11

--- a/solution.py
+++ b/solution.py
@@ -141,20 +141,16 @@
     size = below[0].shape[0]
     rows = lax.broadcasted_iota(jnp.int32, (size, size), 0)
     cols = lax.broadcasted_iota(jnp.int32, (size, size), 1)
-    zero = jnp.zeros((size, size), F32)
-    step = 1
+    apart = rows ^ cols
     solved = None
-    while step < size:
-        joins = (rows // (2 * step) == cols // (2 * step)) & (rows // step > cols // step)
-        parts = [jnp.where(joins, matrix, zero) for matrix in below]
-        if step == 1:
-            solved = [
-                jnp.where(rows == cols, jnp.ones_like(zero), -part).astype(BF16) for part in parts
-            ]
+    for level in range(size.bit_length() - 2):
+        joins = (apart >> level) == 1
+        parts = [jnp.where(joins, matrix, 0.0) for matrix in below]
+        if level == 0:
+            solved = [jnp.where(apart == 0, 1.0, -part).astype(BF16) for part in parts]
         else:
             inner = [dot(part.astype(BF16), now).astype(BF16) for part, now in zip(parts, solved)]
             solved = [now - dot(now, mid).astype(BF16) for now, mid in zip(solved, inner)]
-        step *= 2
     return solved
 
 

time: 56 us -> 55.7 us (level)
  no operation moved by 1% of the time
where the time goes in v12:
time: 55.7 us; the launch traced here: 55.5 us
  waiting for transfers between devices  27.2 us (49%)
  starting transfers between devices  17.2 us (31%)
  Pallas kernels  11 us (20%)
    all_to_all x1, waiting for transfers between devices, per_device(): lax.all_to_all(packed, partner_order(sub, n_head), split_axis=0, concat_a...  13.2 us
    all_to_all x1, starting transfers between devices, per_device(): lax.all_to_all(packed, partner_order(sub, n_head), split_axis=0, concat_a...  6.43 us
    ppermute x3, waiting for transfers between devices, per_device(): lax.ppermute(part, along_sub, [(here, here ^ distance) for here in range(...  5.46 us
    pallas_call x1, Pallas kernels, per_device(): pl.pallas_call(functools.partial(factor_kernel, tokens, ratio, sub, half...  3.9 us
    ppermute x2, waiting for transfers between devices, per_device(): passed_on.append(lax.ppermute(summed, along_head, across))  3.58 us
    ppermute x3, starting transfers between devices, per_device(): lax.ppermute(part, along_sub, [(here, here ^ distance) for here in range(...  3.55 us
    ppermute x1, starting transfers between devices, per_device(): incoming = lax.ppermute(state, 'outer', onward)  2.65 us
    pallas_call x1, Pallas kernels, per_device(): pl.pallas_call(functools.partial(pack_kernel, sub), out_shape=shape((sour...  2.29 us
  transfers between devices with their start and end apart: 14, of which 12 were waited for; matrix products, arithmetic and copies ran while one was open for 0% of the time, Pallas kernels for 6%

profile of v12, /device:TPU:0, one launch (start us, length us, event | category | flops | bytes accessed | tf_op | source)
XLA Modules:
  0.0 55.5 jit_solution(13668226687462258829)
XLA Ops:
  0.0 2.3 %pack.1 = bf16[16,272,128]{2,1,0:T(8,128)(2,1)} custom-call(bf16[64,16,128]{2,1,0:T(8,128)(2,1)} %q_hbm.1, bf16[64,16,128]{2,1,0:T(8,128)(2,1)} %k_hbm.1, bf16[64,32,128]{2,1,0:T(8,128)(2,1)} %v_hbm.1, bf16[32,64]{1,0:T(8,128)(2,1)} %bitcast.4), custom_call_target="tpu_custom_call" | custom-call | tf_op jit(solution)/shard_map/pack/pallas_call | solution.py:391
  2.3 6.4 %all-to-all-start = ((bf16[16,272,128]{2,1,0:T(8,128)(2,1)}), bf16[16,272,128]{2,1,0:T(8,128)(2,1)S(1)}, u32[]{:S(2)}, u32[]{:S(2)}) async-start(bf16[16,272,128]{2,1,0:T(8,128)(2,1)} %pack.1), calls=%async_computation | async-start | bytes 2228224 | tf_op jit(solution)/shard_map/all_to_all | solution.py:407
  8.8 0.6 %gates.1 = (bf16[2,8,64,128]{3,2,1,0:T(8,128)(2,1)S(1)}, bf16[2,8,64,128]{3,2,1,0:T(8,128)(2,1)S(1)}) custom-call(bf16[64,32,128]{2,1,0:T(8,128)(2,1)S(1)} %copy-done.1, bf16[1,128]{1,0:T(2,128)(2,1)S(1)} %bitcast.3), custom_call_target="tpu_custom_call" | custom-call | flops 1 | bytes 1 | tf_op jit(solution)/shard_map/gates/pallas_call | solution.py:414
  9.4 0.5 collective-permute-start
  9.9 1.2 %collective-permute-done.swapped_ref.refs_5_.refs_7_ = bf16[2,8,64,128]{3,2,1,0:T(8,128)(2,1)S(1)} collective-permute-done((bf16[2,8,64,128]{3,2,1,0:T(8,128)(2,1)S(1)}, bf16[2,8,64,128]{3,2,1,0:T(8,128)(2,1)S(1)}, u32[]{:S(2)}, u32[]{:S(2)}) %collective-permute-start) | collective-permute-done | bytes 262176 | tf_op jit(solution)/shard_map/ppermute | solution.py:423
  11.0 13.2 %all-to-all-done.got_ref = bf16[16,272,128]{2,1,0:T(8,128)(2,1)S(1)} async-done(((bf16[16,272,128]{2,1,0:T(8,128)(2,1)}), bf16[16,272,128]{2,1,0:T(8,128)(2,1)S(1)}, u32[]{:S(2)}, u32[]{:S(2)}) %all-to-all-start) | async-done | bytes 1114144 | tf_op jit(solution)/shard_map/all_to_all | solution.py:407
  24.2 3.9 %factors.1 = (bf16[2,128,128]{2,1,0:T(8,128)(2,1)S(1)}, bf16[8,2,128,128]{3,2,1,0:T(8,128)(2,1)S(1)}, f32[8,2,128,128]{3,2,1,0:T(8,128)S(1)}, bf16[8,2,128,128]{...) custom-call(bf16[16,272,128]{2,1,0:T(8,128)(2,1)S(1)} %all-to-all-do, ...), custom_call_target="tpu_custom_call" | custom-call | flops 1 | bytes 1 | tf_op jit(solution)/shard_map/factors/pallas_call | solution.py:449
  28.1 2.7 %collective-permute-start.1 = (bf16[2,128,128]{2,1,0:T(8,128)(2,1)S(1)}, bf16[2,128,128]{2,1,0:T(8,128)(2,1)S(1)}, u32[]{:S(2)}, u32[]{:S(2)}) collective-permute-start(bf16[2,128,128]{2,1,0:T(8,128)(2,1)S(1)} %get-tuple-element.34), channel_id=1, source_target_pairs={{0,16},{16,0},{1,17},{17,1},{2,18},{18,2},{3,19},{19,3},{4,20},{20... | collective-permute-start | bytes 196616 | tf_op jit(solution)/shard_map/ppermute | solution.py:459
  30.8 1.1 %spread.1 = (f32[2,8,128,128]{3,2,1,0:T(8,128)S(1)}, bf16[2,8,128,128]{3,2,1,0:T(8,128)(2,1)S(1)}, bf16[2,8,64,128]{3,2,1,0:T(8,128)(2,1)S(1)}) custom-call(bf16[16,272,128]{2,1,0:T(8,128)(2,1)S(1)} %all-to-all-done.got_ref, bf16[8,2,128,128]{3,2,1,0:T(8,128)(2,1)S(1)} %get-tuple-element.35.w_ref, ...), custom_call_target="tpu_custom_call", output_to_operand_aliasing={{2}: (9, {})} | custom-call | flops 1 | bytes 1 | tf_op jit(solution)/shard_map/spread/pallas_call | solution.py:462
  31.9 1.2 %collective-permute-start.5 = (bf16[2,8,64,128]{3,2,1,0:T(8,128)(2,1)S(1)}, bf16[2,8,64,128]{3,2,1,0:T(8,128)(2,1)S(1)}, u32[]{:S(2)}, u32[]{:S(2)}) collective-permute-start(bf16[2,8,64,128]{3,2,1,0:T(8,128)(2,1)S(1)} %get-tuple-element.49), channel_id=1, source_target_pairs={{0,2},{1,3},{2,0},{3,1},{4,6},{5,7},{6,4},{7,5},{8,10},{9,11},{10,... | collective-permute-start | bytes 786440 | tf_op jit(solution)/shard_map/ppermute | solution.py:478
  33.0 1.8 %collective-permute-done.1.state_ref = bf16[2,128,128]{2,1,0:T(8,128)(2,1)S(1)} collective-permute-done((bf16[2,128,128]{2,1,0:T(8,128)(2,1)S(1)}, bf16[2,128,128]{2,1,0:T(8,128)(2,1)S(1)}, u32[]{:S(2)}, u32[]{:S(2)}) %collective-permute-start.1) | collective-permute-done | bytes 65568 | tf_op jit(solution)/shard_map/ppermute | solution.py:459
  34.8 0.5 join.1
  35.3 1.1 %collective-permute-start.2 = (bf16[2,1,2,128,128]{4,3,2,1,0:T(8,128)(2,1)S(1)}, bf16[2,1,2,128,128]{4,3,2,1,0:T(8,128)(2,1)S(1)}, u32[]{:S(2)}, u32[]{:S(2)}) collective-permute-start(bf16[2,1,2,128,128]{4,3,2,1,0:T(8,128)(2,1)S(1)} %get-tuple-element.46), channel_id=1, source_target_pairs={{0,12},{4,8},{8,4},{12,0},{1,13},{5,9},{9,5},{13,1},{2,14},{6,10},... | collective-permute-start | bytes 393224 | tf_op jit(solution)/shard_map/ppermute | solution.py:500
  36.5 1.7 %collective-permute-start.3 = (bf16[2,1,2,128,128]{4,3,2,1,0:T(8,128)(2,1)S(1)}, bf16[2,1,2,128,128]{4,3,2,1,0:T(8,128)(2,1)S(1)}, u32[]{:S(2)}, u32[]{:S(2)}) collective-permute-start(bf16[2,1,2,128,128]{4,3,2,1,0:T(8,128)(2,1)S(1)} %get-tuple-element.47), channel_id=1, source_target_pairs={{0,8},{4,12},{8,0},{12,4},{1,9},{5,13},{9,1},{13,5},{2,10},{6,14},... | collective-permute-start | bytes 393224 | tf_op jit(solution)/shard_map/ppermute | solution.py:500
  38.1 0.7 %collective-permute-start.4 = (bf16[2,1,2,128,128]{4,3,2,1,0:T(8,128)(2,1)S(1)}, bf16[2,1,2,128,128]{4,3,2,1,0:T(8,128)(2,1)S(1)}, u32[]{:S(2)}, u32[]{:S(2)}) collective-permute-start(bf16[2,1,2,128,128]{4,3,2,1,0:T(8,128)(2,1)S(1)} %get-tuple-element.48), channel_id=1, source_target_pairs={{0,4},{4,0},{8,12},{12,8},{1,5},{5,1},{9,13},{13,9},{2,6},{6,2},{1... | collective-permute-start | bytes 393224 | tf_op jit(solution)/shard_map/ppermute | solution.py:500
  38.9 3.8 %collective-permute-done.2.refs_1_ = bf16[2,1,2,128,128]{4,3,2,1,0:T(8,128)(2,1)S(1)} collective-permute-done((bf16[2,1,2,128,128]{4,3,2,1,0:T(8,128)(2,1)S(1)}, bf16[2,1,2,128,128]{4,3,2,1,0:T(8,128)(2,1)S(1)}, u32[]{:S(2)}, u32[]{:S(2)}) %collective-permute-start.2) | collective-permute-done | bytes 131104 | tf_op jit(solution)/shard_map/ppermute | solution.py:500
  42.7 1.4 %collective-permute-done.3.refs_2_ = bf16[2,1,2,128,128]{4,3,2,1,0:T(8,128)(2,1)S(1)} collective-permute-done((bf16[2,1,2,128,128]{4,3,2,1,0:T(8,128)(2,1)S(1)}, bf16[2,1,2,128,128]{4,3,2,1,0:T(8,128)(2,1)S(1)}, u32[]{:S(2)}, u32[]{:S(2)}) %collective-permute-start.3) | collective-permute-done | bytes 131104 | tf_op jit(solution)/shard_map/ppermute | solution.py:500
  44.1 0.2 collective-permute-done.4.refs_3_
  44.4 0.5 project.3
  45.0 0.4 project_more.1
  45.4 0.6 %collective-permute-start.11 = (bf16[1,64,1024]{2,1,0:T(8,128)(2,1)S(1)}, bf16[1,64,1024]{2,1,0:T(8,128)(2,1)S(1)}, u32[]{:S(2)}, u32[]{:S(2)}) collective-permute-start(bf16[1,64,1024]{2,1,0:T(8,128)(2,1)S(1)} %get-tuple-element.58), channel_id=1, source_target_pairs={{0,1},{1,0},{2,3},{3,2},{4,5},{5,4},{6,7},{7,6},{8,9},{9,8},{10,11... | collective-permute-start | bytes 393224 | tf_op jit(solution)/shard_map/ppermute | solution.py:548
  46.0 0.3 collective-permute-done.9.refs_0_
  46.3 0.1 collective-permute-start.10
  46.4 0.5 collective-permute-done.11.refs_0_
  47.0 1.5 %collective-permute-start.12 = (bf16[1,64,1024]{2,1,0:T(8,128)(2,1)S(1)}, bf16[1,64,1024]{2,1,0:T(8,128)(2,1)S(1)}, u32[]{:S(2)}, u32[]{:S(2)}) collective-permute-start(bf16[1,64,1024]{2,1,0:T(8,128)(2,1)S(1)} %sum.4), channel_id=1, source_target_pairs={{0,2},{1,3},{2,0},{3,1},{4,6},{5,7},{6,4},{7,5},{8,10},{9,11},{10,... | collective-permute-start | bytes 393224 | tf_op jit(solution)/shard_map/ppermute | solution.py:549
  48.5 0.8 %project.2 = (bf16[1,64,768]{2,1,0:T(8,128)(2,1)S(1)}, bf16[1,64,640]{2,1,0:T(8,128)(2,1)S(1)}, bf16[1,64,640]{2,1,0:T(8,128)(2,1)S(1)}, f32[1,64,2048]{2,1,0:T(8,128)S(1)}) custom-call(bf16[2,1,2,128,128]{4,3,2,1,0:T(8,128)(2,1)S(1)} %get-tuple-element.45.refs_0_, bf16[2,1,2,128,128]{4,3,2,1,0:T(8,128)(2,1)S(1)} %collective-permute-done.2.refs_1_, ...), custom_call_target="tpu_custom_call" | custom-call | flops 1 | bytes 1 | tf_op jit(solution)/shard_map/project/pallas_call | solution.py:509
  49.4 0.5 collective-permute-start.7
  50.0 0.8 %collective-permute-done.7.refs_1_ = bf16[1,64,640]{2,1,0:T(8,128)(2,1)S(1)} collective-permute-done((bf16[1,64,640]{2,1,0:T(8,128)(2,1)S(1)}, bf16[1,64,640]{2,1,0:T(8,128)(2,1)S(1)}, u32[]{:S(2)}, u32[]{:S(2)}) %collective-permute-start.7) | collective-permute-done | bytes 81952 | tf_op jit(solution)/shard_map/ppermute | solution.py:552
  50.8 0.4 collective-permute-done.8.refs_2_
  51.2 1.6 %collective-permute-done.10.refs_3_ = bf16[1,64,1024]{2,1,0:T(8,128)(2,1)S(1)} collective-permute-done((bf16[1,64,1024]{2,1,0:T(8,128)(2,1)S(1)}, bf16[1,64,1024]{2,1,0:T(8,128)(2,1)S(1)}, u32[]{:S(2)}, u32[]{:S(2)}) %collective-permute-start.10) | collective-permute-done | bytes 131104 | tf_op jit(solution)/shard_map/ppermute | solution.py:549
  52.7 2.0 %collective-permute-done.12.refs_4_ = bf16[1,64,1024]{2,1,0:T(8,128)(2,1)S(1)} collective-permute-done((bf16[1,64,1024]{2,1,0:T(8,128)(2,1)S(1)}, bf16[1,64,1024]{2,1,0:T(8,128)(2,1)S(1)}, u32[]{:S(2)}, u32[]{:S(2)}) %collective-permute-start.12) | collective-permute-done | bytes 131104 | tf_op jit(solution)/shard_map/ppermute | solution.py:549
  54.7 0.8 %sum.5 = bf16[1,64,2048]{2,1,0:T(8,128)(2,1)} custom-call(f32[1,64,2048]{2,1,0:T(8,128)S(1)} %get-tuple-element.50.keep_ref, bf16[1,64,768]{2,1,0:T(8,128)(2,1)S(1)} %collective-permute-done.6.refs_0_, bf16[1,64,640]{2,1,0:T(8,128)(2,1)S(1)} %collective-permute-done.7.refs_1_, bf16[1,64,640]{2,1,0:T(8,128)(2,1)S(1)} %collective-permute-done.8.refs_2_, ...), custom_call_target="tpu_custom_call" | custom-call | flops 1 | bytes 1 | tf_op jit(solution)/shard_map/sum/pallas_call | solution.py:523
  (14 shorter events, 0.3 us)
Async XLA Ops:
  2.3 6.5 %copy-start.1 = (bf16[64,32,128]{2,1,0:T(8,128)(2,1)S(1)}, bf16[64,32,128]{2,1,0:T(8,128)(2,1)}, u32[]{:S(2)}) copy-start(bf16[64,32,128]{2,1,0:T(8,128)(2,1)} %gate_ref.1) | copy-start | bytes 1572868
  2.3 6.5 %copy-start.2 = (bf16[128]{0:T(256)(128)(2,1)S(1)}, bf16[128]{0:T(256)(128)(2,1)}, u32[]{:S(2)}) copy-start(bf16[128]{0:T(256)(128)(2,1)} %param.12) | copy-start | bytes 772
  2.3 21.9 %all-to-all-start = ((bf16[16,272,128]{2,1,0:T(8,128)(2,1)}), bf16[16,272,128]{2,1,0:T(8,128)(2,1)S(1)}, u32[]{:S(2)}, u32[]{:S(2)}) async-start(bf16[16,272,128]{2,1,0:T(8,128)(2,1)} %pack.1), calls=%async_computation | async-start | bytes 2228224 | tf_op jit(solution)/shard_map/all_to_all | solution.py:407
  9.4 1.6 %collective-permute-start = (bf16[2,8,64,128]{3,2,1,0:T(8,128)(2,1)S(1)}, bf16[2,8,64,128]{3,2,1,0:T(8,128)(2,1)S(1)}, u32[]{:S(2)}, u32[]{:S(2)}) collective-permute-start(bf16[2,8,64,128]{3,2,1,0:T(8,128)(2,1)S(1)} %get-tuple-element.33), channel_id=1, source_target_pairs={{0,1},{1,0},{2,3},{3,2},{4,5},{5,4},{6,7},{7,6},{8,9},{9,8},{10,11... | collective-permute-start | bytes 786440 | tf_op jit(solution)/shard_map/ppermute | solution.py:423
  28.1 6.7 %collective-permute-start.1 = (bf16[2,128,128]{2,1,0:T(8,128)(2,1)S(1)}, bf16[2,128,128]{2,1,0:T(8,128)(2,1)S(1)}, u32[]{:S(2)}, u32[]{:S(2)}) collective-permute-start(bf16[2,128,128]{2,1,0:T(8,128)(2,1)S(1)} %get-tuple-element.34), channel_id=1, source_target_pairs={{0,16},{16,0},{1,17},{17,1},{2,18},{18,2},{3,19},{19,3},{4,20},{20... | collective-permute-start | bytes 196616 | tf_op jit(solution)/shard_map/ppermute | solution.py:459
  31.9 12.5 %collective-permute-start.5 = (bf16[2,8,64,128]{3,2,1,0:T(8,128)(2,1)S(1)}, bf16[2,8,64,128]{3,2,1,0:T(8,128)(2,1)S(1)}, u32[]{:S(2)}, u32[]{:S(2)}) collective-permute-start(bf16[2,8,64,128]{3,2,1,0:T(8,128)(2,1)S(1)} %get-tuple-element.49), channel_id=1, source_target_pairs={{0,2},{1,3},{2,0},{3,1},{4,6},{5,7},{6,4},{7,5},{8,10},{9,11},{10,... | collective-permute-start | bytes 786440 | tf_op jit(solution)/shard_map/ppermute | solution.py:478
  34.8 9.5 %copy-start = (bf16[1024,2048]{1,0:T(8,128)(2,1)S(1)}, bf16[1024,2048]{1,0:T(8,128)(2,1)}, u32[]{:S(2)}) copy-start(bf16[1024,2048]{1,0:T(8,128)(2,1)} %weight_ref.1) | copy-start | bytes 12582916
  35.3 7.4 %collective-permute-start.2 = (bf16[2,1,2,128,128]{4,3,2,1,0:T(8,128)(2,1)S(1)}, bf16[2,1,2,128,128]{4,3,2,1,0:T(8,128)(2,1)S(1)}, u32[]{:S(2)}, u32[]{:S(2)}) collective-permute-start(bf16[2,1,2,128,128]{4,3,2,1,0:T(8,128)(2,1)S(1)} %get-tuple-element.46), channel_id=1, source_target_pairs={{0,12},{4,8},{8,4},{12,0},{1,13},{5,9},{9,5},{13,1},{2,14},{6,10},... | collective-permute-start | bytes 393224 | tf_op jit(solution)/shard_map/ppermute | solution.py:500
  36.5 7.7 %collective-permute-start.3 = (bf16[2,1,2,128,128]{4,3,2,1,0:T(8,128)(2,1)S(1)}, bf16[2,1,2,128,128]{4,3,2,1,0:T(8,128)(2,1)S(1)}, u32[]{:S(2)}, u32[]{:S(2)}) collective-permute-start(bf16[2,1,2,128,128]{4,3,2,1,0:T(8,128)(2,1)S(1)} %get-tuple-element.47), channel_id=1, source_target_pairs={{0,8},{4,12},{8,0},{12,4},{1,9},{5,13},{9,1},{13,5},{2,10},{6,14},... | collective-permute-start | bytes 393224 | tf_op jit(solution)/shard_map/ppermute | solution.py:500
  38.1 6.2 %collective-permute-start.4 = (bf16[2,1,2,128,128]{4,3,2,1,0:T(8,128)(2,1)S(1)}, bf16[2,1,2,128,128]{4,3,2,1,0:T(8,128)(2,1)S(1)}, u32[]{:S(2)}, u32[]{:S(2)}) collective-permute-start(bf16[2,1,2,128,128]{4,3,2,1,0:T(8,128)(2,1)S(1)} %get-tuple-element.48), channel_id=1, source_target_pairs={{0,4},{4,0},{8,12},{12,8},{1,5},{5,1},{9,13},{13,9},{2,6},{6,2},{1... | collective-permute-start | bytes 393224 | tf_op jit(solution)/shard_map/ppermute | solution.py:500
  44.9 1.4 %collective-permute-start.9 = (bf16[1,64,1024]{2,1,0:T(8,128)(2,1)S(1)}, bf16[1,64,1024]{2,1,0:T(8,128)(2,1)S(1)}, u32[]{:S(2)}, u32[]{:S(2)}) collective-permute-start(bf16[1,64,1024]{2,1,0:T(8,128)(2,1)S(1)} %get-tuple-element.55), channel_id=1, source_target_pairs={{0,1},{1,0},{2,3},{3,2},{4,5},{5,4},{6,7},{7,6},{8,9},{9,8},{10,11... | collective-permute-start | bytes 393224 | tf_op jit(solution)/shard_map/ppermute | solution.py:548
  45.4 1.5 %collective-permute-start.11 = (bf16[1,64,1024]{2,1,0:T(8,128)(2,1)S(1)}, bf16[1,64,1024]{2,1,0:T(8,128)(2,1)S(1)}, u32[]{:S(2)}, u32[]{:S(2)}) collective-permute-start(bf16[1,64,1024]{2,1,0:T(8,128)(2,1)S(1)} %get-tuple-element.58), channel_id=1, source_target_pairs={{0,1},{1,0},{2,3},{3,2},{4,5},{5,4},{6,7},{7,6},{8,9},{9,8},{10,11... | collective-permute-start | bytes 393224 | tf_op jit(solution)/shard_map/ppermute | solution.py:548
  46.3 6.4 %collective-permute-start.10 = (bf16[1,64,1024]{2,1,0:T(8,128)(2,1)S(1)}, bf16[1,64,1024]{2,1,0:T(8,128)(2,1)S(1)}, u32[]{:S(2)}, u32[]{:S(2)}) collective-permute-start(bf16[1,64,1024]{2,1,0:T(8,128)(2,1)S(1)} %sum.3), channel_id=1, source_target_pairs={{0,2},{1,3},{2,0},{3,1},{4,6},{5,7},{6,4},{7,5},{8,10},{9,11},{10,... | collective-permute-start | bytes 393224 | tf_op jit(solution)/shard_map/ppermute | solution.py:549
  47.0 7.8 %collective-permute-start.12 = (bf16[1,64,1024]{2,1,0:T(8,128)(2,1)S(1)}, bf16[1,64,1024]{2,1,0:T(8,128)(2,1)S(1)}, u32[]{:S(2)}, u32[]{:S(2)}) collective-permute-start(bf16[1,64,1024]{2,1,0:T(8,128)(2,1)S(1)} %sum.4), channel_id=1, source_target_pairs={{0,2},{1,3},{2,0},{3,1},{4,6},{5,7},{6,4},{7,5},{8,10},{9,11},{10,... | collective-permute-start | bytes 393224 | tf_op jit(solution)/shard_map/ppermute | solution.py:549
  49.3 1.9 %collective-permute-start.6 = (bf16[1,64,768]{2,1,0:T(8,128)(2,1)S(1)}, bf16[1,64,768]{2,1,0:T(8,128)(2,1)S(1)}, u32[]{:S(2)}, u32[]{:S(2)}) collective-permute-start(bf16[1,64,768]{2,1,0:T(8,128)(2,1)S(1)} %get-tuple-element.51), channel_id=1, source_target_pairs={{0,1},{1,0},{2,3},{3,2},{4,5},{5,4},{6,7},{7,6},{8,9},{9,8},{10,11... | collective-permute-start | bytes 294920 | tf_op jit(solution)/shard_map/ppermute | solution.py:552
  49.4 1.4 %collective-permute-start.7 = (bf16[1,64,640]{2,1,0:T(8,128)(2,1)S(1)}, bf16[1,64,640]{2,1,0:T(8,128)(2,1)S(1)}, u32[]{:S(2)}, u32[]{:S(2)}) collective-permute-start(bf16[1,64,640]{2,1,0:T(8,128)(2,1)S(1)} %get-tuple-element.52), channel_id=1, source_target_pairs={{0,1},{1,0},{2,3},{3,2},{4,5},{5,4},{6,7},{7,6},{8,9},{9,8},{10,11... | collective-permute-start | bytes 245768 | tf_op jit(solution)/shard_map/ppermute | solution.py:552
  49.9 1.3 %collective-permute-start.8 = (bf16[1,64,640]{2,1,0:T(8,128)(2,1)S(1)}, bf16[1,64,640]{2,1,0:T(8,128)(2,1)S(1)}, u32[]{:S(2)}, u32[]{:S(2)}) collective-permute-start(bf16[1,64,640]{2,1,0:T(8,128)(2,1)S(1)} %get-tuple-element.53), channel_id=1, source_target_pairs={{0,1},{1,0},{2,3},{3,2},{4,5},{5,4},{6,7},{7,6},{8,9},{9,8},{10,11... | collective-permute-start | bytes 245768 | tf_op jit(solution)/shard_map/ppermute | solution.py:552

commit v13 on v12

--- a/solution.py
+++ b/solution.py
@@ -118,6 +118,12 @@
         pair_ref[1] = swapped_ref[number + 1]
 
 
+def hold_kernel(weight_hbm, after_ref, weight_ref, done):
+    copy = pltpu.make_async_copy(weight_hbm, weight_ref, done)
+    copy.start()
+    copy.wait()
+
+
 def block_slabs(blocks, sub, sources):
     places = [partner(source, sub, sources // sub) for source in range(sources)]
     per = sources // blocks
@@ -142,14 +148,15 @@
     rows = lax.broadcasted_iota(jnp.int32, (size, size), 0)
     cols = lax.broadcasted_iota(jnp.int32, (size, size), 1)
     apart = rows ^ cols
-    solved = None
+    below = [matrix.astype(BF16) for matrix in below]
+    solved = [jnp.where(apart == 0, 1.0, 0.0).astype(BF16)] * len(below)
     for level in range(size.bit_length() - 2):
-        joins = (apart >> level) == 1
-        parts = [jnp.where(joins, matrix, 0.0) for matrix in below]
+        joins = jnp.where((apart >> level) == 1, 1.0, 0.0).astype(BF16)
+        parts = [matrix * joins for matrix in below]
         if level == 0:
-            solved = [jnp.where(apart == 0, 1.0, -part).astype(BF16) for part in parts]
+            solved = [now - part for part, now in zip(parts, solved)]
         else:
-            inner = [dot(part.astype(BF16), now).astype(BF16) for part, now in zip(parts, solved)]
+            inner = [dot(part, now).astype(BF16) for part, now in zip(parts, solved)]
             solved = [now - dot(now, mid).astype(BF16) for now, mid in zip(solved, inner)]
     return solved
 
@@ -431,6 +438,17 @@
             cost_estimate=LIGHT,
         )(own_gates, swapped)
 
+    with jax.named_scope("hold"):
+        held_weight = pl.pallas_call(
+            hold_kernel,
+            out_shape=shape(output_weight.shape, BF16),
+            in_specs=[ANY] * 2,
+            out_specs=VMEM,
+            scratch_shapes=[pltpu.SemaphoreType.DMA],
+            compiler_params=params(),
+            cost_estimate=LIGHT,
+        )(output_weight, own_gates)
+
     state_type = BF16 if outer == 2 else F32
     with jax.named_scope("factors"):
         depths = []
@@ -447,13 +465,13 @@
             shape((blocks, ratio, SPAN, width), F32),
         ] + tree
         state, w, u, *tree = pl.pallas_call(
-            functools.partial(factor_kernel, tokens, ratio, sub, half - 1, outer > 2),
+            functools.partial(factor_kernel, tokens, ratio, sub, half, outer > 2),
             out_shape=out_shape,
-            in_specs=[VMEM] + [ANY] * (half - 1),
+            in_specs=[VMEM] + [ANY] * half,
             out_specs=[VMEM] * len(out_shape),
             compiler_params=params(),
             cost_estimate=LIGHT,
-        )(got, *pairs)
+        )(got, held_weight, *pairs)
 
     onward = [(here, (here + 1) % outer) for here in range(outer)]
     incoming = lax.ppermute(state, "outer", onward)
@@ -516,7 +534,7 @@
                 scratch_shapes=[rows] * (1 - rows_too),
                 compiler_params=params(),
                 cost_estimate=LIGHT,
-            )(*normed, *[array for array, unused in used + others], output_weight)
+            )(*normed, *[array for array, unused in used + others], held_weight)
 
     def add(keep, arrived, kind):
         with jax.named_scope("sum"):
@@ -544,7 +562,7 @@
                     out_specs=[VMEM] * 2,
                     compiler_params=params(),
                     cost_estimate=LIGHT,
-                )(rows, output_weight)
+                )(rows, held_weight)
         summed = add(keep, [lax.ppermute(send, along_head, by_core)], BF16)
         passed_on.append(lax.ppermute(summed, along_head, across))
     third = columns // 3 // width * width

time: 55.7 us -> 57.8 us (1.038)
  local copies, waits for them, and re-layouts: 0.02 us -> 6.33 us
  waiting for transfers between devices: 27.2 us -> 22.8 us
    unnamed x6 -> x12, local copies, waits for them, and re-layouts: 0.02 us -> 6.33 us
    all_to_all x1, waiting for transfers between devices: 13.2 us -> 9.93 us  [per_device(): lax.all_to_all(packed, partner_order(sub, n_head), split_axis=0, concat_a...]
    ppermute x1, waiting for transfers between devices: 1.16 us -> 0.01 us  [per_device(): swapped = lax.ppermute(swap, along_head, by_core)]
    pallas_call x1 -> x2, Pallas kernels: 3.9 us -> 4.1 us  [the longest x1 3.82 us: per_device(): pl.pallas_call(functools.partial(factor_kernel, tokens, ratio, sub, half,...]
  transfers between devices with their start and end apart: 14 -> 14, of which waited for: 12 -> 11; matrix products, arithmetic and copies ran while one was open for 0% -> 0% of each run, Pallas kernels for 6% -> 7%
where the time goes in v13:
time: 57.8 us; the launch traced here: 57.5 us
  waiting for transfers between devices  22.8 us (39%)
  starting transfers between devices  17 us (29%)
  Pallas kernels  11.2 us (19%)
  local copies, waits for them, and re-layouts  6.33 us (11%)
    all_to_all x1, waiting for transfers between devices, per_device(): lax.all_to_all(packed, partner_order(sub, n_head), split_axis=0, concat_a...  9.93 us
    unnamed x12, local copies, waits for them, and re-layouts  6.33 us
    all_to_all x1, starting transfers between devices, per_device(): lax.all_to_all(packed, partner_order(sub, n_head), split_axis=0, concat_a...  6.3 us
    ppermute x3, waiting for transfers between devices, per_device(): lax.ppermute(part, along_sub, [(here, here ^ distance) for here in range(...  5.46 us
    pallas_call x1, Pallas kernels, per_device(): pl.pallas_call(functools.partial(factor_kernel, tokens, ratio, sub, half,...  3.82 us
    ppermute x2, waiting for transfers between devices, per_device(): passed_on.append(lax.ppermute(summed, along_head, across))  3.58 us
    ppermute x3, starting transfers between devices, per_device(): lax.ppermute(part, along_sub, [(here, here ^ distance) for here in range(...  3.55 us
    ppermute x1, starting transfers between devices, per_device(): incoming = lax.ppermute(state, 'outer', onward)  2.66 us
  transfers between devices with their start and end apart: 14, of which 11 were waited for; matrix products, arithmetic and copies ran while one was open for 0% of the time, Pallas kernels for 7%

profile of v13, /device:TPU:0, one launch (start us, length us, event | category | flops | bytes accessed | tf_op | source)
XLA Modules:
  0.0 57.5 jit_solution(7494945566956988415)
XLA Ops:
  0.0 2.3 %pack.1 = bf16[16,272,128]{2,1,0:T(8,128)(2,1)} custom-call(bf16[64,16,128]{2,1,0:T(8,128)(2,1)} %q_hbm.1, bf16[64,16,128]{2,1,0:T(8,128)(2,1)} %k_hbm.1, bf16[64,32,128]{2,1,0:T(8,128)(2,1)} %v_hbm.1, bf16[32,64]{1,0:T(8,128)(2,1)} %bitcast.4), custom_call_target="tpu_custom_call" | custom-call | tf_op jit(solution)/shard_map/pack/pallas_call | solution.py:398
  2.4 6.3 %all-to-all-start = ((bf16[16,272,128]{2,1,0:T(8,128)(2,1)}), bf16[16,272,128]{2,1,0:T(8,128)(2,1)S(1)}, u32[]{:S(2)}, u32[]{:S(2)}) async-start(bf16[16,272,128]{2,1,0:T(8,128)(2,1)} %pack.1), calls=%async_computation | async-start | bytes 2228224 | tf_op jit(solution)/shard_map/all_to_all | solution.py:414
  8.7 0.6 %gates.1 = (bf16[2,8,64,128]{3,2,1,0:T(8,128)(2,1)S(1)}, bf16[2,8,64,128]{3,2,1,0:T(8,128)(2,1)S(1)}) custom-call(bf16[64,32,128]{2,1,0:T(8,128)(2,1)S(1)} %copy-done.4, bf16[1,128]{1,0:T(2,128)(2,1)S(1)} %bitcast.3), custom_call_target="tpu_custom_call" | custom-call | flops 1 | bytes 1 | tf_op jit(solution)/shard_map/gates/pallas_call | solution.py:421
  9.3 0.5 collective-permute-start
  9.8 2.2 %copy-done.3 = bf16[1024,2048]{1,0:T(8,128)(2,1)S(1)} copy-done((bf16[1024,2048]{1,0:T(8,128)(2,1)S(1)}, bf16[1024,2048]{1,0:T(8,128)(2,1)}, u32[]{:S(2)}) %copy-start.3) | copy-done | bytes 4194328
  12.3 1.9 %copy-done = bf16[1024,2048]{1,0:T(8,128)(2,1)} copy-done((bf16[1024,2048]{1,0:T(8,128)(2,1)}, bf16[1024,2048]{1,0:T(8,128)(2,1)S(1)}, u32[]{:S(2)}) %copy-start) | copy-done | bytes 4194328
  14.2 9.9 %all-to-all-done.got_ref = bf16[16,272,128]{2,1,0:T(8,128)(2,1)S(1)} async-done(((bf16[16,272,128]{2,1,0:T(8,128)(2,1)}), bf16[16,272,128]{2,1,0:T(8,128)(2,1)S(1)}, u32[]{:S(2)}, u32[]{:S(2)}) %all-to-all-start) | async-done | bytes 1114144 | tf_op jit(solution)/shard_map/all_to_all | solution.py:414
  24.2 2.2 %copy-done.1 = bf16[1024,2048]{1,0:T(8,128)(2,1)S(1)} copy-done((bf16[1024,2048]{1,0:T(8,128)(2,1)S(1)}, bf16[1024,2048]{1,0:T(8,128)(2,1)}, u32[]{:S(2)}) %copy-start.1) | copy-done | bytes 4194328
  26.3 3.8 %factors.1 = (bf16[2,128,128]{2,1,0:T(8,128)(2,1)S(1)}, bf16[8,2,128,128]{3,2,1,0:T(8,128)(2,1)S(1)}, f32[8,2,128,128]{3,2,1,0:T(8,128)S(1)}, bf16[8,2,128,128]{...) custom-call(bf16[16,272,128]{2,1,0:T(8,128)(2,1)S(1)} %all-to-all-do, ...), custom_call_target="tpu_custom_call" | custom-call | flops 1 | bytes 1 | tf_op jit(solution)/shard_map/factors/pallas_call | solution.py:467
  30.2 2.7 %collective-permute-start.1 = (bf16[2,128,128]{2,1,0:T(8,128)(2,1)S(1)}, bf16[2,128,128]{2,1,0:T(8,128)(2,1)S(1)}, u32[]{:S(2)}, u32[]{:S(2)}) collective-permute-start(bf16[2,128,128]{2,1,0:T(8,128)(2,1)S(1)} %get-tuple-element.34), channel_id=1, source_target_pairs={{0,16},{16,0},{1,17},{17,1},{2,18},{18,2},{3,19},{19,3},{4,20},{20... | collective-permute-start | bytes 196616 | tf_op jit(solution)/shard_map/ppermute | solution.py:477
  32.8 1.1 %spread.1 = (f32[2,8,128,128]{3,2,1,0:T(8,128)S(1)}, bf16[2,8,128,128]{3,2,1,0:T(8,128)(2,1)S(1)}, bf16[2,8,64,128]{3,2,1,0:T(8,128)(2,1)S(1)}) custom-call(bf16[16,272,128]{2,1,0:T(8,128)(2,1)S(1)} %all-to-all-done.got_ref, bf16[8,2,128,128]{3,2,1,0:T(8,128)(2,1)S(1)} %get-tuple-element.35.w_ref, ...), custom_call_target="tpu_custom_call", output_to_operand_aliasing={{2}: (9, {})} | custom-call | flops 1 | bytes 1 | tf_op jit(solution)/shard_map/spread/pallas_call | solution.py:480
  33.9 1.2 %collective-permute-start.5 = (bf16[2,8,64,128]{3,2,1,0:T(8,128)(2,1)S(1)}, bf16[2,8,64,128]{3,2,1,0:T(8,128)(2,1)S(1)}, u32[]{:S(2)}, u32[]{:S(2)}) collective-permute-start(bf16[2,8,64,128]{3,2,1,0:T(8,128)(2,1)S(1)} %get-tuple-element.49), channel_id=1, source_target_pairs={{0,2},{1,3},{2,0},{3,1},{4,6},{5,7},{6,4},{7,5},{8,10},{9,11},{10,... | collective-permute-start | bytes 786440 | tf_op jit(solution)/shard_map/ppermute | solution.py:496
  35.1 1.8 %collective-permute-done.1.state_ref = bf16[2,128,128]{2,1,0:T(8,128)(2,1)S(1)} collective-permute-done((bf16[2,128,128]{2,1,0:T(8,128)(2,1)S(1)}, bf16[2,128,128]{2,1,0:T(8,128)(2,1)S(1)}, u32[]{:S(2)}, u32[]{:S(2)}) %collective-permute-start.1) | collective-permute-done | bytes 65568 | tf_op jit(solution)/shard_map/ppermute | solution.py:477
  36.8 0.5 join.1
  37.3 1.1 %collective-permute-start.2 = (bf16[2,1,2,128,128]{4,3,2,1,0:T(8,128)(2,1)S(1)}, bf16[2,1,2,128,128]{4,3,2,1,0:T(8,128)(2,1)S(1)}, u32[]{:S(2)}, u32[]{:S(2)}) collective-permute-start(bf16[2,1,2,128,128]{4,3,2,1,0:T(8,128)(2,1)S(1)} %get-tuple-element.46), channel_id=1, source_target_pairs={{0,12},{4,8},{8,4},{12,0},{1,13},{5,9},{9,5},{13,1},{2,14},{6,10},... | collective-permute-start | bytes 393224 | tf_op jit(solution)/shard_map/ppermute | solution.py:518
  38.5 1.7 %collective-permute-start.3 = (bf16[2,1,2,128,128]{4,3,2,1,0:T(8,128)(2,1)S(1)}, bf16[2,1,2,128,128]{4,3,2,1,0:T(8,128)(2,1)S(1)}, u32[]{:S(2)}, u32[]{:S(2)}) collective-permute-start(bf16[2,1,2,128,128]{4,3,2,1,0:T(8,128)(2,1)S(1)} %get-tuple-element.47), channel_id=1, source_target_pairs={{0,8},{4,12},{8,0},{12,4},{1,9},{5,13},{9,1},{13,5},{2,10},{6,14},... | collective-permute-start | bytes 393224 | tf_op jit(solution)/shard_map/ppermute | solution.py:518
  40.2 0.7 %collective-permute-start.4 = (bf16[2,1,2,128,128]{4,3,2,1,0:T(8,128)(2,1)S(1)}, bf16[2,1,2,128,128]{4,3,2,1,0:T(8,128)(2,1)S(1)}, u32[]{:S(2)}, u32[]{:S(2)}) collective-permute-start(bf16[2,1,2,128,128]{4,3,2,1,0:T(8,128)(2,1)S(1)} %get-tuple-element.48), channel_id=1, source_target_pairs={{0,4},{4,0},{8,12},{12,8},{1,5},{5,1},{9,13},{13,9},{2,6},{6,2},{1... | collective-permute-start | bytes 393224 | tf_op jit(solution)/shard_map/ppermute | solution.py:518
  40.9 3.8 %collective-permute-done.2.refs_1_ = bf16[2,1,2,128,128]{4,3,2,1,0:T(8,128)(2,1)S(1)} collective-permute-done((bf16[2,1,2,128,128]{4,3,2,1,0:T(8,128)(2,1)S(1)}, bf16[2,1,2,128,128]{4,3,2,1,0:T(8,128)(2,1)S(1)}, u32[]{:S(2)}, u32[]{:S(2)}) %collective-permute-start.2) | collective-permute-done | bytes 131104 | tf_op jit(solution)/shard_map/ppermute | solution.py:518
  44.7 1.4 %collective-permute-done.3.refs_2_ = bf16[2,1,2,128,128]{4,3,2,1,0:T(8,128)(2,1)S(1)} collective-permute-done((bf16[2,1,2,128,128]{4,3,2,1,0:T(8,128)(2,1)S(1)}, bf16[2,1,2,128,128]{4,3,2,1,0:T(8,128)(2,1)S(1)}, u32[]{:S(2)}, u32[]{:S(2)}) %collective-permute-start.3) | collective-permute-done | bytes 131104 | tf_op jit(solution)/shard_map/ppermute | solution.py:518
  46.4 0.5 project.3
  47.0 0.4 project_more.1
  47.4 0.6 collective-permute-start.11
  48.0 0.3 collective-permute-done.9.refs_0_
  48.4 0.5 collective-permute-done.11.refs_0_
  49.0 1.5 %collective-permute-start.12 = (bf16[1,64,1024]{2,1,0:T(8,128)(2,1)S(1)}, bf16[1,64,1024]{2,1,0:T(8,128)(2,1)S(1)}, u32[]{:S(2)}, u32[]{:S(2)}) collective-permute-start(bf16[1,64,1024]{2,1,0:T(8,128)(2,1)S(1)} %sum.4), channel_id=1, source_target_pairs={{0,2},{1,3},{2,0},{3,1},{4,6},{5,7},{6,4},{7,5},{8,10},{9,11},{10,... | collective-permute-start | bytes 393224 | tf_op jit(solution)/shard_map/ppermute | solution.py:567
  50.5 0.8 %project.2 = (bf16[1,64,768]{2,1,0:T(8,128)(2,1)S(1)}, bf16[1,64,640]{2,1,0:T(8,128)(2,1)S(1)}, bf16[1,64,640]{2,1,0:T(8,128)(2,1)S(1)}, f32[1,64,2048]{2,1,0:T(8,128)S(1)}) custom-call(bf16[2,1,2,128,128]{4,3,2,1,0:T(8,128)(2,1)S(1)} %get-tuple-element.45.refs_0_, bf16[2,1,2,128,128]{4,3,2,1,0:T(8,128)(2,1)S(1)} %collective-permute-done.2.refs_1_, ...), custom_call_target="tpu_custom_call" | custom-call | flops 1 | bytes 1 | tf_op jit(solution)/shard_map/project/pallas_call | solution.py:527
  51.4 0.5 collective-permute-start.7
  52.0 0.8 %collective-permute-done.7.refs_1_ = bf16[1,64,640]{2,1,0:T(8,128)(2,1)S(1)} collective-permute-done((bf16[1,64,640]{2,1,0:T(8,128)(2,1)S(1)}, bf16[1,64,640]{2,1,0:T(8,128)(2,1)S(1)}, u32[]{:S(2)}, u32[]{:S(2)}) %collective-permute-start.7) | collective-permute-done | bytes 81952 | tf_op jit(solution)/shard_map/ppermute | solution.py:570
  52.8 0.4 collective-permute-done.8.refs_2_
  53.2 1.6 %collective-permute-done.10.refs_3_ = bf16[1,64,1024]{2,1,0:T(8,128)(2,1)S(1)} collective-permute-done((bf16[1,64,1024]{2,1,0:T(8,128)(2,1)S(1)}, bf16[1,64,1024]{2,1,0:T(8,128)(2,1)S(1)}, u32[]{:S(2)}, u32[]{:S(2)}) %collective-permute-start.10) | collective-permute-done | bytes 131104 | tf_op jit(solution)/shard_map/ppermute | solution.py:567
  54.7 2.0 %collective-permute-done.12.refs_4_ = bf16[1,64,1024]{2,1,0:T(8,128)(2,1)S(1)} collective-permute-done((bf16[1,64,1024]{2,1,0:T(8,128)(2,1)S(1)}, bf16[1,64,1024]{2,1,0:T(8,128)(2,1)S(1)}, u32[]{:S(2)}, u32[]{:S(2)}) %collective-permute-start.12) | collective-permute-done | bytes 131104 | tf_op jit(solution)/shard_map/ppermute | solution.py:567
  56.8 0.8 %sum.5 = bf16[1,64,2048]{2,1,0:T(8,128)(2,1)} custom-call(f32[1,64,2048]{2,1,0:T(8,128)S(1)} %get-tuple-element.50.keep_ref, bf16[1,64,768]{2,1,0:T(8,128)(2,1)S(1)} %collective-permute-done.6.refs_0_, bf16[1,64,640]{2,1,0:T(8,128)(2,1)S(1)} %collective-permute-done.7.refs_1_, bf16[1,64,640]{2,1,0:T(8,128)(2,1)S(1)} %collective-permute-done.8.refs_2_, ...), custom_call_target="tpu_custom_call" | custom-call | flops 1 | bytes 1 | tf_op jit(solution)/shard_map/sum/pallas_call | solution.py:541
  (21 shorter events, 0.9 us)
Async XLA Ops:
  0.0 8.7 %copy-start.5 = (bf16[128]{0:T(256)(128)(2,1)S(1)}, bf16[128]{0:T(256)(128)(2,1)}, u32[]{:S(2)}) copy-start(bf16[128]{0:T(256)(128)(2,1)} %param.12) | copy-start | bytes 772
  0.0 8.7 %copy-start.4 = (bf16[64,32,128]{2,1,0:T(8,128)(2,1)S(1)}, bf16[64,32,128]{2,1,0:T(8,128)(2,1)}, u32[]{:S(2)}) copy-start(bf16[64,32,128]{2,1,0:T(8,128)(2,1)} %gate_ref.1) | copy-start | bytes 1572868
  2.4 21.8 %all-to-all-start = ((bf16[16,272,128]{2,1,0:T(8,128)(2,1)}), bf16[16,272,128]{2,1,0:T(8,128)(2,1)S(1)}, u32[]{:S(2)}, u32[]{:S(2)}) async-start(bf16[16,272,128]{2,1,0:T(8,128)(2,1)} %pack.1), calls=%async_computation | async-start | bytes 2228224 | tf_op jit(solution)/shard_map/all_to_all | solution.py:414
  9.3 4.9 %collective-permute-start = (bf16[2,8,64,128]{3,2,1,0:T(8,128)(2,1)S(1)}, bf16[2,8,64,128]{3,2,1,0:T(8,128)(2,1)S(1)}, u32[]{:S(2)}, u32[]{:S(2)}) collective-permute-start(bf16[2,8,64,128]{3,2,1,0:T(8,128)(2,1)S(1)} %get-tuple-element.33), channel_id=1, source_target_pairs={{0,1},{1,0},{2,3},{3,2},{4,5},{5,4},{6,7},{7,6},{8,9},{9,8},{10,11... | collective-permute-start | bytes 786440 | tf_op jit(solution)/shard_map/ppermute | solution.py:430
  9.8 2.2 %copy-start.3 = (bf16[1024,2048]{1,0:T(8,128)(2,1)S(1)}, bf16[1024,2048]{1,0:T(8,128)(2,1)}, u32[]{:S(2)}) copy-start(bf16[1024,2048]{1,0:T(8,128)(2,1)} %weight_hbm.1) | copy-start | bytes 12582916
  12.2 2.0 %copy-start = (bf16[1024,2048]{1,0:T(8,128)(2,1)}, bf16[1024,2048]{1,0:T(8,128)(2,1)S(1)}, u32[]{:S(2)}) copy-start(bf16[1024,2048]{1,0:T(8,128)(2,1)S(1)} %hold.1.refs_0_.refs_8_.weight_ref) | copy-start | bytes 12582916
  24.1 2.2 %copy-start.1 = (bf16[1024,2048]{1,0:T(8,128)(2,1)S(1)}, bf16[1024,2048]{1,0:T(8,128)(2,1)}, u32[]{:S(2)}) copy-start(bf16[1024,2048]{1,0:T(8,128)(2,1)} %copy-done) | copy-start | bytes 12582916
  30.2 6.7 %collective-permute-start.1 = (bf16[2,128,128]{2,1,0:T(8,128)(2,1)S(1)}, bf16[2,128,128]{2,1,0:T(8,128)(2,1)S(1)}, u32[]{:S(2)}, u32[]{:S(2)}) collective-permute-start(bf16[2,128,128]{2,1,0:T(8,128)(2,1)S(1)} %get-tuple-element.34), channel_id=1, source_target_pairs={{0,16},{16,0},{1,17},{17,1},{2,18},{18,2},{3,19},{19,3},{4,20},{20... | collective-permute-start | bytes 196616 | tf_op jit(solution)/shard_map/ppermute | solution.py:477
  33.9 12.5 %copy-start.2 = (bf16[1024,2048]{1,0:T(8,128)(2,1)S(1)}, bf16[1024,2048]{1,0:T(8,128)(2,1)}, u32[]{:S(2)}) copy-start(bf16[1024,2048]{1,0:T(8,128)(2,1)} %copy-done) | copy-start | bytes 12582916
  33.9 12.4 %collective-permute-start.5 = (bf16[2,8,64,128]{3,2,1,0:T(8,128)(2,1)S(1)}, bf16[2,8,64,128]{3,2,1,0:T(8,128)(2,1)S(1)}, u32[]{:S(2)}, u32[]{:S(2)}) collective-permute-start(bf16[2,8,64,128]{3,2,1,0:T(8,128)(2,1)S(1)} %get-tuple-element.49), channel_id=1, source_target_pairs={{0,2},{1,3},{2,0},{3,1},{4,6},{5,7},{6,4},{7,5},{8,10},{9,11},{10,... | collective-permute-start | bytes 786440 | tf_op jit(solution)/shard_map/ppermute | solution.py:496
  37.3 7.4 %collective-permute-start.2 = (bf16[2,1,2,128,128]{4,3,2,1,0:T(8,128)(2,1)S(1)}, bf16[2,1,2,128,128]{4,3,2,1,0:T(8,128)(2,1)S(1)}, u32[]{:S(2)}, u32[]{:S(2)}) collective-permute-start(bf16[2,1,2,128,128]{4,3,2,1,0:T(8,128)(2,1)S(1)} %get-tuple-element.46), channel_id=1, source_target_pairs={{0,12},{4,8},{8,4},{12,0},{1,13},{5,9},{9,5},{13,1},{2,14},{6,10},... | collective-permute-start | bytes 393224 | tf_op jit(solution)/shard_map/ppermute | solution.py:518
  38.5 7.7 %collective-permute-start.3 = (bf16[2,1,2,128,128]{4,3,2,1,0:T(8,128)(2,1)S(1)}, bf16[2,1,2,128,128]{4,3,2,1,0:T(8,128)(2,1)S(1)}, u32[]{:S(2)}, u32[]{:S(2)}) collective-permute-start(bf16[2,1,2,128,128]{4,3,2,1,0:T(8,128)(2,1)S(1)} %get-tuple-element.47), channel_id=1, source_target_pairs={{0,8},{4,12},{8,0},{12,4},{1,9},{5,13},{9,1},{13,5},{2,10},{6,14},... | collective-permute-start | bytes 393224 | tf_op jit(solution)/shard_map/ppermute | solution.py:518
  40.2 6.2 %collective-permute-start.4 = (bf16[2,1,2,128,128]{4,3,2,1,0:T(8,128)(2,1)S(1)}, bf16[2,1,2,128,128]{4,3,2,1,0:T(8,128)(2,1)S(1)}, u32[]{:S(2)}, u32[]{:S(2)}) collective-permute-start(bf16[2,1,2,128,128]{4,3,2,1,0:T(8,128)(2,1)S(1)} %get-tuple-element.48), channel_id=1, source_target_pairs={{0,4},{4,0},{8,12},{12,8},{1,5},{5,1},{9,13},{13,9},{2,6},{6,2},{1... | collective-permute-start | bytes 393224 | tf_op jit(solution)/shard_map/ppermute | solution.py:518
  46.9 1.4 %collective-permute-start.9 = (bf16[1,64,1024]{2,1,0:T(8,128)(2,1)S(1)}, bf16[1,64,1024]{2,1,0:T(8,128)(2,1)S(1)}, u32[]{:S(2)}, u32[]{:S(2)}) collective-permute-start(bf16[1,64,1024]{2,1,0:T(8,128)(2,1)S(1)} %get-tuple-element.55), channel_id=1, source_target_pairs={{0,1},{1,0},{2,3},{3,2},{4,5},{5,4},{6,7},{7,6},{8,9},{9,8},{10,11... | collective-permute-start | bytes 393224 | tf_op jit(solution)/shard_map/ppermute | solution.py:566
  47.4 1.5 %collective-permute-start.11 = (bf16[1,64,1024]{2,1,0:T(8,128)(2,1)S(1)}, bf16[1,64,1024]{2,1,0:T(8,128)(2,1)S(1)}, u32[]{:S(2)}, u32[]{:S(2)}) collective-permute-start(bf16[1,64,1024]{2,1,0:T(8,128)(2,1)S(1)} %get-tuple-element.58), channel_id=1, source_target_pairs={{0,1},{1,0},{2,3},{3,2},{4,5},{5,4},{6,7},{7,6},{8,9},{9,8},{10,11... | collective-permute-start | bytes 393224 | tf_op jit(solution)/shard_map/ppermute | solution.py:566
  48.3 6.4 %collective-permute-start.10 = (bf16[1,64,1024]{2,1,0:T(8,128)(2,1)S(1)}, bf16[1,64,1024]{2,1,0:T(8,128)(2,1)S(1)}, u32[]{:S(2)}, u32[]{:S(2)}) collective-permute-start(bf16[1,64,1024]{2,1,0:T(8,128)(2,1)S(1)} %sum.3), channel_id=1, source_target_pairs={{0,2},{1,3},{2,0},{3,1},{4,6},{5,7},{6,4},{7,5},{8,10},{9,11},{10,... | collective-permute-start | bytes 393224 | tf_op jit(solution)/shard_map/ppermute | solution.py:567
  49.0 7.8 %collective-permute-start.12 = (bf16[1,64,1024]{2,1,0:T(8,128)(2,1)S(1)}, bf16[1,64,1024]{2,1,0:T(8,128)(2,1)S(1)}, u32[]{:S(2)}, u32[]{:S(2)}) collective-permute-start(bf16[1,64,1024]{2,1,0:T(8,128)(2,1)S(1)} %sum.4), channel_id=1, source_target_pairs={{0,2},{1,3},{2,0},{3,1},{4,6},{5,7},{6,4},{7,5},{8,10},{9,11},{10,... | collective-permute-start | bytes 393224 | tf_op jit(solution)/shard_map/ppermute | solution.py:567
  51.3 1.9 %collective-permute-start.6 = (bf16[1,64,768]{2,1,0:T(8,128)(2,1)S(1)}, bf16[1,64,768]{2,1,0:T(8,128)(2,1)S(1)}, u32[]{:S(2)}, u32[]{:S(2)}) collective-permute-start(bf16[1,64,768]{2,1,0:T(8,128)(2,1)S(1)} %get-tuple-element.51), channel_id=1, source_target_pairs={{0,1},{1,0},{2,3},{3,2},{4,5},{5,4},{6,7},{7,6},{8,9},{9,8},{10,11... | collective-permute-start | bytes 294920 | tf_op jit(solution)/shard_map/ppermute | solution.py:570
  51.4 1.4 %collective-permute-start.7 = (bf16[1,64,640]{2,1,0:T(8,128)(2,1)S(1)}, bf16[1,64,640]{2,1,0:T(8,128)(2,1)S(1)}, u32[]{:S(2)}, u32[]{:S(2)}) collective-permute-start(bf16[1,64,640]{2,1,0:T(8,128)(2,1)S(1)} %get-tuple-element.52), channel_id=1, source_target_pairs={{0,1},{1,0},{2,3},{3,2},{4,5},{5,4},{6,7},{7,6},{8,9},{9,8},{10,11... | collective-permute-start | bytes 245768 | tf_op jit(solution)/shard_map/ppermute | solution.py:570
  51.9 1.3 %collective-permute-start.8 = (bf16[1,64,640]{2,1,0:T(8,128)(2,1)S(1)}, bf16[1,64,640]{2,1,0:T(8,128)(2,1)S(1)}, u32[]{:S(2)}, u32[]{:S(2)}) collective-permute-start(bf16[1,64,640]{2,1,0:T(8,128)(2,1)S(1)} %get-tuple-element.53), channel_id=1, source_target_pairs={{0,1},{1,0},{2,3},{3,2},{4,5},{5,4},{6,7},{7,6},{8,9},{9,8},{10,11... | collective-permute-start | bytes 245768 | tf_op jit(solution)/shard_map/ppermute | solution.py:570

commit v14 on v12

--- a/solution.py
+++ b/solution.py
@@ -142,14 +142,15 @@
     rows = lax.broadcasted_iota(jnp.int32, (size, size), 0)
     cols = lax.broadcasted_iota(jnp.int32, (size, size), 1)
     apart = rows ^ cols
-    solved = None
+    below = [matrix.astype(BF16) for matrix in below]
+    solved = [jnp.where(apart == 0, 1.0, 0.0).astype(BF16)] * len(below)
     for level in range(size.bit_length() - 2):
-        joins = (apart >> level) == 1
-        parts = [jnp.where(joins, matrix, 0.0) for matrix in below]
+        joins = jnp.where((apart >> level) == 1, 1.0, 0.0).astype(BF16)
+        parts = [matrix * joins for matrix in below]
         if level == 0:
-            solved = [jnp.where(apart == 0, 1.0, -part).astype(BF16) for part in parts]
+            solved = [now - part for part, now in zip(parts, solved)]
         else:
-            inner = [dot(part.astype(BF16), now).astype(BF16) for part, now in zip(parts, solved)]
+            inner = [dot(part, now).astype(BF16) for part, now in zip(parts, solved)]
             solved = [now - dot(now, mid).astype(BF16) for now, mid in zip(solved, inner)]
     return solved
 
@@ -486,7 +487,7 @@
     columns = output_weight.shape[1]
     quarter = (n_head // 4, tokens, columns)
     half = n_head // 2
-    order = [0] + sorted(range(1, sub), reverse=True)
+    order = list(range(sub))
     with jax.named_scope("join"):
         normed = pl.pallas_call(
             functools.partial(join_kernel, order, n_head),

time: 55.7 us -> 56 us (level)
  no operation moved by 1% of the time
where the time goes in v14:
time: 56 us; the launch traced here: 55.7 us
  waiting for transfers between devices  27.5 us (49%)
  starting transfers between devices  17.1 us (31%)
  Pallas kernels  10.9 us (19%)
    all_to_all x1, waiting for transfers between devices, per_device(): lax.all_to_all(packed, partner_order(sub, n_head), split_axis=0, concat_a...  13.2 us
    all_to_all x1, starting transfers between devices, per_device(): lax.all_to_all(packed, partner_order(sub, n_head), split_axis=0, concat_a...  6.43 us
    ppermute x3, waiting for transfers between devices, per_device(): lax.ppermute(part, along_sub, [(here, here ^ distance) for here in range(...  5.74 us
    pallas_call x1, Pallas kernels, per_device(): pl.pallas_call(functools.partial(factor_kernel, tokens, ratio, sub, half...  3.82 us
    ppermute x2, waiting for transfers between devices, per_device(): passed_on.append(lax.ppermute(summed, along_head, across))  3.59 us
    ppermute x3, starting transfers between devices, per_device(): lax.ppermute(part, along_sub, [(here, here ^ distance) for here in range(...  3.55 us
    ppermute x1, starting transfers between devices, per_device(): incoming = lax.ppermute(state, 'outer', onward)  2.65 us
    pallas_call x1, Pallas kernels, per_device(): pl.pallas_call(functools.partial(pack_kernel, sub), out_shape=shape((sour...  2.29 us
  transfers between devices with their start and end apart: 14, of which 12 were waited for; matrix products, arithmetic and copies ran while one was open for 0% of the time, Pallas kernels for 6%

profile of v14, /device:TPU:0, one launch (start us, length us, event | category | flops | bytes accessed | tf_op | source)
XLA Modules:
  0.0 55.7 jit_solution(7426134393748779485)
XLA Ops:
  0.0 2.3 %pack.1 = bf16[16,272,128]{2,1,0:T(8,128)(2,1)} custom-call(bf16[64,16,128]{2,1,0:T(8,128)(2,1)} %q_hbm.1, bf16[64,16,128]{2,1,0:T(8,128)(2,1)} %k_hbm.1, bf16[64,32,128]{2,1,0:T(8,128)(2,1)} %v_hbm.1, bf16[32,64]{1,0:T(8,128)(2,1)} %bitcast.4), custom_call_target="tpu_custom_call" | custom-call | tf_op jit(solution)/shard_map/pack/pallas_call | solution.py:392
  2.3 6.4 %all-to-all-start = ((bf16[16,272,128]{2,1,0:T(8,128)(2,1)}), bf16[16,272,128]{2,1,0:T(8,128)(2,1)S(1)}, u32[]{:S(2)}, u32[]{:S(2)}) async-start(bf16[16,272,128]{2,1,0:T(8,128)(2,1)} %pack.1), calls=%async_computation | async-start | bytes 2228224 | tf_op jit(solution)/shard_map/all_to_all | solution.py:408
  8.8 0.6 %gates.1 = (bf16[2,8,64,128]{3,2,1,0:T(8,128)(2,1)S(1)}, bf16[2,8,64,128]{3,2,1,0:T(8,128)(2,1)S(1)}) custom-call(bf16[64,32,128]{2,1,0:T(8,128)(2,1)S(1)} %copy-done.1, bf16[1,128]{1,0:T(2,128)(2,1)S(1)} %bitcast.3), custom_call_target="tpu_custom_call" | custom-call | flops 1 | bytes 1 | tf_op jit(solution)/shard_map/gates/pallas_call | solution.py:415
  9.4 0.5 collective-permute-start
  9.9 1.2 %collective-permute-done.swapped_ref.refs_5_.refs_7_ = bf16[2,8,64,128]{3,2,1,0:T(8,128)(2,1)S(1)} collective-permute-done((bf16[2,8,64,128]{3,2,1,0:T(8,128)(2,1)S(1)}, bf16[2,8,64,128]{3,2,1,0:T(8,128)(2,1)S(1)}, u32[]{:S(2)}, u32[]{:S(2)}) %collective-permute-start) | collective-permute-done | bytes 262176 | tf_op jit(solution)/shard_map/ppermute | solution.py:424
  11.0 13.2 %all-to-all-done.got_ref = bf16[16,272,128]{2,1,0:T(8,128)(2,1)S(1)} async-done(((bf16[16,272,128]{2,1,0:T(8,128)(2,1)}), bf16[16,272,128]{2,1,0:T(8,128)(2,1)S(1)}, u32[]{:S(2)}, u32[]{:S(2)}) %all-to-all-start) | async-done | bytes 1114144 | tf_op jit(solution)/shard_map/all_to_all | solution.py:408
  24.2 3.8 %factors.1 = (bf16[2,128,128]{2,1,0:T(8,128)(2,1)S(1)}, bf16[8,2,128,128]{3,2,1,0:T(8,128)(2,1)S(1)}, f32[8,2,128,128]{3,2,1,0:T(8,128)S(1)}, bf16[8,2,128,128]{...) custom-call(bf16[16,272,128]{2,1,0:T(8,128)(2,1)S(1)} %all-to-all-do, ...), custom_call_target="tpu_custom_call" | custom-call | flops 1 | bytes 1 | tf_op jit(solution)/shard_map/factors/pallas_call | solution.py:450
  28.1 2.7 %collective-permute-start.1 = (bf16[2,128,128]{2,1,0:T(8,128)(2,1)S(1)}, bf16[2,128,128]{2,1,0:T(8,128)(2,1)S(1)}, u32[]{:S(2)}, u32[]{:S(2)}) collective-permute-start(bf16[2,128,128]{2,1,0:T(8,128)(2,1)S(1)} %get-tuple-element.34), channel_id=1, source_target_pairs={{0,16},{16,0},{1,17},{17,1},{2,18},{18,2},{3,19},{19,3},{4,20},{20... | collective-permute-start | bytes 196616 | tf_op jit(solution)/shard_map/ppermute | solution.py:460
  30.7 1.1 %spread.1 = (f32[2,8,128,128]{3,2,1,0:T(8,128)S(1)}, bf16[2,8,128,128]{3,2,1,0:T(8,128)(2,1)S(1)}, bf16[2,8,64,128]{3,2,1,0:T(8,128)(2,1)S(1)}) custom-call(bf16[16,272,128]{2,1,0:T(8,128)(2,1)S(1)} %all-to-all-done.got_ref, bf16[8,2,128,128]{3,2,1,0:T(8,128)(2,1)S(1)} %get-tuple-element.35.w_ref, ...), custom_call_target="tpu_custom_call", output_to_operand_aliasing={{2}: (9, {})} | custom-call | flops 1 | bytes 1 | tf_op jit(solution)/shard_map/spread/pallas_call | solution.py:463
  31.8 1.2 %collective-permute-start.5 = (bf16[2,8,64,128]{3,2,1,0:T(8,128)(2,1)S(1)}, bf16[2,8,64,128]{3,2,1,0:T(8,128)(2,1)S(1)}, u32[]{:S(2)}, u32[]{:S(2)}) collective-permute-start(bf16[2,8,64,128]{3,2,1,0:T(8,128)(2,1)S(1)} %get-tuple-element.49), channel_id=1, source_target_pairs={{0,2},{1,3},{2,0},{3,1},{4,6},{5,7},{6,4},{7,5},{8,10},{9,11},{10,... | collective-permute-start | bytes 786440 | tf_op jit(solution)/shard_map/ppermute | solution.py:479
  33.0 1.8 %collective-permute-done.1.state_ref = bf16[2,128,128]{2,1,0:T(8,128)(2,1)S(1)} collective-permute-done((bf16[2,128,128]{2,1,0:T(8,128)(2,1)S(1)}, bf16[2,128,128]{2,1,0:T(8,128)(2,1)S(1)}, u32[]{:S(2)}, u32[]{:S(2)}) %collective-permute-start.1) | collective-permute-done | bytes 65568 | tf_op jit(solution)/shard_map/ppermute | solution.py:460
  34.7 0.5 join.1
  35.3 1.3 %collective-permute-start.2 = (bf16[2,1,2,128,128]{4,3,2,1,0:T(8,128)(2,1)S(1)}, bf16[2,1,2,128,128]{4,3,2,1,0:T(8,128)(2,1)S(1)}, u32[]{:S(2)}, u32[]{:S(2)}) collective-permute-start(bf16[2,1,2,128,128]{4,3,2,1,0:T(8,128)(2,1)S(1)} %get-tuple-element.46), channel_id=1, source_target_pairs={{0,4},{4,0},{8,12},{12,8},{1,5},{5,1},{9,13},{13,9},{2,6},{6,2},{1... | collective-permute-start | bytes 393224 | tf_op jit(solution)/shard_map/ppermute | solution.py:501
  36.6 0.4 collective-permute-start.3
  37.0 1.9 %collective-permute-start.4 = (bf16[2,1,2,128,128]{4,3,2,1,0:T(8,128)(2,1)S(1)}, bf16[2,1,2,128,128]{4,3,2,1,0:T(8,128)(2,1)S(1)}, u32[]{:S(2)}, u32[]{:S(2)}) collective-permute-start(bf16[2,1,2,128,128]{4,3,2,1,0:T(8,128)(2,1)S(1)} %get-tuple-element.48), channel_id=1, source_target_pairs={{0,12},{4,8},{8,4},{12,0},{1,13},{5,9},{9,5},{13,1},{2,14},{6,10},... | collective-permute-start | bytes 393224 | tf_op jit(solution)/shard_map/ppermute | solution.py:501
  38.8 2.0 %collective-permute-done.2.refs_1_ = bf16[2,1,2,128,128]{4,3,2,1,0:T(8,128)(2,1)S(1)} collective-permute-done((bf16[2,1,2,128,128]{4,3,2,1,0:T(8,128)(2,1)S(1)}, bf16[2,1,2,128,128]{4,3,2,1,0:T(8,128)(2,1)S(1)}, u32[]{:S(2)}, u32[]{:S(2)}) %collective-permute-start.2) | collective-permute-done | bytes 131104 | tf_op jit(solution)/shard_map/ppermute | solution.py:501
  40.8 2.1 %collective-permute-done.3.refs_2_ = bf16[2,1,2,128,128]{4,3,2,1,0:T(8,128)(2,1)S(1)} collective-permute-done((bf16[2,1,2,128,128]{4,3,2,1,0:T(8,128)(2,1)S(1)}, bf16[2,1,2,128,128]{4,3,2,1,0:T(8,128)(2,1)S(1)}, u32[]{:S(2)}, u32[]{:S(2)}) %collective-permute-start.3) | collective-permute-done | bytes 131104 | tf_op jit(solution)/shard_map/ppermute | solution.py:501
  42.9 1.6 %collective-permute-done.4.refs_3_ = bf16[2,1,2,128,128]{4,3,2,1,0:T(8,128)(2,1)S(1)} collective-permute-done((bf16[2,1,2,128,128]{4,3,2,1,0:T(8,128)(2,1)S(1)}, bf16[2,1,2,128,128]{4,3,2,1,0:T(8,128)(2,1)S(1)}, u32[]{:S(2)}, u32[]{:S(2)}) %collective-permute-start.4) | collective-permute-done | bytes 131104 | tf_op jit(solution)/shard_map/ppermute | solution.py:501
  44.6 0.5 project.3
  45.2 0.4 project_more.1
  45.6 0.6 %collective-permute-start.11 = (bf16[1,64,1024]{2,1,0:T(8,128)(2,1)S(1)}, bf16[1,64,1024]{2,1,0:T(8,128)(2,1)S(1)}, u32[]{:S(2)}, u32[]{:S(2)}) collective-permute-start(bf16[1,64,1024]{2,1,0:T(8,128)(2,1)S(1)} %get-tuple-element.58), channel_id=1, source_target_pairs={{0,1},{1,0},{2,3},{3,2},{4,5},{5,4},{6,7},{7,6},{8,9},{9,8},{10,11... | collective-permute-start | bytes 393224 | tf_op jit(solution)/shard_map/ppermute | solution.py:549
  46.2 0.3 collective-permute-done.9.refs_0_
  46.6 0.6 %collective-permute-done.11.refs_0_ = bf16[1,64,1024]{2,1,0:T(8,128)(2,1)S(1)} collective-permute-done((bf16[1,64,1024]{2,1,0:T(8,128)(2,1)S(1)}, bf16[1,64,1024]{2,1,0:T(8,128)(2,1)S(1)}, u32[]{:S(2)}, u32[]{:S(2)}) %collective-permute-start.11) | collective-permute-done | bytes 131104 | tf_op jit(solution)/shard_map/ppermute | solution.py:549
  47.2 1.5 %collective-permute-start.12 = (bf16[1,64,1024]{2,1,0:T(8,128)(2,1)S(1)}, bf16[1,64,1024]{2,1,0:T(8,128)(2,1)S(1)}, u32[]{:S(2)}, u32[]{:S(2)}) collective-permute-start(bf16[1,64,1024]{2,1,0:T(8,128)(2,1)S(1)} %sum.4), channel_id=1, source_target_pairs={{0,2},{1,3},{2,0},{3,1},{4,6},{5,7},{6,4},{7,5},{8,10},{9,11},{10,... | collective-permute-start | bytes 393224 | tf_op jit(solution)/shard_map/ppermute | solution.py:550
  48.7 0.8 %project.2 = (bf16[1,64,768]{2,1,0:T(8,128)(2,1)S(1)}, bf16[1,64,640]{2,1,0:T(8,128)(2,1)S(1)}, bf16[1,64,640]{2,1,0:T(8,128)(2,1)S(1)}, f32[1,64,2048]{2,1,0:T(8,128)S(1)}) custom-call(bf16[2,1,2,128,128]{4,3,2,1,0:T(8,128)(2,1)S(1)} %get-tuple-element.45.refs_0_, bf16[2,1,2,128,128]{4,3,2,1,0:T(8,128)(2,1)S(1)} %collective-permute-done.2.refs_1_, ...), custom_call_target="tpu_custom_call" | custom-call | flops 1 | bytes 1 | tf_op jit(solution)/shard_map/project/pallas_call | solution.py:510
  49.6 0.5 collective-permute-start.7
  50.1 0.1 collective-permute-start.8
  50.2 0.8 %collective-permute-done.7.refs_1_ = bf16[1,64,640]{2,1,0:T(8,128)(2,1)S(1)} collective-permute-done((bf16[1,64,640]{2,1,0:T(8,128)(2,1)S(1)}, bf16[1,64,640]{2,1,0:T(8,128)(2,1)S(1)}, u32[]{:S(2)}, u32[]{:S(2)}) %collective-permute-start.7) | collective-permute-done | bytes 81952 | tf_op jit(solution)/shard_map/ppermute | solution.py:553
  51.0 0.4 collective-permute-done.8.refs_2_
  51.4 1.6 %collective-permute-done.10.refs_3_ = bf16[1,64,1024]{2,1,0:T(8,128)(2,1)S(1)} collective-permute-done((bf16[1,64,1024]{2,1,0:T(8,128)(2,1)S(1)}, bf16[1,64,1024]{2,1,0:T(8,128)(2,1)S(1)}, u32[]{:S(2)}, u32[]{:S(2)}) %collective-permute-start.10) | collective-permute-done | bytes 131104 | tf_op jit(solution)/shard_map/ppermute | solution.py:550
  52.9 2.0 %collective-permute-done.12.refs_4_ = bf16[1,64,1024]{2,1,0:T(8,128)(2,1)S(1)} collective-permute-done((bf16[1,64,1024]{2,1,0:T(8,128)(2,1)S(1)}, bf16[1,64,1024]{2,1,0:T(8,128)(2,1)S(1)}, u32[]{:S(2)}, u32[]{:S(2)}) %collective-permute-start.12) | collective-permute-done | bytes 131104 | tf_op jit(solution)/shard_map/ppermute | solution.py:550
  54.9 0.8 %sum.5 = bf16[1,64,2048]{2,1,0:T(8,128)(2,1)} custom-call(f32[1,64,2048]{2,1,0:T(8,128)S(1)} %get-tuple-element.50.keep_ref, bf16[1,64,768]{2,1,0:T(8,128)(2,1)S(1)} %collective-permute-done.6.refs_0_, bf16[1,64,640]{2,1,0:T(8,128)(2,1)S(1)} %collective-permute-done.7.refs_1_, bf16[1,64,640]{2,1,0:T(8,128)(2,1)S(1)} %collective-permute-done.8.refs_2_, ...), custom_call_target="tpu_custom_call" | custom-call | flops 1 | bytes 1 | tf_op jit(solution)/shard_map/sum/pallas_call | solution.py:524
  (14 shorter events, 0.3 us)
Async XLA Ops:
  2.3 6.5 %copy-start.1 = (bf16[64,32,128]{2,1,0:T(8,128)(2,1)S(1)}, bf16[64,32,128]{2,1,0:T(8,128)(2,1)}, u32[]{:S(2)}) copy-start(bf16[64,32,128]{2,1,0:T(8,128)(2,1)} %gate_ref.1) | copy-start | bytes 1572868
  2.3 6.5 %copy-start.2 = (bf16[128]{0:T(256)(128)(2,1)S(1)}, bf16[128]{0:T(256)(128)(2,1)}, u32[]{:S(2)}) copy-start(bf16[128]{0:T(256)(128)(2,1)} %param.12) | copy-start | bytes 772
  2.3 21.9 %all-to-all-start = ((bf16[16,272,128]{2,1,0:T(8,128)(2,1)}), bf16[16,272,128]{2,1,0:T(8,128)(2,1)S(1)}, u32[]{:S(2)}, u32[]{:S(2)}) async-start(bf16[16,272,128]{2,1,0:T(8,128)(2,1)} %pack.1), calls=%async_computation | async-start | bytes 2228224 | tf_op jit(solution)/shard_map/all_to_all | solution.py:408
  9.4 1.6 %collective-permute-start = (bf16[2,8,64,128]{3,2,1,0:T(8,128)(2,1)S(1)}, bf16[2,8,64,128]{3,2,1,0:T(8,128)(2,1)S(1)}, u32[]{:S(2)}, u32[]{:S(2)}) collective-permute-start(bf16[2,8,64,128]{3,2,1,0:T(8,128)(2,1)S(1)} %get-tuple-element.33), channel_id=1, source_target_pairs={{0,1},{1,0},{2,3},{3,2},{4,5},{5,4},{6,7},{7,6},{8,9},{9,8},{10,11... | collective-permute-start | bytes 786440 | tf_op jit(solution)/shard_map/ppermute | solution.py:424
  28.1 6.7 %collective-permute-start.1 = (bf16[2,128,128]{2,1,0:T(8,128)(2,1)S(1)}, bf16[2,128,128]{2,1,0:T(8,128)(2,1)S(1)}, u32[]{:S(2)}, u32[]{:S(2)}) collective-permute-start(bf16[2,128,128]{2,1,0:T(8,128)(2,1)S(1)} %get-tuple-element.34), channel_id=1, source_target_pairs={{0,16},{16,0},{1,17},{17,1},{2,18},{18,2},{3,19},{19,3},{4,20},{20... | collective-permute-start | bytes 196616 | tf_op jit(solution)/shard_map/ppermute | solution.py:460
  31.8 12.7 %collective-permute-start.5 = (bf16[2,8,64,128]{3,2,1,0:T(8,128)(2,1)S(1)}, bf16[2,8,64,128]{3,2,1,0:T(8,128)(2,1)S(1)}, u32[]{:S(2)}, u32[]{:S(2)}) collective-permute-start(bf16[2,8,64,128]{3,2,1,0:T(8,128)(2,1)S(1)} %get-tuple-element.49), channel_id=1, source_target_pairs={{0,2},{1,3},{2,0},{3,1},{4,6},{5,7},{6,4},{7,5},{8,10},{9,11},{10,... | collective-permute-start | bytes 786440 | tf_op jit(solution)/shard_map/ppermute | solution.py:479
  34.7 9.8 %copy-start = (bf16[1024,2048]{1,0:T(8,128)(2,1)S(1)}, bf16[1024,2048]{1,0:T(8,128)(2,1)}, u32[]{:S(2)}) copy-start(bf16[1024,2048]{1,0:T(8,128)(2,1)} %weight_ref.1) | copy-start | bytes 12582916
  35.3 5.6 %collective-permute-start.2 = (bf16[2,1,2,128,128]{4,3,2,1,0:T(8,128)(2,1)S(1)}, bf16[2,1,2,128,128]{4,3,2,1,0:T(8,128)(2,1)S(1)}, u32[]{:S(2)}, u32[]{:S(2)}) collective-permute-start(bf16[2,1,2,128,128]{4,3,2,1,0:T(8,128)(2,1)S(1)} %get-tuple-element.46), channel_id=1, source_target_pairs={{0,4},{4,0},{8,12},{12,8},{1,5},{5,1},{9,13},{13,9},{2,6},{6,2},{1... | collective-permute-start | bytes 393224 | tf_op jit(solution)/shard_map/ppermute | solution.py:501
  36.6 6.3 %collective-permute-start.3 = (bf16[2,1,2,128,128]{4,3,2,1,0:T(8,128)(2,1)S(1)}, bf16[2,1,2,128,128]{4,3,2,1,0:T(8,128)(2,1)S(1)}, u32[]{:S(2)}, u32[]{:S(2)}) collective-permute-start(bf16[2,1,2,128,128]{4,3,2,1,0:T(8,128)(2,1)S(1)} %get-tuple-element.47), channel_id=1, source_target_pairs={{0,8},{4,12},{8,0},{12,4},{1,9},{5,13},{9,1},{13,5},{2,10},{6,14},... | collective-permute-start | bytes 393224 | tf_op jit(solution)/shard_map/ppermute | solution.py:501
  37.0 7.6 %collective-permute-start.4 = (bf16[2,1,2,128,128]{4,3,2,1,0:T(8,128)(2,1)S(1)}, bf16[2,1,2,128,128]{4,3,2,1,0:T(8,128)(2,1)S(1)}, u32[]{:S(2)}, u32[]{:S(2)}) collective-permute-start(bf16[2,1,2,128,128]{4,3,2,1,0:T(8,128)(2,1)S(1)} %get-tuple-element.48), channel_id=1, source_target_pairs={{0,12},{4,8},{8,4},{12,0},{1,13},{5,9},{9,5},{13,1},{2,14},{6,10},... | collective-permute-start | bytes 393224 | tf_op jit(solution)/shard_map/ppermute | solution.py:501
  45.1 1.4 %collective-permute-start.9 = (bf16[1,64,1024]{2,1,0:T(8,128)(2,1)S(1)}, bf16[1,64,1024]{2,1,0:T(8,128)(2,1)S(1)}, u32[]{:S(2)}, u32[]{:S(2)}) collective-permute-start(bf16[1,64,1024]{2,1,0:T(8,128)(2,1)S(1)} %get-tuple-element.55), channel_id=1, source_target_pairs={{0,1},{1,0},{2,3},{3,2},{4,5},{5,4},{6,7},{7,6},{8,9},{9,8},{10,11... | collective-permute-start | bytes 393224 | tf_op jit(solution)/shard_map/ppermute | solution.py:549
  45.6 1.6 %collective-permute-start.11 = (bf16[1,64,1024]{2,1,0:T(8,128)(2,1)S(1)}, bf16[1,64,1024]{2,1,0:T(8,128)(2,1)S(1)}, u32[]{:S(2)}, u32[]{:S(2)}) collective-permute-start(bf16[1,64,1024]{2,1,0:T(8,128)(2,1)S(1)} %get-tuple-element.58), channel_id=1, source_target_pairs={{0,1},{1,0},{2,3},{3,2},{4,5},{5,4},{6,7},{7,6},{8,9},{9,8},{10,11... | collective-permute-start | bytes 393224 | tf_op jit(solution)/shard_map/ppermute | solution.py:549
  46.5 6.4 %collective-permute-start.10 = (bf16[1,64,1024]{2,1,0:T(8,128)(2,1)S(1)}, bf16[1,64,1024]{2,1,0:T(8,128)(2,1)S(1)}, u32[]{:S(2)}, u32[]{:S(2)}) collective-permute-start(bf16[1,64,1024]{2,1,0:T(8,128)(2,1)S(1)} %sum.3), channel_id=1, source_target_pairs={{0,2},{1,3},{2,0},{3,1},{4,6},{5,7},{6,4},{7,5},{8,10},{9,11},{10,... | collective-permute-start | bytes 393224 | tf_op jit(solution)/shard_map/ppermute | solution.py:550
  47.2 7.8 %collective-permute-start.12 = (bf16[1,64,1024]{2,1,0:T(8,128)(2,1)S(1)}, bf16[1,64,1024]{2,1,0:T(8,128)(2,1)S(1)}, u32[]{:S(2)}, u32[]{:S(2)}) collective-permute-start(bf16[1,64,1024]{2,1,0:T(8,128)(2,1)S(1)} %sum.4), channel_id=1, source_target_pairs={{0,2},{1,3},{2,0},{3,1},{4,6},{5,7},{6,4},{7,5},{8,10},{9,11},{10,... | collective-permute-start | bytes 393224 | tf_op jit(solution)/shard_map/ppermute | solution.py:550
  49.5 1.9 %collective-permute-start.6 = (bf16[1,64,768]{2,1,0:T(8,128)(2,1)S(1)}, bf16[1,64,768]{2,1,0:T(8,128)(2,1)S(1)}, u32[]{:S(2)}, u32[]{:S(2)}) collective-permute-start(bf16[1,64,768]{2,1,0:T(8,128)(2,1)S(1)} %get-tuple-element.51), channel_id=1, source_target_pairs={{0,1},{1,0},{2,3},{3,2},{4,5},{5,4},{6,7},{7,6},{8,9},{9,8},{10,11... | collective-permute-start | bytes 294920 | tf_op jit(solution)/shard_map/ppermute | solution.py:553
  49.6 1.4 %collective-permute-start.7 = (bf16[1,64,640]{2,1,0:T(8,128)(2,1)S(1)}, bf16[1,64,640]{2,1,0:T(8,128)(2,1)S(1)}, u32[]{:S(2)}, u32[]{:S(2)}) collective-permute-start(bf16[1,64,640]{2,1,0:T(8,128)(2,1)S(1)} %get-tuple-element.52), channel_id=1, source_target_pairs={{0,1},{1,0},{2,3},{3,2},{4,5},{5,4},{6,7},{7,6},{8,9},{9,8},{10,11... | collective-permute-start | bytes 245768 | tf_op jit(solution)/shard_map/ppermute | solution.py:553
  50.1 1.3 %collective-permute-start.8 = (bf16[1,64,640]{2,1,0:T(8,128)(2,1)S(1)}, bf16[1,64,640]{2,1,0:T(8,128)(2,1)S(1)}, u32[]{:S(2)}, u32[]{:S(2)}) collective-permute-start(bf16[1,64,640]{2,1,0:T(8,128)(2,1)S(1)} %get-tuple-element.53), channel_id=1, source_target_pairs={{0,1},{1,0},{2,3},{3,2},{4,5},{5,4},{6,7},{7,6},{8,9},{9,8},{10,11... | collective-permute-start | bytes 245768 | tf_op jit(solution)/shard_map/ppermute | solution.py:553

commit v15 on v14

--- a/solution.py
+++ b/solution.py
@@ -209,10 +209,10 @@
         weighted.append(inverse * key_col * strengths[r])
     for part, (block, r) in zip(weighted, flat):
         value = block_rows(got_ref, slabs[block], tokens, 2 + r)
-        u_ref[block, r] = dot_two(part, value)
+        u_ref[block, r] = dot(part.astype(BF16), value)
     for part, (block, r) in zip(weighted, flat):
         unused, key, key_col, key_row, strengths = held[block]
-        w_ref[block, r] = dot_two(part * key_row, key).astype(BF16)
+        w_ref[block, r] = dot((part * key_row).astype(BF16), key).astype(BF16)
     turns, adds = [], []
     for block in range(blocks):
         key_t = held[block][1].T
@@ -487,7 +487,7 @@
     columns = output_weight.shape[1]
     quarter = (n_head // 4, tokens, columns)
     half = n_head // 2
-    order = list(range(sub))
+    order = [0] + sorted(range(1, sub), reverse=True)
     with jax.named_scope("join"):
         normed = pl.pallas_call(
             functools.partial(join_kernel, order, n_head),

time: 56 us -> 55.3 us (0.987)
  no operation moved by 1% of the time
where the time goes in v15:
time: 55.3 us; the launch traced here: 55.1 us
  waiting for transfers between devices  27.2 us (49%)
  starting transfers between devices  17.2 us (31%)
  Pallas kernels  10.6 us (19%)
    all_to_all x1, waiting for transfers between devices, per_device(): lax.all_to_all(packed, partner_order(sub, n_head), split_axis=0, concat_a...  13.2 us
    all_to_all x1, starting transfers between devices, per_device(): lax.all_to_all(packed, partner_order(sub, n_head), split_axis=0, concat_a...  6.43 us
    ppermute x3, waiting for transfers between devices, per_device(): lax.ppermute(part, along_sub, [(here, here ^ distance) for here in range(...  5.46 us
    ppermute x2, waiting for transfers between devices, per_device(): passed_on.append(lax.ppermute(summed, along_head, across))  3.58 us
    ppermute x3, starting transfers between devices, per_device(): lax.ppermute(part, along_sub, [(here, here ^ distance) for here in range(...  3.55 us
    pallas_call x1, Pallas kernels, per_device(): pl.pallas_call(functools.partial(factor_kernel, tokens, ratio, sub, half...  3.49 us
    ppermute x1, starting transfers between devices, per_device(): incoming = lax.ppermute(state, 'outer', onward)  2.66 us
    pallas_call x1, Pallas kernels, per_device(): pl.pallas_call(functools.partial(pack_kernel, sub), out_shape=shape((sour...  2.29 us
  transfers between devices with their start and end apart: 14, of which 12 were waited for; matrix products, arithmetic and copies ran while one was open for 0% of the time, Pallas kernels for 6%

profile of v15, /device:TPU:0, one launch (start us, length us, event | category | flops | bytes accessed | tf_op | source)
XLA Modules:
  0.0 55.1 jit_solution(16905718629649694583)
XLA Ops:
  0.0 2.3 %pack.1 = bf16[16,272,128]{2,1,0:T(8,128)(2,1)} custom-call(bf16[64,16,128]{2,1,0:T(8,128)(2,1)} %q_hbm.1, bf16[64,16,128]{2,1,0:T(8,128)(2,1)} %k_hbm.1, bf16[64,32,128]{2,1,0:T(8,128)(2,1)} %v_hbm.1, bf16[32,64]{1,0:T(8,128)(2,1)} %bitcast.4), custom_call_target="tpu_custom_call" | custom-call | tf_op jit(solution)/shard_map/pack/pallas_call | solution.py:392
  2.3 6.4 %all-to-all-start = ((bf16[16,272,128]{2,1,0:T(8,128)(2,1)}), bf16[16,272,128]{2,1,0:T(8,128)(2,1)S(1)}, u32[]{:S(2)}, u32[]{:S(2)}) async-start(bf16[16,272,128]{2,1,0:T(8,128)(2,1)} %pack.1), calls=%async_computation | async-start | bytes 2228224 | tf_op jit(solution)/shard_map/all_to_all | solution.py:408
  8.8 0.6 %gates.1 = (bf16[2,8,64,128]{3,2,1,0:T(8,128)(2,1)S(1)}, bf16[2,8,64,128]{3,2,1,0:T(8,128)(2,1)S(1)}) custom-call(bf16[64,32,128]{2,1,0:T(8,128)(2,1)S(1)} %copy-done.1, bf16[1,128]{1,0:T(2,128)(2,1)S(1)} %bitcast.3), custom_call_target="tpu_custom_call" | custom-call | flops 1 | bytes 1 | tf_op jit(solution)/shard_map/gates/pallas_call | solution.py:415
  9.4 0.5 collective-permute-start
  9.9 1.2 %collective-permute-done.swapped_ref.refs_5_.refs_7_ = bf16[2,8,64,128]{3,2,1,0:T(8,128)(2,1)S(1)} collective-permute-done((bf16[2,8,64,128]{3,2,1,0:T(8,128)(2,1)S(1)}, bf16[2,8,64,128]{3,2,1,0:T(8,128)(2,1)S(1)}, u32[]{:S(2)}, u32[]{:S(2)}) %collective-permute-start) | collective-permute-done | bytes 262176 | tf_op jit(solution)/shard_map/ppermute | solution.py:424
  11.0 13.2 %all-to-all-done.got_ref = bf16[16,272,128]{2,1,0:T(8,128)(2,1)S(1)} async-done(((bf16[16,272,128]{2,1,0:T(8,128)(2,1)}), bf16[16,272,128]{2,1,0:T(8,128)(2,1)S(1)}, u32[]{:S(2)}, u32[]{:S(2)}) %all-to-all-start) | async-done | bytes 1114144 | tf_op jit(solution)/shard_map/all_to_all | solution.py:408
  24.2 3.5 %factors.1 = (bf16[2,128,128]{2,1,0:T(8,128)(2,1)S(1)}, bf16[8,2,128,128]{3,2,1,0:T(8,128)(2,1)S(1)}, f32[8,2,128,128]{3,2,1,0:T(8,128)S(1)}, bf16[8,2,128,128]{...) custom-call(bf16[16,272,128]{2,1,0:T(8,128)(2,1)S(1)} %all-to-all-do, ...), custom_call_target="tpu_custom_call" | custom-call | flops 1 | bytes 1 | tf_op jit(solution)/shard_map/factors/pallas_call | solution.py:450
  27.7 2.7 %collective-permute-start.1 = (bf16[2,128,128]{2,1,0:T(8,128)(2,1)S(1)}, bf16[2,128,128]{2,1,0:T(8,128)(2,1)S(1)}, u32[]{:S(2)}, u32[]{:S(2)}) collective-permute-start(bf16[2,128,128]{2,1,0:T(8,128)(2,1)S(1)} %get-tuple-element.34), channel_id=1, source_target_pairs={{0,16},{16,0},{1,17},{17,1},{2,18},{18,2},{3,19},{19,3},{4,20},{20... | collective-permute-start | bytes 196616 | tf_op jit(solution)/shard_map/ppermute | solution.py:460
  30.4 1.1 %spread.1 = (f32[2,8,128,128]{3,2,1,0:T(8,128)S(1)}, bf16[2,8,128,128]{3,2,1,0:T(8,128)(2,1)S(1)}, bf16[2,8,64,128]{3,2,1,0:T(8,128)(2,1)S(1)}) custom-call(bf16[16,272,128]{2,1,0:T(8,128)(2,1)S(1)} %all-to-all-done.got_ref, bf16[8,2,128,128]{3,2,1,0:T(8,128)(2,1)S(1)} %get-tuple-element.35.w_ref, ...), custom_call_target="tpu_custom_call", output_to_operand_aliasing={{2}: (9, {})} | custom-call | flops 1 | bytes 1 | tf_op jit(solution)/shard_map/spread/pallas_call | solution.py:463
  31.5 1.2 %collective-permute-start.5 = (bf16[2,8,64,128]{3,2,1,0:T(8,128)(2,1)S(1)}, bf16[2,8,64,128]{3,2,1,0:T(8,128)(2,1)S(1)}, u32[]{:S(2)}, u32[]{:S(2)}) collective-permute-start(bf16[2,8,64,128]{3,2,1,0:T(8,128)(2,1)S(1)} %get-tuple-element.49), channel_id=1, source_target_pairs={{0,2},{1,3},{2,0},{3,1},{4,6},{5,7},{6,4},{7,5},{8,10},{9,11},{10,... | collective-permute-start | bytes 786440 | tf_op jit(solution)/shard_map/ppermute | solution.py:479
  32.6 1.8 %collective-permute-done.1.state_ref = bf16[2,128,128]{2,1,0:T(8,128)(2,1)S(1)} collective-permute-done((bf16[2,128,128]{2,1,0:T(8,128)(2,1)S(1)}, bf16[2,128,128]{2,1,0:T(8,128)(2,1)S(1)}, u32[]{:S(2)}, u32[]{:S(2)}) %collective-permute-start.1) | collective-permute-done | bytes 65568 | tf_op jit(solution)/shard_map/ppermute | solution.py:460
  34.4 0.5 join.1
  34.9 1.1 %collective-permute-start.2 = (bf16[2,1,2,128,128]{4,3,2,1,0:T(8,128)(2,1)S(1)}, bf16[2,1,2,128,128]{4,3,2,1,0:T(8,128)(2,1)S(1)}, u32[]{:S(2)}, u32[]{:S(2)}) collective-permute-start(bf16[2,1,2,128,128]{4,3,2,1,0:T(8,128)(2,1)S(1)} %get-tuple-element.46), channel_id=1, source_target_pairs={{0,12},{4,8},{8,4},{12,0},{1,13},{5,9},{9,5},{13,1},{2,14},{6,10},... | collective-permute-start | bytes 393224 | tf_op jit(solution)/shard_map/ppermute | solution.py:501
  36.1 1.7 %collective-permute-start.3 = (bf16[2,1,2,128,128]{4,3,2,1,0:T(8,128)(2,1)S(1)}, bf16[2,1,2,128,128]{4,3,2,1,0:T(8,128)(2,1)S(1)}, u32[]{:S(2)}, u32[]{:S(2)}) collective-permute-start(bf16[2,1,2,128,128]{4,3,2,1,0:T(8,128)(2,1)S(1)} %get-tuple-element.47), channel_id=1, source_target_pairs={{0,8},{4,12},{8,0},{12,4},{1,9},{5,13},{9,1},{13,5},{2,10},{6,14},... | collective-permute-start | bytes 393224 | tf_op jit(solution)/shard_map/ppermute | solution.py:501
  37.7 0.7 %collective-permute-start.4 = (bf16[2,1,2,128,128]{4,3,2,1,0:T(8,128)(2,1)S(1)}, bf16[2,1,2,128,128]{4,3,2,1,0:T(8,128)(2,1)S(1)}, u32[]{:S(2)}, u32[]{:S(2)}) collective-permute-start(bf16[2,1,2,128,128]{4,3,2,1,0:T(8,128)(2,1)S(1)} %get-tuple-element.48), channel_id=1, source_target_pairs={{0,4},{4,0},{8,12},{12,8},{1,5},{5,1},{9,13},{13,9},{2,6},{6,2},{1... | collective-permute-start | bytes 393224 | tf_op jit(solution)/shard_map/ppermute | solution.py:501
  38.5 3.8 %collective-permute-done.2.refs_1_ = bf16[2,1,2,128,128]{4,3,2,1,0:T(8,128)(2,1)S(1)} collective-permute-done((bf16[2,1,2,128,128]{4,3,2,1,0:T(8,128)(2,1)S(1)}, bf16[2,1,2,128,128]{4,3,2,1,0:T(8,128)(2,1)S(1)}, u32[]{:S(2)}, u32[]{:S(2)}) %collective-permute-start.2) | collective-permute-done | bytes 131104 | tf_op jit(solution)/shard_map/ppermute | solution.py:501
  42.3 1.4 %collective-permute-done.3.refs_2_ = bf16[2,1,2,128,128]{4,3,2,1,0:T(8,128)(2,1)S(1)} collective-permute-done((bf16[2,1,2,128,128]{4,3,2,1,0:T(8,128)(2,1)S(1)}, bf16[2,1,2,128,128]{4,3,2,1,0:T(8,128)(2,1)S(1)}, u32[]{:S(2)}, u32[]{:S(2)}) %collective-permute-start.3) | collective-permute-done | bytes 131104 | tf_op jit(solution)/shard_map/ppermute | solution.py:501
  43.7 0.2 collective-permute-done.4.refs_3_
  43.9 0.5 project.3
  44.5 0.4 project_more.1
  45.0 0.6 %collective-permute-start.11 = (bf16[1,64,1024]{2,1,0:T(8,128)(2,1)S(1)}, bf16[1,64,1024]{2,1,0:T(8,128)(2,1)S(1)}, u32[]{:S(2)}, u32[]{:S(2)}) collective-permute-start(bf16[1,64,1024]{2,1,0:T(8,128)(2,1)S(1)} %get-tuple-element.58), channel_id=1, source_target_pairs={{0,1},{1,0},{2,3},{3,2},{4,5},{5,4},{6,7},{7,6},{8,9},{9,8},{10,11... | collective-permute-start | bytes 393224 | tf_op jit(solution)/shard_map/ppermute | solution.py:549
  45.6 0.3 collective-permute-done.9.refs_0_
  45.9 0.1 collective-permute-start.10
  46.0 0.5 collective-permute-done.11.refs_0_
  46.6 1.5 %collective-permute-start.12 = (bf16[1,64,1024]{2,1,0:T(8,128)(2,1)S(1)}, bf16[1,64,1024]{2,1,0:T(8,128)(2,1)S(1)}, u32[]{:S(2)}, u32[]{:S(2)}) collective-permute-start(bf16[1,64,1024]{2,1,0:T(8,128)(2,1)S(1)} %sum.4), channel_id=1, source_target_pairs={{0,2},{1,3},{2,0},{3,1},{4,6},{5,7},{6,4},{7,5},{8,10},{9,11},{10,... | collective-permute-start | bytes 393224 | tf_op jit(solution)/shard_map/ppermute | solution.py:550
  48.1 0.8 %project.2 = (bf16[1,64,768]{2,1,0:T(8,128)(2,1)S(1)}, bf16[1,64,640]{2,1,0:T(8,128)(2,1)S(1)}, bf16[1,64,640]{2,1,0:T(8,128)(2,1)S(1)}, f32[1,64,2048]{2,1,0:T(8,128)S(1)}) custom-call(bf16[2,1,2,128,128]{4,3,2,1,0:T(8,128)(2,1)S(1)} %get-tuple-element.45.refs_0_, bf16[2,1,2,128,128]{4,3,2,1,0:T(8,128)(2,1)S(1)} %collective-permute-done.2.refs_1_, ...), custom_call_target="tpu_custom_call" | custom-call | flops 1 | bytes 1 | tf_op jit(solution)/shard_map/project/pallas_call | solution.py:510
  49.0 0.5 collective-permute-start.7
  49.5 0.8 %collective-permute-done.7.refs_1_ = bf16[1,64,640]{2,1,0:T(8,128)(2,1)S(1)} collective-permute-done((bf16[1,64,640]{2,1,0:T(8,128)(2,1)S(1)}, bf16[1,64,640]{2,1,0:T(8,128)(2,1)S(1)}, u32[]{:S(2)}, u32[]{:S(2)}) %collective-permute-start.7) | collective-permute-done | bytes 81952 | tf_op jit(solution)/shard_map/ppermute | solution.py:553
  50.4 0.4 collective-permute-done.8.refs_2_
  50.8 1.6 %collective-permute-done.10.refs_3_ = bf16[1,64,1024]{2,1,0:T(8,128)(2,1)S(1)} collective-permute-done((bf16[1,64,1024]{2,1,0:T(8,128)(2,1)S(1)}, bf16[1,64,1024]{2,1,0:T(8,128)(2,1)S(1)}, u32[]{:S(2)}, u32[]{:S(2)}) %collective-permute-start.10) | collective-permute-done | bytes 131104 | tf_op jit(solution)/shard_map/ppermute | solution.py:550
  52.3 2.0 %collective-permute-done.12.refs_4_ = bf16[1,64,1024]{2,1,0:T(8,128)(2,1)S(1)} collective-permute-done((bf16[1,64,1024]{2,1,0:T(8,128)(2,1)S(1)}, bf16[1,64,1024]{2,1,0:T(8,128)(2,1)S(1)}, u32[]{:S(2)}, u32[]{:S(2)}) %collective-permute-start.12) | collective-permute-done | bytes 131104 | tf_op jit(solution)/shard_map/ppermute | solution.py:550
  54.3 0.8 %sum.5 = bf16[1,64,2048]{2,1,0:T(8,128)(2,1)} custom-call(f32[1,64,2048]{2,1,0:T(8,128)S(1)} %get-tuple-element.50.keep_ref, bf16[1,64,768]{2,1,0:T(8,128)(2,1)S(1)} %collective-permute-done.6.refs_0_, bf16[1,64,640]{2,1,0:T(8,128)(2,1)S(1)} %collective-permute-done.7.refs_1_, bf16[1,64,640]{2,1,0:T(8,128)(2,1)S(1)} %collective-permute-done.8.refs_2_, ...), custom_call_target="tpu_custom_call" | custom-call | flops 1 | bytes 1 | tf_op jit(solution)/shard_map/sum/pallas_call | solution.py:524
  (14 shorter events, 0.3 us)
Async XLA Ops:
  2.3 6.5 %copy-start.1 = (bf16[64,32,128]{2,1,0:T(8,128)(2,1)S(1)}, bf16[64,32,128]{2,1,0:T(8,128)(2,1)}, u32[]{:S(2)}) copy-start(bf16[64,32,128]{2,1,0:T(8,128)(2,1)} %gate_ref.1) | copy-start | bytes 1572868
  2.3 6.5 %copy-start.2 = (bf16[128]{0:T(256)(128)(2,1)S(1)}, bf16[128]{0:T(256)(128)(2,1)}, u32[]{:S(2)}) copy-start(bf16[128]{0:T(256)(128)(2,1)} %param.12) | copy-start | bytes 772
  2.3 21.9 %all-to-all-start = ((bf16[16,272,128]{2,1,0:T(8,128)(2,1)}), bf16[16,272,128]{2,1,0:T(8,128)(2,1)S(1)}, u32[]{:S(2)}, u32[]{:S(2)}) async-start(bf16[16,272,128]{2,1,0:T(8,128)(2,1)} %pack.1), calls=%async_computation | async-start | bytes 2228224 | tf_op jit(solution)/shard_map/all_to_all | solution.py:408
  9.4 1.6 %collective-permute-start = (bf16[2,8,64,128]{3,2,1,0:T(8,128)(2,1)S(1)}, bf16[2,8,64,128]{3,2,1,0:T(8,128)(2,1)S(1)}, u32[]{:S(2)}, u32[]{:S(2)}) collective-permute-start(bf16[2,8,64,128]{3,2,1,0:T(8,128)(2,1)S(1)} %get-tuple-element.33), channel_id=1, source_target_pairs={{0,1},{1,0},{2,3},{3,2},{4,5},{5,4},{6,7},{7,6},{8,9},{9,8},{10,11... | collective-permute-start | bytes 786440 | tf_op jit(solution)/shard_map/ppermute | solution.py:424
  27.7 6.7 %collective-permute-start.1 = (bf16[2,128,128]{2,1,0:T(8,128)(2,1)S(1)}, bf16[2,128,128]{2,1,0:T(8,128)(2,1)S(1)}, u32[]{:S(2)}, u32[]{:S(2)}) collective-permute-start(bf16[2,128,128]{2,1,0:T(8,128)(2,1)S(1)} %get-tuple-element.34), channel_id=1, source_target_pairs={{0,16},{16,0},{1,17},{17,1},{2,18},{18,2},{3,19},{19,3},{4,20},{20... | collective-permute-start | bytes 196616 | tf_op jit(solution)/shard_map/ppermute | solution.py:460
  31.5 12.5 %collective-permute-start.5 = (bf16[2,8,64,128]{3,2,1,0:T(8,128)(2,1)S(1)}, bf16[2,8,64,128]{3,2,1,0:T(8,128)(2,1)S(1)}, u32[]{:S(2)}, u32[]{:S(2)}) collective-permute-start(bf16[2,8,64,128]{3,2,1,0:T(8,128)(2,1)S(1)} %get-tuple-element.49), channel_id=1, source_target_pairs={{0,2},{1,3},{2,0},{3,1},{4,6},{5,7},{6,4},{7,5},{8,10},{9,11},{10,... | collective-permute-start | bytes 786440 | tf_op jit(solution)/shard_map/ppermute | solution.py:479
  34.4 9.5 %copy-start = (bf16[1024,2048]{1,0:T(8,128)(2,1)S(1)}, bf16[1024,2048]{1,0:T(8,128)(2,1)}, u32[]{:S(2)}) copy-start(bf16[1024,2048]{1,0:T(8,128)(2,1)} %weight_ref.1) | copy-start | bytes 12582916
  34.9 7.4 %collective-permute-start.2 = (bf16[2,1,2,128,128]{4,3,2,1,0:T(8,128)(2,1)S(1)}, bf16[2,1,2,128,128]{4,3,2,1,0:T(8,128)(2,1)S(1)}, u32[]{:S(2)}, u32[]{:S(2)}) collective-permute-start(bf16[2,1,2,128,128]{4,3,2,1,0:T(8,128)(2,1)S(1)} %get-tuple-element.46), channel_id=1, source_target_pairs={{0,12},{4,8},{8,4},{12,0},{1,13},{5,9},{9,5},{13,1},{2,14},{6,10},... | collective-permute-start | bytes 393224 | tf_op jit(solution)/shard_map/ppermute | solution.py:501
  36.1 7.7 %collective-permute-start.3 = (bf16[2,1,2,128,128]{4,3,2,1,0:T(8,128)(2,1)S(1)}, bf16[2,1,2,128,128]{4,3,2,1,0:T(8,128)(2,1)S(1)}, u32[]{:S(2)}, u32[]{:S(2)}) collective-permute-start(bf16[2,1,2,128,128]{4,3,2,1,0:T(8,128)(2,1)S(1)} %get-tuple-element.47), channel_id=1, source_target_pairs={{0,8},{4,12},{8,0},{12,4},{1,9},{5,13},{9,1},{13,5},{2,10},{6,14},... | collective-permute-start | bytes 393224 | tf_op jit(solution)/shard_map/ppermute | solution.py:501
  37.7 6.2 %collective-permute-start.4 = (bf16[2,1,2,128,128]{4,3,2,1,0:T(8,128)(2,1)S(1)}, bf16[2,1,2,128,128]{4,3,2,1,0:T(8,128)(2,1)S(1)}, u32[]{:S(2)}, u32[]{:S(2)}) collective-permute-start(bf16[2,1,2,128,128]{4,3,2,1,0:T(8,128)(2,1)S(1)} %get-tuple-element.48), channel_id=1, source_target_pairs={{0,4},{4,0},{8,12},{12,8},{1,5},{5,1},{9,13},{13,9},{2,6},{6,2},{1... | collective-permute-start | bytes 393224 | tf_op jit(solution)/shard_map/ppermute | solution.py:501
  44.5 1.4 %collective-permute-start.9 = (bf16[1,64,1024]{2,1,0:T(8,128)(2,1)S(1)}, bf16[1,64,1024]{2,1,0:T(8,128)(2,1)S(1)}, u32[]{:S(2)}, u32[]{:S(2)}) collective-permute-start(bf16[1,64,1024]{2,1,0:T(8,128)(2,1)S(1)} %get-tuple-element.55), channel_id=1, source_target_pairs={{0,1},{1,0},{2,3},{3,2},{4,5},{5,4},{6,7},{7,6},{8,9},{9,8},{10,11... | collective-permute-start | bytes 393224 | tf_op jit(solution)/shard_map/ppermute | solution.py:549
  45.0 1.5 %collective-permute-start.11 = (bf16[1,64,1024]{2,1,0:T(8,128)(2,1)S(1)}, bf16[1,64,1024]{2,1,0:T(8,128)(2,1)S(1)}, u32[]{:S(2)}, u32[]{:S(2)}) collective-permute-start(bf16[1,64,1024]{2,1,0:T(8,128)(2,1)S(1)} %get-tuple-element.58), channel_id=1, source_target_pairs={{0,1},{1,0},{2,3},{3,2},{4,5},{5,4},{6,7},{7,6},{8,9},{9,8},{10,11... | collective-permute-start | bytes 393224 | tf_op jit(solution)/shard_map/ppermute | solution.py:549
  45.9 6.4 %collective-permute-start.10 = (bf16[1,64,1024]{2,1,0:T(8,128)(2,1)S(1)}, bf16[1,64,1024]{2,1,0:T(8,128)(2,1)S(1)}, u32[]{:S(2)}, u32[]{:S(2)}) collective-permute-start(bf16[1,64,1024]{2,1,0:T(8,128)(2,1)S(1)} %sum.3), channel_id=1, source_target_pairs={{0,2},{1,3},{2,0},{3,1},{4,6},{5,7},{6,4},{7,5},{8,10},{9,11},{10,... | collective-permute-start | bytes 393224 | tf_op jit(solution)/shard_map/ppermute | solution.py:550
  46.6 7.8 %collective-permute-start.12 = (bf16[1,64,1024]{2,1,0:T(8,128)(2,1)S(1)}, bf16[1,64,1024]{2,1,0:T(8,128)(2,1)S(1)}, u32[]{:S(2)}, u32[]{:S(2)}) collective-permute-start(bf16[1,64,1024]{2,1,0:T(8,128)(2,1)S(1)} %sum.4), channel_id=1, source_target_pairs={{0,2},{1,3},{2,0},{3,1},{4,6},{5,7},{6,4},{7,5},{8,10},{9,11},{10,... | collective-permute-start | bytes 393224 | tf_op jit(solution)/shard_map/ppermute | solution.py:550
  48.9 1.9 %collective-permute-start.6 = (bf16[1,64,768]{2,1,0:T(8,128)(2,1)S(1)}, bf16[1,64,768]{2,1,0:T(8,128)(2,1)S(1)}, u32[]{:S(2)}, u32[]{:S(2)}) collective-permute-start(bf16[1,64,768]{2,1,0:T(8,128)(2,1)S(1)} %get-tuple-element.51), channel_id=1, source_target_pairs={{0,1},{1,0},{2,3},{3,2},{4,5},{5,4},{6,7},{7,6},{8,9},{9,8},{10,11... | collective-permute-start | bytes 294920 | tf_op jit(solution)/shard_map/ppermute | solution.py:553
  49.0 1.4 %collective-permute-start.7 = (bf16[1,64,640]{2,1,0:T(8,128)(2,1)S(1)}, bf16[1,64,640]{2,1,0:T(8,128)(2,1)S(1)}, u32[]{:S(2)}, u32[]{:S(2)}) collective-permute-start(bf16[1,64,640]{2,1,0:T(8,128)(2,1)S(1)} %get-tuple-element.52), channel_id=1, source_target_pairs={{0,1},{1,0},{2,3},{3,2},{4,5},{5,4},{6,7},{7,6},{8,9},{9,8},{10,11... | collective-permute-start | bytes 245768 | tf_op jit(solution)/shard_map/ppermute | solution.py:553
  49.5 1.3 %collective-permute-start.8 = (bf16[1,64,640]{2,1,0:T(8,128)(2,1)S(1)}, bf16[1,64,640]{2,1,0:T(8,128)(2,1)S(1)}, u32[]{:S(2)}, u32[]{:S(2)}) collective-permute-start(bf16[1,64,640]{2,1,0:T(8,128)(2,1)S(1)} %get-tuple-element.53), channel_id=1, source_target_pairs={{0,1},{1,0},{2,3},{3,2},{4,5},{5,4},{6,7},{7,6},{8,9},{9,8},{10,11... | collective-permute-start | bytes 245768 | tf_op jit(solution)/shard_map/ppermute | solution.py:553

commit v16 on v15

--- a/solution.py
+++ b/solution.py
@@ -40,7 +40,7 @@
 
 def partner_order(sub, n_head):
     heads = split_axis("head", n_head)
-    return heads[-1:] + heads[:-1] + split_axis("sub", sub)
+    return heads[-1:] + split_axis("sub", sub) + heads[:-1]
 
 
 def partner(source, sub, n_head):

time: 55.3 us -> 54.8 us (level)
    all_to_all x1, waiting for transfers between devices: 13.2 us -> 15.4 us  [per_device(): lax.all_to_all(packed, partner_order(sub, n_head), split_axis=0, concat_a...]
    ppermute x3, waiting for transfers between devices: 5.46 us -> 3.95 us  [per_device(): lax.ppermute(part, along_sub, [(here, here ^ distance) for here in range(...]
    ppermute x1, waiting for transfers between devices: 1.77 us -> 1.02 us  [per_device(): incoming = lax.ppermute(state, 'outer', onward)]
  transfers between devices with their start and end apart: 14 -> 14, of which waited for: 12 -> 11; matrix products, arithmetic and copies ran while one was open for 0% -> 0% of each run, Pallas kernels for 6% -> 6%
where the time goes in v16:
time: 54.8 us; the launch traced here: 54.6 us
  waiting for transfers between devices  26.7 us (49%)
  starting transfers between devices  17.2 us (31%)
  Pallas kernels  10.6 us (19%)
    all_to_all x1, waiting for transfers between devices, per_device(): lax.all_to_all(packed, partner_order(sub, n_head), split_axis=0, concat_a...  15.4 us
    all_to_all x1, starting transfers between devices, per_device(): lax.all_to_all(packed, partner_order(sub, n_head), split_axis=0, concat_a...  6.43 us
    ppermute x3, waiting for transfers between devices, per_device(): lax.ppermute(part, along_sub, [(here, here ^ distance) for here in range(...  3.95 us
    ppermute x2, waiting for transfers between devices, per_device(): passed_on.append(lax.ppermute(summed, along_head, across))  3.58 us
    ppermute x3, starting transfers between devices, per_device(): lax.ppermute(part, along_sub, [(here, here ^ distance) for here in range(...  3.55 us
    pallas_call x1, Pallas kernels, per_device(): pl.pallas_call(functools.partial(factor_kernel, tokens, ratio, sub, half...  3.49 us
    ppermute x1, starting transfers between devices, per_device(): incoming = lax.ppermute(state, 'outer', onward)  2.65 us
    pallas_call x1, Pallas kernels, per_device(): pl.pallas_call(functools.partial(pack_kernel, sub), out_shape=shape((sour...  2.3 us
  transfers between devices with their start and end apart: 14, of which 11 were waited for; matrix products, arithmetic and copies ran while one was open for 0% of the time, Pallas kernels for 6%

profile of v16, /device:TPU:0, one launch (start us, length us, event | category | flops | bytes accessed | tf_op | source)
XLA Modules:
  0.0 54.6 jit_solution(9038011397262511943)
XLA Ops:
  0.0 2.3 %pack.1 = bf16[16,272,128]{2,1,0:T(8,128)(2,1)} custom-call(bf16[64,16,128]{2,1,0:T(8,128)(2,1)} %q_hbm.1, bf16[64,16,128]{2,1,0:T(8,128)(2,1)} %k_hbm.1, bf16[64,32,128]{2,1,0:T(8,128)(2,1)} %v_hbm.1, bf16[32,64]{1,0:T(8,128)(2,1)} %bitcast.4), custom_call_target="tpu_custom_call" | custom-call | tf_op jit(solution)/shard_map/pack/pallas_call | solution.py:392
  2.3 6.4 %all-to-all-start = ((bf16[16,272,128]{2,1,0:T(8,128)(2,1)}), bf16[16,272,128]{2,1,0:T(8,128)(2,1)S(1)}, u32[]{:S(2)}, u32[]{:S(2)}) async-start(bf16[16,272,128]{2,1,0:T(8,128)(2,1)} %pack.1), calls=%async_computation | async-start | bytes 2228224 | tf_op jit(solution)/shard_map/all_to_all | solution.py:408
  8.8 0.6 %gates.1 = (bf16[2,8,64,128]{3,2,1,0:T(8,128)(2,1)S(1)}, bf16[2,8,64,128]{3,2,1,0:T(8,128)(2,1)S(1)}) custom-call(bf16[64,32,128]{2,1,0:T(8,128)(2,1)S(1)} %copy-done.1, bf16[1,128]{1,0:T(2,128)(2,1)S(1)} %bitcast.3), custom_call_target="tpu_custom_call" | custom-call | flops 1 | bytes 1 | tf_op jit(solution)/shard_map/gates/pallas_call | solution.py:415
  9.4 0.5 collective-permute-start
  9.9 1.2 %collective-permute-done.swapped_ref.refs_5_.refs_7_ = bf16[2,8,64,128]{3,2,1,0:T(8,128)(2,1)S(1)} collective-permute-done((bf16[2,8,64,128]{3,2,1,0:T(8,128)(2,1)S(1)}, bf16[2,8,64,128]{3,2,1,0:T(8,128)(2,1)S(1)}, u32[]{:S(2)}, u32[]{:S(2)}) %collective-permute-start) | collective-permute-done | bytes 262176 | tf_op jit(solution)/shard_map/ppermute | solution.py:424
  11.1 15.4 %all-to-all-done.got_ref = bf16[16,272,128]{2,1,0:T(8,128)(2,1)S(1)} async-done(((bf16[16,272,128]{2,1,0:T(8,128)(2,1)}), bf16[16,272,128]{2,1,0:T(8,128)(2,1)S(1)}, u32[]{:S(2)}, u32[]{:S(2)}) %all-to-all-start) | async-done | bytes 1114144 | tf_op jit(solution)/shard_map/all_to_all | solution.py:408
  26.5 3.5 %factors.1 = (bf16[2,128,128]{2,1,0:T(8,128)(2,1)S(1)}, bf16[8,2,128,128]{3,2,1,0:T(8,128)(2,1)S(1)}, f32[8,2,128,128]{3,2,1,0:T(8,128)S(1)}, bf16[8,2,128,128]{...) custom-call(bf16[16,272,128]{2,1,0:T(8,128)(2,1)S(1)} %all-to-all-do, ...), custom_call_target="tpu_custom_call" | custom-call | flops 1 | bytes 1 | tf_op jit(solution)/shard_map/factors/pallas_call | solution.py:450
  30.0 2.7 %collective-permute-start.1 = (bf16[2,128,128]{2,1,0:T(8,128)(2,1)S(1)}, bf16[2,128,128]{2,1,0:T(8,128)(2,1)S(1)}, u32[]{:S(2)}, u32[]{:S(2)}) collective-permute-start(bf16[2,128,128]{2,1,0:T(8,128)(2,1)S(1)} %get-tuple-element.34), channel_id=1, source_target_pairs={{0,16},{16,0},{1,17},{17,1},{2,18},{18,2},{3,19},{19,3},{4,20},{20... | collective-permute-start | bytes 196616 | tf_op jit(solution)/shard_map/ppermute | solution.py:460
  32.6 1.1 %spread.1 = (f32[2,8,128,128]{3,2,1,0:T(8,128)S(1)}, bf16[2,8,128,128]{3,2,1,0:T(8,128)(2,1)S(1)}, bf16[2,8,64,128]{3,2,1,0:T(8,128)(2,1)S(1)}) custom-call(bf16[16,272,128]{2,1,0:T(8,128)(2,1)S(1)} %all-to-all-done.got_ref, bf16[8,2,128,128]{3,2,1,0:T(8,128)(2,1)S(1)} %get-tuple-element.35.w_ref, ...), custom_call_target="tpu_custom_call", output_to_operand_aliasing={{2}: (9, {})} | custom-call | flops 1 | bytes 1 | tf_op jit(solution)/shard_map/spread/pallas_call | solution.py:463
  33.7 0.6 %collective-permute-start.5 = (bf16[2,8,64,128]{3,2,1,0:T(8,128)(2,1)S(1)}, bf16[2,8,64,128]{3,2,1,0:T(8,128)(2,1)S(1)}, u32[]{:S(2)}, u32[]{:S(2)}) collective-permute-start(bf16[2,8,64,128]{3,2,1,0:T(8,128)(2,1)S(1)} %get-tuple-element.49), channel_id=1, source_target_pairs={{0,2},{1,3},{2,0},{3,1},{4,6},{5,7},{6,4},{7,5},{8,10},{9,11},{10,... | collective-permute-start | bytes 786440 | tf_op jit(solution)/shard_map/ppermute | solution.py:479
  34.3 1.0 %collective-permute-done.1.state_ref = bf16[2,128,128]{2,1,0:T(8,128)(2,1)S(1)} collective-permute-done((bf16[2,128,128]{2,1,0:T(8,128)(2,1)S(1)}, bf16[2,128,128]{2,1,0:T(8,128)(2,1)S(1)}, u32[]{:S(2)}, u32[]{:S(2)}) %collective-permute-start.1) | collective-permute-done | bytes 65568 | tf_op jit(solution)/shard_map/ppermute | solution.py:460
  35.4 0.5 join.1
  35.9 0.8 %collective-permute-start.2 = (bf16[2,1,2,128,128]{4,3,2,1,0:T(8,128)(2,1)S(1)}, bf16[2,1,2,128,128]{4,3,2,1,0:T(8,128)(2,1)S(1)}, u32[]{:S(2)}, u32[]{:S(2)}) collective-permute-start(bf16[2,1,2,128,128]{4,3,2,1,0:T(8,128)(2,1)S(1)} %get-tuple-element.46), channel_id=1, source_target_pairs={{0,12},{4,8},{8,4},{12,0},{1,13},{5,9},{9,5},{13,1},{2,14},{6,10},... | collective-permute-start | bytes 393224 | tf_op jit(solution)/shard_map/ppermute | solution.py:501
  36.7 1.5 %collective-permute-start.3 = (bf16[2,1,2,128,128]{4,3,2,1,0:T(8,128)(2,1)S(1)}, bf16[2,1,2,128,128]{4,3,2,1,0:T(8,128)(2,1)S(1)}, u32[]{:S(2)}, u32[]{:S(2)}) collective-permute-start(bf16[2,1,2,128,128]{4,3,2,1,0:T(8,128)(2,1)S(1)} %get-tuple-element.47), channel_id=1, source_target_pairs={{0,8},{4,12},{8,0},{12,4},{1,9},{5,13},{9,1},{13,5},{2,10},{6,14},... | collective-permute-start | bytes 393224 | tf_op jit(solution)/shard_map/ppermute | solution.py:501
  38.2 1.2 %collective-permute-start.4 = (bf16[2,1,2,128,128]{4,3,2,1,0:T(8,128)(2,1)S(1)}, bf16[2,1,2,128,128]{4,3,2,1,0:T(8,128)(2,1)S(1)}, u32[]{:S(2)}, u32[]{:S(2)}) collective-permute-start(bf16[2,1,2,128,128]{4,3,2,1,0:T(8,128)(2,1)S(1)} %get-tuple-element.48), channel_id=1, source_target_pairs={{0,4},{4,0},{8,12},{12,8},{1,5},{5,1},{9,13},{13,9},{2,6},{6,2},{1... | collective-permute-start | bytes 393224 | tf_op jit(solution)/shard_map/ppermute | solution.py:501
  39.4 2.6 %collective-permute-done.2.refs_1_ = bf16[2,1,2,128,128]{4,3,2,1,0:T(8,128)(2,1)S(1)} collective-permute-done((bf16[2,1,2,128,128]{4,3,2,1,0:T(8,128)(2,1)S(1)}, bf16[2,1,2,128,128]{4,3,2,1,0:T(8,128)(2,1)S(1)}, u32[]{:S(2)}, u32[]{:S(2)}) %collective-permute-start.2) | collective-permute-done | bytes 131104 | tf_op jit(solution)/shard_map/ppermute | solution.py:501
  42.0 0.6 %collective-permute-done.3.refs_2_ = bf16[2,1,2,128,128]{4,3,2,1,0:T(8,128)(2,1)S(1)} collective-permute-done((bf16[2,1,2,128,128]{4,3,2,1,0:T(8,128)(2,1)S(1)}, bf16[2,1,2,128,128]{4,3,2,1,0:T(8,128)(2,1)S(1)}, u32[]{:S(2)}, u32[]{:S(2)}) %collective-permute-start.3) | collective-permute-done | bytes 131104 | tf_op jit(solution)/shard_map/ppermute | solution.py:501
  42.6 0.8 %collective-permute-done.4.refs_3_ = bf16[2,1,2,128,128]{4,3,2,1,0:T(8,128)(2,1)S(1)} collective-permute-done((bf16[2,1,2,128,128]{4,3,2,1,0:T(8,128)(2,1)S(1)}, bf16[2,1,2,128,128]{4,3,2,1,0:T(8,128)(2,1)S(1)}, u32[]{:S(2)}, u32[]{:S(2)}) %collective-permute-start.4) | collective-permute-done | bytes 131104 | tf_op jit(solution)/shard_map/ppermute | solution.py:501
  43.4 0.5 project.3
  44.0 0.4 project_more.1
  44.5 0.6 %collective-permute-start.11 = (bf16[1,64,1024]{2,1,0:T(8,128)(2,1)S(1)}, bf16[1,64,1024]{2,1,0:T(8,128)(2,1)S(1)}, u32[]{:S(2)}, u32[]{:S(2)}) collective-permute-start(bf16[1,64,1024]{2,1,0:T(8,128)(2,1)S(1)} %get-tuple-element.58), channel_id=1, source_target_pairs={{0,1},{1,0},{2,3},{3,2},{4,5},{5,4},{6,7},{7,6},{8,9},{9,8},{10,11... | collective-permute-start | bytes 393224 | tf_op jit(solution)/shard_map/ppermute | solution.py:549
  45.0 0.3 collective-permute-done.9.refs_0_
  45.4 1.3 %collective-permute-start.10 = (bf16[1,64,1024]{2,1,0:T(8,128)(2,1)S(1)}, bf16[1,64,1024]{2,1,0:T(8,128)(2,1)S(1)}, u32[]{:S(2)}, u32[]{:S(2)}) collective-permute-start(bf16[1,64,1024]{2,1,0:T(8,128)(2,1)S(1)} %sum.3), channel_id=1, source_target_pairs={{0,2},{1,3},{2,0},{3,1},{4,6},{5,7},{6,4},{7,5},{8,10},{9,11},{10,... | collective-permute-start | bytes 393224 | tf_op jit(solution)/shard_map/ppermute | solution.py:550
  46.7 0.9 %collective-permute-start.12 = (bf16[1,64,1024]{2,1,0:T(8,128)(2,1)S(1)}, bf16[1,64,1024]{2,1,0:T(8,128)(2,1)S(1)}, u32[]{:S(2)}, u32[]{:S(2)}) collective-permute-start(bf16[1,64,1024]{2,1,0:T(8,128)(2,1)S(1)} %sum.4), channel_id=1, source_target_pairs={{0,2},{1,3},{2,0},{3,1},{4,6},{5,7},{6,4},{7,5},{8,10},{9,11},{10,... | collective-permute-start | bytes 393224 | tf_op jit(solution)/shard_map/ppermute | solution.py:550
  47.6 0.8 %project.2 = (bf16[1,64,768]{2,1,0:T(8,128)(2,1)S(1)}, bf16[1,64,640]{2,1,0:T(8,128)(2,1)S(1)}, bf16[1,64,640]{2,1,0:T(8,128)(2,1)S(1)}, f32[1,64,2048]{2,1,0:T(8,128)S(1)}) custom-call(bf16[2,1,2,128,128]{4,3,2,1,0:T(8,128)(2,1)S(1)} %get-tuple-element.45.refs_0_, bf16[2,1,2,128,128]{4,3,2,1,0:T(8,128)(2,1)S(1)} %collective-permute-done.2.refs_1_, ...), custom_call_target="tpu_custom_call" | custom-call | flops 1 | bytes 1 | tf_op jit(solution)/shard_map/project/pallas_call | solution.py:510
  48.4 0.5 collective-permute-start.7
  48.9 0.1 collective-permute-start.8
  49.0 0.8 %collective-permute-done.7.refs_1_ = bf16[1,64,640]{2,1,0:T(8,128)(2,1)S(1)} collective-permute-done((bf16[1,64,640]{2,1,0:T(8,128)(2,1)S(1)}, bf16[1,64,640]{2,1,0:T(8,128)(2,1)S(1)}, u32[]{:S(2)}, u32[]{:S(2)}) %collective-permute-start.7) | collective-permute-done | bytes 81952 | tf_op jit(solution)/shard_map/ppermute | solution.py:553
  49.8 0.4 collective-permute-done.8.refs_2_
  50.2 1.6 %collective-permute-done.10.refs_3_ = bf16[1,64,1024]{2,1,0:T(8,128)(2,1)S(1)} collective-permute-done((bf16[1,64,1024]{2,1,0:T(8,128)(2,1)S(1)}, bf16[1,64,1024]{2,1,0:T(8,128)(2,1)S(1)}, u32[]{:S(2)}, u32[]{:S(2)}) %collective-permute-start.10) | collective-permute-done | bytes 131104 | tf_op jit(solution)/shard_map/ppermute | solution.py:550
  51.8 2.0 %collective-permute-done.12.refs_4_ = bf16[1,64,1024]{2,1,0:T(8,128)(2,1)S(1)} collective-permute-done((bf16[1,64,1024]{2,1,0:T(8,128)(2,1)S(1)}, bf16[1,64,1024]{2,1,0:T(8,128)(2,1)S(1)}, u32[]{:S(2)}, u32[]{:S(2)}) %collective-permute-start.12) | collective-permute-done | bytes 131104 | tf_op jit(solution)/shard_map/ppermute | solution.py:550
  53.8 0.8 %sum.5 = bf16[1,64,2048]{2,1,0:T(8,128)(2,1)} custom-call(f32[1,64,2048]{2,1,0:T(8,128)S(1)} %get-tuple-element.50.keep_ref, bf16[1,64,768]{2,1,0:T(8,128)(2,1)S(1)} %collective-permute-done.6.refs_0_, bf16[1,64,640]{2,1,0:T(8,128)(2,1)S(1)} %collective-permute-done.7.refs_1_, bf16[1,64,640]{2,1,0:T(8,128)(2,1)S(1)} %collective-permute-done.8.refs_2_, ...), custom_call_target="tpu_custom_call" | custom-call | flops 1 | bytes 1 | tf_op jit(solution)/shard_map/sum/pallas_call | solution.py:524
  (14 shorter events, 0.2 us)
Async XLA Ops:
  2.3 6.5 %copy-start.1 = (bf16[64,32,128]{2,1,0:T(8,128)(2,1)S(1)}, bf16[64,32,128]{2,1,0:T(8,128)(2,1)}, u32[]{:S(2)}) copy-start(bf16[64,32,128]{2,1,0:T(8,128)(2,1)} %gate_ref.1) | copy-start | bytes 1572868
  2.3 6.5 %copy-start.2 = (bf16[128]{0:T(256)(128)(2,1)S(1)}, bf16[128]{0:T(256)(128)(2,1)}, u32[]{:S(2)}) copy-start(bf16[128]{0:T(256)(128)(2,1)} %param.12) | copy-start | bytes 772
  2.3 24.2 %all-to-all-start = ((bf16[16,272,128]{2,1,0:T(8,128)(2,1)}), bf16[16,272,128]{2,1,0:T(8,128)(2,1)S(1)}, u32[]{:S(2)}, u32[]{:S(2)}) async-start(bf16[16,272,128]{2,1,0:T(8,128)(2,1)} %pack.1), calls=%async_computation | async-start | bytes 2228224 | tf_op jit(solution)/shard_map/all_to_all | solution.py:408
  9.4 1.6 %collective-permute-start = (bf16[2,8,64,128]{3,2,1,0:T(8,128)(2,1)S(1)}, bf16[2,8,64,128]{3,2,1,0:T(8,128)(2,1)S(1)}, u32[]{:S(2)}, u32[]{:S(2)}) collective-permute-start(bf16[2,8,64,128]{3,2,1,0:T(8,128)(2,1)S(1)} %get-tuple-element.33), channel_id=1, source_target_pairs={{0,1},{1,0},{2,3},{3,2},{4,5},{5,4},{6,7},{7,6},{8,9},{9,8},{10,11... | collective-permute-start | bytes 786440 | tf_op jit(solution)/shard_map/ppermute | solution.py:424
  30.0 5.4 %collective-permute-start.1 = (bf16[2,128,128]{2,1,0:T(8,128)(2,1)S(1)}, bf16[2,128,128]{2,1,0:T(8,128)(2,1)S(1)}, u32[]{:S(2)}, u32[]{:S(2)}) collective-permute-start(bf16[2,128,128]{2,1,0:T(8,128)(2,1)S(1)} %get-tuple-element.34), channel_id=1, source_target_pairs={{0,16},{16,0},{1,17},{17,1},{2,18},{18,2},{3,19},{19,3},{4,20},{20... | collective-permute-start | bytes 196616 | tf_op jit(solution)/shard_map/ppermute | solution.py:460
  33.7 9.7 %collective-permute-start.5 = (bf16[2,8,64,128]{3,2,1,0:T(8,128)(2,1)S(1)}, bf16[2,8,64,128]{3,2,1,0:T(8,128)(2,1)S(1)}, u32[]{:S(2)}, u32[]{:S(2)}) collective-permute-start(bf16[2,8,64,128]{3,2,1,0:T(8,128)(2,1)S(1)} %get-tuple-element.49), channel_id=1, source_target_pairs={{0,2},{1,3},{2,0},{3,1},{4,6},{5,7},{6,4},{7,5},{8,10},{9,11},{10,... | collective-permute-start | bytes 786440 | tf_op jit(solution)/shard_map/ppermute | solution.py:479
  35.4 8.0 %copy-start = (bf16[1024,2048]{1,0:T(8,128)(2,1)S(1)}, bf16[1024,2048]{1,0:T(8,128)(2,1)}, u32[]{:S(2)}) copy-start(bf16[1024,2048]{1,0:T(8,128)(2,1)} %weight_ref.1) | copy-start | bytes 12582916
  35.9 6.1 %collective-permute-start.2 = (bf16[2,1,2,128,128]{4,3,2,1,0:T(8,128)(2,1)S(1)}, bf16[2,1,2,128,128]{4,3,2,1,0:T(8,128)(2,1)S(1)}, u32[]{:S(2)}, u32[]{:S(2)}) collective-permute-start(bf16[2,1,2,128,128]{4,3,2,1,0:T(8,128)(2,1)S(1)} %get-tuple-element.46), channel_id=1, source_target_pairs={{0,12},{4,8},{8,4},{12,0},{1,13},{5,9},{9,5},{13,1},{2,14},{6,10},... | collective-permute-start | bytes 393224 | tf_op jit(solution)/shard_map/ppermute | solution.py:501
  36.7 5.9 %collective-permute-start.3 = (bf16[2,1,2,128,128]{4,3,2,1,0:T(8,128)(2,1)S(1)}, bf16[2,1,2,128,128]{4,3,2,1,0:T(8,128)(2,1)S(1)}, u32[]{:S(2)}, u32[]{:S(2)}) collective-permute-start(bf16[2,1,2,128,128]{4,3,2,1,0:T(8,128)(2,1)S(1)} %get-tuple-element.47), channel_id=1, source_target_pairs={{0,8},{4,12},{8,0},{12,4},{1,9},{5,13},{9,1},{13,5},{2,10},{6,14},... | collective-permute-start | bytes 393224 | tf_op jit(solution)/shard_map/ppermute | solution.py:501
  38.2 5.2 %collective-permute-start.4 = (bf16[2,1,2,128,128]{4,3,2,1,0:T(8,128)(2,1)S(1)}, bf16[2,1,2,128,128]{4,3,2,1,0:T(8,128)(2,1)S(1)}, u32[]{:S(2)}, u32[]{:S(2)}) collective-permute-start(bf16[2,1,2,128,128]{4,3,2,1,0:T(8,128)(2,1)S(1)} %get-tuple-element.48), channel_id=1, source_target_pairs={{0,4},{4,0},{8,12},{12,8},{1,5},{5,1},{9,13},{13,9},{2,6},{6,2},{1... | collective-permute-start | bytes 393224 | tf_op jit(solution)/shard_map/ppermute | solution.py:501
  43.9 1.4 %collective-permute-start.9 = (bf16[1,64,1024]{2,1,0:T(8,128)(2,1)S(1)}, bf16[1,64,1024]{2,1,0:T(8,128)(2,1)S(1)}, u32[]{:S(2)}, u32[]{:S(2)}) collective-permute-start(bf16[1,64,1024]{2,1,0:T(8,128)(2,1)S(1)} %get-tuple-element.55), channel_id=1, source_target_pairs={{0,1},{1,0},{2,3},{3,2},{4,5},{5,4},{6,7},{7,6},{8,9},{9,8},{10,11... | collective-permute-start | bytes 393224 | tf_op jit(solution)/shard_map/ppermute | solution.py:549
  44.5 2.2 %collective-permute-start.11 = (bf16[1,64,1024]{2,1,0:T(8,128)(2,1)S(1)}, bf16[1,64,1024]{2,1,0:T(8,128)(2,1)S(1)}, u32[]{:S(2)}, u32[]{:S(2)}) collective-permute-start(bf16[1,64,1024]{2,1,0:T(8,128)(2,1)S(1)} %get-tuple-element.58), channel_id=1, source_target_pairs={{0,1},{1,0},{2,3},{3,2},{4,5},{5,4},{6,7},{7,6},{8,9},{9,8},{10,11... | collective-permute-start | bytes 393224 | tf_op jit(solution)/shard_map/ppermute | solution.py:549
  45.4 6.4 %collective-permute-start.10 = (bf16[1,64,1024]{2,1,0:T(8,128)(2,1)S(1)}, bf16[1,64,1024]{2,1,0:T(8,128)(2,1)S(1)}, u32[]{:S(2)}, u32[]{:S(2)}) collective-permute-start(bf16[1,64,1024]{2,1,0:T(8,128)(2,1)S(1)} %sum.3), channel_id=1, source_target_pairs={{0,2},{1,3},{2,0},{3,1},{4,6},{5,7},{6,4},{7,5},{8,10},{9,11},{10,... | collective-permute-start | bytes 393224 | tf_op jit(solution)/shard_map/ppermute | solution.py:550
  46.7 7.1 %collective-permute-start.12 = (bf16[1,64,1024]{2,1,0:T(8,128)(2,1)S(1)}, bf16[1,64,1024]{2,1,0:T(8,128)(2,1)S(1)}, u32[]{:S(2)}, u32[]{:S(2)}) collective-permute-start(bf16[1,64,1024]{2,1,0:T(8,128)(2,1)S(1)} %sum.4), channel_id=1, source_target_pairs={{0,2},{1,3},{2,0},{3,1},{4,6},{5,7},{6,4},{7,5},{8,10},{9,11},{10,... | collective-permute-start | bytes 393224 | tf_op jit(solution)/shard_map/ppermute | solution.py:550
  48.3 1.9 %collective-permute-start.6 = (bf16[1,64,768]{2,1,0:T(8,128)(2,1)S(1)}, bf16[1,64,768]{2,1,0:T(8,128)(2,1)S(1)}, u32[]{:S(2)}, u32[]{:S(2)}) collective-permute-start(bf16[1,64,768]{2,1,0:T(8,128)(2,1)S(1)} %get-tuple-element.51), channel_id=1, source_target_pairs={{0,1},{1,0},{2,3},{3,2},{4,5},{5,4},{6,7},{7,6},{8,9},{9,8},{10,11... | collective-permute-start | bytes 294920 | tf_op jit(solution)/shard_map/ppermute | solution.py:553
  48.4 1.4 %collective-permute-start.7 = (bf16[1,64,640]{2,1,0:T(8,128)(2,1)S(1)}, bf16[1,64,640]{2,1,0:T(8,128)(2,1)S(1)}, u32[]{:S(2)}, u32[]{:S(2)}) collective-permute-start(bf16[1,64,640]{2,1,0:T(8,128)(2,1)S(1)} %get-tuple-element.52), channel_id=1, source_target_pairs={{0,1},{1,0},{2,3},{3,2},{4,5},{5,4},{6,7},{7,6},{8,9},{9,8},{10,11... | collective-permute-start | bytes 245768 | tf_op jit(solution)/shard_map/ppermute | solution.py:553
  48.9 1.3 %collective-permute-start.8 = (bf16[1,64,640]{2,1,0:T(8,128)(2,1)S(1)}, bf16[1,64,640]{2,1,0:T(8,128)(2,1)S(1)}, u32[]{:S(2)}, u32[]{:S(2)}) collective-permute-start(bf16[1,64,640]{2,1,0:T(8,128)(2,1)S(1)} %get-tuple-element.53), channel_id=1, source_target_pairs={{0,1},{1,0},{2,3},{3,2},{4,5},{5,4},{6,7},{7,6},{8,9},{9,8},{10,11... | collective-permute-start | bytes 245768 | tf_op jit(solution)/shard_map/ppermute | solution.py:553
